TPU v7x, 32 devices: a whole 2x2x4 slice. The times are simulated.
32 devices in a mesh: groups: 2 (over y), dp: 4 (over z), cuts: 2 (over x), grad: 2 (over core).
Axes of the slice: x: 2, y: 2, z: 4, core: 2. Of those that a mesh axis runs over, the one named last changes fastest.
Arguments:
- acts: bfloat16 [1, 6144, 1024], P(None, ('groups', 'dp', 'grad'), 'cuts'), parts along dimension 1, may hold values from -20 to 20
- outgrads: bfloat16 [1, 6144, 1024], P(None, ('groups', 'dp', 'grad'), 'cuts'), parts along dimension 1, may hold values from -20 to 20
- grads: float32 [2, 1024, 1024], P('groups', ('dp', 'grad'), 'cuts'), parts along dimension 0, may hold values from -6 to 6
Outputs:
- precond: float32 [2, 1024, 1024], P('groups', ('dp', 'grad'), 'cuts'), parts along dimension 0
There are 2 independent parts, one for each index of `groups`. A program takes and returns all parts, laid end to end along the dimension named above; each array names one. Nothing has to cross between parts.
All inputs are finite; a program needn't handle non-finite values. Where the computation divides by a largest or mean magnitude, that divisor is 1e-20 or more.
Results may differ from a plain program's by a relative error of at most 0.0003.
Values sent between devices are 32-bit elements; how exact they have to be, the bound alone decides.
No kernel may reach another device: no remote copies, remote signals or barrier semaphores. Data moves between devices by JAX's collectives and lax.ppermute only.
A program may use at most 64 MiB of HBM per device.

v0:
```python
import jax
import jax.numpy as jnp
from jax import lax
from jax.sharding import PartitionSpec as P

ITERS = 4


DAMPING = 0.5
START = 1.9
HIGH = lax.Precision.HIGHEST


def swapped(array, axis, distance):
    return lax.ppermute(array, axis, [(i, i ^ 1 << distance) for i in range(lax.axis_size(axis))])


def from_root(array, axis, root):
    mine = lax.axis_index(axis) == root
    return lax.psum(jnp.where(mine, array, jnp.zeros_like(array)), axis)


def start_rows(factor, count):
    order = factor.shape[0]
    bound = jnp.max(jnp.sum(jnp.abs(factor), axis=1)) + 1e-06
    rows = lax.broadcasted_iota(jnp.int32, (count, order), 0)
    cols = lax.broadcasted_iota(jnp.int32, (count, order), 1)
    return jnp.where(rows == cols, START / bound, 0.0)


def block_rows(local, position, spread):
    joined = local
    for bit in range(spread.bit_length() - 1):
        other = swapped(joined, ("dp", "grad"), bit)
        upper = position // (1 << bit) % 2
        joined = jnp.where(
            upper == 0, jnp.concatenate((joined, other), 1), jnp.concatenate((other, joined), 1)
        )
    return joined


def per_device(acts, outgrads, grads):
    layers = acts.shape[0]
    tok_rows = acts.shape[1]
    order = acts.shape[2]
    dev_count = lax.axis_size(("dp", "grad"))
    spread = dev_count // lax.axis_size("cuts")
    position = lax.axis_index(("dp", "grad"))
    count_blocks = 2 * layers
    pair_size = lax.axis_size("grad")
    partials = []
    partials.append(jnp.einsum("tb,td->bd", acts[0], acts[0], preferred_element_type=jnp.float32))
    partials.append(
        jnp.einsum("tb,td->bd", outgrads[0], outgrads[0], preferred_element_type=jnp.float32)
    )
    eye = jnp.eye(order, dtype=jnp.float32)
    scale = 1.0 / (tok_rows * dev_count)
    sums = lax.psum(jnp.stack(partials), ("dp", "grad"))
    mine = position // pair_size % count_blocks
    factor = lax.dynamic_index_in_dim(sums, mine, 0, keepdims=False) * scale + DAMPING * eye
    finished = start_rows(factor, order)
    for step in range(ITERS):
        product = jnp.dot(factor, finished, precision=HIGH)
        finished = 2.0 * finished - jnp.dot(finished, product, precision=HIGH)
    collected = jnp.stack(
        [
            from_root(finished, ("dp", "grad"), block * pair_size + pair_size - 1)
            for block in range(count_blocks)
        ]
    )
    left_all = collected[0::2]
    right_all = collected[1::2]
    rows_dev = grads.shape[1]
    offset = position % spread * rows_dev
    left_piece = lax.dynamic_slice_in_dim(left_all, offset, rows_dev, 1)
    left_rows = from_root(left_piece, "cuts", position // spread)
    mixed = jnp.einsum("lrk,lkc->lrc", grads, right_all, precision=HIGH)
    gathered = block_rows(mixed, position, spread)
    return jnp.einsum("lrk,lkc->lrc", left_rows, gathered, precision=HIGH)


def solution(mesh):
    in_specs = (
        P(None, ("groups", "dp", "grad"), "cuts"),
        P(None, ("groups", "dp", "grad"), "cuts"),
        P("groups", ("dp", "grad"), "cuts"),
    )
    out_specs = P("groups", ("dp", "grad"), "cuts")
    return jax.shard_map(
        per_device, mesh=mesh, in_specs=in_specs, out_specs=out_specs, check_vma=False
    )
```

profile of v0, /device:TPU:0, one launch (start us, length us, event | category | flops | bytes accessed | tf_op | source)
XLA Modules:
  0.0 202.0 jit_solution(5188906220188909777)
XLA Ops:
  6.5 0.0 copy-start
  6.5 0.0 all-reduce.5.cloned.1.call-start
  6.5 1.0 copy-done
  7.5 0.5 convolution_bitcast_fusion.1
  8.0 1.6 convolution_bitcast_fusion
  9.6 1.5 pad_maximum_fusion
  11.0 0.0 all-reduce.5.cloned.1.call-update
  11.1 0.0 all-reduce.9.cloned.1.call-start
  11.2 67.7 %all-reduce.5.cloned.1.call-done = f32[2,512,512]{2,1,0:T(8,128)} async-done(((f32[2,512,512]{2,1,0:T(8,128)}), f32[2,512,512]{2,1,0:T(8,128)}) %all-reduce.5.cloned.1.call-update) | async-done | bytes 2097168 | tf_op jit(solution)/shard_map/psum | solution.py:58
  78.8 1.4 abs_reduce_fusion
  80.3 0.6 reduce_max.9
  81.6 3.0 %fusion.2 = f32[512,512]{1,0:T(8,128)S(1)} fusion(f32[]{:T(128)S(6)} %div.26, f32[2,512,512]{2,1,0:T(8,128)} %all-reduce.5.cloned.1.call-done, s32[]{:T(128)S(6)} %select_n.100), kind=kOutput, calls=%fused_computation.3 | convolution fusion | flops 1612185600 | bytes 2097160 | tf_op jit(solution)/shard_map/dot_general | solution.py:63
  84.6 0.0 copy-start.1
  84.6 1.8 fusion.4
  86.4 0.0 copy-done.1
  86.5 1.9 fusion.26
  88.4 1.9 convolution_subtract_fusion.2
  90.2 1.9 fusion.25
  92.1 1.9 convolution_subtract_fusion.1
  94.0 1.9 fusion.24
  95.9 3.4 %broadcast_select_fusion = (f32[512,512]{1,0:T(8,128)}, f32[512,512]{1,0:T(8,128)}) fusion(pred[]{:T(512)S(6)} %eq.31, pred[]{:T(512)S(6)} %eq.27, f32[512,512]{1,0:T(8,128)S(1)} %convolution_subtract_fusion.1, f32[512,512]{1,0:T(8,128)S(1)} %fusion.24), kind=kOutput, calls=%fused_computation.27 | convolution fusion | flops 1611661312 | bytes 4194306 | tf_op jit(solution)/shard_map/dot_general | solution.py:64
  99.3 0.0 copy-start.2
  99.3 0.0 all-reduce.9.cloned.1.call-update
  99.3 0.0 all-reduce.7.cloned.1.call-start
  99.4 64.5 %all-reduce.9.cloned.1.call-done = (f32[512,512]{1,0:T(8,128)}, f32[512,512]{1,0:T(8,128)}) async-done(((f32[512,512]{1,0:T(8,128)}, f32[512,512]{1,0:T(8,128)}), (f32[512,512]{1,0:T(8,128)}, f32[512,512]{1,0:T(8,128)})) %all-reduce.9.cloned.1.call-update) | async-done | bytes 2097168 | tf_op jit(solution)/shard_map/psum | solution.py:20
  163.9 0.0 copy-done.2
  163.9 1.9 fusion.19
  165.8 0.1 collective-permute-start
  165.9 1.5 collective-permute-done
  167.5 1.3 collective-permute-start.1
  168.7 1.7 dynamic-slice_select_fusion
  170.4 0.0 all-reduce.7.cloned.1.call-update
  170.5 22.6 %all-reduce.7.cloned.1.call-done = f32[128,512]{1,0:T(8,128)} async-done(((f32[128,512]{1,0:T(8,128)}), f32[128,512]{1,0:T(8,128)}) %all-reduce.7.cloned.1.call-update) | async-done | bytes 262160 | tf_op jit(solution)/shard_map/psum | solution.py:20
  193.1 0.0 collective-permute-done.1
  193.1 2.4 %convolution_bitcast_fusion.2 = f32[1,128,512]{2,1,0:T(8,128)} fusion(f32[128,512]{1,0:T(8,128)} %all-reduce.7.cloned.1.call-done, f32[256,512]{1,0:T(8,128)S(1)} %bitcast.44, f32[256,512]{1,0:T(8,128)S(1)} %maximum_select_fusion.2, pred[]{:T(512)S(6)} %eq.29), kind=kOutput, calls=%fused_computation.12 | convolution fusion | flops 403439616 | bytes 1572865 | tf_op jit(solution)/shard_map/lrk,lkc->lrc/dot_general | solution.py:79
  (2 shorter events, 0.1 us)
Async XLA Ops:
  6.5 1.0 copy-start
  6.5 72.3 %all-reduce.5.cloned.1.call-start = ((), (), s32[]{:S(2)}) async-start(), calls=%async_computation | async-start | bytes 4194304 | tf_op jit(solution)/shard_map/psum | solution.py:58
  11.1 152.8 %all-reduce.9.cloned.1.call-start = ((), (), s32[]{:S(2)}) async-start(), calls=%async_computation.2 | async-start | bytes 4194304 | tf_op jit(solution)/shard_map/psum | solution.py:20
  84.6 1.8 copy-start.1
  99.3 64.6 %copy-start.2 = (f32[1,128,512]{2,1,0:T(8,128)S(1)}, f32[1,128,512]{2,1,0:T(8,128)}, u32[]{:S(2)}) copy-start(f32[1,128,512]{2,1,0:T(8,128)} %param.5) | copy-start | bytes 786436
  99.3 93.8 %all-reduce.7.cloned.1.call-start = ((), (), s32[]{:S(2)}) async-start(), calls=%async_computation.1 | async-start | bytes 524288 | tf_op jit(solution)/shard_map/psum | solution.py:20
  165.8 1.6 collective-permute-start
  167.5 25.6 %collective-permute-start.1 = (f32[1,256,512]{2,1,0:T(8,128)S(1)}, f32[1,256,512]{2,1,0:T(8,128)S(1)}, u32[]{:S(2)}, u32[]{:S(2)}) collective-permute-start(f32[1,256,512]{2,1,0:T(8,128)S(1)} %maximum_select_fusion.3), channel_id=1, source_target_pairs={{0,4},{1,5},{4,0},{5,1},{8,12},{9,13},{12,8},{13,9},{2,6},{3,7},{6... | collective-permute-start | bytes 1572872 | tf_op jit(solution)/shard_map/ppermute | solution.py:15
Sparse Core Ops, SparseCore 0:
  11.2 67.5 all-reduce.4
  99.5 64.3 all-reduce.8
  170.6 22.4 all-reduce.6
where the time goes:
time: 202 us
  waiting for transfers between devices  156 us (77%)
  matrix products  24 us (12%)
  between operations  14 us (7%)
  other arithmetic  5.29 us (3%)
    psum x2, waiting for transfers between devices, from_root(): return lax.psum(jnp.where(mine, array, jnp.zeros_like(array)), axis)  87.1 us
    psum x1, waiting for transfers between devices, per_device(): sums = lax.psum(jnp.stack(partials), ('dp', 'grad'))  67.7 us
    dot_general x4, matrix products, per_device(): finished = 2.0 * finished - jnp.dot(finished, product, precision=HIGH)  8.93 us
    dot_general x4, matrix products, per_device(): product = jnp.dot(factor, finished, precision=HIGH)  8.76 us
  transfers between devices with their start and end apart: 5, of which 4 were waited for; matrix products, arithmetic and copies ran while one was open for 1% of the time, Pallas kernels for 0%

commit v1 on v0

v1 whole, which is shorter than its diff:
```python
import functools
import jax
import jax.numpy as jnp
from jax import lax
from jax.experimental import pallas as pl
from jax.experimental.pallas import tpu as pltpu
from jax.sharding import PartitionSpec as P

ITERS = 4
DAMPING = 0.5
START = 1.9
LANE = 128
QUAD = 4
AXES = ("dp", "cuts", "grad")
PARAMS = pltpu.CompilerParams(vmem_limit_bytes=48 * 1024 * 1024)


def slots(order):
    count = order // LANE
    above = [(i, j) for i in range(count) for j in range(i + 1, count)]
    return above, count // 2


def packed_rows(order):
    above, pairs = slots(order)
    return (len(above) + pairs) * LANE + -(-pairs // 8) * 8


def places():
    rows = lax.broadcasted_iota(jnp.int32, (LANE, LANE), 0)
    cols = lax.broadcasted_iota(jnp.int32, (LANE, LANE), 1)
    return rows, cols


def pack(block, order, out_ref):
    above, pairs = slots(order)
    rows, cols = places()
    for slot, (i, j) in enumerate(above):
        out_ref[slot * LANE : (slot + 1) * LANE, :] = block(i, j)
    diagonals = []
    for pair in range(pairs):
        slot = len(above) + pair
        first, second = block(2 * pair, 2 * pair), block(2 * pair + 1, 2 * pair + 1)
        out_ref[slot * LANE : (slot + 1) * LANE, :] = jnp.where(rows <= cols, first, second)
        diagonals.append(jnp.sum(jnp.where(rows == cols, second, 0.0), axis=0, keepdims=True))
    top = (len(above) + pairs) * LANE
    spare = out_ref.shape[0] - top - pairs
    out_ref[top:, :] = jnp.concatenate(diagonals + [jnp.zeros((spare, LANE), jnp.float32)], 0)


def unpack(piece, order, out_ref, scale=1.0, shift=0.0):
    above, pairs = slots(order)
    rows, cols = places()

    def put(i, j, value):
        out_ref[i * LANE : (i + 1) * LANE, j * LANE : (j + 1) * LANE] = value

    for slot, (i, j) in enumerate(above):
        value = piece(slot * LANE, (slot + 1) * LANE) * scale
        put(i, j, value)
        put(j, i, value.T)
    top = (len(above) + pairs) * LANE
    diagonals = piece(top, top + -(-pairs // 8) * 8)
    damping = jnp.where(rows == cols, shift, 0.0)
    for pair in range(pairs):
        slot = len(above) + pair
        both = piece(slot * LANE, (slot + 1) * LANE)
        turned = both.T
        put(2 * pair, 2 * pair, jnp.where(rows <= cols, both, turned) * scale + damping)
        second = jnp.where(rows > cols, both, jnp.where(rows < cols, turned, diagonals[pair : pair + 1, :]))
        put(2 * pair + 1, 2 * pair + 1, second * scale + damping)


def halves(value):
    high = value.astype(jnp.bfloat16)
    return high, (value - high.astype(jnp.float32)).astype(jnp.bfloat16)


def times(left, right):
    dot = functools.partial(jnp.dot, preferred_element_type=jnp.float32)
    return dot(left[0], right[0]) + (dot(left[0], right[1]) + dot(left[1], right[0]))


def square(x_ref):
    x = x_ref[...]
    return lax.dot_general(x, x, (((0,), (0,)), ((), ())), preferred_element_type=jnp.float32)


def block_of(value):
    return lambda i, j: value[i * LANE : (i + 1) * LANE, j * LANE : (j + 1) * LANE]


def cov_send_kernel(acts_ref, outgrads_ref, out_ref):
    core = lax.axis_index("grad")

    @pl.when(core == 0)
    def _():
        pack(block_of(square(outgrads_ref)), outgrads_ref.shape[1], out_ref)

    @pl.when(core != 0)
    def _():
        pack(block_of(square(acts_ref)), acts_ref.shape[1], out_ref)


def cov_keep_kernel(acts_ref, outgrads_ref, other_ref, out_ref):
    core = lax.axis_index("grad")

    @pl.when(core == 0)
    def _():
        pack(block_of(square(acts_ref)), acts_ref.shape[1], out_ref)

    @pl.when(core != 0)
    def _():
        pack(block_of(square(outgrads_ref)), outgrads_ref.shape[1], out_ref)

    out_ref[...] += other_ref[...]


def inverse_kernel(scale, order, *refs):
    *sums, out_ref, factor_ref = refs

    def piece(start, stop):
        total = sums[0][start:stop, :]
        for ref in sums[1:]:
            total = total + ref[start:stop, :]
        return total

    unpack(piece, order, factor_ref, scale, DAMPING)
    factor = factor_ref[...]
    bound = jnp.max(jnp.sum(jnp.abs(factor), axis=0, keepdims=True), axis=1, keepdims=True) + 1e-06
    start = START / bound
    rows = lax.broadcasted_iota(jnp.int32, (order, order), 0)
    cols = lax.broadcasted_iota(jnp.int32, (order, order), 1)
    eye = jnp.where(rows == cols, 1.0, 0.0)
    power = eye - start * factor
    total = power
    power_halves = halves(power)
    power = times(power_halves, power_halves)
    for step in range(1, ITERS):
        power_halves = halves(power)
        total = total + power + times(halves(total), power_halves)
        if step < ITERS - 1:
            power = times(power_halves, power_halves)
    pack(block_of(start * (eye + total)), order, out_ref)


def final_kernel(order, spread, *refs):
    own_ref, other_ref, *rest = refs
    pieces = rest[:spread]
    out_ref, left_ref, right_ref, tile_ref = rest[spread:]
    core = lax.axis_index("grad")
    position = lax.axis_index("dp") * lax.axis_size("grad") + core
    mine = lax.rem(position, spread)
    rows_dev = out_ref.shape[0]

    @pl.when(core == 0)
    def _():
        unpack(lambda a, b: own_ref[a:b, :], order, left_ref)
        unpack(lambda a, b: other_ref[a:b, :], order, right_ref)

    @pl.when(core != 0)
    def _():
        unpack(lambda a, b: other_ref[a:b, :], order, left_ref)
        unpack(lambda a, b: own_ref[a:b, :], order, right_ref)

    for turn, ref in enumerate(pieces):
        tile_ref[pl.ds(pl.multiple_of((mine ^ turn) * rows_dev, rows_dev), rows_dev), :] = ref[...]
    left = left_ref[pl.ds(pl.multiple_of(mine * rows_dev, rows_dev), rows_dev), :]
    middle = times(halves(left), halves(tile_ref[...]))
    out_ref[...] = times(halves(middle), halves(right_ref[...]))


def call(kernel, shape, scratch, *args):
    return pl.pallas_call(
        kernel,
        out_shape=jax.ShapeDtypeStruct(shape, jnp.float32),
        scratch_shapes=scratch,
        compiler_params=PARAMS,
    )(*args)


class Plan:
    def __init__(self, dp, cuts):
        self.dp, self.cuts = dp, cuts
        self.rounds = max(QUAD - 1, 2 * cuts - 1)

    def index(self, z, x, core):
        return (z * self.cuts + x) * 2 + core

    def root(self, z, x, core):
        return z // QUAD * QUAD + 1 + (x + core) % 2

    def across(self, bit):
        return [
            (self.index(z, x, core), self.index(z ^ bit, x, core))
            for z in range(self.dp)
            for x in range(self.cuts)
            for core in range(2)
        ]

    def gather(self, turn):
        pairs = []
        for x in range(self.cuts):
            for core in range(2):
                for base in range(0, self.dp, QUAD):
                    root = self.root(base, x, core)
                    others = sorted((z for z in range(base, base + QUAD) if z != root), key=lambda z: -abs(z - root))
                    pairs.append((self.index(others[turn], x, core), self.index(root, x, core)))
        return pairs

    def spread(self, turn):
        pairs = []
        for x in range(self.cuts):
            for base in range(0, self.dp, QUAD):
                root = self.root(base, x, 1)
                others = sorted((z for z in range(base, base + QUAD) if z != root), key=lambda z: -abs(z - root))
                if turn < len(others):
                    pairs.append((self.index(root, x, 1), self.index(others[turn], x, 1)))
                if x // 2 != base // QUAD:
                    continue
                root = self.root(base, x, 0)
                targets = [(z, x + d) for d in range(self.cuts) for z in (root ^ 1, root)]
                targets = [(z, other % self.cuts) for z, other in targets if (z, other) != (root, x)]
                if turn < len(targets):
                    z, other = targets[turn]
                    pairs.append((self.index(root, x, 0), self.index(z, other, 0)))
        return pairs


def swap_cores(array):
    return lax.ppermute(array, "grad", [(0, 1), (1, 0)])


def per_device(acts, outgrads, grads):
    dp, cuts, cores = (lax.axis_size(name) for name in AXES)
    tok_rows, order = acts.shape[1:]
    dev_count = dp * cores
    spread = dev_count // cuts
    plan = Plan(dp, cuts)
    shape = (packed_rows(order), LANE)
    acts, outgrads, grads = acts[0], outgrads[0], grads[0]

    pieces = [grads, swap_cores(grads)]
    while len(pieces) < spread:
        moved = [lax.ppermute(piece, AXES, plan.across(len(pieces) // 2)) for piece in pieces]
        pieces += moved

    sent = call(cov_send_kernel, shape, [], acts, outgrads)
    chip = call(cov_keep_kernel, shape, [], acts, outgrads, swap_cores(sent))
    bit = QUAD
    while bit < dp:
        chip = chip + lax.ppermute(chip, AXES, plan.across(bit))
        bit *= 2
    sums = [chip] + [lax.ppermute(chip, AXES, plan.gather(turn)) for turn in range(QUAD - 1)]
    scale = 1.0 / (tok_rows * dev_count)
    inverse = call(
        functools.partial(inverse_kernel, scale, order), shape, [pltpu.VMEM((order, order), jnp.float32)], *sums
    )
    z, x, core = (lax.axis_index(name) for name in AXES)
    is_root = z % QUAD == 1 + (x + core) % 2
    needed = jnp.logical_or(core == 1, x // 2 == z // QUAD)
    mine = jnp.where(jnp.logical_and(is_root, needed), inverse, 0.0)
    for turn in range(plan.rounds):
        mine = mine + lax.ppermute(inverse, AXES, plan.spread(turn))
    other = swap_cores(mine)
    square_scratch = pltpu.VMEM((order, order), jnp.float32)
    out = call(
        functools.partial(final_kernel, order, spread), grads.shape, [square_scratch] * 3, mine, other, *pieces
    )
    return out[None]


def solution(mesh):
    in_specs = (
        P(None, ("groups", "dp", "grad"), "cuts"),
        P(None, ("groups", "dp", "grad"), "cuts"),
        P("groups", ("dp", "grad"), "cuts"),
    )
    out_specs = P("groups", ("dp", "grad"), "cuts")
    return jax.shard_map(
        per_device, mesh=mesh, in_specs=in_specs, out_specs=out_specs, check_vma=False
    )
```

time: 202 us -> 70.8 us (0.35)
  waiting for transfers between devices: 156 us -> 48.7 us
  matrix products: 24 us -> 0 us
  between operations: 14 us -> 0.17 us
  starting transfers between devices: 1.41 us -> 10.9 us
  Pallas kernels: 0 us -> 8.63 us
  other arithmetic: 5.29 us -> 0.14 us
    psum x3 -> x0, waiting for transfers between devices: 155 us -> none  [the longest x2 87.1 us: from_root(): return lax.psum(jnp.where(mine, array, jnp.zeros_like(array)), axis)]
    ppermute x2 -> x11, waiting for transfers between devices: 1.51 us -> 48.7 us  [the longest x3 23 us: per_device(): mine = mine + lax.ppermute(inverse, AXES, plan.spread(turn))]
    dot_general x12 -> x0, matrix products: 24 us -> none  [the longest x4 8.93 us: per_device(): finished = 2.0 * finished - jnp.dot(finished, product, precision=HIGH)]
    ppermute x2 -> x11, starting transfers between devices: 1.33 us -> 10.9 us  [the longest x3 6.88 us: per_device(): lax.ppermute(chip, AXES, plan.gather(turn))]
    pallas_call x0 -> x4, Pallas kernels: none -> 8.63 us  [call(): pl.pallas_call(kernel, out_shape=jax.ShapeDtypeStruct(shape, jnp.float32)...]
  transfers between devices with their start and end apart: 5 -> 11, of which waited for: 4 -> 6; matrix products, arithmetic and copies ran while one was open for 1% -> 0% of each run, Pallas kernels for 0% -> 0%
where the time goes in v1:
time: 70.8 us; the launch traced here: 70.5 us
  waiting for transfers between devices  48.7 us (69%)
  starting transfers between devices  10.9 us (15%)
  Pallas kernels  8.63 us (12%)
  local copies, waits for them, and re-layouts  2 us (3%)
    ppermute x3, waiting for transfers between devices, per_device(): mine = mine + lax.ppermute(inverse, AXES, plan.spread(turn))  23 us
    ppermute x2, waiting for transfers between devices, per_device(): lax.ppermute(piece, AXES, plan.across(len(pieces) // 2))  11.9 us
    ppermute x3, waiting for transfers between devices, per_device(): lax.ppermute(chip, AXES, plan.gather(turn))  10.5 us
    pallas_call x4, Pallas kernels, call(): pl.pallas_call(kernel, out_shape=jax.ShapeDtypeStruct(shape, jnp.float32)...  8.63 us
    ppermute x3, starting transfers between devices, per_device(): lax.ppermute(chip, AXES, plan.gather(turn))  6.88 us
    ppermute x3, waiting for transfers between devices, swap_cores(): return lax.ppermute(array, 'grad', [(0, 1), (1, 0)])  3.32 us
    ppermute x3, starting transfers between devices, per_device(): mine = mine + lax.ppermute(inverse, AXES, plan.spread(turn))  2.68 us
    unnamed x6, local copies, waits for them, and re-layouts  2 us
  transfers between devices with their start and end apart: 11, of which 6 were waited for; matrix products, arithmetic and copies ran while one was open for 0% of the time, Pallas kernels for 0%

profile of v1, /device:TPU:0, one launch (start us, length us, event | category | flops | bytes accessed | tf_op | source)
XLA Modules:
  0.0 70.5 jit_solution(12313255911872170996)
XLA Ops:
  0.0 0.0 copy-start
  0.0 1.0 %copy-done = bf16[1,384,512]{2,1,0:T(8,128)(2,1)S(1)} copy-done((bf16[1,384,512]{2,1,0:T(8,128)(2,1)S(1)}, bf16[1,384,512]{2,1,0:T(8,128)(2,1)}, u32[]{:S(2)}) %copy-start) | copy-done | bytes 393240
  1.0 0.0 copy-start.1
  1.0 1.0 %copy-done.1 = bf16[1,384,512]{2,1,0:T(8,128)(2,1)S(1)} copy-done((bf16[1,384,512]{2,1,0:T(8,128)(2,1)S(1)}, bf16[1,384,512]{2,1,0:T(8,128)(2,1)}, u32[]{:S(2)}) %copy-start.1) | copy-done | bytes 393240
  2.0 0.5 shard_map.37
  2.5 0.5 collective-permute-start
  3.0 1.5 %collective-permute-done.other_ref = f32[1032,128]{1,0:T(8,128)S(1)} collective-permute-done((f32[1032,128]{1,0:T(8,128)S(1)}, f32[1032,128]{1,0:T(8,128)S(1)}, u32[]{:S(2)}, u32[]{:S(2)}) %collective-permute-start) | collective-permute-done | bytes 528416 | tf_op jit(solution)/shard_map/ppermute | solution.py:231
  4.5 0.5 shard_map.38.refs_0_
  5.1 0.7 collective-permute-start.1
  5.8 5.5 %collective-permute-start.2 = (f32[1032,128]{1,0:T(8,128)S(1)}, f32[1032,128]{1,0:T(8,128)S(1)}, u32[]{:S(2)}, u32[]{:S(2)}) collective-permute-start(f32[1032,128]{1,0:T(8,128)S(1)} %shard_map.38.refs_0_), channel_id=1, source_target_pairs={{0,4},{5,9},{6,10},{3,7},{16,20},{21,25},{22,26},{19,23}} | collective-permute-start | bytes 1585160 | tf_op jit(solution)/shard_map/ppermute | solution.py:254
  11.3 0.7 collective-permute-start.3
  12.0 0.0 collective-permute-done.1.refs_1_
  12.0 10.5 %collective-permute-done.2.refs_2_ = f32[1032,128]{1,0:T(8,128)S(1)} collective-permute-done((f32[1032,128]{1,0:T(8,128)S(1)}, f32[1032,128]{1,0:T(8,128)S(1)}, u32[]{:S(2)}, u32[]{:S(2)}) %collective-permute-start.2) | collective-permute-done | bytes 528416 | tf_op jit(solution)/shard_map/ppermute | solution.py:254
  22.5 0.0 collective-permute-done.3.refs_3_
  22.5 5.8 %shard_map.39 = f32[1032,128]{1,0:T(8,128)S(1)} custom-call(f32[1032,128]{1,0:T(8,128)S(1)} %shard_map.38.refs_0_, f32[1032,128]{1,0:T(8,128)S(1)} %collective-permute-done.1.refs_1_, f32[1032,128]{1,0:T(8,128)S(1)} %collective-permute-done.2.refs_2_, f32[1032,128]{1,0:T(8,128)S(1)} %collective-permute-done.3.refs_3_), custom_call_target="tpu_custom_call" | custom-call | tf_op jit(solution)/shard_map/pallas_call | solution.py:174
  28.2 0.7 collective-permute-start.6
  29.0 0.7 collective-permute-start.5
  29.7 1.3 %collective-permute-start.4 = (f32[1032,128]{1,0:T(8,128)S(1)}, f32[1032,128]{1,0:T(8,128)S(1)}, u32[]{:S(2)}, u32[]{:S(2)}) collective-permute-start(f32[1032,128]{1,0:T(8,128)S(1)} %shard_map.39), channel_id=1, source_target_pairs={{9,1},{4,0},{7,15},{10,14},{25,17},{20,16},{23,31},{26,30}} | collective-permute-start | bytes 1585160 | tf_op jit(solution)/shard_map/ppermute | solution.py:264
  31.0 0.0 copy-start.2
  31.0 0.0 collective-permute-done.6
  31.0 0.0 collective-permute-done.5
  31.0 23.0 %collective-permute-done.4 = f32[1032,128]{1,0:T(8,128)S(1)} collective-permute-done((f32[1032,128]{1,0:T(8,128)S(1)}, f32[1032,128]{1,0:T(8,128)S(1)}, u32[]{:S(2)}, u32[]{:S(2)}) %collective-permute-start.4) | collective-permute-done | bytes 528416 | tf_op jit(solution)/shard_map/ppermute | solution.py:264
  54.0 0.1 add_add_fusion.refs_0_
  54.1 0.1 collective-permute-start.7
  54.2 0.0 copy-done.2
  54.2 0.5 collective-permute-start.8
  54.7 0.0 collective-permute-start.9
  54.7 1.8 %collective-permute-done.8.refs_3_ = f32[128,512]{1,0:T(8,128)S(1)} collective-permute-done((f32[128,512]{1,0:T(8,128)S(1)}, f32[128,512]{1,0:T(8,128)S(1)}, u32[]{:S(2)}, u32[]{:S(2)}) %collective-permute-start.8) | collective-permute-done | bytes 262176 | tf_op jit(solution)/shard_map/ppermute | solution.py:231
  56.5 0.3 collective-permute-start.10
  56.7 7.1 %collective-permute-done.9.refs_4_ = f32[128,512]{1,0:T(8,128)S(1)} collective-permute-done((f32[128,512]{1,0:T(8,128)S(1)}, f32[128,512]{1,0:T(8,128)S(1)}, u32[]{:S(2)}, u32[]{:S(2)}) %collective-permute-start.9) | collective-permute-done | bytes 262176 | tf_op jit(solution)/shard_map/ppermute | solution.py:245
  63.9 4.8 %collective-permute-done.10.refs_5_ = f32[128,512]{1,0:T(8,128)S(1)} collective-permute-done((f32[128,512]{1,0:T(8,128)S(1)}, f32[128,512]{1,0:T(8,128)S(1)}, u32[]{:S(2)}, u32[]{:S(2)}) %collective-permute-start.10) | collective-permute-done | bytes 262176 | tf_op jit(solution)/shard_map/ppermute | solution.py:245
  68.6 0.0 collective-permute-done.7.refs_1_
  68.6 1.9 %shard_map.40 = f32[128,512]{1,0:T(8,128)} custom-call(f32[1032,128]{1,0:T(8,128)S(1)} %add_add_fusion.refs_0_, f32[1032,128]{1,0:T(8,128)S(1)} %collective-permute-done.7.refs_1_, f32[128,512]{1,0:T(8,128)S(1)} %bitcast.10, f32[128,512]{1,0:T(8,128)S(1)} %collective-permute-done.8.refs_3_, f32[128,512]{1,0:T(8,128)S(1)} %collective-permute-done.9.refs_4_, ...), custom_call_target="tpu_custom_call" | custom-call | tf_op jit(solution)/shard_map/pallas_call | solution.py:174
Async XLA Ops:
  0.0 1.0 %copy-start = (bf16[1,384,512]{2,1,0:T(8,128)(2,1)S(1)}, bf16[1,384,512]{2,1,0:T(8,128)(2,1)}, u32[]{:S(2)}) copy-start(bf16[1,384,512]{2,1,0:T(8,128)(2,1)} %param.3) | copy-start | bytes 1179652
  1.0 1.0 %copy-start.1 = (bf16[1,384,512]{2,1,0:T(8,128)(2,1)S(1)}, bf16[1,384,512]{2,1,0:T(8,128)(2,1)}, u32[]{:S(2)}) copy-start(bf16[1,384,512]{2,1,0:T(8,128)(2,1)} %param.4) | copy-start | bytes 1179652
  2.5 2.1 %collective-permute-start = (f32[1032,128]{1,0:T(8,128)S(1)}, f32[1032,128]{1,0:T(8,128)S(1)}, u32[]{:S(2)}, u32[]{:S(2)}) collective-permute-start(f32[1032,128]{1,0:T(8,128)S(1)} %shard_map.37), channel_id=1, source_target_pairs={{0,1},{1,0},{2,3},{3,2},{4,5},{5,4},{6,7},{7,6},{8,9},{9,8},{10,11... | collective-permute-start | bytes 1585160 | tf_op jit(solution)/shard_map/ppermute | solution.py:231
  5.1 6.9 %collective-permute-start.1 = (f32[1032,128]{1,0:T(8,128)S(1)}, f32[1032,128]{1,0:T(8,128)S(1)}, u32[]{:S(2)}, u32[]{:S(2)}) collective-permute-start(f32[1032,128]{1,0:T(8,128)S(1)} %shard_map.38.refs_0_), channel_id=1, source_target_pairs={{12,4},{1,9},{2,10},{15,7},{28,20},{17,25},{18,26},{31,23}} | collective-permute-start | bytes 1585160 | tf_op jit(solution)/shard_map/ppermute | solution.py:254
  5.8 16.7 %collective-permute-start.2 = (f32[1032,128]{1,0:T(8,128)S(1)}, f32[1032,128]{1,0:T(8,128)S(1)}, u32[]{:S(2)}, u32[]{:S(2)}) collective-permute-start(f32[1032,128]{1,0:T(8,128)S(1)} %shard_map.38.refs_0_), channel_id=1, source_target_pairs={{0,4},{5,9},{6,10},{3,7},{16,20},{21,25},{22,26},{19,23}} | collective-permute-start | bytes 1585160 | tf_op jit(solution)/shard_map/ppermute | solution.py:254
  11.3 11.2 %collective-permute-start.3 = (f32[1032,128]{1,0:T(8,128)S(1)}, f32[1032,128]{1,0:T(8,128)S(1)}, u32[]{:S(2)}, u32[]{:S(2)}) collective-permute-start(f32[1032,128]{1,0:T(8,128)S(1)} %shard_map.38.refs_0_), channel_id=1, source_target_pairs={{8,4},{13,9},{14,10},{11,7},{24,20},{29,25},{30,26},{27,23}} | collective-permute-start | bytes 1585160 | tf_op jit(solution)/shard_map/ppermute | solution.py:254
  28.2 2.8 %collective-permute-start.6 = (f32[1032,128]{1,0:T(8,128)S(1)}, f32[1032,128]{1,0:T(8,128)S(1)}, u32[]{:S(2)}, u32[]{:S(2)}) collective-permute-start(f32[1032,128]{1,0:T(8,128)S(1)} %shard_map.39), channel_id=1, source_target_pairs={{9,13},{4,6},{7,11},{10,8},{25,29},{20,22},{23,27},{26,24}} | collective-permute-start | bytes 1585160 | tf_op jit(solution)/shard_map/ppermute | solution.py:264
  29.0 2.1 %collective-permute-start.5 = (f32[1032,128]{1,0:T(8,128)S(1)}, f32[1032,128]{1,0:T(8,128)S(1)}, u32[]{:S(2)}, u32[]{:S(2)}) collective-permute-start(f32[1032,128]{1,0:T(8,128)S(1)} %shard_map.39), channel_id=1, source_target_pairs={{9,5},{4,2},{7,3},{10,12},{25,21},{20,18},{23,19},{26,28}} | collective-permute-start | bytes 1585160 | tf_op jit(solution)/shard_map/ppermute | solution.py:264
  29.7 24.3 %collective-permute-start.4 = (f32[1032,128]{1,0:T(8,128)S(1)}, f32[1032,128]{1,0:T(8,128)S(1)}, u32[]{:S(2)}, u32[]{:S(2)}) collective-permute-start(f32[1032,128]{1,0:T(8,128)S(1)} %shard_map.39), channel_id=1, source_target_pairs={{9,1},{4,0},{7,15},{10,14},{25,17},{20,16},{23,31},{26,30}} | collective-permute-start | bytes 1585160 | tf_op jit(solution)/shard_map/ppermute | solution.py:264
  31.0 23.2 %copy-start.2 = (f32[1,128,512]{2,1,0:T(8,128)S(1)}, f32[1,128,512]{2,1,0:T(8,128)}, u32[]{:S(2)}) copy-start(f32[1,128,512]{2,1,0:T(8,128)} %param.5) | copy-start | bytes 786436
  54.1 14.5 %collective-permute-start.7 = (f32[1032,128]{1,0:T(8,128)S(1)}, f32[1032,128]{1,0:T(8,128)S(1)}, u32[]{:S(2)}, u32[]{:S(2)}) collective-permute-start(f32[1032,128]{1,0:T(8,128)S(1)} %add_add_fusion.refs_0_), channel_id=1, source_target_pairs={{0,1},{1,0},{2,3},{3,2},{4,5},{5,4},{6,7},{7,6},{8,9},{9,8},{10,11... | collective-permute-start | bytes 1585160 | tf_op jit(solution)/shard_map/ppermute | solution.py:231
  54.2 2.3 %collective-permute-start.8 = (f32[128,512]{1,0:T(8,128)S(1)}, f32[128,512]{1,0:T(8,128)S(1)}, u32[]{:S(2)}, u32[]{:S(2)}) collective-permute-start(f32[128,512]{1,0:T(8,128)S(1)} %bitcast.8), channel_id=1, source_target_pairs={{0,1},{1,0},{2,3},{3,2},{4,5},{5,4},{6,7},{7,6},{8,9},{9,8},{10,11... | collective-permute-start | bytes 786440 | tf_op jit(solution)/shard_map/ppermute | solution.py:231
  54.7 9.2 %collective-permute-start.9 = (f32[128,512]{1,0:T(8,128)S(1)}, f32[128,512]{1,0:T(8,128)S(1)}, u32[]{:S(2)}, u32[]{:S(2)}) collective-permute-start(f32[128,512]{1,0:T(8,128)S(1)} %bitcast.9), channel_id=1, source_target_pairs={{0,4},{1,5},{2,6},{3,7},{4,0},{5,1},{6,2},{7,3},{8,12},{9,13},{10,... | collective-permute-start | bytes 786440 | tf_op jit(solution)/shard_map/ppermute | solution.py:245
  56.5 12.1 %collective-permute-start.10 = (f32[128,512]{1,0:T(8,128)S(1)}, f32[128,512]{1,0:T(8,128)S(1)}, u32[]{:S(2)}, u32[]{:S(2)}) collective-permute-start(f32[128,512]{1,0:T(8,128)S(1)} %collective-permute-done.8.refs_3_), channel_id=1, source_target_pairs={{0,4},{1,5},{2,6},{3,7},{4,0},{5,1},{6,2},{7,3},{8,12},{9,13},{10,... | collective-permute-start | bytes 786440 | tf_op jit(solution)/shard_map/ppermute | solution.py:245

commit v2 on v1

--- a/solution.py
+++ b/solution.py
@@ -81,39 +81,25 @@
     return dot(left[0], right[0]) + (dot(left[0], right[1]) + dot(left[1], right[0]))
 
 
-def square(x_ref):
-    x = x_ref[...]
-    return lax.dot_general(x, x, (((0,), (0,)), ((), ())), preferred_element_type=jnp.float32)
+def cov_kernel(keep, acts_ref, outgrads_ref, out_ref):
+    core = lax.axis_index("grad")
+
+    def write(x_ref):
+        x = x_ref[...]
+        total = lax.dot_general(x, x, (((0,), (0,)), ((), ())), preferred_element_type=jnp.float32)
+        pack(block_of(total), x.shape[1], out_ref)
+
+    @pl.when((core == 0) == keep)
+    def _():
+        write(acts_ref)
+
+    @pl.when((core == 0) != keep)
+    def _():
+        write(outgrads_ref)
 
 
 def block_of(value):
     return lambda i, j: value[i * LANE : (i + 1) * LANE, j * LANE : (j + 1) * LANE]
-
-
-def cov_send_kernel(acts_ref, outgrads_ref, out_ref):
-    core = lax.axis_index("grad")
-
-    @pl.when(core == 0)
-    def _():
-        pack(block_of(square(outgrads_ref)), outgrads_ref.shape[1], out_ref)
-
-    @pl.when(core != 0)
-    def _():
-        pack(block_of(square(acts_ref)), acts_ref.shape[1], out_ref)
-
-
-def cov_keep_kernel(acts_ref, outgrads_ref, other_ref, out_ref):
-    core = lax.axis_index("grad")
-
-    @pl.when(core == 0)
-    def _():
-        pack(block_of(square(acts_ref)), acts_ref.shape[1], out_ref)
-
-    @pl.when(core != 0)
-    def _():
-        pack(block_of(square(outgrads_ref)), outgrads_ref.shape[1], out_ref)
-
-    out_ref[...] += other_ref[...]
 
 
 def inverse_kernel(scale, order, *refs):
@@ -182,13 +168,16 @@
 class Plan:
     def __init__(self, dp, cuts):
         self.dp, self.cuts = dp, cuts
-        self.rounds = max(QUAD - 1, 2 * cuts - 1)
+        self.bases = range(0, dp, QUAD)
 
     def index(self, z, x, core):
-        return (z * self.cuts + x) * 2 + core
-
-    def root(self, z, x, core):
-        return z // QUAD * QUAD + 1 + (x + core) % 2
+        return (z * self.cuts + x % self.cuts) * 2 + core
+
+    def root(self, base, x, core):
+        return base + 1 + (x + core) % 2
+
+    def needed(self, base, x):
+        return x // 2 == base // QUAD
 
     def across(self, bit):
         return [
@@ -198,32 +187,44 @@
             for core in range(2)
         ]
 
-    def gather(self, turn):
+    def neighbours(self, outward):
+        middle = (1, 2) if outward else (0, 3)
+        return [pair for pair in self.across(1) if pair[0] // (2 * self.cuts) % QUAD in middle]
+
+    def collect(self, turn):
         pairs = []
         for x in range(self.cuts):
             for core in range(2):
-                for base in range(0, self.dp, QUAD):
+                for base in self.bases:
                     root = self.root(base, x, core)
-                    others = sorted((z for z in range(base, base + QUAD) if z != root), key=lambda z: -abs(z - root))
-                    pairs.append((self.index(others[turn], x, core), self.index(root, x, core)))
+                    middle = 2 * base + QUAD - 1 - root
+                    source = (middle ^ 1, middle, root ^ 1)[turn]
+                    pairs.append((self.index(source, x, core), self.index(root, x, core)))
         return pairs
 
-    def spread(self, turn):
+    def first(self, turn):
         pairs = []
         for x in range(self.cuts):
-            for base in range(0, self.dp, QUAD):
-                root = self.root(base, x, 1)
-                others = sorted((z for z in range(base, base + QUAD) if z != root), key=lambda z: -abs(z - root))
-                if turn < len(others):
-                    pairs.append((self.index(root, x, 1), self.index(others[turn], x, 1)))
-                if x // 2 != base // QUAD:
-                    continue
-                root = self.root(base, x, 0)
-                targets = [(z, x + d) for d in range(self.cuts) for z in (root ^ 1, root)]
-                targets = [(z, other % self.cuts) for z, other in targets if (z, other) != (root, x)]
-                if turn < len(targets):
-                    z, other = targets[turn]
-                    pairs.append((self.index(root, x, 0), self.index(z, other, 0)))
+            for base in self.bases:
+                if self.needed(base, x):
+                    root = self.root(base, x, 0)
+                    pairs.append((self.index(root, x, 0), self.index(root, x + turn, 0)))
+                if turn == 1:
+                    root = self.root(base, x, 1)
+                    pairs.append((self.index(root, x, 1), self.index(2 * base + QUAD - 1 - root, x, 1)))
+        return pairs
+
+    def outward(self, turn):
+        pairs = []
+        for x in range(self.cuts):
+            for base in self.bases:
+                if self.needed(base, x):
+                    root = self.root(base, x, 0)
+                    pairs.append((self.index(root, x + turn, 0), self.index(root ^ 1, x + turn, 0)))
+                if turn < 2:
+                    root = self.root(base, x, 1)
+                    chip = root if turn == 0 else 2 * base + QUAD - 1 - root
+                    pairs.append((self.index(chip, x, 1), self.index(chip ^ 1, x, 1)))
         return pairs
 
 
@@ -240,28 +241,40 @@
     shape = (packed_rows(order), LANE)
     acts, outgrads, grads = acts[0], outgrads[0], grads[0]
 
-    pieces = [grads, swap_cores(grads)]
-    while len(pieces) < spread:
-        moved = [lax.ppermute(piece, AXES, plan.across(len(pieces) // 2)) for piece in pieces]
-        pieces += moved
-
-    sent = call(cov_send_kernel, shape, [], acts, outgrads)
-    chip = call(cov_keep_kernel, shape, [], acts, outgrads, swap_cores(sent))
+    sent, kept = (
+        call(functools.partial(cov_kernel, keep), shape, [], acts, outgrads) for keep in (False, True)
+    )
+    chip = kept + swap_cores(sent)
     bit = QUAD
     while bit < dp:
         chip = chip + lax.ppermute(chip, AXES, plan.across(bit))
         bit *= 2
-    sums = [chip] + [lax.ppermute(chip, AXES, plan.gather(turn)) for turn in range(QUAD - 1)]
+    grads, chip = lax.optimization_barrier((grads, chip))
+    sums = [chip] + [lax.ppermute(chip, AXES, plan.collect(turn)) for turn in range(QUAD - 1)]
+    outward = lax.ppermute(grads, AXES, plan.neighbours(True))
+    pieces = [grads, swap_cores(grads)]
+    sums, outward, pieces = lax.optimization_barrier((sums, outward, pieces))
     scale = 1.0 / (tok_rows * dev_count)
     inverse = call(
         functools.partial(inverse_kernel, scale, order), shape, [pltpu.VMEM((order, order), jnp.float32)], *sums
     )
+    inverse, grads = lax.optimization_barrier((inverse, grads))
     z, x, core = (lax.axis_index(name) for name in AXES)
     is_root = z % QUAD == 1 + (x + core) % 2
     needed = jnp.logical_or(core == 1, x // 2 == z // QUAD)
+    arrived = [lax.ppermute(inverse, AXES, plan.first(turn)) for turn in range(1, cuts)]
+    outer = [lax.ppermute(inverse, AXES, plan.outward(0))]
+    inward = lax.ppermute(grads, AXES, plan.neighbours(False))
+    outer += [lax.ppermute(array, AXES, plan.outward(turn + 1)) for turn, array in enumerate(arrived)]
+    neighbour = outward + inward
+    pieces += [neighbour, swap_cores(neighbour)]
+    while len(pieces) < spread:
+        pieces += [lax.ppermute(piece, AXES, plan.across(len(pieces) // 2)) for piece in pieces]
+    pieces = pieces[:spread]
+    arrived, outer, pieces = lax.optimization_barrier((arrived, outer, pieces))
     mine = jnp.where(jnp.logical_and(is_root, needed), inverse, 0.0)
-    for turn in range(plan.rounds):
-        mine = mine + lax.ppermute(inverse, AXES, plan.spread(turn))
+    for array in arrived + outer:
+        mine = mine + array
     other = swap_cores(mine)
     square_scratch = pltpu.VMEM((order, order), jnp.float32)
     out = call(

time: 70.8 us -> 54.7 us (0.77)
  waiting for transfers between devices: 48.7 us -> 18.6 us
  starting transfers between devices: 10.9 us -> 24.7 us
    ppermute x8, waiting for transfers between devices: 45.4 us -> 14.3 us  [the longest x1 8.82 us: per_device(): outward = lax.ppermute(grads, AXES, plan.neighbours(True))]
    ppermute x8, starting transfers between devices: 9.81 us -> 21.8 us  [the longest x1 11.6 us: per_device(): inward = lax.ppermute(grads, AXES, plan.neighbours(False))]
    ppermute x3 -> x4, starting transfers between devices: 1.08 us -> 2.92 us  [swap_cores(): return lax.ppermute(array, 'grad', [(0, 1), (1, 0)])]
    ppermute x3 -> x4, waiting for transfers between devices: 3.32 us -> 4.31 us  [swap_cores(): return lax.ppermute(array, 'grad', [(0, 1), (1, 0)])]
  transfers between devices with their start and end apart: 11 -> 12, of which waited for: 6 -> 5; matrix products, arithmetic and copies ran while one was open for 0% -> 0% of each run, Pallas kernels for 0% -> 1%
where the time goes in v2:
time: 54.7 us; the launch traced here: 54.4 us
  starting transfers between devices  24.7 us (45%)
  waiting for transfers between devices  18.6 us (34%)
  Pallas kernels  8.56 us (16%)
  local copies, waits for them, and re-layouts  2 us (4%)
    ppermute x1, starting transfers between devices, per_device(): inward = lax.ppermute(grads, AXES, plan.neighbours(False))  11.6 us
    ppermute x1, waiting for transfers between devices, per_device(): outward = lax.ppermute(grads, AXES, plan.neighbours(True))  8.82 us
    pallas_call x4, Pallas kernels, call(): pl.pallas_call(kernel, out_shape=jax.ShapeDtypeStruct(shape, jnp.float32)...  8.56 us
    ppermute x3, starting transfers between devices, per_device(): lax.ppermute(chip, AXES, plan.collect(turn))  6.27 us
    ppermute x1, waiting for transfers between devices, per_device(): inward = lax.ppermute(grads, AXES, plan.neighbours(False))  5.44 us
    ppermute x4, waiting for transfers between devices, swap_cores(): return lax.ppermute(array, 'grad', [(0, 1), (1, 0)])  4.31 us
    ppermute x4, starting transfers between devices, swap_cores(): return lax.ppermute(array, 'grad', [(0, 1), (1, 0)])  2.92 us
    unnamed x6, local copies, waits for them, and re-layouts  2 us
  transfers between devices with their start and end apart: 12, of which 5 were waited for; matrix products, arithmetic and copies ran while one was open for 0% of the time, Pallas kernels for 1%

profile of v2, /device:TPU:0, one launch (start us, length us, event | category | flops | bytes accessed | tf_op | source)
XLA Modules:
  0.0 54.4 jit_solution(13731394291955063121)
XLA Ops:
  0.0 0.0 copy-start
  0.0 1.0 %copy-done = bf16[1,384,512]{2,1,0:T(8,128)(2,1)S(1)} copy-done((bf16[1,384,512]{2,1,0:T(8,128)(2,1)S(1)}, bf16[1,384,512]{2,1,0:T(8,128)(2,1)}, u32[]{:S(2)}) %copy-start) | copy-done | bytes 393240
  1.0 0.0 copy-start.1
  1.0 1.0 %copy-done.1 = bf16[1,384,512]{2,1,0:T(8,128)(2,1)S(1)} copy-done((bf16[1,384,512]{2,1,0:T(8,128)(2,1)S(1)}, bf16[1,384,512]{2,1,0:T(8,128)(2,1)}, u32[]{:S(2)}) %copy-start.1) | copy-done | bytes 393240
  2.0 0.5 shard_map.38
  2.5 0.5 collective-permute-start
  3.0 0.5 shard_map.37
  3.5 0.0 copy-start.2
  3.5 1.1 %collective-permute-done = f32[1032,128]{1,0:T(8,128)S(1)} collective-permute-done((f32[1032,128]{1,0:T(8,128)S(1)}, f32[1032,128]{1,0:T(8,128)S(1)}, u32[]{:S(2)}, u32[]{:S(2)}) %collective-permute-start) | collective-permute-done | bytes 528416 | tf_op jit(solution)/shard_map/ppermute | solution.py:232
  4.5 0.1 add.34.refs_0_
  4.6 4.9 %collective-permute-start.3 = (f32[1032,128]{1,0:T(8,128)S(1)}, f32[1032,128]{1,0:T(8,128)S(1)}, u32[]{:S(2)}, u32[]{:S(2)}) collective-permute-start(f32[1032,128]{1,0:T(8,128)S(1)} %add.34.refs_0_), channel_id=1, source_target_pairs={{0,4},{13,9},{14,10},{3,7},{16,20},{29,25},{30,26},{19,23}} | collective-permute-start | bytes 1585160 | tf_op jit(solution)/shard_map/ppermute | solution.py:253
  9.5 0.7 %collective-permute-start.2 = (f32[1032,128]{1,0:T(8,128)S(1)}, f32[1032,128]{1,0:T(8,128)S(1)}, u32[]{:S(2)}, u32[]{:S(2)}) collective-permute-start(f32[1032,128]{1,0:T(8,128)S(1)} %add.34.refs_0_), channel_id=1, source_target_pairs={{8,4},{5,9},{6,10},{11,7},{24,20},{21,25},{22,26},{27,23}} | collective-permute-start | bytes 1585160 | tf_op jit(solution)/shard_map/ppermute | solution.py:253
  10.2 0.7 %collective-permute-start.1 = (f32[1032,128]{1,0:T(8,128)S(1)}, f32[1032,128]{1,0:T(8,128)S(1)}, u32[]{:S(2)}, u32[]{:S(2)}) collective-permute-start(f32[1032,128]{1,0:T(8,128)S(1)} %add.34.refs_0_), channel_id=1, source_target_pairs={{12,4},{1,9},{2,10},{15,7},{28,20},{17,25},{18,26},{31,23}} | collective-permute-start | bytes 1585160 | tf_op jit(solution)/shard_map/ppermute | solution.py:253
  10.9 0.0 copy-done.2
  10.9 2.1 %collective-permute-start.5 = (f32[128,512]{1,0:T(8,128)S(1)}, f32[128,512]{1,0:T(8,128)S(1)}, u32[]{:S(2)}, u32[]{:S(2)}) collective-permute-start(f32[128,512]{1,0:T(8,128)S(1)} %bitcast.8), channel_id=1, source_target_pairs={{0,1},{1,0},{2,3},{3,2},{4,5},{5,4},{6,7},{7,6},{8,9},{9,8},{10,11... | collective-permute-start | bytes 786440 | tf_op jit(solution)/shard_map/ppermute | solution.py:232
  13.0 1.3 %collective-permute-start.4 = (f32[128,512]{1,0:T(8,128)S(1)}, f32[128,512]{1,0:T(8,128)S(1)}, u32[]{:S(2)}, u32[]{:S(2)}) collective-permute-start(f32[128,512]{1,0:T(8,128)S(1)} %bitcast.9), channel_id=1, source_target_pairs={{4,0},{5,1},{6,2},{7,3},{8,12},{9,13},{10,14},{11,15},{20,16},{21,... | collective-permute-start | bytes 786440 | tf_op jit(solution)/shard_map/ppermute | solution.py:254
  14.3 0.0 collective-permute-done.5.refs_3_
  14.3 8.8 %collective-permute-done.4 = f32[128,512]{1,0:T(8,128)S(1)} collective-permute-done((f32[128,512]{1,0:T(8,128)S(1)}, f32[128,512]{1,0:T(8,128)S(1)}, u32[]{:S(2)}, u32[]{:S(2)}) %collective-permute-start.4) | collective-permute-done | bytes 262176 | tf_op jit(solution)/shard_map/ppermute | solution.py:254
  23.1 0.0 collective-permute-done.3.refs_3_
  23.2 0.0 collective-permute-done.2.refs_2_
  23.2 0.0 collective-permute-done.1.refs_1_
  23.2 5.8 %shard_map.39 = f32[1032,128]{1,0:T(8,128)S(1)} custom-call(f32[1032,128]{1,0:T(8,128)S(1)} %add.34.refs_0_, f32[1032,128]{1,0:T(8,128)S(1)} %collective-permute-done.1.refs_1_, f32[1032,128]{1,0:T(8,128)S(1)} %collective-permute-done.2.refs_2_, f32[1032,128]{1,0:T(8,128)S(1)} %collective-permute-done.3.refs_3_), custom_call_target="tpu_custom_call" | custom-call | tf_op jit(solution)/shard_map/pallas_call | solution.py:160
  28.9 0.7 %collective-permute-start.6 = (f32[1032,128]{1,0:T(8,128)S(1)}, f32[1032,128]{1,0:T(8,128)S(1)}, u32[]{:S(2)}, u32[]{:S(2)}) collective-permute-start(f32[1032,128]{1,0:T(8,128)S(1)} %shard_map.39), channel_id=1, source_target_pairs={{4,6},{9,5},{10,8},{7,11},{20,22},{25,21},{26,24},{23,27}} | collective-permute-start | bytes 1585160 | tf_op jit(solution)/shard_map/ppermute | solution.py:265
  29.6 1.3 %collective-permute-start.7 = (f32[1032,128]{1,0:T(8,128)S(1)}, f32[1032,128]{1,0:T(8,128)S(1)}, u32[]{:S(2)}, u32[]{:S(2)}) collective-permute-start(f32[1032,128]{1,0:T(8,128)S(1)} %shard_map.39), channel_id=1, source_target_pairs={{4,0},{9,13},{10,14},{7,3},{20,16},{25,29},{26,30},{23,19}} | collective-permute-start | bytes 1585160 | tf_op jit(solution)/shard_map/ppermute | solution.py:266
  30.9 0.0 collective-permute-done.6
  30.9 0.7 %collective-permute-start.8 = (f32[1032,128]{1,0:T(8,128)S(1)}, f32[1032,128]{1,0:T(8,128)S(1)}, u32[]{:S(2)}, u32[]{:S(2)}) collective-permute-start(f32[1032,128]{1,0:T(8,128)S(1)} %collective-permute-done.6), channel_id=1, source_target_pairs={{6,2},{5,1},{8,12},{11,15},{22,18},{21,17},{24,28},{27,31}} | collective-permute-start | bytes 1585160 | tf_op jit(solution)/shard_map/ppermute | solution.py:268
  31.6 11.6 %collective-permute-start.9 = (f32[128,512]{1,0:T(8,128)S(1)}, f32[128,512]{1,0:T(8,128)S(1)}, u32[]{:S(2)}, u32[]{:S(2)}) collective-permute-start(f32[128,512]{1,0:T(8,128)S(1)} %bitcast.10), channel_id=1, source_target_pairs={{0,4},{1,5},{2,6},{3,7},{12,8},{13,9},{14,10},{15,11},{16,20},{17,... | collective-permute-start | bytes 786440 | tf_op jit(solution)/shard_map/ppermute | solution.py:267
  43.2 5.4 %collective-permute-done.9 = f32[128,512]{1,0:T(8,128)S(1)} collective-permute-done((f32[128,512]{1,0:T(8,128)S(1)}, f32[128,512]{1,0:T(8,128)S(1)}, u32[]{:S(2)}, u32[]{:S(2)}) %collective-permute-start.9) | collective-permute-done | bytes 262176 | tf_op jit(solution)/shard_map/ppermute | solution.py:267
  48.7 0.1 collective-permute-start.10
  48.8 1.5 %collective-permute-done.10.refs_5_ = f32[128,512]{1,0:T(8,128)S(1)} collective-permute-done((f32[128,512]{1,0:T(8,128)S(1)}, f32[128,512]{1,0:T(8,128)S(1)}, u32[]{:S(2)}, u32[]{:S(2)}) %collective-permute-start.10) | collective-permute-done | bytes 262176 | tf_op jit(solution)/shard_map/ppermute | solution.py:232
  50.3 0.0 collective-permute-done.7
  50.3 0.0 collective-permute-done.8
  50.3 0.2 add_add_fusion.refs_0_
  50.5 0.2 collective-permute-start.11
  50.7 1.8 %collective-permute-done.11.refs_1_ = f32[1032,128]{1,0:T(8,128)S(1)} collective-permute-done((f32[1032,128]{1,0:T(8,128)S(1)}, f32[1032,128]{1,0:T(8,128)S(1)}, u32[]{:S(2)}, u32[]{:S(2)}) %collective-permute-start.11) | collective-permute-done | bytes 528416 | tf_op jit(solution)/shard_map/ppermute | solution.py:232
  52.5 1.9 %shard_map.40 = f32[128,512]{1,0:T(8,128)} custom-call(f32[1032,128]{1,0:T(8,128)S(1)} %add_add_fusion.refs_0_, f32[1032,128]{1,0:T(8,128)S(1)} %collective-permute-done.11.refs_1_, f32[128,512]{1,0:T(8,128)S(1)} %bitcast.11, f32[128,512]{1,0:T(8,128)S(1)} %collective-permute-done.5.refs_3_, f32[128,512]{1,0:T(8,128)S(1)} %add.35.refs_4_, ...), custom_call_target="tpu_custom_call" | custom-call | tf_op jit(solution)/shard_map/pallas_call | solution.py:160
  (1 shorter events, 0.0 us)
Async XLA Ops:
  0.0 1.0 %copy-start = (bf16[1,384,512]{2,1,0:T(8,128)(2,1)S(1)}, bf16[1,384,512]{2,1,0:T(8,128)(2,1)}, u32[]{:S(2)}) copy-start(bf16[1,384,512]{2,1,0:T(8,128)(2,1)} %param.3) | copy-start | bytes 1179652
  1.0 1.0 %copy-start.1 = (bf16[1,384,512]{2,1,0:T(8,128)(2,1)S(1)}, bf16[1,384,512]{2,1,0:T(8,128)(2,1)}, u32[]{:S(2)}) copy-start(bf16[1,384,512]{2,1,0:T(8,128)(2,1)} %param.4) | copy-start | bytes 1179652
  2.5 2.1 %collective-permute-start = (f32[1032,128]{1,0:T(8,128)S(1)}, f32[1032,128]{1,0:T(8,128)S(1)}, u32[]{:S(2)}, u32[]{:S(2)}) collective-permute-start(f32[1032,128]{1,0:T(8,128)S(1)} %shard_map.38), channel_id=1, source_target_pairs={{0,1},{1,0},{2,3},{3,2},{4,5},{5,4},{6,7},{7,6},{8,9},{9,8},{10,11... | collective-permute-start | bytes 1585160 | tf_op jit(solution)/shard_map/ppermute | solution.py:232
  3.5 7.4 %copy-start.2 = (f32[1,128,512]{2,1,0:T(8,128)S(1)}, f32[1,128,512]{2,1,0:T(8,128)}, u32[]{:S(2)}) copy-start(f32[1,128,512]{2,1,0:T(8,128)} %param.5) | copy-start | bytes 786436
  4.6 18.5 %collective-permute-start.3 = (f32[1032,128]{1,0:T(8,128)S(1)}, f32[1032,128]{1,0:T(8,128)S(1)}, u32[]{:S(2)}, u32[]{:S(2)}) collective-permute-start(f32[1032,128]{1,0:T(8,128)S(1)} %add.34.refs_0_), channel_id=1, source_target_pairs={{0,4},{13,9},{14,10},{3,7},{16,20},{29,25},{30,26},{19,23}} | collective-permute-start | bytes 1585160 | tf_op jit(solution)/shard_map/ppermute | solution.py:253
  9.5 13.7 %collective-permute-start.2 = (f32[1032,128]{1,0:T(8,128)S(1)}, f32[1032,128]{1,0:T(8,128)S(1)}, u32[]{:S(2)}, u32[]{:S(2)}) collective-permute-start(f32[1032,128]{1,0:T(8,128)S(1)} %add.34.refs_0_), channel_id=1, source_target_pairs={{8,4},{5,9},{6,10},{11,7},{24,20},{21,25},{22,26},{27,23}} | collective-permute-start | bytes 1585160 | tf_op jit(solution)/shard_map/ppermute | solution.py:253
  10.2 13.0 %collective-permute-start.1 = (f32[1032,128]{1,0:T(8,128)S(1)}, f32[1032,128]{1,0:T(8,128)S(1)}, u32[]{:S(2)}, u32[]{:S(2)}) collective-permute-start(f32[1032,128]{1,0:T(8,128)S(1)} %add.34.refs_0_), channel_id=1, source_target_pairs={{12,4},{1,9},{2,10},{15,7},{28,20},{17,25},{18,26},{31,23}} | collective-permute-start | bytes 1585160 | tf_op jit(solution)/shard_map/ppermute | solution.py:253
  10.9 3.4 %collective-permute-start.5 = (f32[128,512]{1,0:T(8,128)S(1)}, f32[128,512]{1,0:T(8,128)S(1)}, u32[]{:S(2)}, u32[]{:S(2)}) collective-permute-start(f32[128,512]{1,0:T(8,128)S(1)} %bitcast.8), channel_id=1, source_target_pairs={{0,1},{1,0},{2,3},{3,2},{4,5},{5,4},{6,7},{7,6},{8,9},{9,8},{10,11... | collective-permute-start | bytes 786440 | tf_op jit(solution)/shard_map/ppermute | solution.py:232
  13.0 10.1 %collective-permute-start.4 = (f32[128,512]{1,0:T(8,128)S(1)}, f32[128,512]{1,0:T(8,128)S(1)}, u32[]{:S(2)}, u32[]{:S(2)}) collective-permute-start(f32[128,512]{1,0:T(8,128)S(1)} %bitcast.9), channel_id=1, source_target_pairs={{4,0},{5,1},{6,2},{7,3},{8,12},{9,13},{10,14},{11,15},{20,16},{21,... | collective-permute-start | bytes 786440 | tf_op jit(solution)/shard_map/ppermute | solution.py:254
  28.9 2.0 %collective-permute-start.6 = (f32[1032,128]{1,0:T(8,128)S(1)}, f32[1032,128]{1,0:T(8,128)S(1)}, u32[]{:S(2)}, u32[]{:S(2)}) collective-permute-start(f32[1032,128]{1,0:T(8,128)S(1)} %shard_map.39), channel_id=1, source_target_pairs={{4,6},{9,5},{10,8},{7,11},{20,22},{25,21},{26,24},{23,27}} | collective-permute-start | bytes 1585160 | tf_op jit(solution)/shard_map/ppermute | solution.py:265
  29.6 20.7 %collective-permute-start.7 = (f32[1032,128]{1,0:T(8,128)S(1)}, f32[1032,128]{1,0:T(8,128)S(1)}, u32[]{:S(2)}, u32[]{:S(2)}) collective-permute-start(f32[1032,128]{1,0:T(8,128)S(1)} %shard_map.39), channel_id=1, source_target_pairs={{4,0},{9,13},{10,14},{7,3},{20,16},{25,29},{26,30},{23,19}} | collective-permute-start | bytes 1585160 | tf_op jit(solution)/shard_map/ppermute | solution.py:266
  30.9 19.4 %collective-permute-start.8 = (f32[1032,128]{1,0:T(8,128)S(1)}, f32[1032,128]{1,0:T(8,128)S(1)}, u32[]{:S(2)}, u32[]{:S(2)}) collective-permute-start(f32[1032,128]{1,0:T(8,128)S(1)} %collective-permute-done.6), channel_id=1, source_target_pairs={{6,2},{5,1},{8,12},{11,15},{22,18},{21,17},{24,28},{27,31}} | collective-permute-start | bytes 1585160 | tf_op jit(solution)/shard_map/ppermute | solution.py:268
  31.6 17.0 %collective-permute-start.9 = (f32[128,512]{1,0:T(8,128)S(1)}, f32[128,512]{1,0:T(8,128)S(1)}, u32[]{:S(2)}, u32[]{:S(2)}) collective-permute-start(f32[128,512]{1,0:T(8,128)S(1)} %bitcast.10), channel_id=1, source_target_pairs={{0,4},{1,5},{2,6},{3,7},{12,8},{13,9},{14,10},{15,11},{16,20},{17,... | collective-permute-start | bytes 786440 | tf_op jit(solution)/shard_map/ppermute | solution.py:267
  48.7 1.6 %collective-permute-start.10 = (f32[128,512]{1,0:T(8,128)S(1)}, f32[128,512]{1,0:T(8,128)S(1)}, u32[]{:S(2)}, u32[]{:S(2)}) collective-permute-start(f32[128,512]{1,0:T(8,128)S(1)} %add.35.refs_4_), channel_id=1, source_target_pairs={{0,1},{1,0},{2,3},{3,2},{4,5},{5,4},{6,7},{7,6},{8,9},{9,8},{10,11... | collective-permute-start | bytes 786440 | tf_op jit(solution)/shard_map/ppermute | solution.py:232
  50.5 2.0 %collective-permute-start.11 = (f32[1032,128]{1,0:T(8,128)S(1)}, f32[1032,128]{1,0:T(8,128)S(1)}, u32[]{:S(2)}, u32[]{:S(2)}) collective-permute-start(f32[1032,128]{1,0:T(8,128)S(1)} %add_add_fusion.refs_0_), channel_id=1, source_target_pairs={{0,1},{1,0},{2,3},{3,2},{4,5},{5,4},{6,7},{7,6},{8,9},{9,8},{10,11... | collective-permute-start | bytes 1585160 | tf_op jit(solution)/shard_map/ppermute | solution.py:232

commit v3 on v2

v3 whole, which is shorter than its diff:
```python
import functools
import jax
import jax.numpy as jnp
from jax import lax
from jax.experimental import pallas as pl
from jax.experimental.pallas import tpu as pltpu
from jax.sharding import PartitionSpec as P

ITERS = 4
DAMPING = 0.5
START = 1.9
LANE = 128
QUAD = 4
AXES = ("groups", "dp", "cuts", "grad")
PARAMS = pltpu.CompilerParams(vmem_limit_bytes=48 * 1024 * 1024)


def half_blocks(order, half):
    count = order // LANE // 2
    own = range(half * count, (half + 1) * count)
    return [(i, j) for i in own for j in own if i < j], [(i, i + 1) for i in own[::2]]


def joining_blocks(order):
    count = order // LANE
    return [(i, j) for i in range(count // 2) for j in range(count // 2, count)]


def part_rows(order):
    above, pairs = half_blocks(order, 0)
    own = (len(above) + len(pairs)) * LANE + -(-len(pairs) // 8) * 8
    return len(joining_blocks(order)) * LANE + own, own


def places():
    rows = lax.broadcasted_iota(jnp.int32, (LANE, LANE), 0)
    cols = lax.broadcasted_iota(jnp.int32, (LANE, LANE), 1)
    return rows, cols


def pack(block, order, a_ref, b_ref, second=None):
    rows, cols = places()

    def own(half):
        above, pairs = half_blocks(order, half)
        values = [block(i, j) for i, j in above]
        values += [jnp.where(rows <= cols, block(i, i), block(j, j)) for i, j in pairs]
        last = [jnp.sum(jnp.where(rows == cols, block(j, j), 0.0), axis=0, keepdims=True) for _, j in pairs]
        return values + [jnp.concatenate(last + [jnp.zeros((-len(pairs) % 8, LANE), jnp.float32)], 0)]

    def put(ref, values):
        top = 0
        for value in values:
            ref[top : top + value.shape[0], :] = value
            top += value.shape[0]

    joining = [block(i, j) for i, j in joining_blocks(order)]
    here, there = own(0), own(1)
    if second is not None:
        here, there = (
            [jnp.where(second, q, p) for p, q in zip(here, there)],
            [jnp.where(second, p, q) for p, q in zip(here, there)],
        )
    put(a_ref, joining + here)
    put(b_ref, there)


def unpack(a_piece, b_piece, order, out_ref, second=None, scale=1.0, shift=0.0):
    rows, cols = places()
    damping = jnp.where(rows == cols, shift, 0.0)

    def put(i, j, value):
        out_ref[i * LANE : (i + 1) * LANE, j * LANE : (j + 1) * LANE] = value

    joining = joining_blocks(order)
    for slot, (i, j) in enumerate(joining):
        value = a_piece(slot * LANE, (slot + 1) * LANE) * scale
        put(i, j, value)
        put(j, i, value.T)

    def own(piece, top):
        above, pairs = half_blocks(order, 0)
        count = len(above) + len(pairs)
        values = [piece(top + k * LANE, top + (k + 1) * LANE) for k in range(count)]
        top += count * LANE
        return values + [piece(top, top + -(-len(pairs) // 8) * 8)]

    here, there = own(a_piece, len(joining) * LANE), own(b_piece, 0)
    if second is not None:
        here, there = (
            [jnp.where(second, q, p) for p, q in zip(here, there)],
            [jnp.where(second, p, q) for p, q in zip(here, there)],
        )
    for half, values in ((0, here), (1, there)):
        above, pairs = half_blocks(order, half)
        for k, (i, j) in enumerate(above):
            value = values[k] * scale
            put(i, j, value)
            put(j, i, value.T)
        for k, (i, j) in enumerate(pairs):
            both = values[len(above) + k]
            turned = both.T
            put(i, i, jnp.where(rows <= cols, both, turned) * scale + damping)
            last = jnp.where(rows > cols, both, jnp.where(rows < cols, turned, values[-1][k : k + 1, :]))
            put(j, j, last * scale + damping)


def halves(value):
    high = value.astype(jnp.bfloat16)
    return high, (value - high.astype(jnp.float32)).astype(jnp.bfloat16)


def times(left, right):
    dot = functools.partial(jnp.dot, preferred_element_type=jnp.float32)
    return dot(left[0], right[0]) + (dot(left[0], right[1]) + dot(left[1], right[0]))


def rows_of(pair, start, stop):
    return pair[0][start:stop, :], pair[1][start:stop, :]


def upper_times(left, right):
    middle = left[0].shape[0] // 2
    top = times(rows_of(left, 0, middle), right)
    corner = times(rows_of(left, middle, 2 * middle), (right[0][:, middle:], right[1][:, middle:]))
    return top, corner


def whole(top, corner):
    middle = corner.shape[0]
    return jnp.concatenate([top, jnp.concatenate([top[:, middle:].T, corner], 1)], 0)


def cov_kernel(keep, acts_ref, outgrads_ref, out_ref):
    core = lax.axis_index("grad")

    def write(x_ref):
        x = x_ref[...]
        order = x.shape[1]
        split = part_rows(order)[0]
        total = lax.dot_general(x, x, (((0,), (0,)), ((), ())), preferred_element_type=jnp.float32)
        pack(block_of(total), order, out_ref.at[:split], out_ref.at[split:])

    @pl.when((core == 0) == keep)
    def _():
        write(acts_ref)

    @pl.when((core == 0) != keep)
    def _():
        write(outgrads_ref)


def block_of(value):
    return lambda i, j: value[i * LANE : (i + 1) * LANE, j * LANE : (j + 1) * LANE]


def chip_kernel(kept_ref, other_ref, own_rows_ref, other_rows_ref, chip_ref, rows_ref, outer_ref):
    chip_ref[...] = kept_ref[...] + other_ref[...]
    core = lax.axis_index("grad")
    rows, columns = own_rows_ref.shape

    def put(start, ref):
        for column in range(columns // LANE):
            rows_ref[start : start + rows, :] = ref[:, column * LANE : (column + 1) * LANE]
            start += rows

    for own in range(2):

        @pl.when(core == own)
        def _():
            put(own * rows * columns // LANE, own_rows_ref)
            put((1 - own) * rows * columns // LANE, other_rows_ref)

    used = 2 * rows * columns // LANE
    rows_ref[used:, :] = jnp.zeros((rows_ref.shape[0] - used, LANE), jnp.float32)

    @pl.when(is_middle())
    def _():
        outer_ref[...] = rows_ref[...]

    @pl.when(jnp.logical_not(is_middle()))
    def _():
        outer_ref[...] = chip_ref[...]


def inverse_kernel(scale, order, *refs):
    *sums, rows_ref, out_ref, direct_ref, factor_ref = refs
    split = part_rows(order)[0]

    def piece(start, stop):
        total = sums[0][start:stop, :]
        for ref in sums[1:]:
            total = total + ref[start:stop, :]
        return total

    unpack(piece, lambda a, b: piece(split + a, split + b), order, factor_ref, None, scale, DAMPING)
    factor = factor_ref[...]
    bound = jnp.max(jnp.sum(jnp.abs(factor), axis=0, keepdims=True), axis=1, keepdims=True) + 1e-06
    start = START / bound
    rows = lax.broadcasted_iota(jnp.int32, (order, order), 0)
    cols = lax.broadcasted_iota(jnp.int32, (order, order), 1)
    eye = jnp.where(rows == cols, 1.0, 0.0)
    total = eye - start * factor
    power_halves = halves(total)
    middle = order // 2
    for step in range(1, ITERS):
        power = whole(*upper_times(power_halves, power_halves))
        power_halves = halves(power)
        top, corner = upper_times(halves(total), power_halves)
        known = total + power
        top, corner = top + known[:middle], corner + known[middle:, middle:]
        if step < ITERS - 1:
            total = whole(top, corner)

    def block(i, j):
        if i < middle // LANE:
            value = block_of(top)(i, j)
        else:
            value = block_of(corner)(i - middle // LANE, j - middle // LANE)
        return start * (value + block_of(eye)(i, j))

    pack(block, order, out_ref.at[:split], out_ref.at[split:], lax.axis_index("cuts") % 2 == 1)

    @pl.when(is_middle())
    def _():
        direct_ref[...] = out_ref[...]

    @pl.when(jnp.logical_not(is_middle()))
    def _():
        direct_ref[...] = rows_ref[...]


def choose_kernel(which, *refs):
    *arrays, out_ref = refs
    index = which()
    for place, ref in enumerate(arrays):

        @pl.when(index == place)
        def _():
            out_ref[...] = ref[...]


def final_kernel(
    order,
    spread,
    own_ref,
    other_ref,
    own_rows_ref,
    other_rows_ref,
    outer_ref,
    outer_other_ref,
    direct_ref,
    direct_other_ref,
    out_ref,
    left_ref,
    right_ref,
    tile_ref,
):
    core = lax.axis_index("grad")
    position = lax.axis_index("dp") * lax.axis_size("grad") + core
    mine = lax.rem(position, spread)
    rows_dev = out_ref.shape[0]
    split = part_rows(order)[0]

    def reader(ref, top):
        return lambda start, stop: ref[top + start : top + stop, :]

    def fill(packed_ref, out_ref, second):
        unpack(reader(packed_ref, 0), reader(packed_ref, split), order, out_ref, second)

    left_second = lax.rem(lax.div(position, spread), 2) == 1
    right_second = lax.rem(lax.axis_index("cuts"), 2) == 1

    @pl.when(core != 0)
    def _():
        fill(own_ref, left_ref, left_second)
        fill(other_ref, right_ref, right_second)

    @pl.when(core == 0)
    def _():
        fill(other_ref, left_ref, left_second)
        fill(own_ref, right_ref, right_second)

    def place(position):
        return pl.ds(pl.multiple_of(position * rows_dev, rows_dev), rows_dev)

    tile_ref[place(mine), :] = own_rows_ref[...]
    tile_ref[place(mine ^ 1), :] = other_rows_ref[...]
    here = core == rows_core()
    for middle, refs in ((False, (outer_ref, outer_other_ref)), (True, (direct_ref, direct_other_ref))):
        for own, ref in zip((True, False), refs):

            @pl.when(jnp.logical_and(is_middle() == middle, here == own))
            def _():
                start = 0
                for turn in range(2):
                    for column in range(order // LANE):
                        tile_ref[place((mine // 2 ^ 1) * 2 + turn), column * LANE : (column + 1) * LANE] = ref[
                            start : start + rows_dev, :
                        ]
                        start += rows_dev

    left = left_ref[pl.ds(pl.multiple_of(mine * rows_dev, rows_dev), rows_dev), :]
    middle = times(halves(left), halves(tile_ref[...]))
    out_ref[...] = times(halves(middle), halves(right_ref[...]))


def call(kernel, shapes, scratch, *args):
    return pl.pallas_call(
        kernel,
        out_shape=[jax.ShapeDtypeStruct(shape, jnp.float32) for shape in shapes],
        scratch_shapes=scratch,
        compiler_params=PARAMS,
    )(*args)


class Plan:
    def __init__(self, groups, dp, cuts):
        self.groups, self.dp, self.cuts = groups, dp, cuts
        self.bases = range(0, dp, QUAD)

    def index(self, z, x, core):
        return (z * self.cuts + x % self.cuts) * 2 + core

    def roots(self, base, x):
        return base + 1 + x % 2, base + 2 - x % 2

    def one_way(self, pairs):
        pairs = list(pairs)
        size = self.dp * self.cuts * 2
        return [(group * size + a, group * size + b) for group in range(self.groups) for a, b in pairs]

    def swaps(self, pairs):
        size = self.dp * self.cuts * 2
        partner = {}
        for a, b in self.one_way(pairs):
            partner[a], partner[b] = b, a
        for device in range(size * self.groups):
            other = device ^ 1
            if other in partner:
                other = (device + size) % (2 * size) + device // (2 * size) * 2 * size
            if device not in partner and other not in partner and other < size * self.groups:
                partner[device], partner[other] = other, device
        return sorted(partner.items())

    def across(self, bit):
        return self.one_way(
            (self.index(z, x, core), self.index(z ^ bit, x, core))
            for z in range(self.dp)
            for x in range(self.cuts)
            for core in range(2)
        )

    def collect(self):
        far, near, outer = [], [], []
        for x in range(self.cuts):
            for base in self.bases:
                left, right = self.roots(base, x)
                left_root, right_root = self.index(left, x, 1), self.index(right, x, 0)
                far.append((self.index(right ^ 1, x, 0), left_root))
                far.append((self.index(left ^ 1, x, 1), right_root))
                near.append((self.index(right, x, 0), left_root))
                outer.append((self.index(left ^ 1, x, 0), left_root))
                outer.append((self.index(right ^ 1, x, 1), right_root))
        return self.one_way(far), self.swaps(near), self.swaps(outer)

    def spread(self):
        hops = [[] for turn in range(1, self.cuts)]
        direct = []
        relays = [[] for turn in range(1, self.cuts)]
        for x in range(self.cuts):
            for base in self.bases:
                left, right = self.roots(base, x)
                right_root, middle = self.index(right, x, 0), self.index(left, x, 0)
                hops[0].append((right_root, middle))
                left_root = self.index(left, x, 1)
                direct.append((right_root, self.index(right ^ 1, x, 0)))
                direct.append((left_root, self.index(left ^ 1, x, 1)))
                relays[0].append((middle, self.index(left ^ 1, x, 0)))
                if x // 2 != base // QUAD:
                    continue
                for turn in range(1, self.cuts):
                    abreast = self.index(left, x + turn, 1)
                    hops[turn - 1].append((left_root, abreast))
                    relays[turn - 1].append((abreast, self.index(left ^ 1, x + turn, 1)))
        return [self.swaps(pairs) for pairs in hops], self.swaps(direct), [self.swaps(pairs) for pairs in relays]

    def which(self):
        z, x, core = (lax.axis_index(name) for name in AXES[1:])
        zq, middle = lax.rem(z, QUAD), is_middle()
        block = lax.div(z, 2)
        turn = lax.rem(x + self.cuts - block, self.cuts)
        left = jnp.where(middle, turn, jnp.where(turn == 0, self.cuts, self.cuts + turn))
        right_root = 2 - lax.rem(x, 2)
        right = jnp.where(
            zq == right_root, 0, jnp.where(middle, 1, jnp.where((zq ^ 1) == right_root, self.cuts, self.cuts + 1))
        )
        return jnp.where(core == 1, left, right)


def is_middle():
    zq = lax.rem(lax.axis_index("dp"), QUAD)
    return jnp.logical_or(zq == 1, zq == 2)


def rows_core():
    zq = lax.rem(lax.axis_index("dp"), QUAD)
    left = 1 + lax.rem(lax.axis_index("cuts"), 2)
    return jnp.where(is_middle(), zq == left, (zq ^ 1) != left).astype(jnp.int32)


def swap_cores(array):
    return lax.ppermute(array, "grad", [(0, 1), (1, 0)])


def per_device(acts, outgrads, grads):
    groups, dp, cuts, cores = (lax.axis_size(name) for name in AXES)
    tok_rows, order = acts.shape[1:]
    dev_count = dp * cores
    spread = dev_count // cuts
    plan = Plan(groups, dp, cuts)
    split, rest = part_rows(order)
    shape = (split + rest, LANE)
    acts, outgrads, grads = acts[0], outgrads[0], grads[0]

    (sent,), (kept,) = (
        call(functools.partial(cov_kernel, keep), [shape], [], acts, outgrads) for keep in (False, True)
    )
    other_rows = swap_cores(grads)
    chip, rows, outer = call(chip_kernel, [shape] * 3, [], kept, swap_cores(sent), grads, other_rows)
    bit = QUAD
    while bit < dp:
        chip = chip + lax.ppermute(chip, AXES, plan.across(bit))
        outer = jnp.where(is_middle(), outer, chip)
        bit *= 2
    far, near, outward = plan.collect()
    sums = [lax.ppermute(array, AXES, pairs) for array, pairs in ((chip, far), (chip, near), (outer, outward))]
    outer_rows = sums[2]
    sums.append(swap_cores(chip))
    scale = 1.0 / (tok_rows * dev_count)
    square_scratch = pltpu.VMEM((order, order), jnp.float32)
    inverse, direct = call(
        functools.partial(inverse_kernel, scale, order), [shape] * 2, [square_scratch], *sums, rows
    )

    hops, outward, relays = plan.spread()
    hopped = [lax.ppermute(inverse, AXES, pairs) for pairs in hops]
    direct = lax.ppermute(direct, AXES, outward)
    relayed = [lax.ppermute(array, AXES, pairs) for array, pairs in zip(hopped, relays)]
    (own,) = call(functools.partial(choose_kernel, plan.which), [shape], [], inverse, *hopped, direct, *relayed)
    (out,) = call(
        functools.partial(final_kernel, order, spread),
        [grads.shape],
        [square_scratch] * 3,
        own,
        swap_cores(own),
        grads,
        other_rows,
        outer_rows,
        swap_cores(outer_rows),
        direct,
        swap_cores(direct),
    )
    return out[None]


def solution(mesh):
    in_specs = (
        P(None, ("groups", "dp", "grad"), "cuts"),
        P(None, ("groups", "dp", "grad"), "cuts"),
        P("groups", ("dp", "grad"), "cuts"),
    )
    out_specs = P("groups", ("dp", "grad"), "cuts")
    return jax.shard_map(
        per_device, mesh=mesh, in_specs=in_specs, out_specs=out_specs, check_vma=False
    )
```

time: 54.7 us -> 50.7 us (0.927)
  the two profiles are of different devices: /device:TPU:0 before, /device:TPU:11 now
where the time goes in v3:
time: 50.7 us; the launch traced here: 50.5 us
  waiting for transfers between devices  22 us (43%)
  starting transfers between devices  18.3 us (36%)
  Pallas kernels  8.13 us (16%)
  local copies, waits for them, and re-layouts  1.99 us (4%)
    ppermute x4, waiting for transfers between devices, per_device(): lax.ppermute(array, AXES, pairs)  13.7 us
    ppermute x6, starting transfers between devices, swap_cores(): return lax.ppermute(array, 'grad', [(0, 1), (1, 0)])  12.2 us
    pallas_call x6, Pallas kernels, call(): pl.pallas_call(kernel, out_shape=[jax.ShapeDtypeStruct(shape, jnp.float32...  8.13 us
    ppermute x1, waiting for transfers between devices, per_device(): hopped = [lax.ppermute(inverse, AXES, pairs) for pairs in hops]  5.71 us
    ppermute x6, waiting for transfers between devices, swap_cores(): return lax.ppermute(array, 'grad', [(0, 1), (1, 0)])  2.59 us
    ppermute x1, starting transfers between devices, per_device(): hopped = [lax.ppermute(inverse, AXES, pairs) for pairs in hops]  2.58 us
    ppermute x4, starting transfers between devices, per_device(): lax.ppermute(array, AXES, pairs)  2.23 us
    unnamed x6, local copies, waits for them, and re-layouts  1.99 us
  transfers between devices with their start and end apart: 12, of which 6 were waited for; matrix products, arithmetic and copies ran while one was open for 0% of the time, Pallas kernels for 1%

profile of v3, /device:TPU:11, one launch (start us, length us, event | category | flops | bytes accessed | tf_op | source)
XLA Modules:
  0.0 50.5 jit_solution(7360522952909396715)
XLA Ops:
  0.0 0.0 copy-start
  0.0 1.0 %copy-done = bf16[1,384,512]{2,1,0:T(8,128)(2,1)S(1)} copy-done((bf16[1,384,512]{2,1,0:T(8,128)(2,1)S(1)}, bf16[1,384,512]{2,1,0:T(8,128)(2,1)}, u32[]{:S(2)}) %copy-start) | copy-done | bytes 393240
  1.0 0.0 copy-start.1
  1.0 1.0 %copy-done.1 = bf16[1,384,512]{2,1,0:T(8,128)(2,1)S(1)} copy-done((bf16[1,384,512]{2,1,0:T(8,128)(2,1)S(1)}, bf16[1,384,512]{2,1,0:T(8,128)(2,1)}, u32[]{:S(2)}) %copy-start.1) | copy-done | bytes 393240
  2.0 0.0 copy-start.2
  2.0 0.5 shard_map.38
  2.5 0.7 %collective-permute-start = (f32[1040,128]{1,0:T(8,128)S(1)}, f32[1040,128]{1,0:T(8,128)S(1)}, u32[]{:S(2)}, u32[]{:S(2)}) collective-permute-start(f32[1040,128]{1,0:T(8,128)S(1)} %shard_map.38), channel_id=1, source_target_pairs={{0,1},{1,0},{2,3},{3,2},{4,5},{5,4},{6,7},{7,6},{8,9},{9,8},{10,11... | collective-permute-start | bytes 1597448 | tf_op jit(solution)/shard_map/ppermute | solution.py:413
  3.2 0.0 copy-done.2
  3.2 0.4 collective-permute-start.1
  3.6 0.5 shard_map.37.kept_ref
  4.1 1.0 %collective-permute-done.1.other_rows_ref = f32[128,512]{1,0:T(8,128)S(1)} collective-permute-done((f32[128,512]{1,0:T(8,128)S(1)}, f32[128,512]{1,0:T(8,128)S(1)}, u32[]{:S(2)}, u32[]{:S(2)}) %collective-permute-start.1) | collective-permute-done | bytes 262176 | tf_op jit(solution)/shard_map/ppermute | solution.py:413
  5.1 0.0 collective-permute-done.other_ref
  5.1 0.1 shard_map.39
  5.3 0.7 %collective-permute-start.2 = (f32[1040,128]{1,0:T(8,128)S(1)}, f32[1040,128]{1,0:T(8,128)S(1)}, u32[]{:S(2)}, u32[]{:S(2)}) collective-permute-start(f32[1040,128]{1,0:T(8,128)S(1)} %get-tuple-element.10), channel_id=1, source_target_pairs={{12,5},{1,8},{2,11},{15,6},{28,21},{17,24},{18,27},{31,22}} | collective-permute-start | bytes 1597448 | tf_op jit(solution)/shard_map/ppermute | solution.py:437
  6.0 1.3 %collective-permute-start.3 = (f32[1040,128]{1,0:T(8,128)S(1)}, f32[1040,128]{1,0:T(8,128)S(1)}, u32[]{:S(2)}, u32[]{:S(2)}) collective-permute-start(f32[1040,128]{1,0:T(8,128)S(1)} %get-tuple-element.10), channel_id=1, source_target_pairs={{0,1},{1,0},{2,3},{3,2},{4,20},{5,8},{6,11},{7,23},{8,5},{9,25},{1... | collective-permute-start | bytes 1597448 | tf_op jit(solution)/shard_map/ppermute | solution.py:437
  7.3 0.2 collective-permute-start.4
  7.5 3.0 %collective-permute-start.5 = (f32[1040,128]{1,0:T(8,128)S(1)}, f32[1040,128]{1,0:T(8,128)S(1)}, u32[]{:S(2)}, u32[]{:S(2)}) collective-permute-start(f32[1040,128]{1,0:T(8,128)S(1)} %get-tuple-element.10), channel_id=1, source_target_pairs={{0,1},{1,0},{2,3},{3,2},{4,5},{5,4},{6,7},{7,6},{8,9},{9,8},{10,11... | collective-permute-start | bytes 1597448 | tf_op jit(solution)/shard_map/ppermute | solution.py:413
  10.6 0.0 collective-permute-done.2.refs_0_
  10.6 3.9 %collective-permute-done.3.refs_1_ = f32[1040,128]{1,0:T(8,128)S(1)} collective-permute-done((f32[1040,128]{1,0:T(8,128)S(1)}, f32[1040,128]{1,0:T(8,128)S(1)}, u32[]{:S(2)}, u32[]{:S(2)}) %collective-permute-start.3) | collective-permute-done | bytes 532512 | tf_op jit(solution)/shard_map/ppermute | solution.py:437
  14.5 5.7 %collective-permute-done.4.refs_2_.outer_ref = f32[1040,128]{1,0:T(8,128)S(1)} collective-permute-done((f32[1040,128]{1,0:T(8,128)S(1)}, f32[1040,128]{1,0:T(8,128)S(1)}, u32[]{:S(2)}, u32[]{:S(2)}) %collective-permute-start.4) | collective-permute-done | bytes 532512 | tf_op jit(solution)/shard_map/ppermute | solution.py:437
  20.2 0.0 collective-permute-done.5.refs_3_
  20.2 5.1 %shard_map.40 = (f32[1040,128]{1,0:T(8,128)S(1)}, f32[1040,128]{1,0:T(8,128)S(1)}) custom-call(f32[1040,128]{1,0:T(8,128)S(1)} %collective-permute-done.2.refs_0_, f32[1040,128]{1,0:T(8,128)S(1)} %collective-permute-done.3.refs_1_, f32[1040,128]{1,0:T(8,128)S(1)} %collective-permute-done.4.refs_2_.outer_ref, f32[1040,128]{1,0:T(8,128)S(1)} %collective-permute-done.5.refs_3_, ...), custom_call_target="tpu_custom_call" | custom-call | tf_op jit(solution)/shard_map/pallas_call | solution.py:309
  25.3 2.6 %collective-permute-start.6 = (f32[1040,128]{1,0:T(8,128)S(1)}, f32[1040,128]{1,0:T(8,128)S(1)}, u32[]{:S(2)}, u32[]{:S(2)}) collective-permute-start(f32[1040,128]{1,0:T(8,128)S(1)} %get-tuple-element.13.refs_0_), channel_id=1, source_target_pairs={{0,1},{1,0},{2,3},{3,2},{4,8},{5,7},{6,10},{7,5},{8,4},{9,11},{10,... | collective-permute-start | bytes 1597448 | tf_op jit(solution)/shard_map/ppermute | solution.py:447
  27.9 1.2 %collective-permute-start.7 = (f32[1040,128]{1,0:T(8,128)S(1)}, f32[1040,128]{1,0:T(8,128)S(1)}, u32[]{:S(2)}, u32[]{:S(2)}) collective-permute-start(f32[1040,128]{1,0:T(8,128)S(1)} %get-tuple-element.14), channel_id=1, source_target_pairs={{0,16},{1,5},{2,6},{3,19},{4,20},{5,1},{6,2},{7,23},{8,12},{9,25},... | collective-permute-start | bytes 1597448 | tf_op jit(solution)/shard_map/ppermute | solution.py:448
  29.1 5.7 %collective-permute-done.6.refs_1_ = f32[1040,128]{1,0:T(8,128)S(1)} collective-permute-done((f32[1040,128]{1,0:T(8,128)S(1)}, f32[1040,128]{1,0:T(8,128)S(1)}, u32[]{:S(2)}, u32[]{:S(2)}) %collective-permute-start.6) | collective-permute-done | bytes 532512 | tf_op jit(solution)/shard_map/ppermute | solution.py:447
  34.8 0.0 collective-permute-start.8
  34.8 4.3 %collective-permute-start.10 = (f32[1040,128]{1,0:T(8,128)S(1)}, f32[1040,128]{1,0:T(8,128)S(1)}, u32[]{:S(2)}, u32[]{:S(2)}) collective-permute-start(f32[1040,128]{1,0:T(8,128)S(1)} %collective-permute-done.4.refs_2_.outer_ref), channel_id=1, source_target_pairs={{0,1},{1,0},{2,3},{3,2},{4,5},{5,4},{6,7},{7,6},{8,9},{9,8},{10,11... | collective-permute-start | bytes 1597448 | tf_op jit(solution)/shard_map/ppermute | solution.py:413
  39.1 0.0 collective-permute-done.7.refs_2_.direct_ref
  39.1 0.0 collective-permute-start.11
  39.1 4.1 %collective-permute-done.8.refs_3_ = f32[1040,128]{1,0:T(8,128)S(1)} collective-permute-done((f32[1040,128]{1,0:T(8,128)S(1)}, f32[1040,128]{1,0:T(8,128)S(1)}, u32[]{:S(2)}, u32[]{:S(2)}) %collective-permute-start.8) | collective-permute-done | bytes 532512 | tf_op jit(solution)/shard_map/ppermute | solution.py:449
  43.3 3.7 %collective-permute-start.9 = (f32[1040,128]{1,0:T(8,128)S(1)}, f32[1040,128]{1,0:T(8,128)S(1)}, u32[]{:S(2)}, u32[]{:S(2)}) collective-permute-start(f32[1040,128]{1,0:T(8,128)S(1)} %shard_map.41.own_ref), channel_id=1, source_target_pairs={{0,1},{1,0},{2,3},{3,2},{4,5},{5,4},{6,7},{7,6},{8,9},{9,8},{10,11... | collective-permute-start | bytes 1597448 | tf_op jit(solution)/shard_map/ppermute | solution.py:413
  47.0 0.0 collective-permute-done.10.outer_other_ref
  47.0 0.0 collective-permute-done.11.direct_other_ref
  47.0 1.5 %collective-permute-done.9.other_ref = f32[1040,128]{1,0:T(8,128)S(1)} collective-permute-done((f32[1040,128]{1,0:T(8,128)S(1)}, f32[1040,128]{1,0:T(8,128)S(1)}, u32[]{:S(2)}, u32[]{:S(2)}) %collective-permute-start.9) | collective-permute-done | bytes 532512 | tf_op jit(solution)/shard_map/ppermute | solution.py:413
  48.5 1.9 %shard_map.42 = f32[128,512]{1,0:T(8,128)} custom-call(f32[1040,128]{1,0:T(8,128)S(1)} %shard_map.41.own_ref, f32[1040,128]{1,0:T(8,128)S(1)} %collective-permute-done.9.other_ref, f32[128,512]{1,0:T(8,128)S(1)} %bitcast.10, f32[128,512]{1,0:T(8,128)S(1)} %collective-permute-done.1.other_rows_ref, f32[1040,128]{1,0:T(8,128)S(1)} %collective-permute-done.4.refs_2_.outer_ref, ...), custom_call_target="tpu_custom_call" | custom-call | tf_op jit(solution)/shard_map/pallas_call | solution.py:309
  (1 shorter events, 0.0 us)
Async XLA Ops:
  0.0 1.0 %copy-start = (bf16[1,384,512]{2,1,0:T(8,128)(2,1)S(1)}, bf16[1,384,512]{2,1,0:T(8,128)(2,1)}, u32[]{:S(2)}) copy-start(bf16[1,384,512]{2,1,0:T(8,128)(2,1)} %param.3) | copy-start | bytes 1179652
  1.0 1.0 %copy-start.1 = (bf16[1,384,512]{2,1,0:T(8,128)(2,1)S(1)}, bf16[1,384,512]{2,1,0:T(8,128)(2,1)}, u32[]{:S(2)}) copy-start(bf16[1,384,512]{2,1,0:T(8,128)(2,1)} %param.4) | copy-start | bytes 1179652
  2.0 1.2 %copy-start.2 = (f32[1,128,512]{2,1,0:T(8,128)S(1)}, f32[1,128,512]{2,1,0:T(8,128)}, u32[]{:S(2)}) copy-start(f32[1,128,512]{2,1,0:T(8,128)} %param.5) | copy-start | bytes 786436
  2.5 2.7 %collective-permute-start = (f32[1040,128]{1,0:T(8,128)S(1)}, f32[1040,128]{1,0:T(8,128)S(1)}, u32[]{:S(2)}, u32[]{:S(2)}) collective-permute-start(f32[1040,128]{1,0:T(8,128)S(1)} %shard_map.38), channel_id=1, source_target_pairs={{0,1},{1,0},{2,3},{3,2},{4,5},{5,4},{6,7},{7,6},{8,9},{9,8},{10,11... | collective-permute-start | bytes 1597448 | tf_op jit(solution)/shard_map/ppermute | solution.py:413
  3.2 1.9 %collective-permute-start.1 = (f32[128,512]{1,0:T(8,128)S(1)}, f32[128,512]{1,0:T(8,128)S(1)}, u32[]{:S(2)}, u32[]{:S(2)}) collective-permute-start(f32[128,512]{1,0:T(8,128)S(1)} %bitcast.8), channel_id=1, source_target_pairs={{0,1},{1,0},{2,3},{3,2},{4,5},{5,4},{6,7},{7,6},{8,9},{9,8},{10,11... | collective-permute-start | bytes 786440 | tf_op jit(solution)/shard_map/ppermute | solution.py:413
  5.3 5.3 %collective-permute-start.2 = (f32[1040,128]{1,0:T(8,128)S(1)}, f32[1040,128]{1,0:T(8,128)S(1)}, u32[]{:S(2)}, u32[]{:S(2)}) collective-permute-start(f32[1040,128]{1,0:T(8,128)S(1)} %get-tuple-element.10), channel_id=1, source_target_pairs={{12,5},{1,8},{2,11},{15,6},{28,21},{17,24},{18,27},{31,22}} | collective-permute-start | bytes 1597448 | tf_op jit(solution)/shard_map/ppermute | solution.py:437
  6.0 8.5 %collective-permute-start.3 = (f32[1040,128]{1,0:T(8,128)S(1)}, f32[1040,128]{1,0:T(8,128)S(1)}, u32[]{:S(2)}, u32[]{:S(2)}) collective-permute-start(f32[1040,128]{1,0:T(8,128)S(1)} %get-tuple-element.10), channel_id=1, source_target_pairs={{0,1},{1,0},{2,3},{3,2},{4,20},{5,8},{6,11},{7,23},{8,5},{9,25},{1... | collective-permute-start | bytes 1597448 | tf_op jit(solution)/shard_map/ppermute | solution.py:437
  7.3 12.9 %collective-permute-start.4 = (f32[1040,128]{1,0:T(8,128)S(1)}, f32[1040,128]{1,0:T(8,128)S(1)}, u32[]{:S(2)}, u32[]{:S(2)}) collective-permute-start(f32[1040,128]{1,0:T(8,128)S(1)} %get-tuple-element.11), channel_id=1, source_target_pairs={{0,5},{1,17},{2,18},{3,6},{4,20},{5,0},{6,3},{7,23},{8,13},{9,25},... | collective-permute-start | bytes 1597448 | tf_op jit(solution)/shard_map/ppermute | solution.py:437
  7.5 12.7 %collective-permute-start.5 = (f32[1040,128]{1,0:T(8,128)S(1)}, f32[1040,128]{1,0:T(8,128)S(1)}, u32[]{:S(2)}, u32[]{:S(2)}) collective-permute-start(f32[1040,128]{1,0:T(8,128)S(1)} %get-tuple-element.10), channel_id=1, source_target_pairs={{0,1},{1,0},{2,3},{3,2},{4,5},{5,4},{6,7},{7,6},{8,9},{9,8},{10,11... | collective-permute-start | bytes 1597448 | tf_op jit(solution)/shard_map/ppermute | solution.py:413
  25.3 9.5 %collective-permute-start.6 = (f32[1040,128]{1,0:T(8,128)S(1)}, f32[1040,128]{1,0:T(8,128)S(1)}, u32[]{:S(2)}, u32[]{:S(2)}) collective-permute-start(f32[1040,128]{1,0:T(8,128)S(1)} %get-tuple-element.13.refs_0_), channel_id=1, source_target_pairs={{0,1},{1,0},{2,3},{3,2},{4,8},{5,7},{6,10},{7,5},{8,4},{9,11},{10,... | collective-permute-start | bytes 1597448 | tf_op jit(solution)/shard_map/ppermute | solution.py:447
  27.9 11.3 %collective-permute-start.7 = (f32[1040,128]{1,0:T(8,128)S(1)}, f32[1040,128]{1,0:T(8,128)S(1)}, u32[]{:S(2)}, u32[]{:S(2)}) collective-permute-start(f32[1040,128]{1,0:T(8,128)S(1)} %get-tuple-element.14), channel_id=1, source_target_pairs={{0,16},{1,5},{2,6},{3,19},{4,20},{5,1},{6,2},{7,23},{8,12},{9,25},... | collective-permute-start | bytes 1597448 | tf_op jit(solution)/shard_map/ppermute | solution.py:448
  34.8 8.4 %collective-permute-start.8 = (f32[1040,128]{1,0:T(8,128)S(1)}, f32[1040,128]{1,0:T(8,128)S(1)}, u32[]{:S(2)}, u32[]{:S(2)}) collective-permute-start(f32[1040,128]{1,0:T(8,128)S(1)} %collective-permute-done.6.refs_1_), channel_id=1, source_target_pairs={{0,4},{1,17},{2,18},{3,7},{4,0},{5,21},{6,22},{7,3},{8,24},{9,13},... | collective-permute-start | bytes 1597448 | tf_op jit(solution)/shard_map/ppermute | solution.py:449
  34.8 12.2 %collective-permute-start.10 = (f32[1040,128]{1,0:T(8,128)S(1)}, f32[1040,128]{1,0:T(8,128)S(1)}, u32[]{:S(2)}, u32[]{:S(2)}) collective-permute-start(f32[1040,128]{1,0:T(8,128)S(1)} %collective-permute-done.4.refs_2_.outer_ref), channel_id=1, source_target_pairs={{0,1},{1,0},{2,3},{3,2},{4,5},{5,4},{6,7},{7,6},{8,9},{9,8},{10,11... | collective-permute-start | bytes 1597448 | tf_op jit(solution)/shard_map/ppermute | solution.py:413
  39.1 7.9 %collective-permute-start.11 = (f32[1040,128]{1,0:T(8,128)S(1)}, f32[1040,128]{1,0:T(8,128)S(1)}, u32[]{:S(2)}, u32[]{:S(2)}) collective-permute-start(f32[1040,128]{1,0:T(8,128)S(1)} %collective-permute-done.7.refs_2_.direct_ref), channel_id=1, source_target_pairs={{0,1},{1,0},{2,3},{3,2},{4,5},{5,4},{6,7},{7,6},{8,9},{9,8},{10,11... | collective-permute-start | bytes 1597448 | tf_op jit(solution)/shard_map/ppermute | solution.py:413
  43.3 5.3 %collective-permute-start.9 = (f32[1040,128]{1,0:T(8,128)S(1)}, f32[1040,128]{1,0:T(8,128)S(1)}, u32[]{:S(2)}, u32[]{:S(2)}) collective-permute-start(f32[1040,128]{1,0:T(8,128)S(1)} %shard_map.41.own_ref), channel_id=1, source_target_pairs={{0,1},{1,0},{2,3},{3,2},{4,5},{5,4},{6,7},{7,6},{8,9},{9,8},{10,11... | collective-permute-start | bytes 1597448 | tf_op jit(solution)/shard_map/ppermute | solution.py:413

commit v4 on v3

--- a/solution.py
+++ b/solution.py
@@ -29,7 +29,7 @@
 def part_rows(order):
     above, pairs = half_blocks(order, 0)
     own = (len(above) + len(pairs)) * LANE + -(-len(pairs) // 8) * 8
-    return len(joining_blocks(order)) * LANE + own, own
+    return len(joining_blocks(order)) * LANE, 2 * own
 
 
 def places():
@@ -38,71 +38,51 @@
     return rows, cols
 
 
-def pack(block, order, a_ref, b_ref, second=None):
+def pack(block, order, a_ref, b_ref):
     rows, cols = places()
-
-    def own(half):
+    for slot, (i, j) in enumerate(joining_blocks(order)):
+        a_ref[slot * LANE : (slot + 1) * LANE, :] = block(i, j)
+    top = 0
+    for half in range(2):
         above, pairs = half_blocks(order, half)
         values = [block(i, j) for i, j in above]
         values += [jnp.where(rows <= cols, block(i, i), block(j, j)) for i, j in pairs]
         last = [jnp.sum(jnp.where(rows == cols, block(j, j), 0.0), axis=0, keepdims=True) for _, j in pairs]
-        return values + [jnp.concatenate(last + [jnp.zeros((-len(pairs) % 8, LANE), jnp.float32)], 0)]
-
-    def put(ref, values):
-        top = 0
+        values.append(jnp.concatenate(last + [jnp.zeros((-len(pairs) % 8, LANE), jnp.float32)], 0))
         for value in values:
-            ref[top : top + value.shape[0], :] = value
+            b_ref[top : top + value.shape[0], :] = value
             top += value.shape[0]
 
-    joining = [block(i, j) for i, j in joining_blocks(order)]
-    here, there = own(0), own(1)
-    if second is not None:
-        here, there = (
-            [jnp.where(second, q, p) for p, q in zip(here, there)],
-            [jnp.where(second, p, q) for p, q in zip(here, there)],
-        )
-    put(a_ref, joining + here)
-    put(b_ref, there)
-
-
-def unpack(a_piece, b_piece, order, out_ref, second=None, scale=1.0, shift=0.0):
+
+def unpack(a_piece, b_piece, order, out_ref, scale=1.0, shift=0.0):
     rows, cols = places()
     damping = jnp.where(rows == cols, shift, 0.0)
 
     def put(i, j, value):
         out_ref[i * LANE : (i + 1) * LANE, j * LANE : (j + 1) * LANE] = value
 
-    joining = joining_blocks(order)
-    for slot, (i, j) in enumerate(joining):
-        value = a_piece(slot * LANE, (slot + 1) * LANE) * scale
+    def put_both(i, j, value):
         put(i, j, value)
         put(j, i, value.T)
 
-    def own(piece, top):
-        above, pairs = half_blocks(order, 0)
-        count = len(above) + len(pairs)
-        values = [piece(top + k * LANE, top + (k + 1) * LANE) for k in range(count)]
-        top += count * LANE
-        return values + [piece(top, top + -(-len(pairs) // 8) * 8)]
-
-    here, there = own(a_piece, len(joining) * LANE), own(b_piece, 0)
-    if second is not None:
-        here, there = (
-            [jnp.where(second, q, p) for p, q in zip(here, there)],
-            [jnp.where(second, p, q) for p, q in zip(here, there)],
-        )
-    for half, values in ((0, here), (1, there)):
+    for slot, (i, j) in enumerate(joining_blocks(order)):
+        put_both(i, j, a_piece(slot * LANE, (slot + 1) * LANE) * scale)
+    top = 0
+    for half in range(2):
         above, pairs = half_blocks(order, half)
-        for k, (i, j) in enumerate(above):
-            value = values[k] * scale
-            put(i, j, value)
-            put(j, i, value.T)
+        for i, j in above:
+            put_both(i, j, b_piece(top, top + LANE) * scale)
+            top += LANE
+        after = top + len(pairs) * LANE
+        last = b_piece(after, after + -(-len(pairs) // 8) * 8)
         for k, (i, j) in enumerate(pairs):
-            both = values[len(above) + k]
+            both = b_piece(top, top + LANE)
             turned = both.T
             put(i, i, jnp.where(rows <= cols, both, turned) * scale + damping)
-            last = jnp.where(rows > cols, both, jnp.where(rows < cols, turned, values[-1][k : k + 1, :]))
-            put(j, j, last * scale + damping)
+            second = jnp.where(rows > cols, both, jnp.where(rows < cols, turned, last[k : k + 1, :]))
+            put(j, j, second * scale + damping)
+            top += LANE
+        top += last.shape[0]
 
 
 def halves(value):
@@ -126,28 +106,27 @@
     return top, corner
 
 
+def upper_square(value):
+    dot = functools.partial(jnp.dot, preferred_element_type=jnp.float32)
+    high, low = value
+    middle = high.shape[0] // 2
+    mixed = dot(high, low)
+    top = dot(high[:middle], high) + (mixed[:middle] + mixed[:, :middle].T)
+    corner = mixed[middle:, middle:]
+    return top, dot(high[middle:], high[:, middle:]) + (corner + corner.T)
+
+
 def whole(top, corner):
     middle = corner.shape[0]
     return jnp.concatenate([top, jnp.concatenate([top[:, middle:].T, corner], 1)], 0)
 
 
-def cov_kernel(keep, acts_ref, outgrads_ref, out_ref):
-    core = lax.axis_index("grad")
-
-    def write(x_ref):
-        x = x_ref[...]
-        order = x.shape[1]
-        split = part_rows(order)[0]
-        total = lax.dot_general(x, x, (((0,), (0,)), ((), ())), preferred_element_type=jnp.float32)
-        pack(block_of(total), order, out_ref.at[:split], out_ref.at[split:])
-
-    @pl.when((core == 0) == keep)
-    def _():
-        write(acts_ref)
-
-    @pl.when((core == 0) != keep)
-    def _():
-        write(outgrads_ref)
+def cov_kernel(x_ref, out_ref):
+    x = x_ref[...]
+    order = x.shape[1]
+    split = part_rows(order)[0]
+    total = lax.dot_general(x, x, (((0,), (0,)), ((), ())), preferred_element_type=jnp.float32)
+    pack(block_of(total), order, out_ref.at[:split], out_ref.at[split:])
 
 
 def block_of(value):
@@ -184,7 +163,7 @@
 
 
 def inverse_kernel(scale, order, *refs):
-    *sums, rows_ref, out_ref, direct_ref, factor_ref = refs
+    *sums, rows_ref, a_ref, b_ref, direct_ref, factor_ref = refs
     split = part_rows(order)[0]
 
     def piece(start, stop):
@@ -193,7 +172,7 @@
             total = total + ref[start:stop, :]
         return total
 
-    unpack(piece, lambda a, b: piece(split + a, split + b), order, factor_ref, None, scale, DAMPING)
+    unpack(piece, lambda a, b: piece(split + a, split + b), order, factor_ref, scale, DAMPING)
     factor = factor_ref[...]
     bound = jnp.max(jnp.sum(jnp.abs(factor), axis=0, keepdims=True), axis=1, keepdims=True) + 1e-06
     start = START / bound
@@ -204,7 +183,7 @@
     power_halves = halves(total)
     middle = order // 2
     for step in range(1, ITERS):
-        power = whole(*upper_times(power_halves, power_halves))
+        power = whole(*upper_square(power_halves))
         power_halves = halves(power)
         top, corner = upper_times(halves(total), power_halves)
         known = total + power
@@ -219,67 +198,52 @@
             value = block_of(corner)(i - middle // LANE, j - middle // LANE)
         return start * (value + block_of(eye)(i, j))
 
-    pack(block, order, out_ref.at[:split], out_ref.at[split:], lax.axis_index("cuts") % 2 == 1)
-
     @pl.when(is_middle())
     def _():
-        direct_ref[...] = out_ref[...]
+        pack(block, order, a_ref, b_ref)
+        direct_ref[:split, :] = a_ref[...]
+        direct_ref[split:, :] = b_ref[...]
 
     @pl.when(jnp.logical_not(is_middle()))
     def _():
+        a_ref[...] = rows_ref[:split, :]
+        b_ref[...] = rows_ref[split:, :]
         direct_ref[...] = rows_ref[...]
 
 
-def choose_kernel(which, *refs):
+def choose_kernel(which, start, *refs):
     *arrays, out_ref = refs
     index = which()
+    rows = out_ref.shape[0]
     for place, ref in enumerate(arrays):
+        first = 0 if ref.shape[0] == rows else start
 
         @pl.when(index == place)
         def _():
-            out_ref[...] = ref[...]
-
-
-def final_kernel(
-    order,
-    spread,
-    own_ref,
-    other_ref,
-    own_rows_ref,
-    other_rows_ref,
-    outer_ref,
-    outer_other_ref,
-    direct_ref,
-    direct_other_ref,
-    out_ref,
-    left_ref,
-    right_ref,
-    tile_ref,
-):
+            out_ref[...] = ref[first : first + rows, :]
+
+
+def final_kernel(order, spread, *refs):
+    own, other, refs = refs[:2], refs[2:4], refs[4:]
+    own_rows_ref, other_rows_ref, outer_ref, outer_other_ref, direct_ref, relayed_a, relayed_b, *refs = refs
+    out_ref, left_ref, right_ref, tile_ref = refs
     core = lax.axis_index("grad")
     position = lax.axis_index("dp") * lax.axis_size("grad") + core
     mine = lax.rem(position, spread)
     rows_dev = out_ref.shape[0]
-    split = part_rows(order)[0]
-
-    def reader(ref, top):
-        return lambda start, stop: ref[top + start : top + stop, :]
-
-    def fill(packed_ref, out_ref, second):
-        unpack(reader(packed_ref, 0), reader(packed_ref, split), order, out_ref, second)
-
-    left_second = lax.rem(lax.div(position, spread), 2) == 1
-    right_second = lax.rem(lax.axis_index("cuts"), 2) == 1
+    def fill(parts, out_ref):
+        a_ref, b_ref = parts
+        unpack(lambda start, stop: a_ref[start:stop, :], lambda start, stop: b_ref[start:stop, :], order, out_ref)
 
     @pl.when(core != 0)
     def _():
-        fill(own_ref, left_ref, left_second)
-        fill(other_ref, right_ref, right_second)
+        fill(own, left_ref)
+        fill(other, right_ref)
 
     @pl.when(core == 0)
     def _():
-        fill(other_ref, left_ref, left_second)
-        fill(own_ref, right_ref, right_second)
+        fill(other, left_ref)
+        fill(own, right_ref)
 
     def place(position):
         return pl.ds(pl.multiple_of(position * rows_dev, rows_dev), rows_dev)
@@ -287,18 +251,25 @@
     tile_ref[place(mine), :] = own_rows_ref[...]
     tile_ref[place(mine ^ 1), :] = other_rows_ref[...]
     here = core == rows_core()
-    for middle, refs in ((False, (outer_ref, outer_other_ref)), (True, (direct_ref, direct_other_ref))):
-        for own, ref in zip((True, False), refs):
-
-            @pl.when(jnp.logical_and(is_middle() == middle, here == own))
-            def _():
-                start = 0
-                for turn in range(2):
-                    for column in range(order // LANE):
-                        tile_ref[place((mine // 2 ^ 1) * 2 + turn), column * LANE : (column + 1) * LANE] = ref[
-                            start : start + rows_dev, :
-                        ]
-                        start += rows_dev
+    cases = (
+        (False, True, (outer_ref,)),
+        (False, False, (outer_other_ref,)),
+        (True, True, (direct_ref,)),
+        (True, False, (relayed_a, relayed_b)),
+    )
+    for middle, arrived, parts in cases:
+
+        @pl.when(jnp.logical_and(is_middle() == middle, here == arrived))
+        def _():
+            start, part = 0, 0
+            for turn in range(2):
+                for column in range(order // LANE):
+                    if start == parts[part].shape[0]:
+                        start, part = 0, part + 1
+                    tile_ref[place((mine // 2 ^ 1) * 2 + turn), column * LANE : (column + 1) * LANE] = parts[part][
+                        start : start + rows_dev, :
+                    ]
+                    start += rows_dev
 
     left = left_ref[pl.ds(pl.multiple_of(mine * rows_dev, rows_dev), rows_dev), :]
     middle = times(halves(left), halves(tile_ref[...]))
@@ -423,9 +394,9 @@
     shape = (split + rest, LANE)
     acts, outgrads, grads = acts[0], outgrads[0], grads[0]
 
-    (sent,), (kept,) = (
-        call(functools.partial(cov_kernel, keep), [shape], [], acts, outgrads) for keep in (False, True)
-    )
+    core = lax.axis_index("grad")
+    (sent,) = call(cov_kernel, [shape], [], jnp.where(core == 0, outgrads, acts))
+    (kept,) = call(cov_kernel, [shape], [], jnp.where(core == 0, acts, outgrads))
     other_rows = swap_cores(grads)
     chip, rows, outer = call(chip_kernel, [shape] * 3, [], kept, swap_cores(sent), grads, other_rows)
     bit = QUAD
@@ -439,27 +410,44 @@
     sums.append(swap_cores(chip))
     scale = 1.0 / (tok_rows * dev_count)
     square_scratch = pltpu.VMEM((order, order), jnp.float32)
-    inverse, direct = call(
-        functools.partial(inverse_kernel, scale, order), [shape] * 2, [square_scratch], *sums, rows
+    *inverse, direct = call(
+        functools.partial(inverse_kernel, scale, order),
+        [(split, LANE), (rest, LANE), shape],
+        [square_scratch],
+        *sums,
+        rows,
     )
 
     hops, outward, relays = plan.spread()
-    hopped = [lax.ppermute(inverse, AXES, pairs) for pairs in hops]
+    hopped = [[lax.ppermute(inverse[0], AXES, pairs) for pairs in hops]]
     direct = lax.ppermute(direct, AXES, outward)
-    relayed = [lax.ppermute(array, AXES, pairs) for array, pairs in zip(hopped, relays)]
-    (own,) = call(functools.partial(choose_kernel, plan.which), [shape], [], inverse, *hopped, direct, *relayed)
+    hopped.append([lax.ppermute(inverse[1], AXES, pairs) for pairs in hops])
+    own, relayed = [], []
+    for part, start in ((0, 0), (1, split)):
+        arrived = [lax.ppermute(array, AXES, pairs) for array, pairs in zip(hopped[part], relays)]
+        (chosen,) = call(
+            functools.partial(choose_kernel, plan.which, start),
+            [inverse[part].shape],
+            [],
+            inverse[part],
+            *hopped[part],
+            direct,
+            *arrived,
+        )
+        own.append(chosen)
+        relayed.append(arrived[0])
     (out,) = call(
         functools.partial(final_kernel, order, spread),
         [grads.shape],
         [square_scratch] * 3,
-        own,
-        swap_cores(own),
+        *own,
+        *map(swap_cores, own),
         grads,
         other_rows,
         outer_rows,
         swap_cores(outer_rows),
         direct,
-        swap_cores(direct),
+        *relayed,
     )
     return out[None]
 

time: 50.7 us -> 46.4 us (0.915)
  the two profiles are of different devices: /device:TPU:11 before, /device:TPU:0 now
where the time goes in v4:
time: 46.4 us; the launch traced here: 45.9 us
  starting transfers between devices  19.6 us (42%)
  waiting for transfers between devices  17.2 us (37%)
  Pallas kernels  7.85 us (17%)
  other arithmetic  1.17 us (3%)
    ppermute x5, starting transfers between devices, per_device(): lax.ppermute(array, AXES, pairs)  14.9 us
    ppermute x5, waiting for transfers between devices, per_device(): lax.ppermute(array, AXES, pairs)  12.1 us
    pallas_call x7, Pallas kernels, call(): pl.pallas_call(kernel, out_shape=[jax.ShapeDtypeStruct(shape, jnp.float32...  7.85 us
    ppermute x6, waiting for transfers between devices, swap_cores(): return lax.ppermute(array, 'grad', [(0, 1), (1, 0)])  2.57 us
    ppermute x1, waiting for transfers between devices, per_device(): direct = lax.ppermute(direct, AXES, outward)  2.56 us
    ppermute x6, starting transfers between devices, swap_cores(): return lax.ppermute(array, 'grad', [(0, 1), (1, 0)])  2.38 us
    ppermute x1, starting transfers between devices, per_device(): direct = lax.ppermute(direct, AXES, outward)  1.58 us
    select_n x1, other arithmetic, per_device(): sent, = call(cov_kernel, [shape], [], jnp.where(core == 0, outgrads, acts))  1.17 us
  transfers between devices with their start and end apart: 14, of which 6 were waited for; matrix products, arithmetic and copies ran while one was open for 0% of the time, Pallas kernels for 1%

profile of v4, /device:TPU:0, one launch (start us, length us, event | category | flops | bytes accessed | tf_op | source)
XLA Modules:
  0.0 45.9 jit_solution(720220452704659525)
XLA Ops:
  0.0 1.2 %select_bitcast_fusion = (bf16[384,512]{1,0:T(8,128)(2,1)S(1)}, bf16[384,512]{1,0:T(8,128)(2,1)S(1)}) fusion(bf16[1,384,512]{2,1,0:T(8,128)(2,1)} %param.4, bf16[1,384,512]{2,1,0:T(8,128)(2,1)} %param.3, pred[]{:T(512)S(6)} %eq.4), kind=kLoop, calls=%fused_computation | loop fusion | flops 393216 | bytes 1572865 | tf_op jit(solution)/shard_map/jit(_where)/select_n | solution.py:398
  1.2 0.0 copy-start
  1.2 0.5 %shard_map.38 = f32[1040,128]{1,0:T(8,128)S(1)} custom-call(bf16[384,512]{1,0:T(8,128)(2,1)S(1)} %get-tuple-element.17.x_ref), custom_call_target="tpu_custom_call" | custom-call | tf_op jit(solution)/shard_map/pallas_call | solution.py:280
  1.7 0.5 %collective-permute-start = (f32[1040,128]{1,0:T(8,128)S(1)}, f32[1040,128]{1,0:T(8,128)S(1)}, u32[]{:S(2)}, u32[]{:S(2)}) collective-permute-start(f32[1040,128]{1,0:T(8,128)S(1)} %shard_map.38), channel_id=1, source_target_pairs={{0,1},{1,0},{2,3},{3,2},{4,5},{5,4},{6,7},{7,6},{8,9},{9,8},{10,11... | collective-permute-start | bytes 1597448 | tf_op jit(solution)/shard_map/ppermute | solution.py:384
  2.2 0.0 copy-done
  2.2 0.4 collective-permute-start.1
  2.6 0.5 %shard_map.37.kept_ref = f32[1040,128]{1,0:T(8,128)S(1)} custom-call(bf16[384,512]{1,0:T(8,128)(2,1)S(1)} %get-tuple-element.18.x_ref), custom_call_target="tpu_custom_call" | custom-call | tf_op jit(solution)/shard_map/pallas_call | solution.py:280
  3.0 1.1 %collective-permute-done.1.other_rows_ref.refs_5_ = f32[128,512]{1,0:T(8,128)S(1)} collective-permute-done((f32[128,512]{1,0:T(8,128)S(1)}, f32[128,512]{1,0:T(8,128)S(1)}, u32[]{:S(2)}, u32[]{:S(2)}) %collective-permute-start.1) | collective-permute-done | bytes 262176 | tf_op jit(solution)/shard_map/ppermute | solution.py:384
  4.1 0.0 collective-permute-done.other_ref
  4.1 0.2 shard_map.39
  4.3 0.7 %collective-permute-start.2 = (f32[1040,128]{1,0:T(8,128)S(1)}, f32[1040,128]{1,0:T(8,128)S(1)}, u32[]{:S(2)}, u32[]{:S(2)}) collective-permute-start(f32[1040,128]{1,0:T(8,128)S(1)} %get-tuple-element.11), channel_id=1, source_target_pairs={{12,5},{1,8},{2,11},{15,6},{28,21},{17,24},{18,27},{31,22}} | collective-permute-start | bytes 1597448 | tf_op jit(solution)/shard_map/ppermute | solution.py:408
  5.0 5.4 %collective-permute-start.3 = (f32[1040,128]{1,0:T(8,128)S(1)}, f32[1040,128]{1,0:T(8,128)S(1)}, u32[]{:S(2)}, u32[]{:S(2)}) collective-permute-start(f32[1040,128]{1,0:T(8,128)S(1)} %get-tuple-element.11), channel_id=1, source_target_pairs={{0,1},{1,0},{2,3},{3,2},{4,20},{5,8},{6,11},{7,23},{8,5},{9,25},{1... | collective-permute-start | bytes 1597448 | tf_op jit(solution)/shard_map/ppermute | solution.py:408
  10.3 0.0 collective-permute-start.4
  10.3 1.3 %collective-permute-start.5 = (f32[1040,128]{1,0:T(8,128)S(1)}, f32[1040,128]{1,0:T(8,128)S(1)}, u32[]{:S(2)}, u32[]{:S(2)}) collective-permute-start(f32[1040,128]{1,0:T(8,128)S(1)} %get-tuple-element.11), channel_id=1, source_target_pairs={{0,1},{1,0},{2,3},{3,2},{4,5},{5,4},{6,7},{7,6},{8,9},{9,8},{10,11... | collective-permute-start | bytes 1597448 | tf_op jit(solution)/shard_map/ppermute | solution.py:384
  11.7 0.0 collective-permute-done.2.refs_0_
  11.7 0.2 collective-permute-done.3.refs_1_
  11.9 10.1 %collective-permute-done.4.refs_2_.refs_6_ = f32[1040,128]{1,0:T(8,128)S(1)} collective-permute-done((f32[1040,128]{1,0:T(8,128)S(1)}, f32[1040,128]{1,0:T(8,128)S(1)}, u32[]{:S(2)}, u32[]{:S(2)}) %collective-permute-start.4) | collective-permute-done | bytes 532512 | tf_op jit(solution)/shard_map/ppermute | solution.py:408
  22.0 0.0 collective-permute-done.5.refs_3_
  22.0 4.8 %shard_map.40 = (f32[512,128]{1,0:T(8,128)S(1)}, f32[528,128]{1,0:T(8,128)S(1)}, f32[1040,128]{1,0:T(8,128)S(1)}) custom-call(f32[1040,128]{1,0:T(8,128)S(1)} %collective-permute-done.2.refs_0_, f32[1040,128]{1,0:T(8,128)S(1)} %collective-permute-done.3.refs_1_, f32[1040,128]{1,0:T(8,128)S(1)} %collective-permute-done.4.refs_2_.refs_6_, ...), custom_call_target="tpu_custom_call" | custom-call | tf_op jit(solution)/shard_map/pallas_call | solution.py:280
  26.9 0.1 collective-permute-start.9
  27.0 1.6 %collective-permute-start.7 = (f32[1040,128]{1,0:T(8,128)S(1)}, f32[1040,128]{1,0:T(8,128)S(1)}, u32[]{:S(2)}, u32[]{:S(2)}) collective-permute-start(f32[1040,128]{1,0:T(8,128)S(1)} %get-tuple-element.15), channel_id=1, source_target_pairs={{0,16},{1,5},{2,6},{3,19},{4,20},{5,1},{6,2},{7,23},{8,12},{9,25},... | collective-permute-start | bytes 1597448 | tf_op jit(solution)/shard_map/ppermute | solution.py:423
  28.5 0.7 %collective-permute-start.6 = (f32[512,128]{1,0:T(8,128)S(1)}, f32[512,128]{1,0:T(8,128)S(1)}, u32[]{:S(2)}, u32[]{:S(2)}) collective-permute-start(f32[512,128]{1,0:T(8,128)S(1)} %get-tuple-element.14.refs_0_), channel_id=1, source_target_pairs={{0,1},{1,0},{2,3},{3,2},{4,8},{5,7},{6,10},{7,5},{8,4},{9,11},{10,... | collective-permute-start | bytes 786440 | tf_op jit(solution)/shard_map/ppermute | solution.py:422
  29.2 0.0 collective-permute-done.9.refs_1_
  29.2 5.4 %collective-permute-start.10 = (f32[528,128]{1,0:T(8,128)S(1)}, f32[528,128]{1,0:T(8,128)S(1)}, u32[]{:S(2)}, u32[]{:S(2)}) collective-permute-start(f32[528,128]{1,0:T(8,128)S(1)} %collective-permute-done.9.refs_1_), channel_id=1, source_target_pairs={{0,4},{1,17},{2,18},{3,7},{4,0},{5,21},{6,22},{7,3},{8,24},{9,13},... | collective-permute-start | bytes 811016 | tf_op jit(solution)/shard_map/ppermute | solution.py:427
  34.6 0.0 collective-permute-start.13
  34.6 0.0 collective-permute-done.6.refs_1_
  34.6 3.4 %collective-permute-start.8 = (f32[512,128]{1,0:T(8,128)S(1)}, f32[512,128]{1,0:T(8,128)S(1)}, u32[]{:S(2)}, u32[]{:S(2)}) collective-permute-start(f32[512,128]{1,0:T(8,128)S(1)} %collective-permute-done.6.refs_1_), channel_id=1, source_target_pairs={{0,4},{1,17},{2,18},{3,7},{4,0},{5,21},{6,22},{7,3},{8,24},{9,13},... | collective-permute-start | bytes 786440 | tf_op jit(solution)/shard_map/ppermute | solution.py:427
  38.0 2.6 %collective-permute-done.7.refs_2_.refs_8_ = f32[1040,128]{1,0:T(8,128)S(1)} collective-permute-done((f32[1040,128]{1,0:T(8,128)S(1)}, f32[1040,128]{1,0:T(8,128)S(1)}, u32[]{:S(2)}, u32[]{:S(2)}) %collective-permute-start.7) | collective-permute-done | bytes 532512 | tf_op jit(solution)/shard_map/ppermute | solution.py:423
  40.6 0.0 collective-permute-done.10.refs_3_.refs_10_
  40.6 0.1 collective-permute-start.12
  40.7 1.7 %collective-permute-done.8.refs_3_.refs_9_ = f32[512,128]{1,0:T(8,128)S(1)} collective-permute-done((f32[512,128]{1,0:T(8,128)S(1)}, f32[512,128]{1,0:T(8,128)S(1)}, u32[]{:S(2)}, u32[]{:S(2)}) %collective-permute-start.8) | collective-permute-done | bytes 262176 | tf_op jit(solution)/shard_map/ppermute | solution.py:427
  42.4 0.1 collective-permute-start.11
  42.5 0.0 collective-permute-done.13.refs_7_
  42.5 1.5 %collective-permute-done.11.refs_2_ = f32[512,128]{1,0:T(8,128)S(1)} collective-permute-done((f32[512,128]{1,0:T(8,128)S(1)}, f32[512,128]{1,0:T(8,128)S(1)}, u32[]{:S(2)}, u32[]{:S(2)}) %collective-permute-start.11) | collective-permute-done | bytes 262176 | tf_op jit(solution)/shard_map/ppermute | solution.py:384
  44.0 0.0 collective-permute-done.12.refs_3_
  44.0 1.9 %shard_map.43 = f32[128,512]{1,0:T(8,128)} custom-call(f32[512,128]{1,0:T(8,128)S(1)} %shard_map.41.refs_0_, f32[528,128]{1,0:T(8,128)S(1)} %shard_map.42.refs_1_, f32[512,128]{1,0:T(8,128)S(1)} %collective-permute-done.11.refs_2_, f32[528,128]{1,0:T(8,128)S(1)} %collective-permute-done.12.refs_3_, f32[128,512]{1,0:T(8,128)S(1)} %bitcast.8, ...), custom_call_target="tpu_custom_call" | custom-call | tf_op jit(solution)/shard_map/pallas_call | solution.py:280
  (2 shorter events, 0.0 us)
Async XLA Ops:
  1.2 1.0 %copy-start = (f32[1,128,512]{2,1,0:T(8,128)S(1)}, f32[1,128,512]{2,1,0:T(8,128)}, u32[]{:S(2)}) copy-start(f32[1,128,512]{2,1,0:T(8,128)} %param.5) | copy-start | bytes 786436
  1.7 2.4 %collective-permute-start = (f32[1040,128]{1,0:T(8,128)S(1)}, f32[1040,128]{1,0:T(8,128)S(1)}, u32[]{:S(2)}, u32[]{:S(2)}) collective-permute-start(f32[1040,128]{1,0:T(8,128)S(1)} %shard_map.38), channel_id=1, source_target_pairs={{0,1},{1,0},{2,3},{3,2},{4,5},{5,4},{6,7},{7,6},{8,9},{9,8},{10,11... | collective-permute-start | bytes 1597448 | tf_op jit(solution)/shard_map/ppermute | solution.py:384
  2.2 1.9 %collective-permute-start.1 = (f32[128,512]{1,0:T(8,128)S(1)}, f32[128,512]{1,0:T(8,128)S(1)}, u32[]{:S(2)}, u32[]{:S(2)}) collective-permute-start(f32[128,512]{1,0:T(8,128)S(1)} %bitcast.6), channel_id=1, source_target_pairs={{0,1},{1,0},{2,3},{3,2},{4,5},{5,4},{6,7},{7,6},{8,9},{9,8},{10,11... | collective-permute-start | bytes 786440 | tf_op jit(solution)/shard_map/ppermute | solution.py:384
  4.3 7.4 %collective-permute-start.2 = (f32[1040,128]{1,0:T(8,128)S(1)}, f32[1040,128]{1,0:T(8,128)S(1)}, u32[]{:S(2)}, u32[]{:S(2)}) collective-permute-start(f32[1040,128]{1,0:T(8,128)S(1)} %get-tuple-element.11), channel_id=1, source_target_pairs={{12,5},{1,8},{2,11},{15,6},{28,21},{17,24},{18,27},{31,22}} | collective-permute-start | bytes 1597448 | tf_op jit(solution)/shard_map/ppermute | solution.py:408
  5.0 6.9 %collective-permute-start.3 = (f32[1040,128]{1,0:T(8,128)S(1)}, f32[1040,128]{1,0:T(8,128)S(1)}, u32[]{:S(2)}, u32[]{:S(2)}) collective-permute-start(f32[1040,128]{1,0:T(8,128)S(1)} %get-tuple-element.11), channel_id=1, source_target_pairs={{0,1},{1,0},{2,3},{3,2},{4,20},{5,8},{6,11},{7,23},{8,5},{9,25},{1... | collective-permute-start | bytes 1597448 | tf_op jit(solution)/shard_map/ppermute | solution.py:408
  10.3 11.7 %collective-permute-start.4 = (f32[1040,128]{1,0:T(8,128)S(1)}, f32[1040,128]{1,0:T(8,128)S(1)}, u32[]{:S(2)}, u32[]{:S(2)}) collective-permute-start(f32[1040,128]{1,0:T(8,128)S(1)} %get-tuple-element.12), channel_id=1, source_target_pairs={{0,5},{1,17},{2,18},{3,6},{4,20},{5,0},{6,3},{7,23},{8,13},{9,25},... | collective-permute-start | bytes 1597448 | tf_op jit(solution)/shard_map/ppermute | solution.py:408
  10.3 11.7 %collective-permute-start.5 = (f32[1040,128]{1,0:T(8,128)S(1)}, f32[1040,128]{1,0:T(8,128)S(1)}, u32[]{:S(2)}, u32[]{:S(2)}) collective-permute-start(f32[1040,128]{1,0:T(8,128)S(1)} %get-tuple-element.11), channel_id=1, source_target_pairs={{0,1},{1,0},{2,3},{3,2},{4,5},{5,4},{6,7},{7,6},{8,9},{9,8},{10,11... | collective-permute-start | bytes 1597448 | tf_op jit(solution)/shard_map/ppermute | solution.py:384
  26.9 2.4 %collective-permute-start.9 = (f32[528,128]{1,0:T(8,128)S(1)}, f32[528,128]{1,0:T(8,128)S(1)}, u32[]{:S(2)}, u32[]{:S(2)}) collective-permute-start(f32[528,128]{1,0:T(8,128)S(1)} %get-tuple-element.16.refs_0_), channel_id=1, source_target_pairs={{0,1},{1,0},{2,3},{3,2},{4,8},{5,7},{6,10},{7,5},{8,4},{9,11},{10,... | collective-permute-start | bytes 811016 | tf_op jit(solution)/shard_map/ppermute | solution.py:424
  27.0 13.6 %collective-permute-start.7 = (f32[1040,128]{1,0:T(8,128)S(1)}, f32[1040,128]{1,0:T(8,128)S(1)}, u32[]{:S(2)}, u32[]{:S(2)}) collective-permute-start(f32[1040,128]{1,0:T(8,128)S(1)} %get-tuple-element.15), channel_id=1, source_target_pairs={{0,16},{1,5},{2,6},{3,19},{4,20},{5,1},{6,2},{7,23},{8,12},{9,25},... | collective-permute-start | bytes 1597448 | tf_op jit(solution)/shard_map/ppermute | solution.py:423
  28.5 6.1 %collective-permute-start.6 = (f32[512,128]{1,0:T(8,128)S(1)}, f32[512,128]{1,0:T(8,128)S(1)}, u32[]{:S(2)}, u32[]{:S(2)}) collective-permute-start(f32[512,128]{1,0:T(8,128)S(1)} %get-tuple-element.14.refs_0_), channel_id=1, source_target_pairs={{0,1},{1,0},{2,3},{3,2},{4,8},{5,7},{6,10},{7,5},{8,4},{9,11},{10,... | collective-permute-start | bytes 786440 | tf_op jit(solution)/shard_map/ppermute | solution.py:422
  29.2 11.4 %collective-permute-start.10 = (f32[528,128]{1,0:T(8,128)S(1)}, f32[528,128]{1,0:T(8,128)S(1)}, u32[]{:S(2)}, u32[]{:S(2)}) collective-permute-start(f32[528,128]{1,0:T(8,128)S(1)} %collective-permute-done.9.refs_1_), channel_id=1, source_target_pairs={{0,4},{1,17},{2,18},{3,7},{4,0},{5,21},{6,22},{7,3},{8,24},{9,13},... | collective-permute-start | bytes 811016 | tf_op jit(solution)/shard_map/ppermute | solution.py:427
  34.6 7.9 %collective-permute-start.13 = (f32[1040,128]{1,0:T(8,128)S(1)}, f32[1040,128]{1,0:T(8,128)S(1)}, u32[]{:S(2)}, u32[]{:S(2)}) collective-permute-start(f32[1040,128]{1,0:T(8,128)S(1)} %collective-permute-done.4.refs_2_.refs_6_), channel_id=1, source_target_pairs={{0,1},{1,0},{2,3},{3,2},{4,5},{5,4},{6,7},{7,6},{8,9},{9,8},{10,11... | collective-permute-start | bytes 1597448 | tf_op jit(solution)/shard_map/ppermute | solution.py:384
  34.6 7.8 %collective-permute-start.8 = (f32[512,128]{1,0:T(8,128)S(1)}, f32[512,128]{1,0:T(8,128)S(1)}, u32[]{:S(2)}, u32[]{:S(2)}) collective-permute-start(f32[512,128]{1,0:T(8,128)S(1)} %collective-permute-done.6.refs_1_), channel_id=1, source_target_pairs={{0,4},{1,17},{2,18},{3,7},{4,0},{5,21},{6,22},{7,3},{8,24},{9,13},... | collective-permute-start | bytes 786440 | tf_op jit(solution)/shard_map/ppermute | solution.py:427
  40.6 3.4 %collective-permute-start.12 = (f32[528,128]{1,0:T(8,128)S(1)}, f32[528,128]{1,0:T(8,128)S(1)}, u32[]{:S(2)}, u32[]{:S(2)}) collective-permute-start(f32[528,128]{1,0:T(8,128)S(1)} %shard_map.42.refs_1_), channel_id=1, source_target_pairs={{0,1},{1,0},{2,3},{3,2},{4,5},{5,4},{6,7},{7,6},{8,9},{9,8},{10,11... | collective-permute-start | bytes 811016 | tf_op jit(solution)/shard_map/ppermute | solution.py:384
  42.4 1.6 %collective-permute-start.11 = (f32[512,128]{1,0:T(8,128)S(1)}, f32[512,128]{1,0:T(8,128)S(1)}, u32[]{:S(2)}, u32[]{:S(2)}) collective-permute-start(f32[512,128]{1,0:T(8,128)S(1)} %shard_map.41.refs_0_), channel_id=1, source_target_pairs={{0,1},{1,0},{2,3},{3,2},{4,5},{5,4},{6,7},{7,6},{8,9},{9,8},{10,11... | collective-permute-start | bytes 786440 | tf_op jit(solution)/shard_map/ppermute | solution.py:384

commit v5 on v4

--- a/solution.py
+++ b/solution.py
@@ -85,6 +85,28 @@
         top += last.shape[0]
 
 
+def stored_block(a_ref, b_ref, order, i, j):
+    if i > j:
+        return stored_block(a_ref, b_ref, order, j, i).T
+    if (i, j) in joining_blocks(order):
+        start = joining_blocks(order).index((i, j)) * LANE
+        return a_ref[start : start + LANE, :]
+    half = i // (order // LANE // 2)
+    above, pairs = half_blocks(order, half)
+    top = half * part_rows(order)[1] // 2
+    if i < j:
+        start = top + above.index((i, j)) * LANE
+        return b_ref[start : start + LANE, :]
+    place = next(k for k, pair in enumerate(pairs) if i in pair)
+    start = top + (len(above) + place) * LANE
+    both = b_ref[start : start + LANE, :]
+    rows, cols = places()
+    if i == pairs[place][0]:
+        return jnp.where(rows <= cols, both, both.T)
+    start = top + (len(above) + len(pairs)) * LANE + place
+    return jnp.where(rows > cols, both, jnp.where(rows < cols, both.T, b_ref[start : start + 1, :]))
+
+
 def halves(value):
     high = value.astype(jnp.bfloat16)
     return high, (value - high.astype(jnp.float32)).astype(jnp.bfloat16)
@@ -92,7 +114,9 @@
 
 def times(left, right):
     dot = functools.partial(jnp.dot, preferred_element_type=jnp.float32)
-    return dot(left[0], right[0]) + (dot(left[0], right[1]) + dot(left[1], right[0]))
+    rows = left[0].shape[0]
+    both = dot(jnp.concatenate(left, 0), right[0])
+    return both[:rows] + (dot(left[0], right[1]) + both[rows:])
 
 
 def rows_of(pair, start, stop):
@@ -226,24 +250,30 @@
 def final_kernel(order, spread, *refs):
     own, other, refs = refs[:2], refs[2:4], refs[4:]
     own_rows_ref, other_rows_ref, outer_ref, outer_other_ref, direct_ref, relayed_a, relayed_b, *refs = refs
-    out_ref, left_ref, right_ref, tile_ref = refs
+    out_ref, left_ref, right_ref, tile_ref, result_ref, sems = refs
     core = lax.axis_index("grad")
     position = lax.axis_index("dp") * lax.axis_size("grad") + core
     mine = lax.rem(position, spread)
     rows_dev = out_ref.shape[0]
-    def fill(parts, out_ref):
-        a_ref, b_ref = parts
-        unpack(lambda start, stop: a_ref[start:stop, :], lambda start, stop: b_ref[start:stop, :], order, out_ref)
+
+    def fill(left, right):
+        a_ref, b_ref = right
+        unpack(lambda start, stop: a_ref[start:stop, :], lambda start, stop: b_ref[start:stop, :], order, right_ref)
+        for row in range(order // LANE):
+
+            @pl.when(mine == row)
+            def _():
+                for column in range(order // LANE):
+                    block = stored_block(*left, order, row, column)
+                    left_ref[:, column * LANE : (column + 1) * LANE] = block
 
     @pl.when(core != 0)
     def _():
-        fill(own, left_ref)
-        fill(other, right_ref)
+        fill(own, other)
 
     @pl.when(core == 0)
     def _():
-        fill(other, left_ref)
-        fill(own, right_ref)
+        fill(other, own)
 
     def place(position):
         return pl.ds(pl.multiple_of(position * rows_dev, rows_dev), rows_dev)
@@ -271,15 +301,23 @@
                     ]
                     start += rows_dev
 
-    left = left_ref[pl.ds(pl.multiple_of(mine * rows_dev, rows_dev), rows_dev), :]
-    middle = times(halves(left), halves(tile_ref[...]))
-    out_ref[...] = times(halves(middle), halves(right_ref[...]))
-
-
-def call(kernel, shapes, scratch, *args):
+    middle = halves(times(halves(left_ref[...]), halves(tile_ref[...])))
+    step = order // 2
+    copies = []
+    for turn in range(2):
+        columns = pl.ds(turn * step, step)
+        result_ref[turn] = times(middle, halves(right_ref[:, turn * step : (turn + 1) * step]))
+        copies.append(pltpu.make_async_copy(result_ref.at[turn], out_ref.at[:, columns], sems.at[turn]))
+        copies[-1].start()
+    for copy in copies:
+        copy.wait()
+
+
+def call(kernel, shapes, scratch, *args, space=pltpu.VMEM):
     return pl.pallas_call(
         kernel,
         out_shape=[jax.ShapeDtypeStruct(shape, jnp.float32) for shape in shapes],
+        out_specs=[pl.BlockSpec(memory_space=space) for shape in shapes],
         scratch_shapes=scratch,
         compiler_params=PARAMS,
     )(*args)
@@ -301,17 +339,22 @@
         size = self.dp * self.cuts * 2
         return [(group * size + a, group * size + b) for group in range(self.groups) for a, b in pairs]
 
-    def swaps(self, pairs):
+    def swaps(self, pairs, abreast=False):
         size = self.dp * self.cuts * 2
         partner = {}
         for a, b in self.one_way(pairs):
             partner[a], partner[b] = b, a
-        for device in range(size * self.groups):
-            other = device ^ 1
-            if other in partner:
-                other = (device + size) % (2 * size) + device // (2 * size) * 2 * size
-            if device not in partner and other not in partner and other < size * self.groups:
-                partner[device], partner[other] = other, device
+
+        def pair_up(other):
+            for device in range(size * self.groups):
+                chosen = other(device)
+                if device not in partner and chosen not in partner and chosen < size * self.groups:
+                    partner[device], partner[chosen] = chosen, device
+
+        pair_up(lambda device: device ^ 1)
+        if abreast and self.cuts % 2 == 0:
+            pair_up(lambda device: device ^ 3)
+        pair_up(lambda device: (device + size) % (2 * size) + device // (2 * size) * 2 * size)
         return sorted(partner.items())
 
     def across(self, bit):
@@ -354,17 +397,18 @@
                     abreast = self.index(left, x + turn, 1)
                     hops[turn - 1].append((left_root, abreast))
                     relays[turn - 1].append((abreast, self.index(left ^ 1, x + turn, 1)))
-        return [self.swaps(pairs) for pairs in hops], self.swaps(direct), [self.swaps(pairs) for pairs in relays]
+        return [self.swaps(pairs) for pairs in hops], self.swaps(direct), [self.swaps(pairs, True) for pairs in relays]
 
     def which(self):
         z, x, core = (lax.axis_index(name) for name in AXES[1:])
         zq, middle = lax.rem(z, QUAD), is_middle()
         block = lax.div(z, 2)
         turn = lax.rem(x + self.cuts - block, self.cuts)
-        left = jnp.where(middle, turn, jnp.where(turn == 0, self.cuts, self.cuts + turn))
+        direct = 2 * self.cuts - 1
+        left = jnp.where(middle, turn, jnp.where(turn == 0, direct, self.cuts - 1 + turn))
         right_root = 2 - lax.rem(x, 2)
         right = jnp.where(
-            zq == right_root, 0, jnp.where(middle, 1, jnp.where((zq ^ 1) == right_root, self.cuts, self.cuts + 1))
+            zq == right_root, 0, jnp.where(middle, 1, jnp.where((zq ^ 1) == right_root, direct, self.cuts))
         )
         return jnp.where(core == 1, left, right)
 
@@ -405,9 +449,13 @@
         outer = jnp.where(is_middle(), outer, chip)
         bit *= 2
     far, near, outward = plan.collect()
-    sums = [lax.ppermute(array, AXES, pairs) for array, pairs in ((chip, far), (chip, near), (outer, outward))]
-    outer_rows = sums[2]
-    sums.append(swap_cores(chip))
+    sums = [
+        lax.ppermute(outer, AXES, outward),
+        lax.ppermute(chip, AXES, near),
+        lax.ppermute(chip, AXES, far),
+        swap_cores(chip),
+    ]
+    outer_rows = sums[0]
     scale = 1.0 / (tok_rows * dev_count)
     square_scratch = pltpu.VMEM((order, order), jnp.float32)
     *inverse, direct = call(
@@ -422,24 +470,29 @@
     hopped = [[lax.ppermute(inverse[0], AXES, pairs) for pairs in hops]]
     direct = lax.ppermute(direct, AXES, outward)
     hopped.append([lax.ppermute(inverse[1], AXES, pairs) for pairs in hops])
-    own, relayed = [], []
+    relayed = [[lax.ppermute(array, AXES, pairs) for array, pairs in zip(arrays, relays)] for arrays in hopped]
+    relayed[1], direct = lax.optimization_barrier((relayed[1], direct))
+    own = []
     for part, start in ((0, 0), (1, split)):
-        arrived = [lax.ppermute(array, AXES, pairs) for array, pairs in zip(hopped[part], relays)]
-        (chosen,) = call(
+        own += call(
             functools.partial(choose_kernel, plan.which, start),
             [inverse[part].shape],
             [],
             inverse[part],
             *hopped[part],
+            *relayed[part],
             direct,
-            *arrived,
         )
-        own.append(chosen)
-        relayed.append(arrived[0])
     (out,) = call(
         functools.partial(final_kernel, order, spread),
         [grads.shape],
-        [square_scratch] * 3,
+        [
+            pltpu.VMEM((LANE, order), jnp.float32),
+            square_scratch,
+            square_scratch,
+            pltpu.VMEM((2, LANE, order // 2), jnp.float32),
+            pltpu.SemaphoreType.DMA((2,)),
+        ],
         *own,
         *map(swap_cores, own),
         grads,
@@ -447,7 +500,9 @@
         outer_rows,
         swap_cores(outer_rows),
         direct,
-        *relayed,
+        relayed[0][0],
+        relayed[1][0],
+        space=pl.ANY,
     )
     return out[None]
 

time: 46.4 us -> 45.2 us (0.974)
  waiting for transfers between devices: 17.2 us -> 10.6 us
  starting transfers between devices: 19.6 us -> 25.5 us
    ppermute x5 -> x2, waiting for transfers between devices: 12.1 us -> 4.24 us  [per_device(): lax.ppermute(array, AXES, pairs)]
    ppermute x5 -> x2, starting transfers between devices: 14.9 us -> 9.71 us  [per_device(): lax.ppermute(array, AXES, pairs)]
    ppermute x1, starting transfers between devices: 0.07 us -> 4.18 us  [per_device(): hopped.append([lax.ppermute(inverse[1], AXES, pairs) for pairs in hops])]
    ppermute x0 -> x3, waiting for transfers between devices: none -> 3.82 us  [the longest x1 3.82 us: per_device(): lax.ppermute(outer, AXES, outward)]
    ppermute x0 -> x3, starting transfers between devices: none -> 3.49 us  [the longest x1 2.75 us: per_device(): lax.ppermute(outer, AXES, outward)]
    ppermute x6, starting transfers between devices: 2.38 us -> 5.02 us  [swap_cores(): return lax.ppermute(array, 'grad', [(0, 1), (1, 0)])]
    ppermute x1, waiting for transfers between devices: 2.56 us -> 0.01 us  [per_device(): direct = lax.ppermute(direct, AXES, outward)]
    ppermute x1, starting transfers between devices: 0.69 us -> 1.59 us  [per_device(): hopped = [[lax.ppermute(inverse[0], AXES, pairs) for pairs in hops]]]
  transfers between devices with their start and end apart: 14 -> 14, of which waited for: 6 -> 5; matrix products, arithmetic and copies ran while one was open for 0% -> 0% of each run, Pallas kernels for 1% -> 1%
where the time goes in v5:
time: 45.2 us; the launch traced here: 45.1 us
  starting transfers between devices  25.5 us (56%)
  waiting for transfers between devices  10.6 us (23%)
  Pallas kernels  7.65 us (17%)
  other arithmetic  1.17 us (3%)
    ppermute x2, starting transfers between devices, per_device(): lax.ppermute(array, AXES, pairs)  9.71 us
    pallas_call x7, Pallas kernels, call(): pl.pallas_call(kernel, out_shape=[jax.ShapeDtypeStruct(shape, jnp.float32...  7.65 us
    ppermute x6, starting transfers between devices, swap_cores(): return lax.ppermute(array, 'grad', [(0, 1), (1, 0)])  5.02 us
    ppermute x2, waiting for transfers between devices, per_device(): lax.ppermute(array, AXES, pairs)  4.24 us
    ppermute x1, starting transfers between devices, per_device(): hopped.append([lax.ppermute(inverse[1], AXES, pairs) for pairs in hops])  4.18 us
    ppermute x1, waiting for transfers between devices, per_device(): lax.ppermute(outer, AXES, outward)  3.82 us
    ppermute x1, starting transfers between devices, per_device(): lax.ppermute(outer, AXES, outward)  2.75 us
    ppermute x6, waiting for transfers between devices, swap_cores(): return lax.ppermute(array, 'grad', [(0, 1), (1, 0)])  2.57 us
  transfers between devices with their start and end apart: 14, of which 5 were waited for; matrix products, arithmetic and copies ran while one was open for 0% of the time, Pallas kernels for 1%

profile of v5, /device:TPU:0, one launch (start us, length us, event | category | flops | bytes accessed | tf_op | source)
XLA Modules:
  0.0 45.1 jit_solution(4874236015562847484)
XLA Ops:
  0.0 1.2 %select_bitcast_fusion = (bf16[384,512]{1,0:T(8,128)(2,1)S(1)}, bf16[384,512]{1,0:T(8,128)(2,1)S(1)}) fusion(bf16[1,384,512]{2,1,0:T(8,128)(2,1)} %param.4, bf16[1,384,512]{2,1,0:T(8,128)(2,1)} %param.3, pred[]{:T(512)S(6)} %eq.4), kind=kLoop, calls=%fused_computation | loop fusion | flops 393216 | bytes 1572865 | tf_op jit(solution)/shard_map/jit(_where)/select_n | solution.py:442
  1.2 0.0 copy-start
  1.2 0.5 %shard_map.38 = f32[1040,128]{1,0:T(8,128)S(1)} custom-call(bf16[384,512]{1,0:T(8,128)(2,1)S(1)} %get-tuple-element.21.x_ref), custom_call_target="tpu_custom_call" | custom-call | tf_op jit(solution)/shard_map/pallas_call | solution.py:317
  1.7 0.5 %collective-permute-start = (f32[1040,128]{1,0:T(8,128)S(1)}, f32[1040,128]{1,0:T(8,128)S(1)}, u32[]{:S(2)}, u32[]{:S(2)}) collective-permute-start(f32[1040,128]{1,0:T(8,128)S(1)} %shard_map.38), channel_id=1, source_target_pairs={{0,1},{1,0},{2,3},{3,2},{4,5},{5,4},{6,7},{7,6},{8,9},{9,8},{10,11... | collective-permute-start | bytes 1597448 | tf_op jit(solution)/shard_map/ppermute | solution.py:428
  2.2 0.0 copy-done
  2.2 0.4 collective-permute-start.1
  2.6 0.5 %shard_map.37.kept_ref = f32[1040,128]{1,0:T(8,128)S(1)} custom-call(bf16[384,512]{1,0:T(8,128)(2,1)S(1)} %get-tuple-element.22.x_ref), custom_call_target="tpu_custom_call" | custom-call | tf_op jit(solution)/shard_map/pallas_call | solution.py:317
  3.0 1.1 %collective-permute-done.1.other_rows_ref.refs_5_ = f32[128,512]{1,0:T(8,128)S(1)} collective-permute-done((f32[128,512]{1,0:T(8,128)S(1)}, f32[128,512]{1,0:T(8,128)S(1)}, u32[]{:S(2)}, u32[]{:S(2)}) %collective-permute-start.1) | collective-permute-done | bytes 262176 | tf_op jit(solution)/shard_map/ppermute | solution.py:428
  4.1 0.0 collective-permute-done.other_ref
  4.1 0.2 shard_map.39
  4.3 2.7 %collective-permute-start.2 = (f32[1040,128]{1,0:T(8,128)S(1)}, f32[1040,128]{1,0:T(8,128)S(1)}, u32[]{:S(2)}, u32[]{:S(2)}) collective-permute-start(f32[1040,128]{1,0:T(8,128)S(1)} %get-tuple-element.13), channel_id=1, source_target_pairs={{0,5},{1,17},{2,18},{3,6},{4,20},{5,0},{6,3},{7,23},{8,13},{9,25},... | collective-permute-start | bytes 1597448 | tf_op jit(solution)/shard_map/ppermute | solution.py:453
  7.0 0.1 collective-permute-start.3
  7.1 0.7 %collective-permute-start.4 = (f32[1040,128]{1,0:T(8,128)S(1)}, f32[1040,128]{1,0:T(8,128)S(1)}, u32[]{:S(2)}, u32[]{:S(2)}) collective-permute-start(f32[1040,128]{1,0:T(8,128)S(1)} %get-tuple-element.14), channel_id=1, source_target_pairs={{12,5},{1,8},{2,11},{15,6},{28,21},{17,24},{18,27},{31,22}} | collective-permute-start | bytes 1597448 | tf_op jit(solution)/shard_map/ppermute | solution.py:455
  7.8 4.0 %collective-permute-start.5 = (f32[1040,128]{1,0:T(8,128)S(1)}, f32[1040,128]{1,0:T(8,128)S(1)}, u32[]{:S(2)}, u32[]{:S(2)}) collective-permute-start(f32[1040,128]{1,0:T(8,128)S(1)} %get-tuple-element.14), channel_id=1, source_target_pairs={{0,1},{1,0},{2,3},{3,2},{4,5},{5,4},{6,7},{7,6},{8,9},{9,8},{10,11... | collective-permute-start | bytes 1597448 | tf_op jit(solution)/shard_map/ppermute | solution.py:428
  11.7 3.8 %collective-permute-done.2.refs_0_.refs_6_ = f32[1040,128]{1,0:T(8,128)S(1)} collective-permute-done((f32[1040,128]{1,0:T(8,128)S(1)}, f32[1040,128]{1,0:T(8,128)S(1)}, u32[]{:S(2)}, u32[]{:S(2)}) %collective-permute-start.2) | collective-permute-done | bytes 532512 | tf_op jit(solution)/shard_map/ppermute | solution.py:453
  15.5 0.0 collective-permute-done.3.refs_1_
  15.5 0.0 collective-permute-done.4.refs_2_
  15.5 0.0 collective-permute-done.5.refs_3_
  15.5 4.7 %shard_map.40 = (f32[512,128]{1,0:T(8,128)S(1)}, f32[528,128]{1,0:T(8,128)S(1)}, f32[1040,128]{1,0:T(8,128)S(1)}) custom-call(f32[1040,128]{1,0:T(8,128)S(1)} %collective-permute-done.2.refs_0_.refs_6_, f32[1040,128]{1,0:T(8,128)S(1)} %collective-permute-done.3.refs_1_, f32[1040,128]{1,0:T(8,128)S(1)} %collective-permute-done.4.refs_2_, ...), custom_call_target="tpu_custom_call" | custom-call | tf_op jit(solution)/shard_map/pallas_call | solution.py:317
  20.2 4.2 %collective-permute-start.8 = (f32[528,128]{1,0:T(8,128)S(1)}, f32[528,128]{1,0:T(8,128)S(1)}, u32[]{:S(2)}, u32[]{:S(2)}) collective-permute-start(f32[528,128]{1,0:T(8,128)S(1)} %get-tuple-element.17.refs_0_), channel_id=1, source_target_pairs={{0,1},{1,0},{2,3},{3,2},{4,8},{5,7},{6,10},{7,5},{8,4},{9,11},{10,... | collective-permute-start | bytes 811016 | tf_op jit(solution)/shard_map/ppermute | solution.py:472
  24.4 1.5 %collective-permute-start.10 = (f32[1040,128]{1,0:T(8,128)S(1)}, f32[1040,128]{1,0:T(8,128)S(1)}, u32[]{:S(2)}, u32[]{:S(2)}) collective-permute-start(f32[1040,128]{1,0:T(8,128)S(1)} %get-tuple-element.18), channel_id=1, source_target_pairs={{0,16},{1,5},{2,6},{3,19},{4,20},{5,1},{6,2},{7,23},{8,12},{9,25},... | collective-permute-start | bytes 1597448 | tf_op jit(solution)/shard_map/ppermute | solution.py:471
  25.9 1.6 %collective-permute-start.6 = (f32[512,128]{1,0:T(8,128)S(1)}, f32[512,128]{1,0:T(8,128)S(1)}, u32[]{:S(2)}, u32[]{:S(2)}) collective-permute-start(f32[512,128]{1,0:T(8,128)S(1)} %get-tuple-element.16.refs_0_), channel_id=1, source_target_pairs={{0,1},{1,0},{2,3},{3,2},{4,8},{5,7},{6,10},{7,5},{8,4},{9,11},{10,... | collective-permute-start | bytes 786440 | tf_op jit(solution)/shard_map/ppermute | solution.py:470
  27.5 0.0 collective-permute-done.8.refs_1_
  27.5 6.3 %collective-permute-start.9 = (f32[528,128]{1,0:T(8,128)S(1)}, f32[528,128]{1,0:T(8,128)S(1)}, u32[]{:S(2)}, u32[]{:S(2)}) collective-permute-start(f32[528,128]{1,0:T(8,128)S(1)} %collective-permute-done.8.refs_1_), channel_id=1, source_target_pairs={{0,4},{1,2},{2,1},{3,7},{4,0},{5,6},{6,5},{7,3},{8,11},{9,13},{10,... | collective-permute-start | bytes 811016 | tf_op jit(solution)/shard_map/ppermute | solution.py:473
  33.8 0.0 collective-permute-start.13
  33.8 0.0 collective-permute-done.6.refs_1_
  33.8 3.4 %collective-permute-start.7 = (f32[512,128]{1,0:T(8,128)S(1)}, f32[512,128]{1,0:T(8,128)S(1)}, u32[]{:S(2)}, u32[]{:S(2)}) collective-permute-start(f32[512,128]{1,0:T(8,128)S(1)} %collective-permute-done.6.refs_1_), channel_id=1, source_target_pairs={{0,4},{1,2},{2,1},{3,7},{4,0},{5,6},{6,5},{7,3},{8,11},{9,13},{10,... | collective-permute-start | bytes 786440 | tf_op jit(solution)/shard_map/ppermute | solution.py:473
  37.3 0.0 collective-permute-done.10.refs_3_.refs_8_
  37.3 1.0 %collective-permute-done.9.refs_2_.refs_10_ = f32[528,128]{1,0:T(8,128)S(1)} collective-permute-done((f32[528,128]{1,0:T(8,128)S(1)}, f32[528,128]{1,0:T(8,128)S(1)}, u32[]{:S(2)}, u32[]{:S(2)}) %collective-permute-start.9) | collective-permute-done | bytes 270368 | tf_op jit(solution)/shard_map/ppermute | solution.py:473
  38.3 0.1 collective-permute-start.12
  38.4 3.3 %collective-permute-done.7.refs_2_.refs_9_ = f32[512,128]{1,0:T(8,128)S(1)} collective-permute-done((f32[512,128]{1,0:T(8,128)S(1)}, f32[512,128]{1,0:T(8,128)S(1)}, u32[]{:S(2)}, u32[]{:S(2)}) %collective-permute-start.7) | collective-permute-done | bytes 262176 | tf_op jit(solution)/shard_map/ppermute | solution.py:473
  41.6 0.1 collective-permute-start.11
  41.7 0.0 collective-permute-done.13.refs_7_
  41.7 1.5 %collective-permute-done.11.refs_2_ = f32[512,128]{1,0:T(8,128)S(1)} collective-permute-done((f32[512,128]{1,0:T(8,128)S(1)}, f32[512,128]{1,0:T(8,128)S(1)}, u32[]{:S(2)}, u32[]{:S(2)}) %collective-permute-start.11) | collective-permute-done | bytes 262176 | tf_op jit(solution)/shard_map/ppermute | solution.py:428
  43.2 0.0 collective-permute-done.12.refs_3_
  43.2 1.8 %shard_map.43 = f32[128,512]{1,0:T(8,128)} custom-call(f32[512,128]{1,0:T(8,128)S(1)} %shard_map.41.refs_0_, f32[528,128]{1,0:T(8,128)S(1)} %shard_map.42.refs_1_, f32[512,128]{1,0:T(8,128)S(1)} %collective-permute-done.11.refs_2_, f32[528,128]{1,0:T(8,128)S(1)} %collective-permute-done.12.refs_3_, f32[128,512]{1,0:T(8,128)S(1)} %bitcast.8, ...), custom_call_target="tpu_custom_call" | custom-call | tf_op jit(solution)/shard_map/pallas_call | solution.py:317
  (2 shorter events, 0.0 us)
Async XLA Ops:
  1.2 1.0 %copy-start = (f32[1,128,512]{2,1,0:T(8,128)S(1)}, f32[1,128,512]{2,1,0:T(8,128)}, u32[]{:S(2)}) copy-start(f32[1,128,512]{2,1,0:T(8,128)} %param.5) | copy-start | bytes 786436
  1.7 2.4 %collective-permute-start = (f32[1040,128]{1,0:T(8,128)S(1)}, f32[1040,128]{1,0:T(8,128)S(1)}, u32[]{:S(2)}, u32[]{:S(2)}) collective-permute-start(f32[1040,128]{1,0:T(8,128)S(1)} %shard_map.38), channel_id=1, source_target_pairs={{0,1},{1,0},{2,3},{3,2},{4,5},{5,4},{6,7},{7,6},{8,9},{9,8},{10,11... | collective-permute-start | bytes 1597448 | tf_op jit(solution)/shard_map/ppermute | solution.py:428
  2.2 1.9 %collective-permute-start.1 = (f32[128,512]{1,0:T(8,128)S(1)}, f32[128,512]{1,0:T(8,128)S(1)}, u32[]{:S(2)}, u32[]{:S(2)}) collective-permute-start(f32[128,512]{1,0:T(8,128)S(1)} %bitcast.6), channel_id=1, source_target_pairs={{0,1},{1,0},{2,3},{3,2},{4,5},{5,4},{6,7},{7,6},{8,9},{9,8},{10,11... | collective-permute-start | bytes 786440 | tf_op jit(solution)/shard_map/ppermute | solution.py:428
  4.3 11.3 %collective-permute-start.2 = (f32[1040,128]{1,0:T(8,128)S(1)}, f32[1040,128]{1,0:T(8,128)S(1)}, u32[]{:S(2)}, u32[]{:S(2)}) collective-permute-start(f32[1040,128]{1,0:T(8,128)S(1)} %get-tuple-element.13), channel_id=1, source_target_pairs={{0,5},{1,17},{2,18},{3,6},{4,20},{5,0},{6,3},{7,23},{8,13},{9,25},... | collective-permute-start | bytes 1597448 | tf_op jit(solution)/shard_map/ppermute | solution.py:453
  7.0 8.5 %collective-permute-start.3 = (f32[1040,128]{1,0:T(8,128)S(1)}, f32[1040,128]{1,0:T(8,128)S(1)}, u32[]{:S(2)}, u32[]{:S(2)}) collective-permute-start(f32[1040,128]{1,0:T(8,128)S(1)} %get-tuple-element.14), channel_id=1, source_target_pairs={{0,1},{1,0},{2,3},{3,2},{4,20},{5,8},{6,11},{7,23},{8,5},{9,25},{1... | collective-permute-start | bytes 1597448 | tf_op jit(solution)/shard_map/ppermute | solution.py:454
  7.1 8.5 %collective-permute-start.4 = (f32[1040,128]{1,0:T(8,128)S(1)}, f32[1040,128]{1,0:T(8,128)S(1)}, u32[]{:S(2)}, u32[]{:S(2)}) collective-permute-start(f32[1040,128]{1,0:T(8,128)S(1)} %get-tuple-element.14), channel_id=1, source_target_pairs={{12,5},{1,8},{2,11},{15,6},{28,21},{17,24},{18,27},{31,22}} | collective-permute-start | bytes 1597448 | tf_op jit(solution)/shard_map/ppermute | solution.py:455
  7.8 7.8 %collective-permute-start.5 = (f32[1040,128]{1,0:T(8,128)S(1)}, f32[1040,128]{1,0:T(8,128)S(1)}, u32[]{:S(2)}, u32[]{:S(2)}) collective-permute-start(f32[1040,128]{1,0:T(8,128)S(1)} %get-tuple-element.14), channel_id=1, source_target_pairs={{0,1},{1,0},{2,3},{3,2},{4,5},{5,4},{6,7},{7,6},{8,9},{9,8},{10,11... | collective-permute-start | bytes 1597448 | tf_op jit(solution)/shard_map/ppermute | solution.py:428
  20.2 7.3 %collective-permute-start.8 = (f32[528,128]{1,0:T(8,128)S(1)}, f32[528,128]{1,0:T(8,128)S(1)}, u32[]{:S(2)}, u32[]{:S(2)}) collective-permute-start(f32[528,128]{1,0:T(8,128)S(1)} %get-tuple-element.17.refs_0_), channel_id=1, source_target_pairs={{0,1},{1,0},{2,3},{3,2},{4,8},{5,7},{6,10},{7,5},{8,4},{9,11},{10,... | collective-permute-start | bytes 811016 | tf_op jit(solution)/shard_map/ppermute | solution.py:472
  24.4 12.8 %collective-permute-start.10 = (f32[1040,128]{1,0:T(8,128)S(1)}, f32[1040,128]{1,0:T(8,128)S(1)}, u32[]{:S(2)}, u32[]{:S(2)}) collective-permute-start(f32[1040,128]{1,0:T(8,128)S(1)} %get-tuple-element.18), channel_id=1, source_target_pairs={{0,16},{1,5},{2,6},{3,19},{4,20},{5,1},{6,2},{7,23},{8,12},{9,25},... | collective-permute-start | bytes 1597448 | tf_op jit(solution)/shard_map/ppermute | solution.py:471
  25.9 7.9 %collective-permute-start.6 = (f32[512,128]{1,0:T(8,128)S(1)}, f32[512,128]{1,0:T(8,128)S(1)}, u32[]{:S(2)}, u32[]{:S(2)}) collective-permute-start(f32[512,128]{1,0:T(8,128)S(1)} %get-tuple-element.16.refs_0_), channel_id=1, source_target_pairs={{0,1},{1,0},{2,3},{3,2},{4,8},{5,7},{6,10},{7,5},{8,4},{9,11},{10,... | collective-permute-start | bytes 786440 | tf_op jit(solution)/shard_map/ppermute | solution.py:470
  27.5 10.7 %collective-permute-start.9 = (f32[528,128]{1,0:T(8,128)S(1)}, f32[528,128]{1,0:T(8,128)S(1)}, u32[]{:S(2)}, u32[]{:S(2)}) collective-permute-start(f32[528,128]{1,0:T(8,128)S(1)} %collective-permute-done.8.refs_1_), channel_id=1, source_target_pairs={{0,4},{1,2},{2,1},{3,7},{4,0},{5,6},{6,5},{7,3},{8,11},{9,13},{10,... | collective-permute-start | bytes 811016 | tf_op jit(solution)/shard_map/ppermute | solution.py:473
  33.8 7.9 %collective-permute-start.13 = (f32[1040,128]{1,0:T(8,128)S(1)}, f32[1040,128]{1,0:T(8,128)S(1)}, u32[]{:S(2)}, u32[]{:S(2)}) collective-permute-start(f32[1040,128]{1,0:T(8,128)S(1)} %collective-permute-done.2.refs_0_.refs_6_), channel_id=1, source_target_pairs={{0,1},{1,0},{2,3},{3,2},{4,5},{5,4},{6,7},{7,6},{8,9},{9,8},{10,11... | collective-permute-start | bytes 1597448 | tf_op jit(solution)/shard_map/ppermute | solution.py:428
  33.8 7.8 %collective-permute-start.7 = (f32[512,128]{1,0:T(8,128)S(1)}, f32[512,128]{1,0:T(8,128)S(1)}, u32[]{:S(2)}, u32[]{:S(2)}) collective-permute-start(f32[512,128]{1,0:T(8,128)S(1)} %collective-permute-done.6.refs_1_), channel_id=1, source_target_pairs={{0,4},{1,2},{2,1},{3,7},{4,0},{5,6},{6,5},{7,3},{8,11},{9,13},{10,... | collective-permute-start | bytes 786440 | tf_op jit(solution)/shard_map/ppermute | solution.py:473
  38.3 5.0 %collective-permute-start.12 = (f32[528,128]{1,0:T(8,128)S(1)}, f32[528,128]{1,0:T(8,128)S(1)}, u32[]{:S(2)}, u32[]{:S(2)}) collective-permute-start(f32[528,128]{1,0:T(8,128)S(1)} %shard_map.42.refs_1_), channel_id=1, source_target_pairs={{0,1},{1,0},{2,3},{3,2},{4,5},{5,4},{6,7},{7,6},{8,9},{9,8},{10,11... | collective-permute-start | bytes 811016 | tf_op jit(solution)/shard_map/ppermute | solution.py:428
  41.6 1.6 %collective-permute-start.11 = (f32[512,128]{1,0:T(8,128)S(1)}, f32[512,128]{1,0:T(8,128)S(1)}, u32[]{:S(2)}, u32[]{:S(2)}) collective-permute-start(f32[512,128]{1,0:T(8,128)S(1)} %shard_map.41.refs_0_), channel_id=1, source_target_pairs={{0,1},{1,0},{2,3},{3,2},{4,5},{5,4},{6,7},{7,6},{8,9},{9,8},{10,11... | collective-permute-start | bytes 786440 | tf_op jit(solution)/shard_map/ppermute | solution.py:428

commit v6 on v5

--- a/solution.py
+++ b/solution.py
@@ -32,29 +32,34 @@
     return len(joining_blocks(order)) * LANE, 2 * own
 
 
+def own_start(order, half, second):
+    rows = part_rows(order)[1] // 2
+    return (half ^ second) * rows if isinstance(second, int) else pl.multiple_of((half ^ second) * rows, 8)
+
+
 def places():
     rows = lax.broadcasted_iota(jnp.int32, (LANE, LANE), 0)
     cols = lax.broadcasted_iota(jnp.int32, (LANE, LANE), 1)
     return rows, cols
 
 
-def pack(block, order, a_ref, b_ref):
+def pack(block, order, a_ref, b_ref, second=0):
     rows, cols = places()
     for slot, (i, j) in enumerate(joining_blocks(order)):
         a_ref[slot * LANE : (slot + 1) * LANE, :] = block(i, j)
-    top = 0
     for half in range(2):
+        top = own_start(order, half, second)
         above, pairs = half_blocks(order, half)
         values = [block(i, j) for i, j in above]
         values += [jnp.where(rows <= cols, block(i, i), block(j, j)) for i, j in pairs]
         last = [jnp.sum(jnp.where(rows == cols, block(j, j), 0.0), axis=0, keepdims=True) for _, j in pairs]
         values.append(jnp.concatenate(last + [jnp.zeros((-len(pairs) % 8, LANE), jnp.float32)], 0))
         for value in values:
-            b_ref[top : top + value.shape[0], :] = value
+            b_ref[pl.ds(top, value.shape[0]), :] = value
             top += value.shape[0]
 
 
-def unpack(a_piece, b_piece, order, out_ref, scale=1.0, shift=0.0):
+def unpack(a_piece, b_piece, order, out_ref, second=0, scale=1.0, shift=0.0):
     rows, cols = places()
     damping = jnp.where(rows == cols, shift, 0.0)
 
@@ -66,45 +71,41 @@
         put(j, i, value.T)
 
     for slot, (i, j) in enumerate(joining_blocks(order)):
-        put_both(i, j, a_piece(slot * LANE, (slot + 1) * LANE) * scale)
-    top = 0
+        put_both(i, j, a_piece(slot * LANE, LANE) * scale)
     for half in range(2):
+        top = own_start(order, half, second)
         above, pairs = half_blocks(order, half)
         for i, j in above:
-            put_both(i, j, b_piece(top, top + LANE) * scale)
+            put_both(i, j, b_piece(top, LANE) * scale)
             top += LANE
-        after = top + len(pairs) * LANE
-        last = b_piece(after, after + -(-len(pairs) // 8) * 8)
+        last = b_piece(top + len(pairs) * LANE, -(-len(pairs) // 8) * 8)
         for k, (i, j) in enumerate(pairs):
-            both = b_piece(top, top + LANE)
+            both = b_piece(top, LANE)
             turned = both.T
             put(i, i, jnp.where(rows <= cols, both, turned) * scale + damping)
-            second = jnp.where(rows > cols, both, jnp.where(rows < cols, turned, last[k : k + 1, :]))
-            put(j, j, second * scale + damping)
+            after = jnp.where(rows > cols, both, jnp.where(rows < cols, turned, last[k : k + 1, :]))
+            put(j, j, after * scale + damping)
             top += LANE
-        top += last.shape[0]
-
-
-def stored_block(a_ref, b_ref, order, i, j):
+
+
+def stored_block(a_ref, b_ref, order, i, j, second):
     if i > j:
-        return stored_block(a_ref, b_ref, order, j, i).T
+        return stored_block(a_ref, b_ref, order, j, i, second).T
     if (i, j) in joining_blocks(order):
         start = joining_blocks(order).index((i, j)) * LANE
         return a_ref[start : start + LANE, :]
     half = i // (order // LANE // 2)
     above, pairs = half_blocks(order, half)
-    top = half * part_rows(order)[1] // 2
+    top = own_start(order, half, second)
     if i < j:
-        start = top + above.index((i, j)) * LANE
-        return b_ref[start : start + LANE, :]
+        return b_ref[pl.ds(top + above.index((i, j)) * LANE, LANE), :]
     place = next(k for k, pair in enumerate(pairs) if i in pair)
-    start = top + (len(above) + place) * LANE
-    both = b_ref[start : start + LANE, :]
+    both = b_ref[pl.ds(top + (len(above) + place) * LANE, LANE), :]
     rows, cols = places()
     if i == pairs[place][0]:
         return jnp.where(rows <= cols, both, both.T)
-    start = top + (len(above) + len(pairs)) * LANE + place
-    return jnp.where(rows > cols, both, jnp.where(rows < cols, both.T, b_ref[start : start + 1, :]))
+    last = b_ref[pl.ds(top + (len(above) + len(pairs)) * LANE, -(-len(pairs) // 8) * 8), :]
+    return jnp.where(rows > cols, both, jnp.where(rows < cols, both.T, last[place : place + 1, :]))
 
 
 def halves(value):
@@ -187,16 +188,16 @@
 
 
 def inverse_kernel(scale, order, *refs):
-    *sums, rows_ref, a_ref, b_ref, direct_ref, factor_ref = refs
+    *sums, rows_ref, a_ref, b_ref, direct_ref, rest_ref, factor_ref = refs
     split = part_rows(order)[0]
 
-    def piece(start, stop):
-        total = sums[0][start:stop, :]
+    def piece(start, size):
+        total = sums[0][start : start + size, :]
         for ref in sums[1:]:
-            total = total + ref[start:stop, :]
+            total = total + ref[start : start + size, :]
         return total
 
-    unpack(piece, lambda a, b: piece(split + a, split + b), order, factor_ref, scale, DAMPING)
+    unpack(piece, lambda start, size: piece(split + start, size), order, factor_ref, 0, scale, DAMPING)
     factor = factor_ref[...]
     bound = jnp.max(jnp.sum(jnp.abs(factor), axis=0, keepdims=True), axis=1, keepdims=True) + 1e-06
     start = START / bound
@@ -222,17 +223,35 @@
             value = block_of(corner)(i - middle // LANE, j - middle // LANE)
         return start * (value + block_of(eye)(i, j))
 
+    used = direct_ref.shape[0] - split
+
     @pl.when(is_middle())
     def _():
-        pack(block, order, a_ref, b_ref)
+        pack(block, order, a_ref, b_ref, lax.rem(lax.axis_index("cuts"), 2))
         direct_ref[:split, :] = a_ref[...]
-        direct_ref[split:, :] = b_ref[...]
+        direct_ref[split:, :] = b_ref[:used, :]
+        rest_ref[...] = b_ref[used:, :]
 
     @pl.when(jnp.logical_not(is_middle()))
     def _():
         a_ref[...] = rows_ref[:split, :]
         b_ref[...] = rows_ref[split:, :]
-        direct_ref[...] = rows_ref[...]
+        direct_ref[...] = rows_ref[: split + used, :]
+        rest_ref[...] = rows_ref[:used, :]
+
+
+def relay_kernel(hopped_ref, rest_ref, out_ref):
+    used = rest_ref.shape[0]
+    out_ref[:used, :] = hopped_ref[:used, :]
+    rest = jnp.logical_and(is_middle(), lax.axis_index("grad") == 1)
+
+    @pl.when(rest)
+    def _():
+        out_ref[used:, :] = rest_ref[...]
+
+    @pl.when(jnp.logical_not(rest))
+    def _():
+        out_ref[used:, :] = hopped_ref[used:, :]
 
 
 def choose_kernel(which, start, *refs):
@@ -240,31 +259,51 @@
     index = which()
     rows = out_ref.shape[0]
     for place, ref in enumerate(arrays):
-        first = 0 if ref.shape[0] == rows else start
+        first = start if place == len(arrays) - 1 else 0
+        size = min(rows, ref.shape[0] - first)
 
         @pl.when(index == place)
         def _():
-            out_ref[...] = ref[first : first + rows, :]
+            out_ref[:size, :] = ref[first : first + size, :]
+            if size < rows:
+                out_ref[size:, :] = jnp.zeros((rows - size, LANE), jnp.float32)
 
 
 def final_kernel(order, spread, *refs):
     own, other, refs = refs[:2], refs[2:4], refs[4:]
-    own_rows_ref, other_rows_ref, outer_ref, outer_other_ref, direct_ref, relayed_a, relayed_b, *refs = refs
-    out_ref, left_ref, right_ref, tile_ref, result_ref, sems = refs
+    own_rows_ref, other_rows_ref, outer_ref, outer_other_ref, direct_ref, relayed_a, relayed_b, other_b, *refs = refs
+    out_ref, left_ref, right_ref, tile_ref, result_ref, b_ref, sems = refs
     core = lax.axis_index("grad")
     position = lax.axis_index("dp") * lax.axis_size("grad") + core
     mine = lax.rem(position, spread)
     rows_dev = out_ref.shape[0]
 
+    cut = lax.axis_index("cuts")
+    zq = lax.rem(lax.axis_index("dp"), QUAD)
+    was_direct = jnp.logical_and(jnp.logical_not(is_middle()), (zq ^ 1) == 2 - lax.rem(cut, 2))
+    left_second = lax.rem(lax.div(position, spread), 2)
+
     def fill(left, right):
-        a_ref, b_ref = right
-        unpack(lambda start, stop: a_ref[start:stop, :], lambda start, stop: b_ref[start:stop, :], order, right_ref)
+        used = b_ref.shape[0] // 2
+        b_ref[...] = right[1][...]
+
+        @pl.when(was_direct)
+        def _():
+            b_ref[used:, :] = left[1][used:, :]
+
+        unpack(
+            lambda start, size: right[0][pl.ds(start, size), :],
+            lambda start, size: b_ref[pl.ds(start, size), :],
+            order,
+            right_ref,
+            lax.rem(cut, 2),
+        )
         for row in range(order // LANE):
 
             @pl.when(mine == row)
             def _():
                 for column in range(order // LANE):
-                    block = stored_block(*left, order, row, column)
+                    block = stored_block(*left, order, row, column, left_second)
                     left_ref[:, column * LANE : (column + 1) * LANE] = block
 
     @pl.when(core != 0)
@@ -284,7 +323,7 @@
     cases = (
         (False, True, (outer_ref,)),
         (False, False, (outer_other_ref,)),
-        (True, True, (direct_ref,)),
+        (True, True, (direct_ref.at[: relayed_a.shape[0]], other_b)),
         (True, False, (relayed_a, relayed_b)),
     )
     for middle, arrived, parts in cases:
@@ -399,6 +438,11 @@
                     relays[turn - 1].append((abreast, self.index(left ^ 1, x + turn, 1)))
         return [self.swaps(pairs) for pairs in hops], self.swaps(direct), [self.swaps(pairs, True) for pairs in relays]
 
+    def turn(self):
+        z, x, core = (lax.axis_index(name) for name in AXES[1:])
+        turn = lax.rem(x + self.cuts - lax.div(z, 2), self.cuts)
+        return jnp.where(core == 1, jnp.maximum(turn - 1, 0), 0)
+
     def which(self):
         z, x, core = (lax.axis_index(name) for name in AXES[1:])
         zq, middle = lax.rem(z, QUAD), is_middle()
@@ -458,9 +502,9 @@
     outer_rows = sums[0]
     scale = 1.0 / (tok_rows * dev_count)
     square_scratch = pltpu.VMEM((order, order), jnp.float32)
-    *inverse, direct = call(
+    *inverse, direct, rest_own = call(
         functools.partial(inverse_kernel, scale, order),
-        [(split, LANE), (rest, LANE), shape],
+        [(split, LANE), (rest, LANE), (split + rest // 2, LANE), (rest // 2, LANE)],
         [square_scratch],
         *sums,
         rows,
@@ -470,8 +514,17 @@
     hopped = [[lax.ppermute(inverse[0], AXES, pairs) for pairs in hops]]
     direct = lax.ppermute(direct, AXES, outward)
     hopped.append([lax.ppermute(inverse[1], AXES, pairs) for pairs in hops])
-    relayed = [[lax.ppermute(array, AXES, pairs) for array, pairs in zip(arrays, relays)] for arrays in hopped]
+    rest_own = swap_cores(rest_own)
+    carried = [
+        hopped[0],
+        [call(relay_kernel, [array.shape], [], array, rest_own)[0] for array in hopped[1]],
+    ]
+    relayed = [[lax.ppermute(array, AXES, pairs) for array, pairs in zip(arrays, relays)] for arrays in carried]
     relayed[1], direct = lax.optimization_barrier((relayed[1], direct))
+    arrived = [
+        arrays[0] if cuts == 2 else call(functools.partial(choose_kernel, plan.turn, 0), [arrays[0].shape], [], *arrays)[0]
+        for arrays in relayed
+    ]
     own = []
     for part, start in ((0, 0), (1, split)):
         own += call(
@@ -491,6 +544,7 @@
             square_scratch,
             square_scratch,
             pltpu.VMEM((2, LANE, order // 2), jnp.float32),
+            pltpu.VMEM((rest, LANE), jnp.float32),
             pltpu.SemaphoreType.DMA((2,)),
         ],
         *own,
@@ -500,8 +554,8 @@
         outer_rows,
         swap_cores(outer_rows),
         direct,
-        relayed[0][0],
-        relayed[1][0],
+        *arrived,
+        swap_cores(arrived[1]),
         space=pl.ANY,
     )
     return out[None]

time: 45.2 us -> 44.8 us (level)
    ppermute x1, starting transfers between devices: 1.59 us -> 0.08 us  [per_device(): hopped = [[lax.ppermute(inverse[0], AXES, pairs) for pairs in hops]]]
    ppermute x6 -> x8, starting transfers between devices: 5.02 us -> 5.95 us  [swap_cores(): return lax.ppermute(array, 'grad', [(0, 1), (1, 0)])]
    pallas_call x7 -> x8, Pallas kernels: 7.65 us -> 7.69 us  [call(): pl.pallas_call(kernel, out_shape=[jax.ShapeDtypeStruct(shape, jnp.float32...]
    ppermute x6 -> x8, waiting for transfers between devices: 2.57 us -> 2.58 us  [swap_cores(): return lax.ppermute(array, 'grad', [(0, 1), (1, 0)])]
  transfers between devices with their start and end apart: 14 -> 16, of which waited for: 5 -> 5; matrix products, arithmetic and copies ran while one was open for 0% -> 0% of each run, Pallas kernels for 1% -> 1%
where the time goes in v6:
time: 44.8 us; the launch traced here: 44.7 us
  starting transfers between devices  25.4 us (57%)
  waiting for transfers between devices  10.3 us (23%)
  Pallas kernels  7.69 us (17%)
  other arithmetic  1.17 us (3%)
    ppermute x2, starting transfers between devices, per_device(): lax.ppermute(array, AXES, pairs)  10.1 us
    pallas_call x8, Pallas kernels, call(): pl.pallas_call(kernel, out_shape=[jax.ShapeDtypeStruct(shape, jnp.float32...  7.69 us
    ppermute x8, starting transfers between devices, swap_cores(): return lax.ppermute(array, 'grad', [(0, 1), (1, 0)])  5.95 us
    ppermute x1, starting transfers between devices, per_device(): hopped.append([lax.ppermute(inverse[1], AXES, pairs) for pairs in hops])  4.18 us
    ppermute x2, waiting for transfers between devices, per_device(): lax.ppermute(array, AXES, pairs)  3.93 us
    ppermute x1, waiting for transfers between devices, per_device(): lax.ppermute(outer, AXES, outward)  3.82 us
    ppermute x1, starting transfers between devices, per_device(): lax.ppermute(outer, AXES, outward)  2.75 us
    ppermute x8, waiting for transfers between devices, swap_cores(): return lax.ppermute(array, 'grad', [(0, 1), (1, 0)])  2.58 us
  transfers between devices with their start and end apart: 16, of which 5 were waited for; matrix products, arithmetic and copies ran while one was open for 0% of the time, Pallas kernels for 1%

profile of v6, /device:TPU:0, one launch (start us, length us, event | category | flops | bytes accessed | tf_op | source)
XLA Modules:
  0.0 44.7 jit_solution(8504881740107895742)
XLA Ops:
  0.0 1.2 %select_bitcast_fusion = (bf16[384,512]{1,0:T(8,128)(2,1)S(1)}, bf16[384,512]{1,0:T(8,128)(2,1)S(1)}) fusion(bf16[1,384,512]{2,1,0:T(8,128)(2,1)} %param.4, bf16[1,384,512]{2,1,0:T(8,128)(2,1)} %param.3, pred[]{:T(512)S(6)} %eq.4), kind=kLoop, calls=%fused_computation | loop fusion | flops 393216 | bytes 1572865 | tf_op jit(solution)/shard_map/jit(_where)/select_n | solution.py:486
  1.2 0.0 copy-start
  1.2 0.5 %shard_map.38 = f32[1040,128]{1,0:T(8,128)S(1)} custom-call(bf16[384,512]{1,0:T(8,128)(2,1)S(1)} %get-tuple-element.23.x_ref), custom_call_target="tpu_custom_call" | custom-call | tf_op jit(solution)/shard_map/pallas_call | solution.py:356
  1.7 0.5 %collective-permute-start = (f32[1040,128]{1,0:T(8,128)S(1)}, f32[1040,128]{1,0:T(8,128)S(1)}, u32[]{:S(2)}, u32[]{:S(2)}) collective-permute-start(f32[1040,128]{1,0:T(8,128)S(1)} %shard_map.38), channel_id=1, source_target_pairs={{0,1},{1,0},{2,3},{3,2},{4,5},{5,4},{6,7},{7,6},{8,9},{9,8},{10,11... | collective-permute-start | bytes 1597448 | tf_op jit(solution)/shard_map/ppermute | solution.py:472
  2.2 0.0 copy-done
  2.2 0.4 collective-permute-start.1
  2.6 0.5 %shard_map.37.kept_ref = f32[1040,128]{1,0:T(8,128)S(1)} custom-call(bf16[384,512]{1,0:T(8,128)(2,1)S(1)} %get-tuple-element.24.x_ref), custom_call_target="tpu_custom_call" | custom-call | tf_op jit(solution)/shard_map/pallas_call | solution.py:356
  3.0 1.1 %collective-permute-done.1.other_rows_ref.refs_5_ = f32[128,512]{1,0:T(8,128)S(1)} collective-permute-done((f32[128,512]{1,0:T(8,128)S(1)}, f32[128,512]{1,0:T(8,128)S(1)}, u32[]{:S(2)}, u32[]{:S(2)}) %collective-permute-start.1) | collective-permute-done | bytes 262176 | tf_op jit(solution)/shard_map/ppermute | solution.py:472
  4.1 0.0 collective-permute-done.other_ref
  4.1 0.2 shard_map.39
  4.3 2.7 %collective-permute-start.2 = (f32[1040,128]{1,0:T(8,128)S(1)}, f32[1040,128]{1,0:T(8,128)S(1)}, u32[]{:S(2)}, u32[]{:S(2)}) collective-permute-start(f32[1040,128]{1,0:T(8,128)S(1)} %get-tuple-element.14), channel_id=1, source_target_pairs={{0,5},{1,17},{2,18},{3,6},{4,20},{5,0},{6,3},{7,23},{8,13},{9,25},... | collective-permute-start | bytes 1597448 | tf_op jit(solution)/shard_map/ppermute | solution.py:497
  7.0 0.1 collective-permute-start.3
  7.1 0.7 %collective-permute-start.4 = (f32[1040,128]{1,0:T(8,128)S(1)}, f32[1040,128]{1,0:T(8,128)S(1)}, u32[]{:S(2)}, u32[]{:S(2)}) collective-permute-start(f32[1040,128]{1,0:T(8,128)S(1)} %get-tuple-element.15), channel_id=1, source_target_pairs={{12,5},{1,8},{2,11},{15,6},{28,21},{17,24},{18,27},{31,22}} | collective-permute-start | bytes 1597448 | tf_op jit(solution)/shard_map/ppermute | solution.py:499
  7.8 4.0 %collective-permute-start.5 = (f32[1040,128]{1,0:T(8,128)S(1)}, f32[1040,128]{1,0:T(8,128)S(1)}, u32[]{:S(2)}, u32[]{:S(2)}) collective-permute-start(f32[1040,128]{1,0:T(8,128)S(1)} %get-tuple-element.15), channel_id=1, source_target_pairs={{0,1},{1,0},{2,3},{3,2},{4,5},{5,4},{6,7},{7,6},{8,9},{9,8},{10,11... | collective-permute-start | bytes 1597448 | tf_op jit(solution)/shard_map/ppermute | solution.py:472
  11.7 3.8 %collective-permute-done.2.refs_0_.refs_6_ = f32[1040,128]{1,0:T(8,128)S(1)} collective-permute-done((f32[1040,128]{1,0:T(8,128)S(1)}, f32[1040,128]{1,0:T(8,128)S(1)}, u32[]{:S(2)}, u32[]{:S(2)}) %collective-permute-start.2) | collective-permute-done | bytes 532512 | tf_op jit(solution)/shard_map/ppermute | solution.py:497
  15.5 0.0 collective-permute-done.3.refs_1_
  15.5 0.0 collective-permute-done.4.refs_2_
  15.5 0.0 collective-permute-done.5.refs_3_
  15.5 4.7 %shard_map.40 = (f32[512,128]{1,0:T(8,128)S(1)}, f32[528,128]{1,0:T(8,128)S(1)}, f32[776,128]{1,0:T(8,128)S(1)}, f32[264,128]{1,0:T(8,128)S(1)}) custom-call(f32[1040,128]{1,0:T(8,128)S(1)} %collective-permute-done.2.refs_0_.refs_6_, f32[1040,128]{1,0:T(8,128)S(1)} %collective-permute-done.3.refs_1_, f32[1040,128]{1,0:T(8,128)S(1)} %collective-permute-done.4.refs_2_, ...), custom_call_target="tpu_custom_call" | custom-call | tf_op jit(solution)/shard_map/pallas_call | solution.py:356
  20.2 4.2 %collective-permute-start.8 = (f32[528,128]{1,0:T(8,128)S(1)}, f32[528,128]{1,0:T(8,128)S(1)}, u32[]{:S(2)}, u32[]{:S(2)}) collective-permute-start(f32[528,128]{1,0:T(8,128)S(1)} %get-tuple-element.18.refs_0_), channel_id=1, source_target_pairs={{0,1},{1,0},{2,3},{3,2},{4,8},{5,7},{6,10},{7,5},{8,4},{9,11},{10,... | collective-permute-start | bytes 811016 | tf_op jit(solution)/shard_map/ppermute | solution.py:516
  24.4 0.1 collective-permute-start.6
  24.5 0.4 collective-permute-start.9
  24.9 1.5 %collective-permute-start.11 = (f32[776,128]{1,0:T(8,128)S(1)}, f32[776,128]{1,0:T(8,128)S(1)}, u32[]{:S(2)}, u32[]{:S(2)}) collective-permute-start(f32[776,128]{1,0:T(8,128)S(1)} %get-tuple-element.20), channel_id=1, source_target_pairs={{0,16},{1,5},{2,6},{3,19},{4,20},{5,1},{6,2},{7,23},{8,12},{9,25},... | collective-permute-start | bytes 1191944 | tf_op jit(solution)/shard_map/ppermute | solution.py:515
  26.5 0.0 collective-permute-done.9.rest_ref
  26.5 0.0 collective-permute-done.8.hopped_ref.refs_1_
  26.5 7.4 %collective-permute-start.10 = (f32[528,128]{1,0:T(8,128)S(1)}, f32[528,128]{1,0:T(8,128)S(1)}, u32[]{:S(2)}, u32[]{:S(2)}) collective-permute-start(f32[528,128]{1,0:T(8,128)S(1)} %shard_map.41), channel_id=1, source_target_pairs={{0,4},{1,2},{2,1},{3,7},{4,0},{5,6},{6,5},{7,3},{8,11},{9,13},{10,... | collective-permute-start | bytes 811016 | tf_op jit(solution)/shard_map/ppermute | solution.py:522
  33.9 0.0 collective-permute-start.14
  33.9 0.0 collective-permute-done.6.refs_1_
  33.9 2.7 %collective-permute-start.7 = (f32[512,128]{1,0:T(8,128)S(1)}, f32[512,128]{1,0:T(8,128)S(1)}, u32[]{:S(2)}, u32[]{:S(2)}) collective-permute-start(f32[512,128]{1,0:T(8,128)S(1)} %collective-permute-done.6.refs_1_), channel_id=1, source_target_pairs={{0,4},{1,2},{2,1},{3,7},{4,0},{5,6},{6,5},{7,3},{8,11},{9,13},{10,... | collective-permute-start | bytes 786440 | tf_op jit(solution)/shard_map/ppermute | solution.py:522
  36.6 0.0 collective-permute-done.11.refs_3_.refs_8_
  36.6 1.7 %collective-permute-done.10.refs_2_.refs_10_ = f32[528,128]{1,0:T(8,128)S(1)} collective-permute-done((f32[528,128]{1,0:T(8,128)S(1)}, f32[528,128]{1,0:T(8,128)S(1)}, u32[]{:S(2)}, u32[]{:S(2)}) %collective-permute-start.10) | collective-permute-done | bytes 270368 | tf_op jit(solution)/shard_map/ppermute | solution.py:522
  38.4 0.1 collective-permute-start.13
  38.5 0.5 %collective-permute-start.15 = (f32[528,128]{1,0:T(8,128)S(1)}, f32[528,128]{1,0:T(8,128)S(1)}, u32[]{:S(2)}, u32[]{:S(2)}) collective-permute-start(f32[528,128]{1,0:T(8,128)S(1)} %collective-permute-done.10.refs_2_.refs_10_), channel_id=1, source_target_pairs={{0,1},{1,0},{2,3},{3,2},{4,5},{5,4},{6,7},{7,6},{8,9},{9,8},{10,11... | collective-permute-start | bytes 811016 | tf_op jit(solution)/shard_map/ppermute | solution.py:472
  39.0 2.2 %collective-permute-done.7.refs_2_.refs_9_ = f32[512,128]{1,0:T(8,128)S(1)} collective-permute-done((f32[512,128]{1,0:T(8,128)S(1)}, f32[512,128]{1,0:T(8,128)S(1)}, u32[]{:S(2)}, u32[]{:S(2)}) %collective-permute-start.7) | collective-permute-done | bytes 262176 | tf_op jit(solution)/shard_map/ppermute | solution.py:522
  41.2 0.1 collective-permute-start.12
  41.3 0.0 collective-permute-done.14.refs_7_
  41.3 1.5 %collective-permute-done.12.refs_2_ = f32[512,128]{1,0:T(8,128)S(1)} collective-permute-done((f32[512,128]{1,0:T(8,128)S(1)}, f32[512,128]{1,0:T(8,128)S(1)}, u32[]{:S(2)}, u32[]{:S(2)}) %collective-permute-start.12) | collective-permute-done | bytes 262176 | tf_op jit(solution)/shard_map/ppermute | solution.py:472
  42.8 0.0 collective-permute-done.13.refs_3_
  42.8 0.0 collective-permute-done.15.refs_11_
  42.8 1.9 %shard_map.44 = f32[128,512]{1,0:T(8,128)} custom-call(f32[512,128]{1,0:T(8,128)S(1)} %shard_map.42.refs_0_, f32[528,128]{1,0:T(8,128)S(1)} %shard_map.43.refs_1_, f32[512,128]{1,0:T(8,128)S(1)} %collective-permute-done.12.refs_2_, f32[528,128]{1,0:T(8,128)S(1)} %collective-permute-done.13.refs_3_, f32[128,512]{1,0:T(8,128)S(1)} %bitcast.8, ...), custom_call_target="tpu_custom_call" | custom-call | tf_op jit(solution)/shard_map/pallas_call | solution.py:356
  (3 shorter events, 0.1 us)
Async XLA Ops:
  1.2 1.0 %copy-start = (f32[1,128,512]{2,1,0:T(8,128)S(1)}, f32[1,128,512]{2,1,0:T(8,128)}, u32[]{:S(2)}) copy-start(f32[1,128,512]{2,1,0:T(8,128)} %param.5) | copy-start | bytes 786436
  1.7 2.4 %collective-permute-start = (f32[1040,128]{1,0:T(8,128)S(1)}, f32[1040,128]{1,0:T(8,128)S(1)}, u32[]{:S(2)}, u32[]{:S(2)}) collective-permute-start(f32[1040,128]{1,0:T(8,128)S(1)} %shard_map.38), channel_id=1, source_target_pairs={{0,1},{1,0},{2,3},{3,2},{4,5},{5,4},{6,7},{7,6},{8,9},{9,8},{10,11... | collective-permute-start | bytes 1597448 | tf_op jit(solution)/shard_map/ppermute | solution.py:472
  2.2 1.9 %collective-permute-start.1 = (f32[128,512]{1,0:T(8,128)S(1)}, f32[128,512]{1,0:T(8,128)S(1)}, u32[]{:S(2)}, u32[]{:S(2)}) collective-permute-start(f32[128,512]{1,0:T(8,128)S(1)} %bitcast.6), channel_id=1, source_target_pairs={{0,1},{1,0},{2,3},{3,2},{4,5},{5,4},{6,7},{7,6},{8,9},{9,8},{10,11... | collective-permute-start | bytes 786440 | tf_op jit(solution)/shard_map/ppermute | solution.py:472
  4.3 11.3 %collective-permute-start.2 = (f32[1040,128]{1,0:T(8,128)S(1)}, f32[1040,128]{1,0:T(8,128)S(1)}, u32[]{:S(2)}, u32[]{:S(2)}) collective-permute-start(f32[1040,128]{1,0:T(8,128)S(1)} %get-tuple-element.14), channel_id=1, source_target_pairs={{0,5},{1,17},{2,18},{3,6},{4,20},{5,0},{6,3},{7,23},{8,13},{9,25},... | collective-permute-start | bytes 1597448 | tf_op jit(solution)/shard_map/ppermute | solution.py:497
  7.0 8.5 %collective-permute-start.3 = (f32[1040,128]{1,0:T(8,128)S(1)}, f32[1040,128]{1,0:T(8,128)S(1)}, u32[]{:S(2)}, u32[]{:S(2)}) collective-permute-start(f32[1040,128]{1,0:T(8,128)S(1)} %get-tuple-element.15), channel_id=1, source_target_pairs={{0,1},{1,0},{2,3},{3,2},{4,20},{5,8},{6,11},{7,23},{8,5},{9,25},{1... | collective-permute-start | bytes 1597448 | tf_op jit(solution)/shard_map/ppermute | solution.py:498
  7.1 8.5 %collective-permute-start.4 = (f32[1040,128]{1,0:T(8,128)S(1)}, f32[1040,128]{1,0:T(8,128)S(1)}, u32[]{:S(2)}, u32[]{:S(2)}) collective-permute-start(f32[1040,128]{1,0:T(8,128)S(1)} %get-tuple-element.15), channel_id=1, source_target_pairs={{12,5},{1,8},{2,11},{15,6},{28,21},{17,24},{18,27},{31,22}} | collective-permute-start | bytes 1597448 | tf_op jit(solution)/shard_map/ppermute | solution.py:499
  7.8 7.8 %collective-permute-start.5 = (f32[1040,128]{1,0:T(8,128)S(1)}, f32[1040,128]{1,0:T(8,128)S(1)}, u32[]{:S(2)}, u32[]{:S(2)}) collective-permute-start(f32[1040,128]{1,0:T(8,128)S(1)} %get-tuple-element.15), channel_id=1, source_target_pairs={{0,1},{1,0},{2,3},{3,2},{4,5},{5,4},{6,7},{7,6},{8,9},{9,8},{10,11... | collective-permute-start | bytes 1597448 | tf_op jit(solution)/shard_map/ppermute | solution.py:472
  20.2 6.2 %collective-permute-start.8 = (f32[528,128]{1,0:T(8,128)S(1)}, f32[528,128]{1,0:T(8,128)S(1)}, u32[]{:S(2)}, u32[]{:S(2)}) collective-permute-start(f32[528,128]{1,0:T(8,128)S(1)} %get-tuple-element.18.refs_0_), channel_id=1, source_target_pairs={{0,1},{1,0},{2,3},{3,2},{4,8},{5,7},{6,10},{7,5},{8,4},{9,11},{10,... | collective-permute-start | bytes 811016 | tf_op jit(solution)/shard_map/ppermute | solution.py:516
  24.4 9.5 %collective-permute-start.6 = (f32[512,128]{1,0:T(8,128)S(1)}, f32[512,128]{1,0:T(8,128)S(1)}, u32[]{:S(2)}, u32[]{:S(2)}) collective-permute-start(f32[512,128]{1,0:T(8,128)S(1)} %get-tuple-element.17.refs_0_), channel_id=1, source_target_pairs={{0,1},{1,0},{2,3},{3,2},{4,8},{5,7},{6,10},{7,5},{8,4},{9,11},{10,... | collective-permute-start | bytes 786440 | tf_op jit(solution)/shard_map/ppermute | solution.py:514
  24.5 2.0 %collective-permute-start.9 = (f32[264,128]{1,0:T(8,128)S(1)}, f32[264,128]{1,0:T(8,128)S(1)}, u32[]{:S(2)}, u32[]{:S(2)}) collective-permute-start(f32[264,128]{1,0:T(8,128)S(1)} %get-tuple-element.19), channel_id=1, source_target_pairs={{0,1},{1,0},{2,3},{3,2},{4,5},{5,4},{6,7},{7,6},{8,9},{9,8},{10,11... | collective-permute-start | bytes 405512 | tf_op jit(solution)/shard_map/ppermute | solution.py:472
  24.9 11.7 %collective-permute-start.11 = (f32[776,128]{1,0:T(8,128)S(1)}, f32[776,128]{1,0:T(8,128)S(1)}, u32[]{:S(2)}, u32[]{:S(2)}) collective-permute-start(f32[776,128]{1,0:T(8,128)S(1)} %get-tuple-element.20), channel_id=1, source_target_pairs={{0,16},{1,5},{2,6},{3,19},{4,20},{5,1},{6,2},{7,23},{8,12},{9,25},... | collective-permute-start | bytes 1191944 | tf_op jit(solution)/shard_map/ppermute | solution.py:515
  26.5 11.9 %collective-permute-start.10 = (f32[528,128]{1,0:T(8,128)S(1)}, f32[528,128]{1,0:T(8,128)S(1)}, u32[]{:S(2)}, u32[]{:S(2)}) collective-permute-start(f32[528,128]{1,0:T(8,128)S(1)} %shard_map.41), channel_id=1, source_target_pairs={{0,4},{1,2},{2,1},{3,7},{4,0},{5,6},{6,5},{7,3},{8,11},{9,13},{10,... | collective-permute-start | bytes 811016 | tf_op jit(solution)/shard_map/ppermute | solution.py:522
  33.9 7.4 %collective-permute-start.14 = (f32[1040,128]{1,0:T(8,128)S(1)}, f32[1040,128]{1,0:T(8,128)S(1)}, u32[]{:S(2)}, u32[]{:S(2)}) collective-permute-start(f32[1040,128]{1,0:T(8,128)S(1)} %collective-permute-done.2.refs_0_.refs_6_), channel_id=1, source_target_pairs={{0,1},{1,0},{2,3},{3,2},{4,5},{5,4},{6,7},{7,6},{8,9},{9,8},{10,11... | collective-permute-start | bytes 1597448 | tf_op jit(solution)/shard_map/ppermute | solution.py:472
  33.9 7.2 %collective-permute-start.7 = (f32[512,128]{1,0:T(8,128)S(1)}, f32[512,128]{1,0:T(8,128)S(1)}, u32[]{:S(2)}, u32[]{:S(2)}) collective-permute-start(f32[512,128]{1,0:T(8,128)S(1)} %collective-permute-done.6.refs_1_), channel_id=1, source_target_pairs={{0,4},{1,2},{2,1},{3,7},{4,0},{5,6},{6,5},{7,3},{8,11},{9,13},{10,... | collective-permute-start | bytes 786440 | tf_op jit(solution)/shard_map/ppermute | solution.py:522
  38.4 4.4 %collective-permute-start.13 = (f32[528,128]{1,0:T(8,128)S(1)}, f32[528,128]{1,0:T(8,128)S(1)}, u32[]{:S(2)}, u32[]{:S(2)}) collective-permute-start(f32[528,128]{1,0:T(8,128)S(1)} %shard_map.43.refs_1_), channel_id=1, source_target_pairs={{0,1},{1,0},{2,3},{3,2},{4,5},{5,4},{6,7},{7,6},{8,9},{9,8},{10,11... | collective-permute-start | bytes 811016 | tf_op jit(solution)/shard_map/ppermute | solution.py:472
  38.5 4.3 %collective-permute-start.15 = (f32[528,128]{1,0:T(8,128)S(1)}, f32[528,128]{1,0:T(8,128)S(1)}, u32[]{:S(2)}, u32[]{:S(2)}) collective-permute-start(f32[528,128]{1,0:T(8,128)S(1)} %collective-permute-done.10.refs_2_.refs_10_), channel_id=1, source_target_pairs={{0,1},{1,0},{2,3},{3,2},{4,5},{5,4},{6,7},{7,6},{8,9},{9,8},{10,11... | collective-permute-start | bytes 811016 | tf_op jit(solution)/shard_map/ppermute | solution.py:472
  41.2 1.6 %collective-permute-start.12 = (f32[512,128]{1,0:T(8,128)S(1)}, f32[512,128]{1,0:T(8,128)S(1)}, u32[]{:S(2)}, u32[]{:S(2)}) collective-permute-start(f32[512,128]{1,0:T(8,128)S(1)} %shard_map.42.refs_0_), channel_id=1, source_target_pairs={{0,1},{1,0},{2,3},{3,2},{4,5},{5,4},{6,7},{7,6},{8,9},{9,8},{10,11... | collective-permute-start | bytes 786440 | tf_op jit(solution)/shard_map/ppermute | solution.py:472

commit v7 on v6

--- a/solution.py
+++ b/solution.py
@@ -269,50 +269,47 @@
                 out_ref[size:, :] = jnp.zeros((rows - size, LANE), jnp.float32)
 
 
-def final_kernel(order, spread, *refs):
-    own, other, refs = refs[:2], refs[2:4], refs[4:]
-    own_rows_ref, other_rows_ref, outer_ref, outer_other_ref, direct_ref, relayed_a, relayed_b, other_b, *refs = refs
-    out_ref, left_ref, right_ref, tile_ref, result_ref, b_ref, sems = refs
-    core = lax.axis_index("grad")
-    position = lax.axis_index("dp") * lax.axis_size("grad") + core
-    mine = lax.rem(position, spread)
-    rows_dev = out_ref.shape[0]
-
+def fill_left(order, mine, a_ref, b_ref, left_ref):
+    second = lax.rem(lax.div(lax.axis_index("dp"), 2), 2)
+    for row in range(order // LANE):
+
+        @pl.when(mine == row)
+        def _():
+            for column in range(order // LANE):
+                block = stored_block(a_ref, b_ref, order, row, column, second)
+                left_ref[:, column * LANE : (column + 1) * LANE] = block
+
+
+def fill_right(order, a_ref, b_ref, left_b_ref, joined_ref, right_ref):
     cut = lax.axis_index("cuts")
     zq = lax.rem(lax.axis_index("dp"), QUAD)
     was_direct = jnp.logical_and(jnp.logical_not(is_middle()), (zq ^ 1) == 2 - lax.rem(cut, 2))
-    left_second = lax.rem(lax.div(position, spread), 2)
-
-    def fill(left, right):
-        used = b_ref.shape[0] // 2
-        b_ref[...] = right[1][...]
-
-        @pl.when(was_direct)
-        def _():
-            b_ref[used:, :] = left[1][used:, :]
-
-        unpack(
-            lambda start, size: right[0][pl.ds(start, size), :],
-            lambda start, size: b_ref[pl.ds(start, size), :],
-            order,
-            right_ref,
-            lax.rem(cut, 2),
-        )
-        for row in range(order // LANE):
-
-            @pl.when(mine == row)
-            def _():
-                for column in range(order // LANE):
-                    block = stored_block(*left, order, row, column, left_second)
-                    left_ref[:, column * LANE : (column + 1) * LANE] = block
-
-    @pl.when(core != 0)
-    def _():
-        fill(own, other)
-
-    @pl.when(core == 0)
-    def _():
-        fill(other, own)
+    used = joined_ref.shape[0] // 2
+    joined_ref[...] = b_ref[...]
+
+    @pl.when(was_direct)
+    def _():
+        joined_ref[used:, :] = left_b_ref[used:, :]
+
+    unpack(
+        lambda start, size: a_ref[pl.ds(start, size), :],
+        lambda start, size: joined_ref[pl.ds(start, size), :],
+        order,
+        right_ref,
+        lax.rem(cut, 2),
+    )
+
+
+def place_of_rows(spread):
+    core = lax.axis_index("grad")
+    return core, lax.rem(lax.axis_index("dp") * lax.axis_size("grad") + core, spread)
+
+
+def first_kernel(order, spread, own_a, own_b, other_b, *refs):
+    own_rows_ref, other_rows_ref, outer_ref, outer_other_ref, direct_ref, relayed_a, relayed_b, relayed_other, *refs = refs
+    left_out, right_out, left_ref, right_ref, tile_ref, joined_ref = refs
+    core, mine = place_of_rows(spread)
+    rows_dev = own_rows_ref.shape[0]
 
     def place(position):
         return pl.ds(pl.multiple_of(position * rows_dev, rows_dev), rows_dev)
@@ -323,7 +320,7 @@
     cases = (
         (False, True, (outer_ref,)),
         (False, False, (outer_other_ref,)),
-        (True, True, (direct_ref.at[: relayed_a.shape[0]], other_b)),
+        (True, True, (direct_ref.at[: relayed_a.shape[0]], relayed_other)),
         (True, False, (relayed_a, relayed_b)),
     )
     for middle, arrived, parts in cases:
@@ -340,16 +337,41 @@
                     ]
                     start += rows_dev
 
-    middle = halves(times(halves(left_ref[...]), halves(tile_ref[...])))
+    @pl.when(core != 0)
+    def _():
+        fill_left(order, mine, own_a, own_b, left_ref)
+        left_out[...] = times(halves(left_ref[...]), halves(tile_ref[...]))
+
+    @pl.when(core == 0)
+    def _():
+        fill_right(order, own_a, own_b, other_b, joined_ref, right_ref)
+        right_out[...] = times(halves(tile_ref[...]), halves(right_ref[...]))
+
+
+def last_kernel(order, spread, own_b, other_a, other_b, first_left, first_right, out_ref, *refs):
+    left_ref, right_ref, joined_ref, result_ref, sems = refs
+    core, mine = place_of_rows(spread)
     step = order // 2
-    copies = []
-    for turn in range(2):
-        columns = pl.ds(turn * step, step)
-        result_ref[turn] = times(middle, halves(right_ref[:, turn * step : (turn + 1) * step]))
-        copies.append(pltpu.make_async_copy(result_ref.at[turn], out_ref.at[:, columns], sems.at[turn]))
-        copies[-1].start()
-    for copy in copies:
-        copy.wait()
+
+    def finish(left, right_ref):
+        copies = []
+        for turn in range(2):
+            columns = pl.ds(turn * step, step)
+            result_ref[turn] = times(left, halves(right_ref[:, turn * step : (turn + 1) * step]))
+            copies.append(pltpu.make_async_copy(result_ref.at[turn], out_ref.at[:, columns], sems.at[turn]))
+            copies[-1].start()
+        for copy in copies:
+            copy.wait()
+
+    @pl.when(core != 0)
+    def _():
+        fill_right(order, other_a, other_b, own_b, joined_ref, right_ref)
+        finish(halves(first_left[...]), right_ref)
+
+    @pl.when(core == 0)
+    def _():
+        fill_left(order, mine, other_a, other_b, left_ref)
+        finish(halves(left_ref[...]), first_right)
 
 
 def call(kernel, shapes, scratch, *args, space=pltpu.VMEM):
@@ -536,19 +558,15 @@
             *relayed[part],
             direct,
         )
-    (out,) = call(
-        functools.partial(final_kernel, order, spread),
-        [grads.shape],
-        [
-            pltpu.VMEM((LANE, order), jnp.float32),
-            square_scratch,
-            square_scratch,
-            pltpu.VMEM((2, LANE, order // 2), jnp.float32),
-            pltpu.VMEM((rest, LANE), jnp.float32),
-            pltpu.SemaphoreType.DMA((2,)),
-        ],
+    other_a, other_b = map(swap_cores, own)
+    left_scratch = pltpu.VMEM((LANE, order), jnp.float32)
+    joined_scratch = pltpu.VMEM((rest, LANE), jnp.float32)
+    first = call(
+        functools.partial(first_kernel, order, spread),
+        [(LANE, order), (order, order)],
+        [left_scratch, square_scratch, square_scratch, joined_scratch],
         *own,
-        *map(swap_cores, own),
+        other_b,
         grads,
         other_rows,
         outer_rows,
@@ -556,6 +574,21 @@
         direct,
         *arrived,
         swap_cores(arrived[1]),
+    )
+    (out,) = call(
+        functools.partial(last_kernel, order, spread),
+        [grads.shape],
+        [
+            left_scratch,
+            square_scratch,
+            joined_scratch,
+            pltpu.VMEM((2, LANE, order // 2), jnp.float32),
+            pltpu.SemaphoreType.DMA((2,)),
+        ],
+        own[1],
+        other_a,
+        other_b,
+        *first,
         space=pl.ANY,
     )
     return out[None]

time: 44.8 us -> 44.2 us (0.987)
  waiting for transfers between devices: 10.3 us -> 9.1 us
  Pallas kernels: 7.69 us -> 8.27 us
    ppermute x8, waiting for transfers between devices: 2.58 us -> 1.34 us  [swap_cores(): return lax.ppermute(array, 'grad', [(0, 1), (1, 0)])]
    pallas_call x8 -> x9, Pallas kernels: 7.69 us -> 8.27 us  [call(): pl.pallas_call(kernel, out_shape=[jax.ShapeDtypeStruct(shape, jnp.float32...]
  transfers between devices with their start and end apart: 16 -> 16, of which waited for: 5 -> 5; matrix products, arithmetic and copies ran while one was open for 0% -> 0% of each run, Pallas kernels for 1% -> 4%
where the time goes in v7:
time: 44.2 us; the launch traced here: 44 us
  starting transfers between devices  25.4 us (57%)
  waiting for transfers between devices  9.1 us (21%)
  Pallas kernels  8.27 us (19%)
  other arithmetic  1.17 us (3%)
    ppermute x2, starting transfers between devices, per_device(): lax.ppermute(array, AXES, pairs)  10.1 us
    pallas_call x9, Pallas kernels, call(): pl.pallas_call(kernel, out_shape=[jax.ShapeDtypeStruct(shape, jnp.float32...  8.27 us
    ppermute x8, starting transfers between devices, swap_cores(): return lax.ppermute(array, 'grad', [(0, 1), (1, 0)])  5.95 us
    ppermute x1, starting transfers between devices, per_device(): hopped.append([lax.ppermute(inverse[1], AXES, pairs) for pairs in hops])  4.17 us
    ppermute x2, waiting for transfers between devices, per_device(): lax.ppermute(array, AXES, pairs)  3.93 us
    ppermute x1, waiting for transfers between devices, per_device(): lax.ppermute(outer, AXES, outward)  3.82 us
    ppermute x1, starting transfers between devices, per_device(): lax.ppermute(outer, AXES, outward)  2.75 us
    ppermute x1, starting transfers between devices, per_device(): direct = lax.ppermute(direct, AXES, outward)  1.53 us
  transfers between devices with their start and end apart: 16, of which 5 were waited for; matrix products, arithmetic and copies ran while one was open for 0% of the time, Pallas kernels for 4%

profile of v7, /device:TPU:0, one launch (start us, length us, event | category | flops | bytes accessed | tf_op | source)
XLA Modules:
  0.0 44.0 jit_solution(9940431420509479583)
XLA Ops:
  0.0 1.2 %select_bitcast_fusion = (bf16[384,512]{1,0:T(8,128)(2,1)S(1)}, bf16[384,512]{1,0:T(8,128)(2,1)S(1)}) fusion(bf16[1,384,512]{2,1,0:T(8,128)(2,1)} %param.4, bf16[1,384,512]{2,1,0:T(8,128)(2,1)} %param.3, pred[]{:T(512)S(6)} %eq.4), kind=kLoop, calls=%fused_computation | loop fusion | flops 393216 | bytes 1572865 | tf_op jit(solution)/shard_map/jit(_where)/select_n | solution.py:508
  1.2 0.0 copy-start
  1.2 0.5 %shard_map.38 = f32[1040,128]{1,0:T(8,128)S(1)} custom-call(bf16[384,512]{1,0:T(8,128)(2,1)S(1)} %get-tuple-element.27.x_ref), custom_call_target="tpu_custom_call" | custom-call | tf_op jit(solution)/shard_map/pallas_call | solution.py:378
  1.7 0.5 %collective-permute-start = (f32[1040,128]{1,0:T(8,128)S(1)}, f32[1040,128]{1,0:T(8,128)S(1)}, u32[]{:S(2)}, u32[]{:S(2)}) collective-permute-start(f32[1040,128]{1,0:T(8,128)S(1)} %shard_map.38), channel_id=1, source_target_pairs={{0,1},{1,0},{2,3},{3,2},{4,5},{5,4},{6,7},{7,6},{8,9},{9,8},{10,11... | collective-permute-start | bytes 1597448 | tf_op jit(solution)/shard_map/ppermute | solution.py:494
  2.2 0.0 copy-done
  2.2 0.4 collective-permute-start.1
  2.6 0.5 %shard_map.37.kept_ref = f32[1040,128]{1,0:T(8,128)S(1)} custom-call(bf16[384,512]{1,0:T(8,128)(2,1)S(1)} %get-tuple-element.28.x_ref), custom_call_target="tpu_custom_call" | custom-call | tf_op jit(solution)/shard_map/pallas_call | solution.py:378
  3.0 1.1 %collective-permute-done.1.other_rows_ref.refs_1_ = f32[128,512]{1,0:T(8,128)S(1)} collective-permute-done((f32[128,512]{1,0:T(8,128)S(1)}, f32[128,512]{1,0:T(8,128)S(1)}, u32[]{:S(2)}, u32[]{:S(2)}) %collective-permute-start.1) | collective-permute-done | bytes 262176 | tf_op jit(solution)/shard_map/ppermute | solution.py:494
  4.1 0.0 collective-permute-done.other_ref
  4.1 0.2 shard_map.39
  4.3 2.7 %collective-permute-start.2 = (f32[1040,128]{1,0:T(8,128)S(1)}, f32[1040,128]{1,0:T(8,128)S(1)}, u32[]{:S(2)}, u32[]{:S(2)}) collective-permute-start(f32[1040,128]{1,0:T(8,128)S(1)} %get-tuple-element.16), channel_id=1, source_target_pairs={{0,5},{1,17},{2,18},{3,6},{4,20},{5,0},{6,3},{7,23},{8,13},{9,25},... | collective-permute-start | bytes 1597448 | tf_op jit(solution)/shard_map/ppermute | solution.py:519
  7.0 0.1 collective-permute-start.3
  7.1 0.7 %collective-permute-start.4 = (f32[1040,128]{1,0:T(8,128)S(1)}, f32[1040,128]{1,0:T(8,128)S(1)}, u32[]{:S(2)}, u32[]{:S(2)}) collective-permute-start(f32[1040,128]{1,0:T(8,128)S(1)} %get-tuple-element.17), channel_id=1, source_target_pairs={{12,5},{1,8},{2,11},{15,6},{28,21},{17,24},{18,27},{31,22}} | collective-permute-start | bytes 1597448 | tf_op jit(solution)/shard_map/ppermute | solution.py:521
  7.8 4.0 %collective-permute-start.5 = (f32[1040,128]{1,0:T(8,128)S(1)}, f32[1040,128]{1,0:T(8,128)S(1)}, u32[]{:S(2)}, u32[]{:S(2)}) collective-permute-start(f32[1040,128]{1,0:T(8,128)S(1)} %get-tuple-element.17), channel_id=1, source_target_pairs={{0,1},{1,0},{2,3},{3,2},{4,5},{5,4},{6,7},{7,6},{8,9},{9,8},{10,11... | collective-permute-start | bytes 1597448 | tf_op jit(solution)/shard_map/ppermute | solution.py:494
  11.7 3.8 %collective-permute-done.2.refs_0_.refs_2_ = f32[1040,128]{1,0:T(8,128)S(1)} collective-permute-done((f32[1040,128]{1,0:T(8,128)S(1)}, f32[1040,128]{1,0:T(8,128)S(1)}, u32[]{:S(2)}, u32[]{:S(2)}) %collective-permute-start.2) | collective-permute-done | bytes 532512 | tf_op jit(solution)/shard_map/ppermute | solution.py:519
  15.5 0.0 collective-permute-done.3.refs_1_
  15.5 0.0 collective-permute-done.4.refs_2_
  15.5 0.0 collective-permute-done.5.refs_3_
  15.5 4.7 %shard_map.40 = (f32[512,128]{1,0:T(8,128)S(1)}, f32[528,128]{1,0:T(8,128)S(1)}, f32[776,128]{1,0:T(8,128)S(1)}, f32[264,128]{1,0:T(8,128)S(1)}) custom-call(f32[1040,128]{1,0:T(8,128)S(1)} %collective-permute-done.2.refs_0_.refs_2_, f32[1040,128]{1,0:T(8,128)S(1)} %collective-permute-done.3.refs_1_, f32[1040,128]{1,0:T(8,128)S(1)} %collective-permute-done.4.refs_2_, ...), custom_call_target="tpu_custom_call" | custom-call | tf_op jit(solution)/shard_map/pallas_call | solution.py:378
  20.2 4.2 %collective-permute-start.6 = (f32[528,128]{1,0:T(8,128)S(1)}, f32[528,128]{1,0:T(8,128)S(1)}, u32[]{:S(2)}, u32[]{:S(2)}) collective-permute-start(f32[528,128]{1,0:T(8,128)S(1)} %get-tuple-element.19.refs_0_), channel_id=1, source_target_pairs={{0,1},{1,0},{2,3},{3,2},{4,8},{5,7},{6,10},{7,5},{8,4},{9,11},{10,... | collective-permute-start | bytes 811016 | tf_op jit(solution)/shard_map/ppermute | solution.py:538
  24.4 0.1 collective-permute-start.10
  24.5 0.4 collective-permute-start.7
  24.9 1.5 %collective-permute-start.9 = (f32[776,128]{1,0:T(8,128)S(1)}, f32[776,128]{1,0:T(8,128)S(1)}, u32[]{:S(2)}, u32[]{:S(2)}) collective-permute-start(f32[776,128]{1,0:T(8,128)S(1)} %get-tuple-element.21), channel_id=1, source_target_pairs={{0,16},{1,5},{2,6},{3,19},{4,20},{5,1},{6,2},{7,23},{8,12},{9,25},... | collective-permute-start | bytes 1191944 | tf_op jit(solution)/shard_map/ppermute | solution.py:537
  26.5 0.0 collective-permute-done.7.rest_ref
  26.5 0.0 collective-permute-done.6.hopped_ref.refs_1_
  26.5 7.4 %collective-permute-start.8 = (f32[528,128]{1,0:T(8,128)S(1)}, f32[528,128]{1,0:T(8,128)S(1)}, u32[]{:S(2)}, u32[]{:S(2)}) collective-permute-start(f32[528,128]{1,0:T(8,128)S(1)} %shard_map.41), channel_id=1, source_target_pairs={{0,4},{1,2},{2,1},{3,7},{4,0},{5,6},{6,5},{7,3},{8,11},{9,13},{10,... | collective-permute-start | bytes 811016 | tf_op jit(solution)/shard_map/ppermute | solution.py:544
  33.9 0.0 collective-permute-start.14
  33.9 0.0 collective-permute-done.10.refs_1_
  33.9 2.7 %collective-permute-start.11 = (f32[512,128]{1,0:T(8,128)S(1)}, f32[512,128]{1,0:T(8,128)S(1)}, u32[]{:S(2)}, u32[]{:S(2)}) collective-permute-start(f32[512,128]{1,0:T(8,128)S(1)} %collective-permute-done.10.refs_1_), channel_id=1, source_target_pairs={{0,4},{1,2},{2,1},{3,7},{4,0},{5,6},{6,5},{7,3},{8,11},{9,13},{10,... | collective-permute-start | bytes 786440 | tf_op jit(solution)/shard_map/ppermute | solution.py:544
  36.6 0.0 collective-permute-done.9.refs_3_.refs_4_
  36.6 1.7 %collective-permute-done.8.refs_2_.refs_6_ = f32[528,128]{1,0:T(8,128)S(1)} collective-permute-done((f32[528,128]{1,0:T(8,128)S(1)}, f32[528,128]{1,0:T(8,128)S(1)}, u32[]{:S(2)}, u32[]{:S(2)}) %collective-permute-start.8) | collective-permute-done | bytes 270368 | tf_op jit(solution)/shard_map/ppermute | solution.py:544
  38.4 0.1 collective-permute-start.13
  38.5 0.5 %collective-permute-start.15 = (f32[528,128]{1,0:T(8,128)S(1)}, f32[528,128]{1,0:T(8,128)S(1)}, u32[]{:S(2)}, u32[]{:S(2)}) collective-permute-start(f32[528,128]{1,0:T(8,128)S(1)} %collective-permute-done.8.refs_2_.refs_6_), channel_id=1, source_target_pairs={{0,1},{1,0},{2,3},{3,2},{4,5},{5,4},{6,7},{7,6},{8,9},{9,8},{10,11... | collective-permute-start | bytes 811016 | tf_op jit(solution)/shard_map/ppermute | solution.py:494
  39.0 2.2 %collective-permute-done.11.refs_2_.refs_5_ = f32[512,128]{1,0:T(8,128)S(1)} collective-permute-done((f32[512,128]{1,0:T(8,128)S(1)}, f32[512,128]{1,0:T(8,128)S(1)}, u32[]{:S(2)}, u32[]{:S(2)}) %collective-permute-start.11) | collective-permute-done | bytes 262176 | tf_op jit(solution)/shard_map/ppermute | solution.py:544
  41.2 0.1 collective-permute-start.12
  41.3 0.0 collective-permute-done.14.refs_3_
  41.3 0.0 collective-permute-done.13.other_b
  41.3 0.0 collective-permute-done.15.refs_7_
  41.3 1.2 %shard_map.44 = (f32[128,512]{1,0:T(8,128)S(1)}, f32[512,512]{1,0:T(8,128)S(1)}) custom-call(f32[512,128]{1,0:T(8,128)S(1)} %shard_map.43.own_a, f32[528,128]{1,0:T(8,128)S(1)} %shard_map.42.own_b, f32[528,128]{1,0:T(8,128)S(1)} %collective-permute-done.13.other_b, f32[128,512]{1,0:T(8,128)S(1)} %bitcast.8, ...), custom_call_target="tpu_custom_call" | custom-call | tf_op jit(solution)/shard_map/pallas_call | solution.py:378
  42.5 0.3 collective-permute-done.12.other_a
  42.8 1.2 %shard_map.45 = f32[128,512]{1,0:T(8,128)} custom-call(f32[528,128]{1,0:T(8,128)S(1)} %shard_map.42.own_b, f32[512,128]{1,0:T(8,128)S(1)} %collective-permute-done.12.other_a, f32[528,128]{1,0:T(8,128)S(1)} %collective-permute-done.13.other_b, f32[128,512]{1,0:T(8,128)S(1)} %get-tuple-element.25.first_left, f32[512,512]{1,0:T(8,128)S(1)} %get-tuple-element.26.first_right), custom_call_target="tpu_custom_call" | custom-call | tf_op jit(solution)/shard_map/pallas_call | solution.py:378
  (3 shorter events, 0.1 us)
Async XLA Ops:
  1.2 1.0 %copy-start = (f32[1,128,512]{2,1,0:T(8,128)S(1)}, f32[1,128,512]{2,1,0:T(8,128)}, u32[]{:S(2)}) copy-start(f32[1,128,512]{2,1,0:T(8,128)} %param.5) | copy-start | bytes 786436
  1.7 2.4 %collective-permute-start = (f32[1040,128]{1,0:T(8,128)S(1)}, f32[1040,128]{1,0:T(8,128)S(1)}, u32[]{:S(2)}, u32[]{:S(2)}) collective-permute-start(f32[1040,128]{1,0:T(8,128)S(1)} %shard_map.38), channel_id=1, source_target_pairs={{0,1},{1,0},{2,3},{3,2},{4,5},{5,4},{6,7},{7,6},{8,9},{9,8},{10,11... | collective-permute-start | bytes 1597448 | tf_op jit(solution)/shard_map/ppermute | solution.py:494
  2.2 1.9 %collective-permute-start.1 = (f32[128,512]{1,0:T(8,128)S(1)}, f32[128,512]{1,0:T(8,128)S(1)}, u32[]{:S(2)}, u32[]{:S(2)}) collective-permute-start(f32[128,512]{1,0:T(8,128)S(1)} %bitcast.6), channel_id=1, source_target_pairs={{0,1},{1,0},{2,3},{3,2},{4,5},{5,4},{6,7},{7,6},{8,9},{9,8},{10,11... | collective-permute-start | bytes 786440 | tf_op jit(solution)/shard_map/ppermute | solution.py:494
  4.3 11.3 %collective-permute-start.2 = (f32[1040,128]{1,0:T(8,128)S(1)}, f32[1040,128]{1,0:T(8,128)S(1)}, u32[]{:S(2)}, u32[]{:S(2)}) collective-permute-start(f32[1040,128]{1,0:T(8,128)S(1)} %get-tuple-element.16), channel_id=1, source_target_pairs={{0,5},{1,17},{2,18},{3,6},{4,20},{5,0},{6,3},{7,23},{8,13},{9,25},... | collective-permute-start | bytes 1597448 | tf_op jit(solution)/shard_map/ppermute | solution.py:519
  7.0 8.5 %collective-permute-start.3 = (f32[1040,128]{1,0:T(8,128)S(1)}, f32[1040,128]{1,0:T(8,128)S(1)}, u32[]{:S(2)}, u32[]{:S(2)}) collective-permute-start(f32[1040,128]{1,0:T(8,128)S(1)} %get-tuple-element.17), channel_id=1, source_target_pairs={{0,1},{1,0},{2,3},{3,2},{4,20},{5,8},{6,11},{7,23},{8,5},{9,25},{1... | collective-permute-start | bytes 1597448 | tf_op jit(solution)/shard_map/ppermute | solution.py:520
  7.1 8.5 %collective-permute-start.4 = (f32[1040,128]{1,0:T(8,128)S(1)}, f32[1040,128]{1,0:T(8,128)S(1)}, u32[]{:S(2)}, u32[]{:S(2)}) collective-permute-start(f32[1040,128]{1,0:T(8,128)S(1)} %get-tuple-element.17), channel_id=1, source_target_pairs={{12,5},{1,8},{2,11},{15,6},{28,21},{17,24},{18,27},{31,22}} | collective-permute-start | bytes 1597448 | tf_op jit(solution)/shard_map/ppermute | solution.py:521
  7.8 7.8 %collective-permute-start.5 = (f32[1040,128]{1,0:T(8,128)S(1)}, f32[1040,128]{1,0:T(8,128)S(1)}, u32[]{:S(2)}, u32[]{:S(2)}) collective-permute-start(f32[1040,128]{1,0:T(8,128)S(1)} %get-tuple-element.17), channel_id=1, source_target_pairs={{0,1},{1,0},{2,3},{3,2},{4,5},{5,4},{6,7},{7,6},{8,9},{9,8},{10,11... | collective-permute-start | bytes 1597448 | tf_op jit(solution)/shard_map/ppermute | solution.py:494
  20.2 6.2 %collective-permute-start.6 = (f32[528,128]{1,0:T(8,128)S(1)}, f32[528,128]{1,0:T(8,128)S(1)}, u32[]{:S(2)}, u32[]{:S(2)}) collective-permute-start(f32[528,128]{1,0:T(8,128)S(1)} %get-tuple-element.19.refs_0_), channel_id=1, source_target_pairs={{0,1},{1,0},{2,3},{3,2},{4,8},{5,7},{6,10},{7,5},{8,4},{9,11},{10,... | collective-permute-start | bytes 811016 | tf_op jit(solution)/shard_map/ppermute | solution.py:538
  24.4 9.5 %collective-permute-start.10 = (f32[512,128]{1,0:T(8,128)S(1)}, f32[512,128]{1,0:T(8,128)S(1)}, u32[]{:S(2)}, u32[]{:S(2)}) collective-permute-start(f32[512,128]{1,0:T(8,128)S(1)} %get-tuple-element.24.refs_0_), channel_id=1, source_target_pairs={{0,1},{1,0},{2,3},{3,2},{4,8},{5,7},{6,10},{7,5},{8,4},{9,11},{10,... | collective-permute-start | bytes 786440 | tf_op jit(solution)/shard_map/ppermute | solution.py:536
  24.5 2.0 %collective-permute-start.7 = (f32[264,128]{1,0:T(8,128)S(1)}, f32[264,128]{1,0:T(8,128)S(1)}, u32[]{:S(2)}, u32[]{:S(2)}) collective-permute-start(f32[264,128]{1,0:T(8,128)S(1)} %get-tuple-element.20), channel_id=1, source_target_pairs={{0,1},{1,0},{2,3},{3,2},{4,5},{5,4},{6,7},{7,6},{8,9},{9,8},{10,11... | collective-permute-start | bytes 405512 | tf_op jit(solution)/shard_map/ppermute | solution.py:494
  24.9 11.7 %collective-permute-start.9 = (f32[776,128]{1,0:T(8,128)S(1)}, f32[776,128]{1,0:T(8,128)S(1)}, u32[]{:S(2)}, u32[]{:S(2)}) collective-permute-start(f32[776,128]{1,0:T(8,128)S(1)} %get-tuple-element.21), channel_id=1, source_target_pairs={{0,16},{1,5},{2,6},{3,19},{4,20},{5,1},{6,2},{7,23},{8,12},{9,25},... | collective-permute-start | bytes 1191944 | tf_op jit(solution)/shard_map/ppermute | solution.py:537
  26.5 11.9 %collective-permute-start.8 = (f32[528,128]{1,0:T(8,128)S(1)}, f32[528,128]{1,0:T(8,128)S(1)}, u32[]{:S(2)}, u32[]{:S(2)}) collective-permute-start(f32[528,128]{1,0:T(8,128)S(1)} %shard_map.41), channel_id=1, source_target_pairs={{0,4},{1,2},{2,1},{3,7},{4,0},{5,6},{6,5},{7,3},{8,11},{9,13},{10,... | collective-permute-start | bytes 811016 | tf_op jit(solution)/shard_map/ppermute | solution.py:544
  33.9 7.4 %collective-permute-start.14 = (f32[1040,128]{1,0:T(8,128)S(1)}, f32[1040,128]{1,0:T(8,128)S(1)}, u32[]{:S(2)}, u32[]{:S(2)}) collective-permute-start(f32[1040,128]{1,0:T(8,128)S(1)} %collective-permute-done.2.refs_0_.refs_2_), channel_id=1, source_target_pairs={{0,1},{1,0},{2,3},{3,2},{4,5},{5,4},{6,7},{7,6},{8,9},{9,8},{10,11... | collective-permute-start | bytes 1597448 | tf_op jit(solution)/shard_map/ppermute | solution.py:494
  33.9 7.2 %collective-permute-start.11 = (f32[512,128]{1,0:T(8,128)S(1)}, f32[512,128]{1,0:T(8,128)S(1)}, u32[]{:S(2)}, u32[]{:S(2)}) collective-permute-start(f32[512,128]{1,0:T(8,128)S(1)} %collective-permute-done.10.refs_1_), channel_id=1, source_target_pairs={{0,4},{1,2},{2,1},{3,7},{4,0},{5,6},{6,5},{7,3},{8,11},{9,13},{10,... | collective-permute-start | bytes 786440 | tf_op jit(solution)/shard_map/ppermute | solution.py:544
  38.4 2.9 %collective-permute-start.13 = (f32[528,128]{1,0:T(8,128)S(1)}, f32[528,128]{1,0:T(8,128)S(1)}, u32[]{:S(2)}, u32[]{:S(2)}) collective-permute-start(f32[528,128]{1,0:T(8,128)S(1)} %shard_map.42.own_b), channel_id=1, source_target_pairs={{0,1},{1,0},{2,3},{3,2},{4,5},{5,4},{6,7},{7,6},{8,9},{9,8},{10,11... | collective-permute-start | bytes 811016 | tf_op jit(solution)/shard_map/ppermute | solution.py:494
  38.5 2.8 %collective-permute-start.15 = (f32[528,128]{1,0:T(8,128)S(1)}, f32[528,128]{1,0:T(8,128)S(1)}, u32[]{:S(2)}, u32[]{:S(2)}) collective-permute-start(f32[528,128]{1,0:T(8,128)S(1)} %collective-permute-done.8.refs_2_.refs_6_), channel_id=1, source_target_pairs={{0,1},{1,0},{2,3},{3,2},{4,5},{5,4},{6,7},{7,6},{8,9},{9,8},{10,11... | collective-permute-start | bytes 811016 | tf_op jit(solution)/shard_map/ppermute | solution.py:494
  41.2 1.6 %collective-permute-start.12 = (f32[512,128]{1,0:T(8,128)S(1)}, f32[512,128]{1,0:T(8,128)S(1)}, u32[]{:S(2)}, u32[]{:S(2)}) collective-permute-start(f32[512,128]{1,0:T(8,128)S(1)} %shard_map.43.own_a), channel_id=1, source_target_pairs={{0,1},{1,0},{2,3},{3,2},{4,5},{5,4},{6,7},{7,6},{8,9},{9,8},{10,11... | collective-permute-start | bytes 786440 | tf_op jit(solution)/shard_map/ppermute | solution.py:494

commit v8 on v7

--- a/solution.py
+++ b/solution.py
@@ -400,23 +400,33 @@
         size = self.dp * self.cuts * 2
         return [(group * size + a, group * size + b) for group in range(self.groups) for a, b in pairs]
 
-    def swaps(self, pairs, abreast=False):
+    def whole(self, edges, abreast=False):
         size = self.dp * self.cuts * 2
-        partner = {}
-        for a, b in self.one_way(pairs):
-            partner[a], partner[b] = b, a
+        target = dict(self.one_way(edges))
 
         def pair_up(other):
             for device in range(size * self.groups):
                 chosen = other(device)
-                if device not in partner and chosen not in partner and chosen < size * self.groups:
-                    partner[device], partner[chosen] = chosen, device
+                if device not in target and chosen not in target and chosen < size * self.groups:
+                    target[device], target[chosen] = chosen, device
 
         pair_up(lambda device: device ^ 1)
         if abreast and self.cuts % 2 == 0:
             pair_up(lambda device: device ^ 3)
         pair_up(lambda device: (device + size) % (2 * size) + device // (2 * size) * 2 * size)
-        return sorted(partner.items())
+        return sorted(target.items())
+
+    def swaps(self, pairs):
+        return self.whole([edge for a, b in pairs for edge in ((a, b), (b, a))])
+
+    def loops(self, pairs):
+        edges = []
+        for a, b in pairs:
+            if (a ^ 1, b ^ 1) in pairs:
+                edges += [(a, b), (b, a)]
+            else:
+                edges += [(a, b), (b, b ^ 1), (b ^ 1, a ^ 1), (a ^ 1, a)]
+        return self.whole(edges)
 
     def across(self, bit):
         return self.one_way(
@@ -432,12 +442,12 @@
             for base in self.bases:
                 left, right = self.roots(base, x)
                 left_root, right_root = self.index(left, x, 1), self.index(right, x, 0)
-                far.append((self.index(right ^ 1, x, 0), left_root))
-                far.append((self.index(left ^ 1, x, 1), right_root))
+                right_far, left_far = self.index(left ^ 1, x, 1), self.index(right ^ 1, x, 0)
+                far += [(left_far, left_root), (left_root, right_far), (right_far, right_root), (right_root, left_far)]
                 near.append((self.index(right, x, 0), left_root))
                 outer.append((self.index(left ^ 1, x, 0), left_root))
                 outer.append((self.index(right ^ 1, x, 1), right_root))
-        return self.one_way(far), self.swaps(near), self.swaps(outer)
+        return self.whole(far, True), self.swaps(near), self.loops(outer)
 
     def spread(self):
         hops = [[] for turn in range(1, self.cuts)]
@@ -458,12 +468,12 @@
                     abreast = self.index(left, x + turn, 1)
                     hops[turn - 1].append((left_root, abreast))
                     relays[turn - 1].append((abreast, self.index(left ^ 1, x + turn, 1)))
-        return [self.swaps(pairs) for pairs in hops], self.swaps(direct), [self.swaps(pairs, True) for pairs in relays]
+        return [self.swaps(pairs) for pairs in hops], self.loops(direct), [self.loops(pairs) for pairs in relays]
 
     def turn(self):
         z, x, core = (lax.axis_index(name) for name in AXES[1:])
         turn = lax.rem(x + self.cuts - lax.div(z, 2), self.cuts)
-        return jnp.where(core == 1, jnp.maximum(turn - 1, 0), 0)
+        return jnp.where(lax.rem(z, QUAD) == 1 + lax.rem(x, 2), 0, jnp.maximum(turn - 1, 0))
 
     def which(self):
         z, x, core = (lax.axis_index(name) for name in AXES[1:])
@@ -487,7 +497,7 @@
 def rows_core():
     zq = lax.rem(lax.axis_index("dp"), QUAD)
     left = 1 + lax.rem(lax.axis_index("cuts"), 2)
-    return jnp.where(is_middle(), zq == left, (zq ^ 1) != left).astype(jnp.int32)
+    return jnp.where(is_middle(), zq != left, (zq ^ 1) == left).astype(jnp.int32)
 
 
 def swap_cores(array):

time: 44.2 us -> 43.9 us (level)
  the two profiles are of different devices: /device:TPU:0 before, /device:TPU:11 now
where the time goes in v8:
time: 43.9 us; the launch traced here: 43.8 us
  starting transfers between devices  22 us (50%)
  waiting for transfers between devices  12.7 us (29%)
  Pallas kernels  7.79 us (18%)
  other arithmetic  1.17 us (3%)
    ppermute x8, starting transfers between devices, swap_cores(): return lax.ppermute(array, 'grad', [(0, 1), (1, 0)])  13.1 us
    pallas_call x9, Pallas kernels, call(): pl.pallas_call(kernel, out_shape=[jax.ShapeDtypeStruct(shape, jnp.float32...  7.79 us
    ppermute x1, waiting for transfers between devices, per_device(): lax.ppermute(outer, AXES, outward)  7.49 us
    ppermute x1, starting transfers between devices, per_device(): hopped.append([lax.ppermute(inverse[1], AXES, pairs) for pairs in hops])  4.77 us
    ppermute x8, waiting for transfers between devices, swap_cores(): return lax.ppermute(array, 'grad', [(0, 1), (1, 0)])  2.53 us
    ppermute x2, starting transfers between devices, per_device(): lax.ppermute(array, AXES, pairs)  1.83 us
    ppermute x1, starting transfers between devices, per_device(): lax.ppermute(chip, AXES, near)  1.24 us
    select_n x1, other arithmetic, per_device(): sent, = call(cov_kernel, [shape], [], jnp.where(core == 0, outgrads, acts))  1.17 us
  transfers between devices with their start and end apart: 16, of which 8 were waited for; matrix products, arithmetic and copies ran while one was open for 0% of the time, Pallas kernels for 3%

profile of v8, /device:TPU:11, one launch (start us, length us, event | category | flops | bytes accessed | tf_op | source)
XLA Modules:
  0.0 43.8 jit_solution(1861195700302368767)
XLA Ops:
  0.0 1.2 %select_bitcast_fusion = (bf16[384,512]{1,0:T(8,128)(2,1)S(1)}, bf16[384,512]{1,0:T(8,128)(2,1)S(1)}) fusion(bf16[1,384,512]{2,1,0:T(8,128)(2,1)} %param.4, bf16[1,384,512]{2,1,0:T(8,128)(2,1)} %param.3, pred[]{:T(512)S(6)} %eq.4), kind=kLoop, calls=%fused_computation | loop fusion | flops 393216 | bytes 1572865 | tf_op jit(solution)/shard_map/jit(_where)/select_n | solution.py:518
  1.2 0.0 copy-start
  1.2 0.5 %shard_map.38 = f32[1040,128]{1,0:T(8,128)S(1)} custom-call(bf16[384,512]{1,0:T(8,128)(2,1)S(1)} %get-tuple-element.27.x_ref), custom_call_target="tpu_custom_call" | custom-call | tf_op jit(solution)/shard_map/pallas_call | solution.py:378
  1.7 0.7 %collective-permute-start = (f32[1040,128]{1,0:T(8,128)S(1)}, f32[1040,128]{1,0:T(8,128)S(1)}, u32[]{:S(2)}, u32[]{:S(2)}) collective-permute-start(f32[1040,128]{1,0:T(8,128)S(1)} %shard_map.38), channel_id=1, source_target_pairs={{0,1},{1,0},{2,3},{3,2},{4,5},{5,4},{6,7},{7,6},{8,9},{9,8},{10,11... | collective-permute-start | bytes 1597448 | tf_op jit(solution)/shard_map/ppermute | solution.py:504
  2.4 0.0 copy-done
  2.4 0.4 collective-permute-start.1
  2.8 0.5 %shard_map.37.kept_ref = f32[1040,128]{1,0:T(8,128)S(1)} custom-call(bf16[384,512]{1,0:T(8,128)(2,1)S(1)} %get-tuple-element.28.x_ref), custom_call_target="tpu_custom_call" | custom-call | tf_op jit(solution)/shard_map/pallas_call | solution.py:378
  3.3 1.0 %collective-permute-done.1.other_rows_ref.refs_1_ = f32[128,512]{1,0:T(8,128)S(1)} collective-permute-done((f32[128,512]{1,0:T(8,128)S(1)}, f32[128,512]{1,0:T(8,128)S(1)}, u32[]{:S(2)}, u32[]{:S(2)}) %collective-permute-start.1) | collective-permute-done | bytes 262176 | tf_op jit(solution)/shard_map/ppermute | solution.py:504
  4.3 0.0 collective-permute-done.other_ref
  4.3 0.1 shard_map.39
  4.5 0.5 %collective-permute-start.2 = (f32[1040,128]{1,0:T(8,128)S(1)}, f32[1040,128]{1,0:T(8,128)S(1)}, u32[]{:S(2)}, u32[]{:S(2)}) collective-permute-start(f32[1040,128]{1,0:T(8,128)S(1)} %get-tuple-element.16), channel_id=1, source_target_pairs={{0,5},{1,0},{2,3},{3,6},{4,1},{5,4},{6,7},{7,2},{8,9},{9,12},{10,1... | collective-permute-start | bytes 1597448 | tf_op jit(solution)/shard_map/ppermute | solution.py:529
  5.0 1.2 %collective-permute-start.3 = (f32[1040,128]{1,0:T(8,128)S(1)}, f32[1040,128]{1,0:T(8,128)S(1)}, u32[]{:S(2)}, u32[]{:S(2)}) collective-permute-start(f32[1040,128]{1,0:T(8,128)S(1)} %get-tuple-element.17), channel_id=1, source_target_pairs={{0,1},{1,0},{2,3},{3,2},{4,20},{5,8},{6,11},{7,23},{8,5},{9,25},{1... | collective-permute-start | bytes 1597448 | tf_op jit(solution)/shard_map/ppermute | solution.py:530
  6.2 0.6 %collective-permute-start.4 = (f32[1040,128]{1,0:T(8,128)S(1)}, f32[1040,128]{1,0:T(8,128)S(1)}, u32[]{:S(2)}, u32[]{:S(2)}) collective-permute-start(f32[1040,128]{1,0:T(8,128)S(1)} %get-tuple-element.17), channel_id=1, source_target_pairs={{0,3},{1,8},{2,11},{3,0},{4,7},{5,1},{6,2},{7,4},{8,12},{9,10},{10... | collective-permute-start | bytes 1597448 | tf_op jit(solution)/shard_map/ppermute | solution.py:531
  6.8 0.3 collective-permute-start.5
  7.1 7.5 %collective-permute-done.2.refs_0_.refs_2_ = f32[1040,128]{1,0:T(8,128)S(1)} collective-permute-done((f32[1040,128]{1,0:T(8,128)S(1)}, f32[1040,128]{1,0:T(8,128)S(1)}, u32[]{:S(2)}, u32[]{:S(2)}) %collective-permute-start.2) | collective-permute-done | bytes 532512 | tf_op jit(solution)/shard_map/ppermute | solution.py:529
  14.5 0.0 collective-permute-done.3.refs_1_
  14.6 0.6 %collective-permute-done.4.refs_2_ = f32[1040,128]{1,0:T(8,128)S(1)} collective-permute-done((f32[1040,128]{1,0:T(8,128)S(1)}, f32[1040,128]{1,0:T(8,128)S(1)}, u32[]{:S(2)}, u32[]{:S(2)}) %collective-permute-start.4) | collective-permute-done | bytes 532512 | tf_op jit(solution)/shard_map/ppermute | solution.py:531
  15.2 0.0 collective-permute-done.5.refs_3_
  15.2 4.7 %shard_map.40 = (f32[512,128]{1,0:T(8,128)S(1)}, f32[528,128]{1,0:T(8,128)S(1)}, f32[776,128]{1,0:T(8,128)S(1)}, f32[264,128]{1,0:T(8,128)S(1)}) custom-call(f32[1040,128]{1,0:T(8,128)S(1)} %collective-permute-done.2.refs_0_.refs_2_, f32[1040,128]{1,0:T(8,128)S(1)} %collective-permute-done.3.refs_1_, f32[1040,128]{1,0:T(8,128)S(1)} %collective-permute-done.4.refs_2_, ...), custom_call_target="tpu_custom_call" | custom-call | tf_op jit(solution)/shard_map/pallas_call | solution.py:378
  20.0 4.8 %collective-permute-start.6 = (f32[528,128]{1,0:T(8,128)S(1)}, f32[528,128]{1,0:T(8,128)S(1)}, u32[]{:S(2)}, u32[]{:S(2)}) collective-permute-start(f32[528,128]{1,0:T(8,128)S(1)} %get-tuple-element.19.refs_0_), channel_id=1, source_target_pairs={{0,1},{1,0},{2,3},{3,2},{4,8},{5,7},{6,10},{7,5},{8,4},{9,11},{10,... | collective-permute-start | bytes 811016 | tf_op jit(solution)/shard_map/ppermute | solution.py:548
  24.7 0.1 collective-permute-start.10
  24.8 2.7 %collective-permute-start.7 = (f32[264,128]{1,0:T(8,128)S(1)}, f32[264,128]{1,0:T(8,128)S(1)}, u32[]{:S(2)}, u32[]{:S(2)}) collective-permute-start(f32[264,128]{1,0:T(8,128)S(1)} %get-tuple-element.20), channel_id=1, source_target_pairs={{0,1},{1,0},{2,3},{3,2},{4,5},{5,4},{6,7},{7,6},{8,9},{9,8},{10,11... | collective-permute-start | bytes 405512 | tf_op jit(solution)/shard_map/ppermute | solution.py:504
  27.5 0.0 collective-permute-start.9
  27.5 1.0 %collective-permute-done.7.rest_ref = f32[264,128]{1,0:T(8,128)S(1)} collective-permute-done((f32[264,128]{1,0:T(8,128)S(1)}, f32[264,128]{1,0:T(8,128)S(1)}, u32[]{:S(2)}, u32[]{:S(2)}) %collective-permute-start.7) | collective-permute-done | bytes 135200 | tf_op jit(solution)/shard_map/ppermute | solution.py:504
  28.5 0.4 collective-permute-done.6.hopped_ref.refs_1_
  28.9 0.2 collective-permute-start.8
  29.1 3.0 %collective-permute-start.14 = (f32[1040,128]{1,0:T(8,128)S(1)}, f32[1040,128]{1,0:T(8,128)S(1)}, u32[]{:S(2)}, u32[]{:S(2)}) collective-permute-start(f32[1040,128]{1,0:T(8,128)S(1)} %collective-permute-done.2.refs_0_.refs_2_), channel_id=1, source_target_pairs={{0,1},{1,0},{2,3},{3,2},{4,5},{5,4},{6,7},{7,6},{8,9},{9,8},{10,11... | collective-permute-start | bytes 1597448 | tf_op jit(solution)/shard_map/ppermute | solution.py:504
  32.1 0.0 collective-permute-done.10.refs_1_
  32.1 1.7 %collective-permute-start.11 = (f32[512,128]{1,0:T(8,128)S(1)}, f32[512,128]{1,0:T(8,128)S(1)}, u32[]{:S(2)}, u32[]{:S(2)}) collective-permute-start(f32[512,128]{1,0:T(8,128)S(1)} %collective-permute-done.10.refs_1_), channel_id=1, source_target_pairs={{0,1},{1,5},{2,6},{3,2},{4,0},{5,4},{6,7},{7,3},{8,9},{9,13},{10,1... | collective-permute-start | bytes 786440 | tf_op jit(solution)/shard_map/ppermute | solution.py:554
  33.8 0.6 %collective-permute-done.9.refs_3_.refs_4_ = f32[776,128]{1,0:T(8,128)S(1)} collective-permute-done((f32[776,128]{1,0:T(8,128)S(1)}, f32[776,128]{1,0:T(8,128)S(1)}, u32[]{:S(2)}, u32[]{:S(2)}) %collective-permute-start.9) | collective-permute-done | bytes 397344 | tf_op jit(solution)/shard_map/ppermute | solution.py:547
  34.3 1.1 %collective-permute-done.8.refs_2_.refs_6_ = f32[528,128]{1,0:T(8,128)S(1)} collective-permute-done((f32[528,128]{1,0:T(8,128)S(1)}, f32[528,128]{1,0:T(8,128)S(1)}, u32[]{:S(2)}, u32[]{:S(2)}) %collective-permute-start.8) | collective-permute-done | bytes 270368 | tf_op jit(solution)/shard_map/ppermute | solution.py:554
  35.4 3.1 %collective-permute-start.13 = (f32[528,128]{1,0:T(8,128)S(1)}, f32[528,128]{1,0:T(8,128)S(1)}, u32[]{:S(2)}, u32[]{:S(2)}) collective-permute-start(f32[528,128]{1,0:T(8,128)S(1)} %shard_map.42.own_b), channel_id=1, source_target_pairs={{0,1},{1,0},{2,3},{3,2},{4,5},{5,4},{6,7},{7,6},{8,9},{9,8},{10,11... | collective-permute-start | bytes 811016 | tf_op jit(solution)/shard_map/ppermute | solution.py:504
  38.6 0.1 collective-permute-start.15
  38.7 0.0 collective-permute-done.11.refs_2_.refs_5_
  38.7 2.7 %collective-permute-start.12 = (f32[512,128]{1,0:T(8,128)S(1)}, f32[512,128]{1,0:T(8,128)S(1)}, u32[]{:S(2)}, u32[]{:S(2)}) collective-permute-start(f32[512,128]{1,0:T(8,128)S(1)} %shard_map.43.own_a), channel_id=1, source_target_pairs={{0,1},{1,0},{2,3},{3,2},{4,5},{5,4},{6,7},{7,6},{8,9},{9,8},{10,11... | collective-permute-start | bytes 786440 | tf_op jit(solution)/shard_map/ppermute | solution.py:504
  41.4 0.0 collective-permute-done.14.refs_3_
  41.4 0.0 collective-permute-done.13.other_b
  41.4 0.0 collective-permute-done.15.refs_7_
  41.4 0.7 %shard_map.44 = (f32[128,512]{1,0:T(8,128)S(1)}, f32[512,512]{1,0:T(8,128)S(1)}) custom-call(f32[512,128]{1,0:T(8,128)S(1)} %shard_map.43.own_a, f32[528,128]{1,0:T(8,128)S(1)} %shard_map.42.own_b, f32[528,128]{1,0:T(8,128)S(1)} %collective-permute-done.13.other_b, f32[128,512]{1,0:T(8,128)S(1)} %bitcast.8, ...), custom_call_target="tpu_custom_call" | custom-call | tf_op jit(solution)/shard_map/pallas_call | solution.py:378
  42.1 0.5 %collective-permute-done.12.other_a = f32[512,128]{1,0:T(8,128)S(1)} collective-permute-done((f32[512,128]{1,0:T(8,128)S(1)}, f32[512,128]{1,0:T(8,128)S(1)}, u32[]{:S(2)}, u32[]{:S(2)}) %collective-permute-start.12) | collective-permute-done | bytes 262176 | tf_op jit(solution)/shard_map/ppermute | solution.py:504
  42.6 1.2 %shard_map.45 = f32[128,512]{1,0:T(8,128)} custom-call(f32[528,128]{1,0:T(8,128)S(1)} %shard_map.42.own_b, f32[512,128]{1,0:T(8,128)S(1)} %collective-permute-done.12.other_a, f32[528,128]{1,0:T(8,128)S(1)} %collective-permute-done.13.other_b, f32[128,512]{1,0:T(8,128)S(1)} %get-tuple-element.25.first_left, f32[512,512]{1,0:T(8,128)S(1)} %get-tuple-element.26.first_right), custom_call_target="tpu_custom_call" | custom-call | tf_op jit(solution)/shard_map/pallas_call | solution.py:378
  (3 shorter events, 0.1 us)
Async XLA Ops:
  1.2 1.2 %copy-start = (f32[1,128,512]{2,1,0:T(8,128)S(1)}, f32[1,128,512]{2,1,0:T(8,128)}, u32[]{:S(2)}) copy-start(f32[1,128,512]{2,1,0:T(8,128)} %param.5) | copy-start | bytes 786436
  1.7 2.7 %collective-permute-start = (f32[1040,128]{1,0:T(8,128)S(1)}, f32[1040,128]{1,0:T(8,128)S(1)}, u32[]{:S(2)}, u32[]{:S(2)}) collective-permute-start(f32[1040,128]{1,0:T(8,128)S(1)} %shard_map.38), channel_id=1, source_target_pairs={{0,1},{1,0},{2,3},{3,2},{4,5},{5,4},{6,7},{7,6},{8,9},{9,8},{10,11... | collective-permute-start | bytes 1597448 | tf_op jit(solution)/shard_map/ppermute | solution.py:504
  2.4 1.9 %collective-permute-start.1 = (f32[128,512]{1,0:T(8,128)S(1)}, f32[128,512]{1,0:T(8,128)S(1)}, u32[]{:S(2)}, u32[]{:S(2)}) collective-permute-start(f32[128,512]{1,0:T(8,128)S(1)} %bitcast.6), channel_id=1, source_target_pairs={{0,1},{1,0},{2,3},{3,2},{4,5},{5,4},{6,7},{7,6},{8,9},{9,8},{10,11... | collective-permute-start | bytes 786440 | tf_op jit(solution)/shard_map/ppermute | solution.py:504
  4.5 10.1 %collective-permute-start.2 = (f32[1040,128]{1,0:T(8,128)S(1)}, f32[1040,128]{1,0:T(8,128)S(1)}, u32[]{:S(2)}, u32[]{:S(2)}) collective-permute-start(f32[1040,128]{1,0:T(8,128)S(1)} %get-tuple-element.16), channel_id=1, source_target_pairs={{0,5},{1,0},{2,3},{3,6},{4,1},{5,4},{6,7},{7,2},{8,9},{9,12},{10,1... | collective-permute-start | bytes 1597448 | tf_op jit(solution)/shard_map/ppermute | solution.py:529
  5.0 9.6 %collective-permute-start.3 = (f32[1040,128]{1,0:T(8,128)S(1)}, f32[1040,128]{1,0:T(8,128)S(1)}, u32[]{:S(2)}, u32[]{:S(2)}) collective-permute-start(f32[1040,128]{1,0:T(8,128)S(1)} %get-tuple-element.17), channel_id=1, source_target_pairs={{0,1},{1,0},{2,3},{3,2},{4,20},{5,8},{6,11},{7,23},{8,5},{9,25},{1... | collective-permute-start | bytes 1597448 | tf_op jit(solution)/shard_map/ppermute | solution.py:530
  6.2 9.0 %collective-permute-start.4 = (f32[1040,128]{1,0:T(8,128)S(1)}, f32[1040,128]{1,0:T(8,128)S(1)}, u32[]{:S(2)}, u32[]{:S(2)}) collective-permute-start(f32[1040,128]{1,0:T(8,128)S(1)} %get-tuple-element.17), channel_id=1, source_target_pairs={{0,3},{1,8},{2,11},{3,0},{4,7},{5,1},{6,2},{7,4},{8,12},{9,10},{10... | collective-permute-start | bytes 1597448 | tf_op jit(solution)/shard_map/ppermute | solution.py:531
  6.8 8.4 %collective-permute-start.5 = (f32[1040,128]{1,0:T(8,128)S(1)}, f32[1040,128]{1,0:T(8,128)S(1)}, u32[]{:S(2)}, u32[]{:S(2)}) collective-permute-start(f32[1040,128]{1,0:T(8,128)S(1)} %get-tuple-element.17), channel_id=1, source_target_pairs={{0,1},{1,0},{2,3},{3,2},{4,5},{5,4},{6,7},{7,6},{8,9},{9,8},{10,11... | collective-permute-start | bytes 1597448 | tf_op jit(solution)/shard_map/ppermute | solution.py:504
  20.0 8.9 %collective-permute-start.6 = (f32[528,128]{1,0:T(8,128)S(1)}, f32[528,128]{1,0:T(8,128)S(1)}, u32[]{:S(2)}, u32[]{:S(2)}) collective-permute-start(f32[528,128]{1,0:T(8,128)S(1)} %get-tuple-element.19.refs_0_), channel_id=1, source_target_pairs={{0,1},{1,0},{2,3},{3,2},{4,8},{5,7},{6,10},{7,5},{8,4},{9,11},{10,... | collective-permute-start | bytes 811016 | tf_op jit(solution)/shard_map/ppermute | solution.py:548
  24.7 7.4 %collective-permute-start.10 = (f32[512,128]{1,0:T(8,128)S(1)}, f32[512,128]{1,0:T(8,128)S(1)}, u32[]{:S(2)}, u32[]{:S(2)}) collective-permute-start(f32[512,128]{1,0:T(8,128)S(1)} %get-tuple-element.24.refs_0_), channel_id=1, source_target_pairs={{0,1},{1,0},{2,3},{3,2},{4,8},{5,7},{6,10},{7,5},{8,4},{9,11},{10,... | collective-permute-start | bytes 786440 | tf_op jit(solution)/shard_map/ppermute | solution.py:546
  24.8 3.7 %collective-permute-start.7 = (f32[264,128]{1,0:T(8,128)S(1)}, f32[264,128]{1,0:T(8,128)S(1)}, u32[]{:S(2)}, u32[]{:S(2)}) collective-permute-start(f32[264,128]{1,0:T(8,128)S(1)} %get-tuple-element.20), channel_id=1, source_target_pairs={{0,1},{1,0},{2,3},{3,2},{4,5},{5,4},{6,7},{7,6},{8,9},{9,8},{10,11... | collective-permute-start | bytes 405512 | tf_op jit(solution)/shard_map/ppermute | solution.py:504
  27.5 6.8 %collective-permute-start.9 = (f32[776,128]{1,0:T(8,128)S(1)}, f32[776,128]{1,0:T(8,128)S(1)}, u32[]{:S(2)}, u32[]{:S(2)}) collective-permute-start(f32[776,128]{1,0:T(8,128)S(1)} %get-tuple-element.21), channel_id=1, source_target_pairs={{0,4},{1,0},{2,3},{3,7},{4,5},{5,1},{6,2},{7,6},{8,12},{9,8},{10,1... | collective-permute-start | bytes 1191944 | tf_op jit(solution)/shard_map/ppermute | solution.py:547
  28.9 6.5 %collective-permute-start.8 = (f32[528,128]{1,0:T(8,128)S(1)}, f32[528,128]{1,0:T(8,128)S(1)}, u32[]{:S(2)}, u32[]{:S(2)}) collective-permute-start(f32[528,128]{1,0:T(8,128)S(1)} %shard_map.41), channel_id=1, source_target_pairs={{0,1},{1,5},{2,6},{3,2},{4,0},{5,4},{6,7},{7,3},{8,9},{9,13},{10,1... | collective-permute-start | bytes 811016 | tf_op jit(solution)/shard_map/ppermute | solution.py:554
  29.1 12.3 %collective-permute-start.14 = (f32[1040,128]{1,0:T(8,128)S(1)}, f32[1040,128]{1,0:T(8,128)S(1)}, u32[]{:S(2)}, u32[]{:S(2)}) collective-permute-start(f32[1040,128]{1,0:T(8,128)S(1)} %collective-permute-done.2.refs_0_.refs_2_), channel_id=1, source_target_pairs={{0,1},{1,0},{2,3},{3,2},{4,5},{5,4},{6,7},{7,6},{8,9},{9,8},{10,11... | collective-permute-start | bytes 1597448 | tf_op jit(solution)/shard_map/ppermute | solution.py:504
  32.1 6.6 %collective-permute-start.11 = (f32[512,128]{1,0:T(8,128)S(1)}, f32[512,128]{1,0:T(8,128)S(1)}, u32[]{:S(2)}, u32[]{:S(2)}) collective-permute-start(f32[512,128]{1,0:T(8,128)S(1)} %collective-permute-done.10.refs_1_), channel_id=1, source_target_pairs={{0,1},{1,5},{2,6},{3,2},{4,0},{5,4},{6,7},{7,3},{8,9},{9,13},{10,1... | collective-permute-start | bytes 786440 | tf_op jit(solution)/shard_map/ppermute | solution.py:554
  35.4 6.0 %collective-permute-start.13 = (f32[528,128]{1,0:T(8,128)S(1)}, f32[528,128]{1,0:T(8,128)S(1)}, u32[]{:S(2)}, u32[]{:S(2)}) collective-permute-start(f32[528,128]{1,0:T(8,128)S(1)} %shard_map.42.own_b), channel_id=1, source_target_pairs={{0,1},{1,0},{2,3},{3,2},{4,5},{5,4},{6,7},{7,6},{8,9},{9,8},{10,11... | collective-permute-start | bytes 811016 | tf_op jit(solution)/shard_map/ppermute | solution.py:504
  38.6 2.8 %collective-permute-start.15 = (f32[528,128]{1,0:T(8,128)S(1)}, f32[528,128]{1,0:T(8,128)S(1)}, u32[]{:S(2)}, u32[]{:S(2)}) collective-permute-start(f32[528,128]{1,0:T(8,128)S(1)} %collective-permute-done.8.refs_2_.refs_6_), channel_id=1, source_target_pairs={{0,1},{1,0},{2,3},{3,2},{4,5},{5,4},{6,7},{7,6},{8,9},{9,8},{10,11... | collective-permute-start | bytes 811016 | tf_op jit(solution)/shard_map/ppermute | solution.py:504
  38.7 3.9 %collective-permute-start.12 = (f32[512,128]{1,0:T(8,128)S(1)}, f32[512,128]{1,0:T(8,128)S(1)}, u32[]{:S(2)}, u32[]{:S(2)}) collective-permute-start(f32[512,128]{1,0:T(8,128)S(1)} %shard_map.43.own_a), channel_id=1, source_target_pairs={{0,1},{1,0},{2,3},{3,2},{4,5},{5,4},{6,7},{7,6},{8,9},{9,8},{10,11... | collective-permute-start | bytes 786440 | tf_op jit(solution)/shard_map/ppermute | solution.py:504

commit v9 on v8

--- a/solution.py
+++ b/solution.py
@@ -418,6 +418,18 @@
 
     def swaps(self, pairs):
         return self.whole([edge for a, b in pairs for edge in ((a, b), (b, a))])
+
+    def chains(self, pairs):
+        to, of = dict(pairs), {b: a for a, b in pairs}
+        edges = list(pairs)
+        for device in sorted(set(to) | set(of)):
+            if device in of and device not in to:
+                if device ^ 1 in of or device ^ 1 not in to:
+                    return self.swaps(pairs)
+                edges.append((device, device ^ 1))
+            elif device in to and device not in of and (device ^ 1 in to or device ^ 1 not in of):
+                return self.swaps(pairs)
+        return self.whole(edges)
 
     def loops(self, pairs):
         edges = []
@@ -468,7 +480,7 @@
                     abreast = self.index(left, x + turn, 1)
                     hops[turn - 1].append((left_root, abreast))
                     relays[turn - 1].append((abreast, self.index(left ^ 1, x + turn, 1)))
-        return [self.swaps(pairs) for pairs in hops], self.loops(direct), [self.loops(pairs) for pairs in relays]
+        return [self.chains(pairs) for pairs in hops], self.loops(direct), [self.loops(pairs) for pairs in relays]
 
     def turn(self):
         z, x, core = (lax.axis_index(name) for name in AXES[1:])

time: 43.9 us -> 43.4 us (0.989)
  the two profiles are of different devices: /device:TPU:11 before, /device:TPU:0 now
where the time goes in v9:
time: 43.4 us; the launch traced here: 43.2 us
  waiting for transfers between devices  19.3 us (44%)
  starting transfers between devices  14.3 us (33%)
  Pallas kernels  8.29 us (19%)
  other arithmetic  1.17 us (3%)
    ppermute x1, waiting for transfers between devices, per_device(): lax.ppermute(outer, AXES, outward)  9.24 us
    pallas_call x9, Pallas kernels, call(): pl.pallas_call(kernel, out_shape=[jax.ShapeDtypeStruct(shape, jnp.float32...  8.29 us
    ppermute x1, waiting for transfers between devices, per_device(): direct = lax.ppermute(direct, AXES, outward)  8.01 us
    ppermute x1, starting transfers between devices, per_device(): direct = lax.ppermute(direct, AXES, outward)  4.23 us
    ppermute x8, starting transfers between devices, swap_cores(): return lax.ppermute(array, 'grad', [(0, 1), (1, 0)])  3.87 us
    ppermute x1, starting transfers between devices, per_device(): lax.ppermute(outer, AXES, outward)  2.73 us
    ppermute x1, starting transfers between devices, per_device(): hopped.append([lax.ppermute(inverse[1], AXES, pairs) for pairs in hops])  1.88 us
    ppermute x1, starting transfers between devices, per_device(): lax.ppermute(chip, AXES, far)  1.48 us
  transfers between devices with their start and end apart: 16, of which 4 were waited for; matrix products, arithmetic and copies ran while one was open for 0% of the time, Pallas kernels for 4%

profile of v9, /device:TPU:0, one launch (start us, length us, event | category | flops | bytes accessed | tf_op | source)
XLA Modules:
  0.0 43.2 jit_solution(6392052121361863044)
XLA Ops:
  0.0 1.2 %select_bitcast_fusion = (bf16[384,512]{1,0:T(8,128)(2,1)S(1)}, bf16[384,512]{1,0:T(8,128)(2,1)S(1)}) fusion(bf16[1,384,512]{2,1,0:T(8,128)(2,1)} %param.4, bf16[1,384,512]{2,1,0:T(8,128)(2,1)} %param.3, pred[]{:T(512)S(6)} %eq.4), kind=kLoop, calls=%fused_computation | loop fusion | flops 393216 | bytes 1572865 | tf_op jit(solution)/shard_map/jit(_where)/select_n | solution.py:530
  1.2 0.0 copy-start
  1.2 0.5 %shard_map.38 = f32[1040,128]{1,0:T(8,128)S(1)} custom-call(bf16[384,512]{1,0:T(8,128)(2,1)S(1)} %get-tuple-element.27.x_ref), custom_call_target="tpu_custom_call" | custom-call | tf_op jit(solution)/shard_map/pallas_call | solution.py:378
  1.7 0.5 %collective-permute-start = (f32[1040,128]{1,0:T(8,128)S(1)}, f32[1040,128]{1,0:T(8,128)S(1)}, u32[]{:S(2)}, u32[]{:S(2)}) collective-permute-start(f32[1040,128]{1,0:T(8,128)S(1)} %shard_map.38), channel_id=1, source_target_pairs={{0,1},{1,0},{2,3},{3,2},{4,5},{5,4},{6,7},{7,6},{8,9},{9,8},{10,11... | collective-permute-start | bytes 1597448 | tf_op jit(solution)/shard_map/ppermute | solution.py:516
  2.2 0.0 copy-done
  2.2 0.4 collective-permute-start.1
  2.6 0.5 %shard_map.37.kept_ref = f32[1040,128]{1,0:T(8,128)S(1)} custom-call(bf16[384,512]{1,0:T(8,128)(2,1)S(1)} %get-tuple-element.28.x_ref), custom_call_target="tpu_custom_call" | custom-call | tf_op jit(solution)/shard_map/pallas_call | solution.py:378
  3.0 1.1 %collective-permute-done.1.other_rows_ref.refs_1_ = f32[128,512]{1,0:T(8,128)S(1)} collective-permute-done((f32[128,512]{1,0:T(8,128)S(1)}, f32[128,512]{1,0:T(8,128)S(1)}, u32[]{:S(2)}, u32[]{:S(2)}) %collective-permute-start.1) | collective-permute-done | bytes 262176 | tf_op jit(solution)/shard_map/ppermute | solution.py:516
  4.1 0.0 collective-permute-done.other_ref
  4.1 0.2 shard_map.39
  4.3 2.7 %collective-permute-start.2 = (f32[1040,128]{1,0:T(8,128)S(1)}, f32[1040,128]{1,0:T(8,128)S(1)}, u32[]{:S(2)}, u32[]{:S(2)}) collective-permute-start(f32[1040,128]{1,0:T(8,128)S(1)} %get-tuple-element.16), channel_id=1, source_target_pairs={{0,5},{1,0},{2,3},{3,6},{4,1},{5,4},{6,7},{7,2},{8,9},{9,12},{10,1... | collective-permute-start | bytes 1597448 | tf_op jit(solution)/shard_map/ppermute | solution.py:541
  7.0 0.0 collective-permute-start.3
  7.0 1.5 %collective-permute-start.4 = (f32[1040,128]{1,0:T(8,128)S(1)}, f32[1040,128]{1,0:T(8,128)S(1)}, u32[]{:S(2)}, u32[]{:S(2)}) collective-permute-start(f32[1040,128]{1,0:T(8,128)S(1)} %get-tuple-element.17), channel_id=1, source_target_pairs={{0,3},{1,8},{2,11},{3,0},{4,7},{5,1},{6,2},{7,4},{8,12},{9,10},{10... | collective-permute-start | bytes 1597448 | tf_op jit(solution)/shard_map/ppermute | solution.py:543
  8.5 0.5 %collective-permute-start.5 = (f32[1040,128]{1,0:T(8,128)S(1)}, f32[1040,128]{1,0:T(8,128)S(1)}, u32[]{:S(2)}, u32[]{:S(2)}) collective-permute-start(f32[1040,128]{1,0:T(8,128)S(1)} %get-tuple-element.17), channel_id=1, source_target_pairs={{0,1},{1,0},{2,3},{3,2},{4,5},{5,4},{6,7},{7,6},{8,9},{9,8},{10,11... | collective-permute-start | bytes 1597448 | tf_op jit(solution)/shard_map/ppermute | solution.py:516
  9.0 9.2 %collective-permute-done.2.refs_0_.refs_2_ = f32[1040,128]{1,0:T(8,128)S(1)} collective-permute-done((f32[1040,128]{1,0:T(8,128)S(1)}, f32[1040,128]{1,0:T(8,128)S(1)}, u32[]{:S(2)}, u32[]{:S(2)}) %collective-permute-start.2) | collective-permute-done | bytes 532512 | tf_op jit(solution)/shard_map/ppermute | solution.py:541
  18.2 0.0 collective-permute-done.3.refs_1_
  18.2 0.0 collective-permute-done.4.refs_2_
  18.2 0.0 collective-permute-done.5.refs_3_
  18.2 4.7 %shard_map.40 = (f32[512,128]{1,0:T(8,128)S(1)}, f32[528,128]{1,0:T(8,128)S(1)}, f32[776,128]{1,0:T(8,128)S(1)}, f32[264,128]{1,0:T(8,128)S(1)}) custom-call(f32[1040,128]{1,0:T(8,128)S(1)} %collective-permute-done.2.refs_0_.refs_2_, f32[1040,128]{1,0:T(8,128)S(1)} %collective-permute-done.3.refs_1_, f32[1040,128]{1,0:T(8,128)S(1)} %collective-permute-done.4.refs_2_, ...), custom_call_target="tpu_custom_call" | custom-call | tf_op jit(solution)/shard_map/pallas_call | solution.py:378
  22.9 1.9 %collective-permute-start.6 = (f32[528,128]{1,0:T(8,128)S(1)}, f32[528,128]{1,0:T(8,128)S(1)}, u32[]{:S(2)}, u32[]{:S(2)}) collective-permute-start(f32[528,128]{1,0:T(8,128)S(1)} %get-tuple-element.19.refs_0_), channel_id=1, source_target_pairs={{0,1},{1,0},{2,3},{3,2},{4,5},{5,7},{6,10},{7,6},{8,4},{9,8},{10,1... | collective-permute-start | bytes 811016 | tf_op jit(solution)/shard_map/ppermute | solution.py:560
  24.8 0.1 collective-permute-start.10
  24.8 0.4 %collective-permute-start.7 = (f32[264,128]{1,0:T(8,128)S(1)}, f32[264,128]{1,0:T(8,128)S(1)}, u32[]{:S(2)}, u32[]{:S(2)}) collective-permute-start(f32[264,128]{1,0:T(8,128)S(1)} %get-tuple-element.20), channel_id=1, source_target_pairs={{0,1},{1,0},{2,3},{3,2},{4,5},{5,4},{6,7},{7,6},{8,9},{9,8},{10,11... | collective-permute-start | bytes 405512 | tf_op jit(solution)/shard_map/ppermute | solution.py:516
  25.3 4.2 %collective-permute-start.9 = (f32[776,128]{1,0:T(8,128)S(1)}, f32[776,128]{1,0:T(8,128)S(1)}, u32[]{:S(2)}, u32[]{:S(2)}) collective-permute-start(f32[776,128]{1,0:T(8,128)S(1)} %get-tuple-element.21), channel_id=1, source_target_pairs={{0,4},{1,0},{2,3},{3,7},{4,5},{5,1},{6,2},{7,6},{8,12},{9,8},{10,1... | collective-permute-start | bytes 1191944 | tf_op jit(solution)/shard_map/ppermute | solution.py:559
  29.5 0.0 collective-permute-done.7.rest_ref
  29.5 0.0 collective-permute-done.6.hopped_ref.refs_1_
  29.6 0.1 collective-permute-start.8
  29.6 1.1 %collective-permute-start.14 = (f32[1040,128]{1,0:T(8,128)S(1)}, f32[1040,128]{1,0:T(8,128)S(1)}, u32[]{:S(2)}, u32[]{:S(2)}) collective-permute-start(f32[1040,128]{1,0:T(8,128)S(1)} %collective-permute-done.2.refs_0_.refs_2_), channel_id=1, source_target_pairs={{0,1},{1,0},{2,3},{3,2},{4,5},{5,4},{6,7},{7,6},{8,9},{9,8},{10,11... | collective-permute-start | bytes 1597448 | tf_op jit(solution)/shard_map/ppermute | solution.py:516
  30.7 0.0 collective-permute-done.10.refs_1_
  30.7 0.0 collective-permute-start.11
  30.7 8.0 %collective-permute-done.9.refs_3_.refs_4_ = f32[776,128]{1,0:T(8,128)S(1)} collective-permute-done((f32[776,128]{1,0:T(8,128)S(1)}, f32[776,128]{1,0:T(8,128)S(1)}, u32[]{:S(2)}, u32[]{:S(2)}) %collective-permute-start.9) | collective-permute-done | bytes 397344 | tf_op jit(solution)/shard_map/ppermute | solution.py:559
  38.7 0.0 collective-permute-done.8.refs_2_.refs_6_
  38.7 0.1 collective-permute-start.13
  38.8 0.5 %collective-permute-start.15 = (f32[528,128]{1,0:T(8,128)S(1)}, f32[528,128]{1,0:T(8,128)S(1)}, u32[]{:S(2)}, u32[]{:S(2)}) collective-permute-start(f32[528,128]{1,0:T(8,128)S(1)} %collective-permute-done.8.refs_2_.refs_6_), channel_id=1, source_target_pairs={{0,1},{1,0},{2,3},{3,2},{4,5},{5,4},{6,7},{7,6},{8,9},{9,8},{10,11... | collective-permute-start | bytes 811016 | tf_op jit(solution)/shard_map/ppermute | solution.py:516
  39.3 1.0 %collective-permute-done.11.refs_2_.refs_5_ = f32[512,128]{1,0:T(8,128)S(1)} collective-permute-done((f32[512,128]{1,0:T(8,128)S(1)}, f32[512,128]{1,0:T(8,128)S(1)}, u32[]{:S(2)}, u32[]{:S(2)}) %collective-permute-start.11) | collective-permute-done | bytes 262176 | tf_op jit(solution)/shard_map/ppermute | solution.py:566
  40.4 0.4 collective-permute-start.12
  40.8 0.0 collective-permute-done.14.refs_3_
  40.8 0.0 collective-permute-done.13.other_b
  40.8 0.0 collective-permute-done.15.refs_7_
  40.8 1.2 %shard_map.44 = (f32[128,512]{1,0:T(8,128)S(1)}, f32[512,512]{1,0:T(8,128)S(1)}) custom-call(f32[512,128]{1,0:T(8,128)S(1)} %shard_map.43.own_a, f32[528,128]{1,0:T(8,128)S(1)} %shard_map.42.own_b, f32[528,128]{1,0:T(8,128)S(1)} %collective-permute-done.13.other_b, f32[128,512]{1,0:T(8,128)S(1)} %bitcast.8, ...), custom_call_target="tpu_custom_call" | custom-call | tf_op jit(solution)/shard_map/pallas_call | solution.py:378
  42.0 0.0 collective-permute-done.12.other_a
  42.0 1.2 %shard_map.45 = f32[128,512]{1,0:T(8,128)} custom-call(f32[528,128]{1,0:T(8,128)S(1)} %shard_map.42.own_b, f32[512,128]{1,0:T(8,128)S(1)} %collective-permute-done.12.other_a, f32[528,128]{1,0:T(8,128)S(1)} %collective-permute-done.13.other_b, f32[128,512]{1,0:T(8,128)S(1)} %get-tuple-element.25.first_left, f32[512,512]{1,0:T(8,128)S(1)} %get-tuple-element.26.first_right), custom_call_target="tpu_custom_call" | custom-call | tf_op jit(solution)/shard_map/pallas_call | solution.py:378
  (3 shorter events, 0.1 us)
Async XLA Ops:
  1.2 1.0 %copy-start = (f32[1,128,512]{2,1,0:T(8,128)S(1)}, f32[1,128,512]{2,1,0:T(8,128)}, u32[]{:S(2)}) copy-start(f32[1,128,512]{2,1,0:T(8,128)} %param.5) | copy-start | bytes 786436
  1.7 2.4 %collective-permute-start = (f32[1040,128]{1,0:T(8,128)S(1)}, f32[1040,128]{1,0:T(8,128)S(1)}, u32[]{:S(2)}, u32[]{:S(2)}) collective-permute-start(f32[1040,128]{1,0:T(8,128)S(1)} %shard_map.38), channel_id=1, source_target_pairs={{0,1},{1,0},{2,3},{3,2},{4,5},{5,4},{6,7},{7,6},{8,9},{9,8},{10,11... | collective-permute-start | bytes 1597448 | tf_op jit(solution)/shard_map/ppermute | solution.py:516
  2.2 1.9 %collective-permute-start.1 = (f32[128,512]{1,0:T(8,128)S(1)}, f32[128,512]{1,0:T(8,128)S(1)}, u32[]{:S(2)}, u32[]{:S(2)}) collective-permute-start(f32[128,512]{1,0:T(8,128)S(1)} %bitcast.6), channel_id=1, source_target_pairs={{0,1},{1,0},{2,3},{3,2},{4,5},{5,4},{6,7},{7,6},{8,9},{9,8},{10,11... | collective-permute-start | bytes 786440 | tf_op jit(solution)/shard_map/ppermute | solution.py:516
  4.3 13.9 %collective-permute-start.2 = (f32[1040,128]{1,0:T(8,128)S(1)}, f32[1040,128]{1,0:T(8,128)S(1)}, u32[]{:S(2)}, u32[]{:S(2)}) collective-permute-start(f32[1040,128]{1,0:T(8,128)S(1)} %get-tuple-element.16), channel_id=1, source_target_pairs={{0,5},{1,0},{2,3},{3,6},{4,1},{5,4},{6,7},{7,2},{8,9},{9,12},{10,1... | collective-permute-start | bytes 1597448 | tf_op jit(solution)/shard_map/ppermute | solution.py:541
  7.0 11.2 %collective-permute-start.3 = (f32[1040,128]{1,0:T(8,128)S(1)}, f32[1040,128]{1,0:T(8,128)S(1)}, u32[]{:S(2)}, u32[]{:S(2)}) collective-permute-start(f32[1040,128]{1,0:T(8,128)S(1)} %get-tuple-element.17), channel_id=1, source_target_pairs={{0,1},{1,0},{2,3},{3,2},{4,20},{5,8},{6,11},{7,23},{8,5},{9,25},{1... | collective-permute-start | bytes 1597448 | tf_op jit(solution)/shard_map/ppermute | solution.py:542
  7.0 11.2 %collective-permute-start.4 = (f32[1040,128]{1,0:T(8,128)S(1)}, f32[1040,128]{1,0:T(8,128)S(1)}, u32[]{:S(2)}, u32[]{:S(2)}) collective-permute-start(f32[1040,128]{1,0:T(8,128)S(1)} %get-tuple-element.17), channel_id=1, source_target_pairs={{0,3},{1,8},{2,11},{3,0},{4,7},{5,1},{6,2},{7,4},{8,12},{9,10},{10... | collective-permute-start | bytes 1597448 | tf_op jit(solution)/shard_map/ppermute | solution.py:543
  8.5 9.7 %collective-permute-start.5 = (f32[1040,128]{1,0:T(8,128)S(1)}, f32[1040,128]{1,0:T(8,128)S(1)}, u32[]{:S(2)}, u32[]{:S(2)}) collective-permute-start(f32[1040,128]{1,0:T(8,128)S(1)} %get-tuple-element.17), channel_id=1, source_target_pairs={{0,1},{1,0},{2,3},{3,2},{4,5},{5,4},{6,7},{7,6},{8,9},{9,8},{10,11... | collective-permute-start | bytes 1597448 | tf_op jit(solution)/shard_map/ppermute | solution.py:516
  22.9 6.6 %collective-permute-start.6 = (f32[528,128]{1,0:T(8,128)S(1)}, f32[528,128]{1,0:T(8,128)S(1)}, u32[]{:S(2)}, u32[]{:S(2)}) collective-permute-start(f32[528,128]{1,0:T(8,128)S(1)} %get-tuple-element.19.refs_0_), channel_id=1, source_target_pairs={{0,1},{1,0},{2,3},{3,2},{4,5},{5,7},{6,10},{7,6},{8,4},{9,8},{10,1... | collective-permute-start | bytes 811016 | tf_op jit(solution)/shard_map/ppermute | solution.py:560
  24.8 5.9 %collective-permute-start.10 = (f32[512,128]{1,0:T(8,128)S(1)}, f32[512,128]{1,0:T(8,128)S(1)}, u32[]{:S(2)}, u32[]{:S(2)}) collective-permute-start(f32[512,128]{1,0:T(8,128)S(1)} %get-tuple-element.24.refs_0_), channel_id=1, source_target_pairs={{0,1},{1,0},{2,3},{3,2},{4,5},{5,7},{6,10},{7,6},{8,4},{9,8},{10,1... | collective-permute-start | bytes 786440 | tf_op jit(solution)/shard_map/ppermute | solution.py:558
  24.8 4.7 %collective-permute-start.7 = (f32[264,128]{1,0:T(8,128)S(1)}, f32[264,128]{1,0:T(8,128)S(1)}, u32[]{:S(2)}, u32[]{:S(2)}) collective-permute-start(f32[264,128]{1,0:T(8,128)S(1)} %get-tuple-element.20), channel_id=1, source_target_pairs={{0,1},{1,0},{2,3},{3,2},{4,5},{5,4},{6,7},{7,6},{8,9},{9,8},{10,11... | collective-permute-start | bytes 405512 | tf_op jit(solution)/shard_map/ppermute | solution.py:516
  25.3 13.4 %collective-permute-start.9 = (f32[776,128]{1,0:T(8,128)S(1)}, f32[776,128]{1,0:T(8,128)S(1)}, u32[]{:S(2)}, u32[]{:S(2)}) collective-permute-start(f32[776,128]{1,0:T(8,128)S(1)} %get-tuple-element.21), channel_id=1, source_target_pairs={{0,4},{1,0},{2,3},{3,7},{4,5},{5,1},{6,2},{7,6},{8,12},{9,8},{10,1... | collective-permute-start | bytes 1191944 | tf_op jit(solution)/shard_map/ppermute | solution.py:559
  29.6 9.2 %collective-permute-start.8 = (f32[528,128]{1,0:T(8,128)S(1)}, f32[528,128]{1,0:T(8,128)S(1)}, u32[]{:S(2)}, u32[]{:S(2)}) collective-permute-start(f32[528,128]{1,0:T(8,128)S(1)} %shard_map.41), channel_id=1, source_target_pairs={{0,1},{1,5},{2,6},{3,2},{4,0},{5,4},{6,7},{7,3},{8,9},{9,13},{10,1... | collective-permute-start | bytes 811016 | tf_op jit(solution)/shard_map/ppermute | solution.py:566
  29.6 11.1 %collective-permute-start.14 = (f32[1040,128]{1,0:T(8,128)S(1)}, f32[1040,128]{1,0:T(8,128)S(1)}, u32[]{:S(2)}, u32[]{:S(2)}) collective-permute-start(f32[1040,128]{1,0:T(8,128)S(1)} %collective-permute-done.2.refs_0_.refs_2_), channel_id=1, source_target_pairs={{0,1},{1,0},{2,3},{3,2},{4,5},{5,4},{6,7},{7,6},{8,9},{9,8},{10,11... | collective-permute-start | bytes 1597448 | tf_op jit(solution)/shard_map/ppermute | solution.py:516
  30.7 9.6 %collective-permute-start.11 = (f32[512,128]{1,0:T(8,128)S(1)}, f32[512,128]{1,0:T(8,128)S(1)}, u32[]{:S(2)}, u32[]{:S(2)}) collective-permute-start(f32[512,128]{1,0:T(8,128)S(1)} %collective-permute-done.10.refs_1_), channel_id=1, source_target_pairs={{0,1},{1,5},{2,6},{3,2},{4,0},{5,4},{6,7},{7,3},{8,9},{9,13},{10,1... | collective-permute-start | bytes 786440 | tf_op jit(solution)/shard_map/ppermute | solution.py:566
  38.7 2.0 %collective-permute-start.13 = (f32[528,128]{1,0:T(8,128)S(1)}, f32[528,128]{1,0:T(8,128)S(1)}, u32[]{:S(2)}, u32[]{:S(2)}) collective-permute-start(f32[528,128]{1,0:T(8,128)S(1)} %shard_map.42.own_b), channel_id=1, source_target_pairs={{0,1},{1,0},{2,3},{3,2},{4,5},{5,4},{6,7},{7,6},{8,9},{9,8},{10,11... | collective-permute-start | bytes 811016 | tf_op jit(solution)/shard_map/ppermute | solution.py:516
  38.8 2.0 %collective-permute-start.15 = (f32[528,128]{1,0:T(8,128)S(1)}, f32[528,128]{1,0:T(8,128)S(1)}, u32[]{:S(2)}, u32[]{:S(2)}) collective-permute-start(f32[528,128]{1,0:T(8,128)S(1)} %collective-permute-done.8.refs_2_.refs_6_), channel_id=1, source_target_pairs={{0,1},{1,0},{2,3},{3,2},{4,5},{5,4},{6,7},{7,6},{8,9},{9,8},{10,11... | collective-permute-start | bytes 811016 | tf_op jit(solution)/shard_map/ppermute | solution.py:516
  40.4 1.6 %collective-permute-start.12 = (f32[512,128]{1,0:T(8,128)S(1)}, f32[512,128]{1,0:T(8,128)S(1)}, u32[]{:S(2)}, u32[]{:S(2)}) collective-permute-start(f32[512,128]{1,0:T(8,128)S(1)} %shard_map.43.own_a), channel_id=1, source_target_pairs={{0,1},{1,0},{2,3},{3,2},{4,5},{5,4},{6,7},{7,6},{8,9},{9,8},{10,11... | collective-permute-start | bytes 786440 | tf_op jit(solution)/shard_map/ppermute | solution.py:516

commit v10 on v9

--- a/solution.py
+++ b/solution.py
@@ -158,29 +158,21 @@
     return lambda i, j: value[i * LANE : (i + 1) * LANE, j * LANE : (j + 1) * LANE]
 
 
-def chip_kernel(kept_ref, other_ref, own_rows_ref, other_rows_ref, chip_ref, rows_ref, outer_ref):
+def put_rows(out_ref, start, rows_ref):
+    rows, columns = rows_ref.shape
+    for column in range(columns // LANE):
+        out_ref[start : start + rows, :] = rows_ref[:, column * LANE : (column + 1) * LANE]
+        start += rows
+
+
+def chip_kernel(kept_ref, other_ref, rows_ref, chip_ref, outer_ref):
     chip_ref[...] = kept_ref[...] + other_ref[...]
-    core = lax.axis_index("grad")
-    rows, columns = own_rows_ref.shape
-
-    def put(start, ref):
-        for column in range(columns // LANE):
-            rows_ref[start : start + rows, :] = ref[:, column * LANE : (column + 1) * LANE]
-            start += rows
-
-    for own in range(2):
-
-        @pl.when(core == own)
-        def _():
-            put(own * rows * columns // LANE, own_rows_ref)
-            put((1 - own) * rows * columns // LANE, other_rows_ref)
-
-    used = 2 * rows * columns // LANE
-    rows_ref[used:, :] = jnp.zeros((rows_ref.shape[0] - used, LANE), jnp.float32)
 
     @pl.when(is_middle())
     def _():
-        outer_ref[...] = rows_ref[...]
+        used = rows_ref.shape[0] * rows_ref.shape[1] // LANE
+        put_rows(outer_ref, 0, rows_ref)
+        outer_ref[used:, :] = jnp.zeros((outer_ref.shape[0] - used, LANE), jnp.float32)
 
     @pl.when(jnp.logical_not(is_middle()))
     def _():
@@ -188,7 +180,7 @@
 
 
 def inverse_kernel(scale, order, *refs):
-    *sums, rows_ref, a_ref, b_ref, direct_ref, rest_ref, factor_ref = refs
+    *sums, own_rows_ref, other_rows_ref, a_ref, b_ref, direct_ref, rest_ref, gathered_ref, factor_ref, rows_ref = refs
     split = part_rows(order)[0]
 
     def piece(start, size):
@@ -234,6 +226,22 @@
 
     @pl.when(jnp.logical_not(is_middle()))
     def _():
+        core = lax.axis_index("grad")
+        size = own_rows_ref.shape[0] * own_rows_ref.shape[1] // LANE
+        rows_ref[2 * size :, :] = jnp.zeros((rows_ref.shape[0] - 2 * size, LANE), jnp.float32)
+        for mine in range(2):
+
+            @pl.when(core == mine)
+            def _():
+                put_rows(rows_ref, mine * size, own_rows_ref)
+                put_rows(rows_ref, (1 - mine) * size, other_rows_ref)
+
+            @pl.when(rows_core() == mine)
+            def _():
+                outer, far = sums[0][:size, :], sums[2][:size, :]
+                gathered_ref[:size, :] = outer if mine else far
+                gathered_ref[size:, :] = far if mine else outer
+
         a_ref[...] = rows_ref[:split, :]
         b_ref[...] = rows_ref[split:, :]
         direct_ref[...] = rows_ref[: split + used, :]
@@ -530,7 +538,7 @@
     (sent,) = call(cov_kernel, [shape], [], jnp.where(core == 0, outgrads, acts))
     (kept,) = call(cov_kernel, [shape], [], jnp.where(core == 0, acts, outgrads))
     other_rows = swap_cores(grads)
-    chip, rows, outer = call(chip_kernel, [shape] * 3, [], kept, swap_cores(sent), grads, other_rows)
+    chip, outer = call(chip_kernel, [shape] * 2, [], kept, swap_cores(sent), grads)
     bit = QUAD
     while bit < dp:
         chip = chip + lax.ppermute(chip, AXES, plan.across(bit))
@@ -540,18 +548,19 @@
     sums = [
         lax.ppermute(outer, AXES, outward),
         lax.ppermute(chip, AXES, near),
-        lax.ppermute(chip, AXES, far),
+        lax.ppermute(outer, AXES, far),
         swap_cores(chip),
     ]
-    outer_rows = sums[0]
     scale = 1.0 / (tok_rows * dev_count)
     square_scratch = pltpu.VMEM((order, order), jnp.float32)
-    *inverse, direct, rest_own = call(
+    gathered = (2 * grads.size // LANE, LANE)
+    *inverse, direct, rest_own, outer_rows = call(
         functools.partial(inverse_kernel, scale, order),
-        [(split, LANE), (rest, LANE), (split + rest // 2, LANE), (rest // 2, LANE)],
-        [square_scratch],
+        [(split, LANE), (rest, LANE), (split + rest - rest // 2, LANE), (rest // 2, LANE), gathered],
+        [square_scratch, pltpu.VMEM(shape, jnp.float32)],
         *sums,
-        rows,
+        grads,
+        other_rows,
     )
 
     hops, outward, relays = plan.spread()

time: 43.4 us -> 43 us (level)
    ppermute x1, waiting for transfers between devices: 9.24 us -> 7.32 us  [per_device(): lax.ppermute(outer, AXES, outward)]
    ppermute x8, waiting for transfers between devices: 1.07 us -> 2.98 us  [swap_cores(): return lax.ppermute(array, 'grad', [(0, 1), (1, 0)])]
  transfers between devices with their start and end apart: 16 -> 16, of which waited for: 4 -> 5; matrix products, arithmetic and copies ran while one was open for 0% -> 0% of each run, Pallas kernels for 4% -> 4%
where the time goes in v10:
time: 43 us; the launch traced here: 42.8 us
  waiting for transfers between devices  19.3 us (45%)
  starting transfers between devices  13.9 us (32%)
  Pallas kernels  8.35 us (19%)
  other arithmetic  1.17 us (3%)
    pallas_call x9, Pallas kernels, call(): pl.pallas_call(kernel, out_shape=[jax.ShapeDtypeStruct(shape, jnp.float32...  8.35 us
    ppermute x1, waiting for transfers between devices, per_device(): direct = lax.ppermute(direct, AXES, outward)  8.01 us
    ppermute x1, waiting for transfers between devices, per_device(): lax.ppermute(outer, AXES, outward)  7.32 us
    ppermute x1, starting transfers between devices, per_device(): direct = lax.ppermute(direct, AXES, outward)  4.14 us
    ppermute x8, starting transfers between devices, swap_cores(): return lax.ppermute(array, 'grad', [(0, 1), (1, 0)])  3.5 us
    ppermute x8, waiting for transfers between devices, swap_cores(): return lax.ppermute(array, 'grad', [(0, 1), (1, 0)])  2.98 us
    ppermute x1, starting transfers between devices, per_device(): lax.ppermute(outer, AXES, outward)  2.74 us
    ppermute x1, starting transfers between devices, per_device(): hopped.append([lax.ppermute(inverse[1], AXES, pairs) for pairs in hops])  1.88 us
  transfers between devices with their start and end apart: 16, of which 5 were waited for; matrix products, arithmetic and copies ran while one was open for 0% of the time, Pallas kernels for 4%

profile of v10, /device:TPU:0, one launch (start us, length us, event | category | flops | bytes accessed | tf_op | source)
XLA Modules:
  0.0 42.8 jit_solution(8871817386342194202)
XLA Ops:
  0.0 1.2 %select_bitcast_fusion = (bf16[384,512]{1,0:T(8,128)(2,1)S(1)}, bf16[384,512]{1,0:T(8,128)(2,1)S(1)}) fusion(bf16[1,384,512]{2,1,0:T(8,128)(2,1)} %param.4, bf16[1,384,512]{2,1,0:T(8,128)(2,1)} %param.3, pred[]{:T(512)S(6)} %eq.4), kind=kLoop, calls=%fused_computation | loop fusion | flops 393216 | bytes 1572865 | tf_op jit(solution)/shard_map/jit(_where)/select_n | solution.py:538
  1.2 0.5 %shard_map.38 = f32[1040,128]{1,0:T(8,128)S(1)} custom-call(bf16[384,512]{1,0:T(8,128)(2,1)S(1)} %get-tuple-element.27.x_ref), custom_call_target="tpu_custom_call" | custom-call | tf_op jit(solution)/shard_map/pallas_call | solution.py:386
  1.6 0.5 %collective-permute-start = (f32[1040,128]{1,0:T(8,128)S(1)}, f32[1040,128]{1,0:T(8,128)S(1)}, u32[]{:S(2)}, u32[]{:S(2)}) collective-permute-start(f32[1040,128]{1,0:T(8,128)S(1)} %shard_map.38), channel_id=1, source_target_pairs={{0,1},{1,0},{2,3},{3,2},{4,5},{5,4},{6,7},{7,6},{8,9},{9,8},{10,11... | collective-permute-start | bytes 1597448 | tf_op jit(solution)/shard_map/ppermute | solution.py:524
  2.2 0.0 copy-start
  2.2 0.5 %shard_map.37.kept_ref = f32[1040,128]{1,0:T(8,128)S(1)} custom-call(bf16[384,512]{1,0:T(8,128)(2,1)S(1)} %get-tuple-element.28.x_ref), custom_call_target="tpu_custom_call" | custom-call | tf_op jit(solution)/shard_map/pallas_call | solution.py:386
  2.6 1.1 %collective-permute-done.other_ref = f32[1040,128]{1,0:T(8,128)S(1)} collective-permute-done((f32[1040,128]{1,0:T(8,128)S(1)}, f32[1040,128]{1,0:T(8,128)S(1)}, u32[]{:S(2)}, u32[]{:S(2)}) %collective-permute-start) | collective-permute-done | bytes 532512 | tf_op jit(solution)/shard_map/ppermute | solution.py:524
  3.7 0.0 copy-done
  3.7 0.1 shard_map.39
  3.8 2.7 %collective-permute-start.1 = (f32[1040,128]{1,0:T(8,128)S(1)}, f32[1040,128]{1,0:T(8,128)S(1)}, u32[]{:S(2)}, u32[]{:S(2)}) collective-permute-start(f32[1040,128]{1,0:T(8,128)S(1)} %get-tuple-element.16), channel_id=1, source_target_pairs={{0,5},{1,0},{2,3},{3,6},{4,1},{5,4},{6,7},{7,2},{8,9},{9,12},{10,1... | collective-permute-start | bytes 1597448 | tf_op jit(solution)/shard_map/ppermute | solution.py:549
  6.6 0.0 collective-permute-start.2
  6.6 1.5 %collective-permute-start.3 = (f32[1040,128]{1,0:T(8,128)S(1)}, f32[1040,128]{1,0:T(8,128)S(1)}, u32[]{:S(2)}, u32[]{:S(2)}) collective-permute-start(f32[1040,128]{1,0:T(8,128)S(1)} %get-tuple-element.16), channel_id=1, source_target_pairs={{0,3},{1,8},{2,11},{3,0},{4,7},{5,1},{6,2},{7,4},{8,12},{9,10},{10... | collective-permute-start | bytes 1597448 | tf_op jit(solution)/shard_map/ppermute | solution.py:551
  8.0 0.5 %collective-permute-start.4 = (f32[1040,128]{1,0:T(8,128)S(1)}, f32[1040,128]{1,0:T(8,128)S(1)}, u32[]{:S(2)}, u32[]{:S(2)}) collective-permute-start(f32[1040,128]{1,0:T(8,128)S(1)} %get-tuple-element.17), channel_id=1, source_target_pairs={{0,1},{1,0},{2,3},{3,2},{4,5},{5,4},{6,7},{7,6},{8,9},{9,8},{10,11... | collective-permute-start | bytes 1597448 | tf_op jit(solution)/shard_map/ppermute | solution.py:524
  8.5 0.0 collective-permute-start.5
  8.5 1.9 %collective-permute-done.5.refs_5_.refs_1_ = f32[128,512]{1,0:T(8,128)S(1)} collective-permute-done((f32[128,512]{1,0:T(8,128)S(1)}, f32[128,512]{1,0:T(8,128)S(1)}, u32[]{:S(2)}, u32[]{:S(2)}) %collective-permute-start.5) | collective-permute-done | bytes 262176 | tf_op jit(solution)/shard_map/ppermute | solution.py:524
  10.4 7.3 %collective-permute-done.1.refs_0_ = f32[1040,128]{1,0:T(8,128)S(1)} collective-permute-done((f32[1040,128]{1,0:T(8,128)S(1)}, f32[1040,128]{1,0:T(8,128)S(1)}, u32[]{:S(2)}, u32[]{:S(2)}) %collective-permute-start.1) | collective-permute-done | bytes 532512 | tf_op jit(solution)/shard_map/ppermute | solution.py:549
  17.8 0.0 collective-permute-done.2.refs_1_
  17.8 0.0 collective-permute-done.3.refs_2_
  17.8 0.0 collective-permute-done.4.refs_3_
  17.8 4.8 %shard_map.40 = (f32[512,128]{1,0:T(8,128)S(1)}, f32[528,128]{1,0:T(8,128)S(1)}, f32[776,128]{1,0:T(8,128)S(1)}, f32[264,128]{1,0:T(8,128)S(1)}, f32[1024,128]{1,0:T(8,128)S(1)}) custom-call(f32[1040,128]{1,0:T(8,128)S(1)} %collective-permute-done.1.refs_0_, f32[1040,128]{1,0:T(8,128)S(1)} %collective-permute-done.2.refs_1_, ...), custom_call_target="tpu_custom_call" | custom-call | tf_op jit(solution)/shard_map/pallas_call | solution.py:386
  22.6 1.9 %collective-permute-start.6 = (f32[528,128]{1,0:T(8,128)S(1)}, f32[528,128]{1,0:T(8,128)S(1)}, u32[]{:S(2)}, u32[]{:S(2)}) collective-permute-start(f32[528,128]{1,0:T(8,128)S(1)} %get-tuple-element.18.refs_0_), channel_id=1, source_target_pairs={{0,1},{1,0},{2,3},{3,2},{4,5},{5,7},{6,10},{7,6},{8,4},{9,8},{10,1... | collective-permute-start | bytes 811016 | tf_op jit(solution)/shard_map/ppermute | solution.py:569
  24.4 0.1 collective-permute-start.10
  24.5 0.4 %collective-permute-start.7 = (f32[264,128]{1,0:T(8,128)S(1)}, f32[264,128]{1,0:T(8,128)S(1)}, u32[]{:S(2)}, u32[]{:S(2)}) collective-permute-start(f32[264,128]{1,0:T(8,128)S(1)} %get-tuple-element.19), channel_id=1, source_target_pairs={{0,1},{1,0},{2,3},{3,2},{4,5},{5,4},{6,7},{7,6},{8,9},{9,8},{10,11... | collective-permute-start | bytes 405512 | tf_op jit(solution)/shard_map/ppermute | solution.py:524
  24.9 4.1 %collective-permute-start.9 = (f32[776,128]{1,0:T(8,128)S(1)}, f32[776,128]{1,0:T(8,128)S(1)}, u32[]{:S(2)}, u32[]{:S(2)}) collective-permute-start(f32[776,128]{1,0:T(8,128)S(1)} %get-tuple-element.20), channel_id=1, source_target_pairs={{0,4},{1,0},{2,3},{3,7},{4,5},{5,1},{6,2},{7,6},{8,12},{9,8},{10,1... | collective-permute-start | bytes 1191944 | tf_op jit(solution)/shard_map/ppermute | solution.py:568
  29.1 0.0 collective-permute-done.7.rest_ref
  29.1 0.0 collective-permute-done.6.hopped_ref.refs_1_
  29.1 0.1 collective-permute-start.8
  29.2 1.1 %collective-permute-start.14 = (f32[1024,128]{1,0:T(8,128)S(1)}, f32[1024,128]{1,0:T(8,128)S(1)}, u32[]{:S(2)}, u32[]{:S(2)}) collective-permute-start(f32[1024,128]{1,0:T(8,128)S(1)} %get-tuple-element.24.refs_2_), channel_id=1, source_target_pairs={{0,1},{1,0},{2,3},{3,2},{4,5},{5,4},{6,7},{7,6},{8,9},{9,8},{10,11... | collective-permute-start | bytes 1572872 | tf_op jit(solution)/shard_map/ppermute | solution.py:524
  30.3 0.0 collective-permute-done.10.refs_1_
  30.3 0.0 collective-permute-start.11
  30.3 8.0 %collective-permute-done.9.refs_3_.refs_4_ = f32[776,128]{1,0:T(8,128)S(1)} collective-permute-done((f32[776,128]{1,0:T(8,128)S(1)}, f32[776,128]{1,0:T(8,128)S(1)}, u32[]{:S(2)}, u32[]{:S(2)}) %collective-permute-start.9) | collective-permute-done | bytes 397344 | tf_op jit(solution)/shard_map/ppermute | solution.py:568
  38.3 0.0 collective-permute-done.8.refs_2_.refs_6_
  38.3 0.1 collective-permute-start.13
  38.4 0.5 %collective-permute-start.15 = (f32[528,128]{1,0:T(8,128)S(1)}, f32[528,128]{1,0:T(8,128)S(1)}, u32[]{:S(2)}, u32[]{:S(2)}) collective-permute-start(f32[528,128]{1,0:T(8,128)S(1)} %collective-permute-done.8.refs_2_.refs_6_), channel_id=1, source_target_pairs={{0,1},{1,0},{2,3},{3,2},{4,5},{5,4},{6,7},{7,6},{8,9},{9,8},{10,11... | collective-permute-start | bytes 811016 | tf_op jit(solution)/shard_map/ppermute | solution.py:524
  38.9 1.0 %collective-permute-done.11.refs_2_.refs_5_ = f32[512,128]{1,0:T(8,128)S(1)} collective-permute-done((f32[512,128]{1,0:T(8,128)S(1)}, f32[512,128]{1,0:T(8,128)S(1)}, u32[]{:S(2)}, u32[]{:S(2)}) %collective-permute-start.11) | collective-permute-done | bytes 262176 | tf_op jit(solution)/shard_map/ppermute | solution.py:575
  39.9 0.4 collective-permute-start.12
  40.3 0.0 collective-permute-done.14.refs_3_
  40.3 0.0 collective-permute-done.13.other_b
  40.3 0.0 collective-permute-done.15.refs_7_
  40.4 1.2 %shard_map.44 = (f32[128,512]{1,0:T(8,128)S(1)}, f32[512,512]{1,0:T(8,128)S(1)}) custom-call(f32[512,128]{1,0:T(8,128)S(1)} %shard_map.43.own_a, f32[528,128]{1,0:T(8,128)S(1)} %shard_map.42.own_b, f32[528,128]{1,0:T(8,128)S(1)} %collective-permute-done.13.other_b, f32[128,512]{1,0:T(8,128)S(1)} %bitcast.9, ...), custom_call_target="tpu_custom_call" | custom-call | tf_op jit(solution)/shard_map/pallas_call | solution.py:386
  41.6 0.0 collective-permute-done.12.other_a
  41.6 1.3 %shard_map.45 = f32[128,512]{1,0:T(8,128)} custom-call(f32[528,128]{1,0:T(8,128)S(1)} %shard_map.42.own_b, f32[512,128]{1,0:T(8,128)S(1)} %collective-permute-done.12.other_a, f32[528,128]{1,0:T(8,128)S(1)} %collective-permute-done.13.other_b, f32[128,512]{1,0:T(8,128)S(1)} %get-tuple-element.25.first_left, f32[512,512]{1,0:T(8,128)S(1)} %get-tuple-element.26.first_right), custom_call_target="tpu_custom_call" | custom-call | tf_op jit(solution)/shard_map/pallas_call | solution.py:386
  (3 shorter events, 0.1 us)
Async XLA Ops:
  1.6 2.1 %collective-permute-start = (f32[1040,128]{1,0:T(8,128)S(1)}, f32[1040,128]{1,0:T(8,128)S(1)}, u32[]{:S(2)}, u32[]{:S(2)}) collective-permute-start(f32[1040,128]{1,0:T(8,128)S(1)} %shard_map.38), channel_id=1, source_target_pairs={{0,1},{1,0},{2,3},{3,2},{4,5},{5,4},{6,7},{7,6},{8,9},{9,8},{10,11... | collective-permute-start | bytes 1597448 | tf_op jit(solution)/shard_map/ppermute | solution.py:524
  2.2 1.6 %copy-start = (f32[1,128,512]{2,1,0:T(8,128)S(1)}, f32[1,128,512]{2,1,0:T(8,128)}, u32[]{:S(2)}) copy-start(f32[1,128,512]{2,1,0:T(8,128)} %param.5) | copy-start | bytes 786436
  3.8 13.9 %collective-permute-start.1 = (f32[1040,128]{1,0:T(8,128)S(1)}, f32[1040,128]{1,0:T(8,128)S(1)}, u32[]{:S(2)}, u32[]{:S(2)}) collective-permute-start(f32[1040,128]{1,0:T(8,128)S(1)} %get-tuple-element.16), channel_id=1, source_target_pairs={{0,5},{1,0},{2,3},{3,6},{4,1},{5,4},{6,7},{7,2},{8,9},{9,12},{10,1... | collective-permute-start | bytes 1597448 | tf_op jit(solution)/shard_map/ppermute | solution.py:549
  6.6 11.2 %collective-permute-start.2 = (f32[1040,128]{1,0:T(8,128)S(1)}, f32[1040,128]{1,0:T(8,128)S(1)}, u32[]{:S(2)}, u32[]{:S(2)}) collective-permute-start(f32[1040,128]{1,0:T(8,128)S(1)} %get-tuple-element.17), channel_id=1, source_target_pairs={{0,1},{1,0},{2,3},{3,2},{4,20},{5,8},{6,11},{7,23},{8,5},{9,25},{1... | collective-permute-start | bytes 1597448 | tf_op jit(solution)/shard_map/ppermute | solution.py:550
  6.6 11.2 %collective-permute-start.3 = (f32[1040,128]{1,0:T(8,128)S(1)}, f32[1040,128]{1,0:T(8,128)S(1)}, u32[]{:S(2)}, u32[]{:S(2)}) collective-permute-start(f32[1040,128]{1,0:T(8,128)S(1)} %get-tuple-element.16), channel_id=1, source_target_pairs={{0,3},{1,8},{2,11},{3,0},{4,7},{5,1},{6,2},{7,4},{8,12},{9,10},{10... | collective-permute-start | bytes 1597448 | tf_op jit(solution)/shard_map/ppermute | solution.py:551
  8.0 9.7 %collective-permute-start.4 = (f32[1040,128]{1,0:T(8,128)S(1)}, f32[1040,128]{1,0:T(8,128)S(1)}, u32[]{:S(2)}, u32[]{:S(2)}) collective-permute-start(f32[1040,128]{1,0:T(8,128)S(1)} %get-tuple-element.17), channel_id=1, source_target_pairs={{0,1},{1,0},{2,3},{3,2},{4,5},{5,4},{6,7},{7,6},{8,9},{9,8},{10,11... | collective-permute-start | bytes 1597448 | tf_op jit(solution)/shard_map/ppermute | solution.py:524
  8.5 1.9 %collective-permute-start.5 = (f32[128,512]{1,0:T(8,128)S(1)}, f32[128,512]{1,0:T(8,128)S(1)}, u32[]{:S(2)}, u32[]{:S(2)}) collective-permute-start(f32[128,512]{1,0:T(8,128)S(1)} %bitcast.7), channel_id=1, source_target_pairs={{0,1},{1,0},{2,3},{3,2},{4,5},{5,4},{6,7},{7,6},{8,9},{9,8},{10,11... | collective-permute-start | bytes 786440 | tf_op jit(solution)/shard_map/ppermute | solution.py:524
  22.6 6.5 %collective-permute-start.6 = (f32[528,128]{1,0:T(8,128)S(1)}, f32[528,128]{1,0:T(8,128)S(1)}, u32[]{:S(2)}, u32[]{:S(2)}) collective-permute-start(f32[528,128]{1,0:T(8,128)S(1)} %get-tuple-element.18.refs_0_), channel_id=1, source_target_pairs={{0,1},{1,0},{2,3},{3,2},{4,5},{5,7},{6,10},{7,6},{8,4},{9,8},{10,1... | collective-permute-start | bytes 811016 | tf_op jit(solution)/shard_map/ppermute | solution.py:569
  24.4 5.8 %collective-permute-start.10 = (f32[512,128]{1,0:T(8,128)S(1)}, f32[512,128]{1,0:T(8,128)S(1)}, u32[]{:S(2)}, u32[]{:S(2)}) collective-permute-start(f32[512,128]{1,0:T(8,128)S(1)} %get-tuple-element.23.refs_0_), channel_id=1, source_target_pairs={{0,1},{1,0},{2,3},{3,2},{4,5},{5,7},{6,10},{7,6},{8,4},{9,8},{10,1... | collective-permute-start | bytes 786440 | tf_op jit(solution)/shard_map/ppermute | solution.py:567
  24.5 4.6 %collective-permute-start.7 = (f32[264,128]{1,0:T(8,128)S(1)}, f32[264,128]{1,0:T(8,128)S(1)}, u32[]{:S(2)}, u32[]{:S(2)}) collective-permute-start(f32[264,128]{1,0:T(8,128)S(1)} %get-tuple-element.19), channel_id=1, source_target_pairs={{0,1},{1,0},{2,3},{3,2},{4,5},{5,4},{6,7},{7,6},{8,9},{9,8},{10,11... | collective-permute-start | bytes 405512 | tf_op jit(solution)/shard_map/ppermute | solution.py:524
  24.9 13.3 %collective-permute-start.9 = (f32[776,128]{1,0:T(8,128)S(1)}, f32[776,128]{1,0:T(8,128)S(1)}, u32[]{:S(2)}, u32[]{:S(2)}) collective-permute-start(f32[776,128]{1,0:T(8,128)S(1)} %get-tuple-element.20), channel_id=1, source_target_pairs={{0,4},{1,0},{2,3},{3,7},{4,5},{5,1},{6,2},{7,6},{8,12},{9,8},{10,1... | collective-permute-start | bytes 1191944 | tf_op jit(solution)/shard_map/ppermute | solution.py:568
  29.1 9.2 %collective-permute-start.8 = (f32[528,128]{1,0:T(8,128)S(1)}, f32[528,128]{1,0:T(8,128)S(1)}, u32[]{:S(2)}, u32[]{:S(2)}) collective-permute-start(f32[528,128]{1,0:T(8,128)S(1)} %shard_map.41), channel_id=1, source_target_pairs={{0,1},{1,5},{2,6},{3,2},{4,0},{5,4},{6,7},{7,3},{8,9},{9,13},{10,1... | collective-permute-start | bytes 811016 | tf_op jit(solution)/shard_map/ppermute | solution.py:575
  29.2 11.1 %collective-permute-start.14 = (f32[1024,128]{1,0:T(8,128)S(1)}, f32[1024,128]{1,0:T(8,128)S(1)}, u32[]{:S(2)}, u32[]{:S(2)}) collective-permute-start(f32[1024,128]{1,0:T(8,128)S(1)} %get-tuple-element.24.refs_2_), channel_id=1, source_target_pairs={{0,1},{1,0},{2,3},{3,2},{4,5},{5,4},{6,7},{7,6},{8,9},{9,8},{10,11... | collective-permute-start | bytes 1572872 | tf_op jit(solution)/shard_map/ppermute | solution.py:524
  30.3 9.6 %collective-permute-start.11 = (f32[512,128]{1,0:T(8,128)S(1)}, f32[512,128]{1,0:T(8,128)S(1)}, u32[]{:S(2)}, u32[]{:S(2)}) collective-permute-start(f32[512,128]{1,0:T(8,128)S(1)} %collective-permute-done.10.refs_1_), channel_id=1, source_target_pairs={{0,1},{1,5},{2,6},{3,2},{4,0},{5,4},{6,7},{7,3},{8,9},{9,13},{10,1... | collective-permute-start | bytes 786440 | tf_op jit(solution)/shard_map/ppermute | solution.py:575
  38.3 2.0 %collective-permute-start.13 = (f32[528,128]{1,0:T(8,128)S(1)}, f32[528,128]{1,0:T(8,128)S(1)}, u32[]{:S(2)}, u32[]{:S(2)}) collective-permute-start(f32[528,128]{1,0:T(8,128)S(1)} %shard_map.42.own_b), channel_id=1, source_target_pairs={{0,1},{1,0},{2,3},{3,2},{4,5},{5,4},{6,7},{7,6},{8,9},{9,8},{10,11... | collective-permute-start | bytes 811016 | tf_op jit(solution)/shard_map/ppermute | solution.py:524
  38.4 2.0 %collective-permute-start.15 = (f32[528,128]{1,0:T(8,128)S(1)}, f32[528,128]{1,0:T(8,128)S(1)}, u32[]{:S(2)}, u32[]{:S(2)}) collective-permute-start(f32[528,128]{1,0:T(8,128)S(1)} %collective-permute-done.8.refs_2_.refs_6_), channel_id=1, source_target_pairs={{0,1},{1,0},{2,3},{3,2},{4,5},{5,4},{6,7},{7,6},{8,9},{9,8},{10,11... | collective-permute-start | bytes 811016 | tf_op jit(solution)/shard_map/ppermute | solution.py:524
  39.9 1.6 %collective-permute-start.12 = (f32[512,128]{1,0:T(8,128)S(1)}, f32[512,128]{1,0:T(8,128)S(1)}, u32[]{:S(2)}, u32[]{:S(2)}) collective-permute-start(f32[512,128]{1,0:T(8,128)S(1)} %shard_map.43.own_a), channel_id=1, source_target_pairs={{0,1},{1,0},{2,3},{3,2},{4,5},{5,4},{6,7},{7,6},{8,9},{9,8},{10,11... | collective-permute-start | bytes 786440 | tf_op jit(solution)/shard_map/ppermute | solution.py:524

commit v11 on v10

--- a/solution.py
+++ b/solution.py
@@ -180,7 +180,7 @@
 
 
 def inverse_kernel(scale, order, *refs):
-    *sums, own_rows_ref, other_rows_ref, a_ref, b_ref, direct_ref, rest_ref, gathered_ref, factor_ref, rows_ref = refs
+    *sums, own_rows_ref, other_rows_ref, a_ref, b_ref, direct_ref, gathered_ref, factor_ref, rows_ref = refs
     split = part_rows(order)[0]
 
     def piece(start, size):
@@ -215,14 +215,11 @@
             value = block_of(corner)(i - middle // LANE, j - middle // LANE)
         return start * (value + block_of(eye)(i, j))
 
-    used = direct_ref.shape[0] - split
-
     @pl.when(is_middle())
     def _():
         pack(block, order, a_ref, b_ref, lax.rem(lax.axis_index("cuts"), 2))
         direct_ref[:split, :] = a_ref[...]
-        direct_ref[split:, :] = b_ref[:used, :]
-        rest_ref[...] = b_ref[used:, :]
+        direct_ref[split:, :] = b_ref[...]
 
     @pl.when(jnp.logical_not(is_middle()))
     def _():
@@ -244,22 +241,7 @@
 
         a_ref[...] = rows_ref[:split, :]
         b_ref[...] = rows_ref[split:, :]
-        direct_ref[...] = rows_ref[: split + used, :]
-        rest_ref[...] = rows_ref[:used, :]
-
-
-def relay_kernel(hopped_ref, rest_ref, out_ref):
-    used = rest_ref.shape[0]
-    out_ref[:used, :] = hopped_ref[:used, :]
-    rest = jnp.logical_and(is_middle(), lax.axis_index("grad") == 1)
-
-    @pl.when(rest)
-    def _():
-        out_ref[used:, :] = rest_ref[...]
-
-    @pl.when(jnp.logical_not(rest))
-    def _():
-        out_ref[used:, :] = hopped_ref[used:, :]
+        direct_ref[...] = rows_ref[...]
 
 
 def choose_kernel(which, start, *refs):
@@ -268,13 +250,10 @@
     rows = out_ref.shape[0]
     for place, ref in enumerate(arrays):
         first = start if place == len(arrays) - 1 else 0
-        size = min(rows, ref.shape[0] - first)
 
         @pl.when(index == place)
         def _():
-            out_ref[:size, :] = ref[first : first + size, :]
-            if size < rows:
-                out_ref[size:, :] = jnp.zeros((rows - size, LANE), jnp.float32)
+            out_ref[...] = ref[first : first + rows, :]
 
 
 def fill_left(order, mine, a_ref, b_ref, left_ref):
@@ -288,23 +267,13 @@
                 left_ref[:, column * LANE : (column + 1) * LANE] = block
 
 
-def fill_right(order, a_ref, b_ref, left_b_ref, joined_ref, right_ref):
-    cut = lax.axis_index("cuts")
-    zq = lax.rem(lax.axis_index("dp"), QUAD)
-    was_direct = jnp.logical_and(jnp.logical_not(is_middle()), (zq ^ 1) == 2 - lax.rem(cut, 2))
-    used = joined_ref.shape[0] // 2
-    joined_ref[...] = b_ref[...]
-
-    @pl.when(was_direct)
-    def _():
-        joined_ref[used:, :] = left_b_ref[used:, :]
-
+def fill_right(order, a_ref, b_ref, right_ref):
     unpack(
         lambda start, size: a_ref[pl.ds(start, size), :],
-        lambda start, size: joined_ref[pl.ds(start, size), :],
+        lambda start, size: b_ref[pl.ds(start, size), :],
         order,
         right_ref,
-        lax.rem(cut, 2),
+        lax.rem(lax.axis_index("cuts"), 2),
     )
 
 
@@ -313,9 +282,9 @@
     return core, lax.rem(lax.axis_index("dp") * lax.axis_size("grad") + core, spread)
 
 
-def first_kernel(order, spread, own_a, own_b, other_b, *refs):
+def first_kernel(order, spread, own_a, own_b, *refs):
     own_rows_ref, other_rows_ref, outer_ref, outer_other_ref, direct_ref, relayed_a, relayed_b, relayed_other, *refs = refs
-    left_out, right_out, left_ref, right_ref, tile_ref, joined_ref = refs
+    left_out, right_out, left_ref, right_ref, tile_ref = refs
     core, mine = place_of_rows(spread)
     rows_dev = own_rows_ref.shape[0]
 
@@ -352,12 +321,12 @@
 
     @pl.when(core == 0)
     def _():
-        fill_right(order, own_a, own_b, other_b, joined_ref, right_ref)
+        fill_right(order, own_a, own_b, right_ref)
         right_out[...] = times(halves(tile_ref[...]), halves(right_ref[...]))
 
 
-def last_kernel(order, spread, own_b, other_a, other_b, first_left, first_right, out_ref, *refs):
-    left_ref, right_ref, joined_ref, result_ref, sems = refs
+def last_kernel(order, spread, other_a, other_b, first_left, first_right, out_ref, *refs):
+    left_ref, right_ref, result_ref, sems = refs
     core, mine = place_of_rows(spread)
     step = order // 2
 
@@ -373,7 +342,7 @@
 
     @pl.when(core != 0)
     def _():
-        fill_right(order, other_a, other_b, own_b, joined_ref, right_ref)
+        fill_right(order, other_a, other_b, right_ref)
         finish(halves(first_left[...]), right_ref)
 
     @pl.when(core == 0)
@@ -554,9 +523,9 @@
     scale = 1.0 / (tok_rows * dev_count)
     square_scratch = pltpu.VMEM((order, order), jnp.float32)
     gathered = (2 * grads.size // LANE, LANE)
-    *inverse, direct, rest_own, outer_rows = call(
+    *inverse, direct, outer_rows = call(
         functools.partial(inverse_kernel, scale, order),
-        [(split, LANE), (rest, LANE), (split + rest - rest // 2, LANE), (rest // 2, LANE), gathered],
+        [(split, LANE), (rest, LANE), shape, gathered],
         [square_scratch, pltpu.VMEM(shape, jnp.float32)],
         *sums,
         grads,
@@ -567,12 +536,7 @@
     hopped = [[lax.ppermute(inverse[0], AXES, pairs) for pairs in hops]]
     direct = lax.ppermute(direct, AXES, outward)
     hopped.append([lax.ppermute(inverse[1], AXES, pairs) for pairs in hops])
-    rest_own = swap_cores(rest_own)
-    carried = [
-        hopped[0],
-        [call(relay_kernel, [array.shape], [], array, rest_own)[0] for array in hopped[1]],
-    ]
-    relayed = [[lax.ppermute(array, AXES, pairs) for array, pairs in zip(arrays, relays)] for arrays in carried]
+    relayed = [[lax.ppermute(array, AXES, pairs) for array, pairs in zip(arrays, relays)] for arrays in hopped]
     relayed[1], direct = lax.optimization_barrier((relayed[1], direct))
     arrived = [
         arrays[0] if cuts == 2 else call(functools.partial(choose_kernel, plan.turn, 0), [arrays[0].shape], [], *arrays)[0]
@@ -591,13 +555,11 @@
         )
     other_a, other_b = map(swap_cores, own)
     left_scratch = pltpu.VMEM((LANE, order), jnp.float32)
-    joined_scratch = pltpu.VMEM((rest, LANE), jnp.float32)
     first = call(
         functools.partial(first_kernel, order, spread),
         [(LANE, order), (order, order)],
-        [left_scratch, square_scratch, square_scratch, joined_scratch],
+        [left_scratch, square_scratch, square_scratch],
         *own,
-        other_b,
         grads,
         other_rows,
         outer_rows,
@@ -612,11 +574,9 @@
         [
             left_scratch,
             square_scratch,
-            joined_scratch,
             pltpu.VMEM((2, LANE, order // 2), jnp.float32),
             pltpu.SemaphoreType.DMA((2,)),
         ],
-        own[1],
         other_a,
         other_b,
         *first,

time: 43 us -> 42.5 us (0.988)
  starting transfers between devices: 13.9 us -> 13.3 us
    ppermute x1, starting transfers between devices: 4.14 us -> 2.43 us  [per_device(): direct = lax.ppermute(direct, AXES, outward)]
    ppermute x1, waiting for transfers between devices: 8.01 us -> 6.85 us  [per_device(): direct = lax.ppermute(direct, AXES, outward)]
    ppermute x2, waiting for transfers between devices: 1.02 us -> 2.05 us  [per_device(): lax.ppermute(array, AXES, pairs)]
    ppermute x8 -> x7, starting transfers between devices: 3.5 us -> 4.28 us  [swap_cores(): return lax.ppermute(array, 'grad', [(0, 1), (1, 0)])]
    ppermute x2, starting transfers between devices: 0.07 us -> 0.51 us  [per_device(): lax.ppermute(array, AXES, pairs)]
    ppermute x8 -> x7, waiting for transfers between devices: 2.98 us -> 3.28 us  [swap_cores(): return lax.ppermute(array, 'grad', [(0, 1), (1, 0)])]
    pallas_call x9 -> x8, Pallas kernels: 8.35 us -> 8.25 us  [call(): pl.pallas_call(kernel, out_shape=[jax.ShapeDtypeStruct(shape, jnp.float32...]
  transfers between devices with their start and end apart: 16 -> 15, of which waited for: 5 -> 6; matrix products, arithmetic and copies ran while one was open for 0% -> 0% of each run, Pallas kernels for 4% -> 4%
where the time goes in v11:
time: 42.5 us; the launch traced here: 42.3 us
  waiting for transfers between devices  19.5 us (46%)
  starting transfers between devices  13.3 us (31%)
  Pallas kernels  8.25 us (19%)
  other arithmetic  1.17 us (3%)
    pallas_call x8, Pallas kernels, call(): pl.pallas_call(kernel, out_shape=[jax.ShapeDtypeStruct(shape, jnp.float32...  8.25 us
    ppermute x1, waiting for transfers between devices, per_device(): lax.ppermute(outer, AXES, outward)  7.32 us
    ppermute x1, waiting for transfers between devices, per_device(): direct = lax.ppermute(direct, AXES, outward)  6.85 us
    ppermute x7, starting transfers between devices, swap_cores(): return lax.ppermute(array, 'grad', [(0, 1), (1, 0)])  4.28 us
    ppermute x7, waiting for transfers between devices, swap_cores(): return lax.ppermute(array, 'grad', [(0, 1), (1, 0)])  3.28 us
    ppermute x1, starting transfers between devices, per_device(): lax.ppermute(outer, AXES, outward)  2.74 us
    ppermute x1, starting transfers between devices, per_device(): direct = lax.ppermute(direct, AXES, outward)  2.43 us
    ppermute x2, waiting for transfers between devices, per_device(): lax.ppermute(array, AXES, pairs)  2.05 us
  transfers between devices with their start and end apart: 15, of which 6 were waited for; matrix products, arithmetic and copies ran while one was open for 0% of the time, Pallas kernels for 4%

profile of v11, /device:TPU:0, one launch (start us, length us, event | category | flops | bytes accessed | tf_op | source)
XLA Modules:
  0.0 42.3 jit_solution(16848696190552047715)
XLA Ops:
  0.0 1.2 %select_bitcast_fusion = (bf16[384,512]{1,0:T(8,128)(2,1)S(1)}, bf16[384,512]{1,0:T(8,128)(2,1)S(1)}) fusion(bf16[1,384,512]{2,1,0:T(8,128)(2,1)} %param.4, bf16[1,384,512]{2,1,0:T(8,128)(2,1)} %param.3, pred[]{:T(512)S(6)} %eq.4), kind=kLoop, calls=%fused_computation | loop fusion | flops 393216 | bytes 1572865 | tf_op jit(solution)/shard_map/jit(_where)/select_n | solution.py:507
  1.2 0.5 %shard_map.38 = f32[1040,128]{1,0:T(8,128)S(1)} custom-call(bf16[384,512]{1,0:T(8,128)(2,1)S(1)} %get-tuple-element.25.x_ref), custom_call_target="tpu_custom_call" | custom-call | tf_op jit(solution)/shard_map/pallas_call | solution.py:355
  1.6 0.5 %collective-permute-start = (f32[1040,128]{1,0:T(8,128)S(1)}, f32[1040,128]{1,0:T(8,128)S(1)}, u32[]{:S(2)}, u32[]{:S(2)}) collective-permute-start(f32[1040,128]{1,0:T(8,128)S(1)} %shard_map.38), channel_id=1, source_target_pairs={{0,1},{1,0},{2,3},{3,2},{4,5},{5,4},{6,7},{7,6},{8,9},{9,8},{10,11... | collective-permute-start | bytes 1597448 | tf_op jit(solution)/shard_map/ppermute | solution.py:493
  2.2 0.0 copy-start
  2.2 0.5 %shard_map.37.kept_ref = f32[1040,128]{1,0:T(8,128)S(1)} custom-call(bf16[384,512]{1,0:T(8,128)(2,1)S(1)} %get-tuple-element.26.x_ref), custom_call_target="tpu_custom_call" | custom-call | tf_op jit(solution)/shard_map/pallas_call | solution.py:355
  2.6 1.1 %collective-permute-done.other_ref = f32[1040,128]{1,0:T(8,128)S(1)} collective-permute-done((f32[1040,128]{1,0:T(8,128)S(1)}, f32[1040,128]{1,0:T(8,128)S(1)}, u32[]{:S(2)}, u32[]{:S(2)}) %collective-permute-start) | collective-permute-done | bytes 532512 | tf_op jit(solution)/shard_map/ppermute | solution.py:493
  3.7 0.0 copy-done
  3.7 0.1 shard_map.39
  3.8 2.7 %collective-permute-start.1 = (f32[1040,128]{1,0:T(8,128)S(1)}, f32[1040,128]{1,0:T(8,128)S(1)}, u32[]{:S(2)}, u32[]{:S(2)}) collective-permute-start(f32[1040,128]{1,0:T(8,128)S(1)} %get-tuple-element.15), channel_id=1, source_target_pairs={{0,5},{1,0},{2,3},{3,6},{4,1},{5,4},{6,7},{7,2},{8,9},{9,12},{10,1... | collective-permute-start | bytes 1597448 | tf_op jit(solution)/shard_map/ppermute | solution.py:518
  6.6 0.0 collective-permute-start.2
  6.6 1.5 %collective-permute-start.3 = (f32[1040,128]{1,0:T(8,128)S(1)}, f32[1040,128]{1,0:T(8,128)S(1)}, u32[]{:S(2)}, u32[]{:S(2)}) collective-permute-start(f32[1040,128]{1,0:T(8,128)S(1)} %get-tuple-element.15), channel_id=1, source_target_pairs={{0,3},{1,8},{2,11},{3,0},{4,7},{5,1},{6,2},{7,4},{8,12},{9,10},{10... | collective-permute-start | bytes 1597448 | tf_op jit(solution)/shard_map/ppermute | solution.py:520
  8.0 0.5 %collective-permute-start.4 = (f32[1040,128]{1,0:T(8,128)S(1)}, f32[1040,128]{1,0:T(8,128)S(1)}, u32[]{:S(2)}, u32[]{:S(2)}) collective-permute-start(f32[1040,128]{1,0:T(8,128)S(1)} %get-tuple-element.16), channel_id=1, source_target_pairs={{0,1},{1,0},{2,3},{3,2},{4,5},{5,4},{6,7},{7,6},{8,9},{9,8},{10,11... | collective-permute-start | bytes 1597448 | tf_op jit(solution)/shard_map/ppermute | solution.py:493
  8.5 0.0 collective-permute-start.5
  8.5 1.9 %collective-permute-done.5.refs_5_.refs_1_ = f32[128,512]{1,0:T(8,128)S(1)} collective-permute-done((f32[128,512]{1,0:T(8,128)S(1)}, f32[128,512]{1,0:T(8,128)S(1)}, u32[]{:S(2)}, u32[]{:S(2)}) %collective-permute-start.5) | collective-permute-done | bytes 262176 | tf_op jit(solution)/shard_map/ppermute | solution.py:493
  10.4 7.3 %collective-permute-done.1.refs_0_ = f32[1040,128]{1,0:T(8,128)S(1)} collective-permute-done((f32[1040,128]{1,0:T(8,128)S(1)}, f32[1040,128]{1,0:T(8,128)S(1)}, u32[]{:S(2)}, u32[]{:S(2)}) %collective-permute-start.1) | collective-permute-done | bytes 532512 | tf_op jit(solution)/shard_map/ppermute | solution.py:518
  17.8 0.0 collective-permute-done.2.refs_1_
  17.8 0.0 collective-permute-done.3.refs_2_
  17.8 0.0 collective-permute-done.4.refs_3_
  17.8 4.8 %shard_map.40 = (f32[512,128]{1,0:T(8,128)S(1)}, f32[528,128]{1,0:T(8,128)S(1)}, f32[1040,128]{1,0:T(8,128)S(1)}, f32[1024,128]{1,0:T(8,128)S(1)}) custom-call(f32[1040,128]{1,0:T(8,128)S(1)} %collective-permute-done.1.refs_0_, f32[1040,128]{1,0:T(8,128)S(1)} %collective-permute-done.2.refs_1_, f32[1040,128]{1,0:T(8,128)S(1)} %collective-permute-done.3.refs_2_, ...), custom_call_target="tpu_custom_call" | custom-call | tf_op jit(solution)/shard_map/pallas_call | solution.py:355
  22.5 1.9 %collective-permute-start.8 = (f32[528,128]{1,0:T(8,128)S(1)}, f32[528,128]{1,0:T(8,128)S(1)}, u32[]{:S(2)}, u32[]{:S(2)}) collective-permute-start(f32[528,128]{1,0:T(8,128)S(1)} %get-tuple-element.18.refs_0_), channel_id=1, source_target_pairs={{0,1},{1,0},{2,3},{3,2},{4,5},{5,7},{6,10},{7,6},{8,4},{9,8},{10,1... | collective-permute-start | bytes 811016 | tf_op jit(solution)/shard_map/ppermute | solution.py:538
  24.4 2.4 %collective-permute-start.10 = (f32[1040,128]{1,0:T(8,128)S(1)}, f32[1040,128]{1,0:T(8,128)S(1)}, u32[]{:S(2)}, u32[]{:S(2)}) collective-permute-start(f32[1040,128]{1,0:T(8,128)S(1)} %get-tuple-element.19), channel_id=1, source_target_pairs={{0,4},{1,0},{2,3},{3,7},{4,5},{5,1},{6,2},{7,6},{8,12},{9,8},{10,1... | collective-permute-start | bytes 1597448 | tf_op jit(solution)/shard_map/ppermute | solution.py:537
  26.9 0.0 collective-permute-start.6
  26.9 0.0 collective-permute-done.8.refs_1_
  26.9 0.5 %collective-permute-start.9 = (f32[528,128]{1,0:T(8,128)S(1)}, f32[528,128]{1,0:T(8,128)S(1)}, u32[]{:S(2)}, u32[]{:S(2)}) collective-permute-start(f32[528,128]{1,0:T(8,128)S(1)} %collective-permute-done.8.refs_1_), channel_id=1, source_target_pairs={{0,1},{1,5},{2,6},{3,2},{4,0},{5,4},{6,7},{7,3},{8,9},{9,13},{10,1... | collective-permute-start | bytes 811016 | tf_op jit(solution)/shard_map/ppermute | solution.py:539
  27.4 2.6 %collective-permute-start.13 = (f32[1024,128]{1,0:T(8,128)S(1)}, f32[1024,128]{1,0:T(8,128)S(1)}, u32[]{:S(2)}, u32[]{:S(2)}) collective-permute-start(f32[1024,128]{1,0:T(8,128)S(1)} %get-tuple-element.22.refs_2_), channel_id=1, source_target_pairs={{0,1},{1,0},{2,3},{3,2},{4,5},{5,4},{6,7},{7,6},{8,9},{9,8},{10,11... | collective-permute-start | bytes 1572872 | tf_op jit(solution)/shard_map/ppermute | solution.py:493
  30.0 0.0 collective-permute-done.6.refs_1_
  30.0 0.0 collective-permute-start.7
  30.0 6.8 %collective-permute-done.10.refs_3_.refs_4_ = f32[1040,128]{1,0:T(8,128)S(1)} collective-permute-done((f32[1040,128]{1,0:T(8,128)S(1)}, f32[1040,128]{1,0:T(8,128)S(1)}, u32[]{:S(2)}, u32[]{:S(2)}) %collective-permute-start.10) | collective-permute-done | bytes 532512 | tf_op jit(solution)/shard_map/ppermute | solution.py:537
  36.8 0.0 collective-permute-done.9.refs_2_.refs_6_
  36.8 0.0 collective-permute-start.14
  36.9 0.6 %collective-permute-start.12 = (f32[528,128]{1,0:T(8,128)S(1)}, f32[528,128]{1,0:T(8,128)S(1)}, u32[]{:S(2)}, u32[]{:S(2)}) collective-permute-start(f32[528,128]{1,0:T(8,128)S(1)} %shard_map.42.own_b), channel_id=1, source_target_pairs={{0,1},{1,0},{2,3},{3,2},{4,5},{5,4},{6,7},{7,6},{8,9},{9,8},{10,11... | collective-permute-start | bytes 811016 | tf_op jit(solution)/shard_map/ppermute | solution.py:493
  37.4 2.0 %collective-permute-done.7.refs_2_.refs_5_ = f32[512,128]{1,0:T(8,128)S(1)} collective-permute-done((f32[512,128]{1,0:T(8,128)S(1)}, f32[512,128]{1,0:T(8,128)S(1)}, u32[]{:S(2)}, u32[]{:S(2)}) %collective-permute-start.7) | collective-permute-done | bytes 262176 | tf_op jit(solution)/shard_map/ppermute | solution.py:539
  39.5 0.1 collective-permute-start.11
  39.6 0.0 collective-permute-done.13.refs_3_
  39.6 0.0 collective-permute-done.14.refs_7_
  39.6 1.2 %shard_map.43 = (f32[128,512]{1,0:T(8,128)S(1)}, f32[512,512]{1,0:T(8,128)S(1)}) custom-call(f32[512,128]{1,0:T(8,128)S(1)} %shard_map.41.own_a, f32[528,128]{1,0:T(8,128)S(1)} %shard_map.42.own_b, f32[128,512]{1,0:T(8,128)S(1)} %bitcast.9, f32[128,512]{1,0:T(8,128)S(1)} %collective-permute-done.5.refs_5_.refs_1_, ...), custom_call_target="tpu_custom_call" | custom-call | tf_op jit(solution)/shard_map/pallas_call | solution.py:355
  40.8 0.3 collective-permute-done.11.other_a
  41.1 0.0 collective-permute-done.12.other_b
  41.1 1.2 %shard_map.44 = f32[128,512]{1,0:T(8,128)} custom-call(f32[512,128]{1,0:T(8,128)S(1)} %collective-permute-done.11.other_a, f32[528,128]{1,0:T(8,128)S(1)} %collective-permute-done.12.other_b, f32[128,512]{1,0:T(8,128)S(1)} %get-tuple-element.23.first_left, f32[512,512]{1,0:T(8,128)S(1)} %get-tuple-element.24.first_right), custom_call_target="tpu_custom_call" | custom-call | tf_op jit(solution)/shard_map/pallas_call | solution.py:355
  (2 shorter events, 0.0 us)
Async XLA Ops:
  1.6 2.1 %collective-permute-start = (f32[1040,128]{1,0:T(8,128)S(1)}, f32[1040,128]{1,0:T(8,128)S(1)}, u32[]{:S(2)}, u32[]{:S(2)}) collective-permute-start(f32[1040,128]{1,0:T(8,128)S(1)} %shard_map.38), channel_id=1, source_target_pairs={{0,1},{1,0},{2,3},{3,2},{4,5},{5,4},{6,7},{7,6},{8,9},{9,8},{10,11... | collective-permute-start | bytes 1597448 | tf_op jit(solution)/shard_map/ppermute | solution.py:493
  2.2 1.6 %copy-start = (f32[1,128,512]{2,1,0:T(8,128)S(1)}, f32[1,128,512]{2,1,0:T(8,128)}, u32[]{:S(2)}) copy-start(f32[1,128,512]{2,1,0:T(8,128)} %param.5) | copy-start | bytes 786436
  3.8 13.9 %collective-permute-start.1 = (f32[1040,128]{1,0:T(8,128)S(1)}, f32[1040,128]{1,0:T(8,128)S(1)}, u32[]{:S(2)}, u32[]{:S(2)}) collective-permute-start(f32[1040,128]{1,0:T(8,128)S(1)} %get-tuple-element.15), channel_id=1, source_target_pairs={{0,5},{1,0},{2,3},{3,6},{4,1},{5,4},{6,7},{7,2},{8,9},{9,12},{10,1... | collective-permute-start | bytes 1597448 | tf_op jit(solution)/shard_map/ppermute | solution.py:518
  6.6 11.2 %collective-permute-start.2 = (f32[1040,128]{1,0:T(8,128)S(1)}, f32[1040,128]{1,0:T(8,128)S(1)}, u32[]{:S(2)}, u32[]{:S(2)}) collective-permute-start(f32[1040,128]{1,0:T(8,128)S(1)} %get-tuple-element.16), channel_id=1, source_target_pairs={{0,1},{1,0},{2,3},{3,2},{4,20},{5,8},{6,11},{7,23},{8,5},{9,25},{1... | collective-permute-start | bytes 1597448 | tf_op jit(solution)/shard_map/ppermute | solution.py:519
  6.6 11.2 %collective-permute-start.3 = (f32[1040,128]{1,0:T(8,128)S(1)}, f32[1040,128]{1,0:T(8,128)S(1)}, u32[]{:S(2)}, u32[]{:S(2)}) collective-permute-start(f32[1040,128]{1,0:T(8,128)S(1)} %get-tuple-element.15), channel_id=1, source_target_pairs={{0,3},{1,8},{2,11},{3,0},{4,7},{5,1},{6,2},{7,4},{8,12},{9,10},{10... | collective-permute-start | bytes 1597448 | tf_op jit(solution)/shard_map/ppermute | solution.py:520
  8.0 9.7 %collective-permute-start.4 = (f32[1040,128]{1,0:T(8,128)S(1)}, f32[1040,128]{1,0:T(8,128)S(1)}, u32[]{:S(2)}, u32[]{:S(2)}) collective-permute-start(f32[1040,128]{1,0:T(8,128)S(1)} %get-tuple-element.16), channel_id=1, source_target_pairs={{0,1},{1,0},{2,3},{3,2},{4,5},{5,4},{6,7},{7,6},{8,9},{9,8},{10,11... | collective-permute-start | bytes 1597448 | tf_op jit(solution)/shard_map/ppermute | solution.py:493
  8.5 1.9 %collective-permute-start.5 = (f32[128,512]{1,0:T(8,128)S(1)}, f32[128,512]{1,0:T(8,128)S(1)}, u32[]{:S(2)}, u32[]{:S(2)}) collective-permute-start(f32[128,512]{1,0:T(8,128)S(1)} %bitcast.7), channel_id=1, source_target_pairs={{0,1},{1,0},{2,3},{3,2},{4,5},{5,4},{6,7},{7,6},{8,9},{9,8},{10,11... | collective-permute-start | bytes 786440 | tf_op jit(solution)/shard_map/ppermute | solution.py:493
  22.5 4.3 %collective-permute-start.8 = (f32[528,128]{1,0:T(8,128)S(1)}, f32[528,128]{1,0:T(8,128)S(1)}, u32[]{:S(2)}, u32[]{:S(2)}) collective-permute-start(f32[528,128]{1,0:T(8,128)S(1)} %get-tuple-element.18.refs_0_), channel_id=1, source_target_pairs={{0,1},{1,0},{2,3},{3,2},{4,5},{5,7},{6,10},{7,6},{8,4},{9,8},{10,1... | collective-permute-start | bytes 811016 | tf_op jit(solution)/shard_map/ppermute | solution.py:538
  24.4 12.4 %collective-permute-start.10 = (f32[1040,128]{1,0:T(8,128)S(1)}, f32[1040,128]{1,0:T(8,128)S(1)}, u32[]{:S(2)}, u32[]{:S(2)}) collective-permute-start(f32[1040,128]{1,0:T(8,128)S(1)} %get-tuple-element.19), channel_id=1, source_target_pairs={{0,4},{1,0},{2,3},{3,7},{4,5},{5,1},{6,2},{7,6},{8,12},{9,8},{10,1... | collective-permute-start | bytes 1597448 | tf_op jit(solution)/shard_map/ppermute | solution.py:537
  26.9 3.1 %collective-permute-start.6 = (f32[512,128]{1,0:T(8,128)S(1)}, f32[512,128]{1,0:T(8,128)S(1)}, u32[]{:S(2)}, u32[]{:S(2)}) collective-permute-start(f32[512,128]{1,0:T(8,128)S(1)} %get-tuple-element.17.refs_0_), channel_id=1, source_target_pairs={{0,1},{1,0},{2,3},{3,2},{4,5},{5,7},{6,10},{7,6},{8,4},{9,8},{10,1... | collective-permute-start | bytes 786440 | tf_op jit(solution)/shard_map/ppermute | solution.py:536
  26.9 10.0 %collective-permute-start.9 = (f32[528,128]{1,0:T(8,128)S(1)}, f32[528,128]{1,0:T(8,128)S(1)}, u32[]{:S(2)}, u32[]{:S(2)}) collective-permute-start(f32[528,128]{1,0:T(8,128)S(1)} %collective-permute-done.8.refs_1_), channel_id=1, source_target_pairs={{0,1},{1,5},{2,6},{3,2},{4,0},{5,4},{6,7},{7,3},{8,9},{9,13},{10,1... | collective-permute-start | bytes 811016 | tf_op jit(solution)/shard_map/ppermute | solution.py:539
  27.4 12.2 %collective-permute-start.13 = (f32[1024,128]{1,0:T(8,128)S(1)}, f32[1024,128]{1,0:T(8,128)S(1)}, u32[]{:S(2)}, u32[]{:S(2)}) collective-permute-start(f32[1024,128]{1,0:T(8,128)S(1)} %get-tuple-element.22.refs_2_), channel_id=1, source_target_pairs={{0,1},{1,0},{2,3},{3,2},{4,5},{5,4},{6,7},{7,6},{8,9},{9,8},{10,11... | collective-permute-start | bytes 1572872 | tf_op jit(solution)/shard_map/ppermute | solution.py:493
  30.0 9.5 %collective-permute-start.7 = (f32[512,128]{1,0:T(8,128)S(1)}, f32[512,128]{1,0:T(8,128)S(1)}, u32[]{:S(2)}, u32[]{:S(2)}) collective-permute-start(f32[512,128]{1,0:T(8,128)S(1)} %collective-permute-done.6.refs_1_), channel_id=1, source_target_pairs={{0,1},{1,5},{2,6},{3,2},{4,0},{5,4},{6,7},{7,3},{8,9},{9,13},{10,1... | collective-permute-start | bytes 786440 | tf_op jit(solution)/shard_map/ppermute | solution.py:539
  36.8 2.8 %collective-permute-start.14 = (f32[528,128]{1,0:T(8,128)S(1)}, f32[528,128]{1,0:T(8,128)S(1)}, u32[]{:S(2)}, u32[]{:S(2)}) collective-permute-start(f32[528,128]{1,0:T(8,128)S(1)} %collective-permute-done.9.refs_2_.refs_6_), channel_id=1, source_target_pairs={{0,1},{1,0},{2,3},{3,2},{4,5},{5,4},{6,7},{7,6},{8,9},{9,8},{10,11... | collective-permute-start | bytes 811016 | tf_op jit(solution)/shard_map/ppermute | solution.py:493
  36.9 4.2 %collective-permute-start.12 = (f32[528,128]{1,0:T(8,128)S(1)}, f32[528,128]{1,0:T(8,128)S(1)}, u32[]{:S(2)}, u32[]{:S(2)}) collective-permute-start(f32[528,128]{1,0:T(8,128)S(1)} %shard_map.42.own_b), channel_id=1, source_target_pairs={{0,1},{1,0},{2,3},{3,2},{4,5},{5,4},{6,7},{7,6},{8,9},{9,8},{10,11... | collective-permute-start | bytes 811016 | tf_op jit(solution)/shard_map/ppermute | solution.py:493
  39.5 1.6 %collective-permute-start.11 = (f32[512,128]{1,0:T(8,128)S(1)}, f32[512,128]{1,0:T(8,128)S(1)}, u32[]{:S(2)}, u32[]{:S(2)}) collective-permute-start(f32[512,128]{1,0:T(8,128)S(1)} %shard_map.41.own_a), channel_id=1, source_target_pairs={{0,1},{1,0},{2,3},{3,2},{4,5},{5,4},{6,7},{7,6},{8,9},{9,8},{10,11... | collective-permute-start | bytes 786440 | tf_op jit(solution)/shard_map/ppermute | solution.py:493

commit v12 on v11

--- a/solution.py
+++ b/solution.py
@@ -60,31 +60,35 @@
 
 
 def unpack(a_piece, b_piece, order, out_ref, second=0, scale=1.0, shift=0.0):
+    for slot, (i, j) in enumerate(joining_blocks(order)):
+        value = a_piece(slot * LANE, LANE) * scale
+        put_block(out_ref, i, j, value)
+        put_block(out_ref, j, i, value.T)
+    unpack_own(b_piece, order, out_ref, second, scale, shift)
+
+
+def put_block(out_ref, i, j, value):
+    out_ref[i * LANE : (i + 1) * LANE, j * LANE : (j + 1) * LANE] = value
+
+
+def unpack_own(b_piece, order, out_ref, second=0, scale=1.0, shift=0.0):
     rows, cols = places()
     damping = jnp.where(rows == cols, shift, 0.0)
-
-    def put(i, j, value):
-        out_ref[i * LANE : (i + 1) * LANE, j * LANE : (j + 1) * LANE] = value
-
-    def put_both(i, j, value):
-        put(i, j, value)
-        put(j, i, value.T)
-
-    for slot, (i, j) in enumerate(joining_blocks(order)):
-        put_both(i, j, a_piece(slot * LANE, LANE) * scale)
     for half in range(2):
         top = own_start(order, half, second)
         above, pairs = half_blocks(order, half)
         for i, j in above:
-            put_both(i, j, b_piece(top, LANE) * scale)
+            value = b_piece(top, LANE) * scale
+            put_block(out_ref, i, j, value)
+            put_block(out_ref, j, i, value.T)
             top += LANE
         last = b_piece(top + len(pairs) * LANE, -(-len(pairs) // 8) * 8)
         for k, (i, j) in enumerate(pairs):
             both = b_piece(top, LANE)
             turned = both.T
-            put(i, i, jnp.where(rows <= cols, both, turned) * scale + damping)
+            put_block(out_ref, i, i, jnp.where(rows <= cols, both, turned) * scale + damping)
             after = jnp.where(rows > cols, both, jnp.where(rows < cols, turned, last[k : k + 1, :]))
-            put(j, j, after * scale + damping)
+            put_block(out_ref, j, j, after * scale + damping)
             top += LANE
 
 
@@ -113,8 +117,9 @@
     return high, (value - high.astype(jnp.float32)).astype(jnp.bfloat16)
 
 
-def times(left, right):
-    dot = functools.partial(jnp.dot, preferred_element_type=jnp.float32)
+def times(left, right, turned=False):
+    dims = (((1,), (1 if turned else 0,)), ((), ()))
+    dot = functools.partial(lax.dot_general, dimension_numbers=dims, preferred_element_type=jnp.float32)
     rows = left[0].shape[0]
     both = dot(jnp.concatenate(left, 0), right[0])
     return both[:rows] + (dot(left[0], right[1]) + both[rows:])
@@ -282,9 +287,9 @@
     return core, lax.rem(lax.axis_index("dp") * lax.axis_size("grad") + core, spread)
 
 
-def first_kernel(order, spread, own_a, own_b, *refs):
+def first_kernel(order, spread, own_a, own_b, other_b, *refs):
     own_rows_ref, other_rows_ref, outer_ref, outer_other_ref, direct_ref, relayed_a, relayed_b, relayed_other, *refs = refs
-    left_out, right_out, left_ref, right_ref, tile_ref = refs
+    left_out, high_out, low_out, left_ref, right_ref, tile_ref = refs
     core, mine = place_of_rows(spread)
     rows_dev = own_rows_ref.shape[0]
 
@@ -318,43 +323,58 @@
     def _():
         fill_left(order, mine, own_a, own_b, left_ref)
         left_out[...] = times(halves(left_ref[...]), halves(tile_ref[...]))
+        second = lax.rem(lax.axis_index("cuts"), 2)
+        unpack_own(lambda start, size: other_b[pl.ds(start, size), :], order, right_ref, second)
+        for own in (slice(0, order // 2), slice(order // 2, order)):
+            high_out[own, own], low_out[own, own] = halves(right_ref[own, own])
 
     @pl.when(core == 0)
     def _():
         fill_right(order, own_a, own_b, right_ref)
-        right_out[...] = times(halves(tile_ref[...]), halves(right_ref[...]))
-
-
-def last_kernel(order, spread, other_a, other_b, first_left, first_right, out_ref, *refs):
-    left_ref, right_ref, result_ref, sems = refs
+        high_out[...], low_out[...] = halves(times(halves(tile_ref[...]), halves(right_ref[...])))
+
+
+def last_kernel(order, spread, other_a, other_b, first_left, high_ref, low_ref, out_ref, left_ref, result_ref, sems):
     core, mine = place_of_rows(spread)
     step = order // 2
-
-    def finish(left, right_ref):
+    parts = (slice(0, step), slice(step, order))
+
+    def finish(columns):
         copies = []
         for turn in range(2):
-            columns = pl.ds(turn * step, step)
-            result_ref[turn] = times(left, halves(right_ref[:, turn * step : (turn + 1) * step]))
-            copies.append(pltpu.make_async_copy(result_ref.at[turn], out_ref.at[:, columns], sems.at[turn]))
+            result_ref[turn] = columns(turn)
+            target = out_ref.at[:, pl.ds(turn * step, step)]
+            copies.append(pltpu.make_async_copy(result_ref.at[turn], target, sems.at[turn]))
             copies[-1].start()
         for copy in copies:
             copy.wait()
 
     @pl.when(core != 0)
     def _():
-        fill_right(order, other_a, other_b, right_ref)
-        finish(halves(first_left[...]), right_ref)
+        count = step // LANE
+        blocks = [other_a[slot * LANE : (slot + 1) * LANE, :] for slot in range(count * count)]
+        rows = [jnp.concatenate(blocks[row * count : (row + 1) * count], 1) for row in range(count)]
+        joining = halves(jnp.concatenate(rows, 0))
+        left = halves(first_left[...])
+        left = [(left[0][:, part], left[1][:, part]) for part in parts]
+
+        def columns(turn):
+            own = high_ref[parts[turn], parts[turn]], low_ref[parts[turn], parts[turn]]
+            return times(left[turn], own) + times(left[1 - turn], joining, turn == 0)
+
+        finish(columns)
 
     @pl.when(core == 0)
     def _():
         fill_left(order, mine, other_a, other_b, left_ref)
-        finish(halves(left_ref[...]), first_right)
+        left = halves(left_ref[...])
+        finish(lambda turn: times(left, (high_ref[:, parts[turn]], low_ref[:, parts[turn]])))
 
 
 def call(kernel, shapes, scratch, *args, space=pltpu.VMEM):
     return pl.pallas_call(
         kernel,
-        out_shape=[jax.ShapeDtypeStruct(shape, jnp.float32) for shape in shapes],
+        out_shape=[jax.ShapeDtypeStruct(shape[:2], *shape[2:] or (jnp.float32,)) for shape in shapes],
         out_specs=[pl.BlockSpec(memory_space=space) for shape in shapes],
         scratch_shapes=scratch,
         compiler_params=PARAMS,
@@ -557,9 +577,10 @@
     left_scratch = pltpu.VMEM((LANE, order), jnp.float32)
     first = call(
         functools.partial(first_kernel, order, spread),
-        [(LANE, order), (order, order)],
+        [(LANE, order), (order, order, jnp.bfloat16), (order, order, jnp.bfloat16)],
         [left_scratch, square_scratch, square_scratch],
         *own,
+        other_b,
         grads,
         other_rows,
         outer_rows,
@@ -573,7 +594,6 @@
         [grads.shape],
         [
             left_scratch,
-            square_scratch,
             pltpu.VMEM((2, LANE, order // 2), jnp.float32),
             pltpu.SemaphoreType.DMA((2,)),
         ],

time: 42.5 us -> 42.5 us (level)
  no operation moved by 1% of the time
where the time goes in v12:
time: 42.5 us; the launch traced here: 42.3 us
  waiting for transfers between devices  19.5 us (46%)
  starting transfers between devices  13.3 us (31%)
  Pallas kernels  8.26 us (19%)
  other arithmetic  1.17 us (3%)
    pallas_call x8, Pallas kernels, call(): pl.pallas_call(kernel, out_shape=[jax.ShapeDtypeStruct(shape[:2], *(shape...  8.26 us
    ppermute x1, waiting for transfers between devices, per_device(): lax.ppermute(outer, AXES, outward)  7.32 us
    ppermute x1, waiting for transfers between devices, per_device(): direct = lax.ppermute(direct, AXES, outward)  6.85 us
    ppermute x7, starting transfers between devices, swap_cores(): return lax.ppermute(array, 'grad', [(0, 1), (1, 0)])  4.28 us
    ppermute x7, waiting for transfers between devices, swap_cores(): return lax.ppermute(array, 'grad', [(0, 1), (1, 0)])  3.26 us
    ppermute x1, starting transfers between devices, per_device(): lax.ppermute(outer, AXES, outward)  2.74 us
    ppermute x1, starting transfers between devices, per_device(): direct = lax.ppermute(direct, AXES, outward)  2.44 us
    ppermute x2, waiting for transfers between devices, per_device(): lax.ppermute(array, AXES, pairs)  2.04 us
  transfers between devices with their start and end apart: 15, of which 6 were waited for; matrix products, arithmetic and copies ran while one was open for 0% of the time, Pallas kernels for 4%

profile of v12, /device:TPU:0, one launch (start us, length us, event | category | flops | bytes accessed | tf_op | source)
XLA Modules:
  0.0 42.3 jit_solution(4503325349153065417)
XLA Ops:
  0.0 1.2 %select_bitcast_fusion = (bf16[384,512]{1,0:T(8,128)(2,1)S(1)}, bf16[384,512]{1,0:T(8,128)(2,1)S(1)}) fusion(bf16[1,384,512]{2,1,0:T(8,128)(2,1)} %param.4, bf16[1,384,512]{2,1,0:T(8,128)(2,1)} %param.3, pred[]{:T(512)S(6)} %eq.4), kind=kLoop, calls=%fused_computation | loop fusion | flops 393216 | bytes 1572865 | tf_op jit(solution)/shard_map/jit(_where)/select_n | solution.py:527
  1.2 0.5 %shard_map.38 = f32[1040,128]{1,0:T(8,128)S(1)} custom-call(bf16[384,512]{1,0:T(8,128)(2,1)S(1)} %get-tuple-element.27.x_ref), custom_call_target="tpu_custom_call" | custom-call | tf_op jit(solution)/shard_map/pallas_call | solution.py:375
  1.6 0.5 %collective-permute-start = (f32[1040,128]{1,0:T(8,128)S(1)}, f32[1040,128]{1,0:T(8,128)S(1)}, u32[]{:S(2)}, u32[]{:S(2)}) collective-permute-start(f32[1040,128]{1,0:T(8,128)S(1)} %shard_map.38), channel_id=1, source_target_pairs={{0,1},{1,0},{2,3},{3,2},{4,5},{5,4},{6,7},{7,6},{8,9},{9,8},{10,11... | collective-permute-start | bytes 1597448 | tf_op jit(solution)/shard_map/ppermute | solution.py:513
  2.2 0.0 copy-start
  2.2 0.5 %shard_map.37.kept_ref = f32[1040,128]{1,0:T(8,128)S(1)} custom-call(bf16[384,512]{1,0:T(8,128)(2,1)S(1)} %get-tuple-element.28.x_ref), custom_call_target="tpu_custom_call" | custom-call | tf_op jit(solution)/shard_map/pallas_call | solution.py:375
  2.6 1.1 %collective-permute-done.other_ref = f32[1040,128]{1,0:T(8,128)S(1)} collective-permute-done((f32[1040,128]{1,0:T(8,128)S(1)}, f32[1040,128]{1,0:T(8,128)S(1)}, u32[]{:S(2)}, u32[]{:S(2)}) %collective-permute-start) | collective-permute-done | bytes 532512 | tf_op jit(solution)/shard_map/ppermute | solution.py:513
  3.7 0.0 copy-done
  3.7 0.1 shard_map.39
  3.8 2.7 %collective-permute-start.1 = (f32[1040,128]{1,0:T(8,128)S(1)}, f32[1040,128]{1,0:T(8,128)S(1)}, u32[]{:S(2)}, u32[]{:S(2)}) collective-permute-start(f32[1040,128]{1,0:T(8,128)S(1)} %get-tuple-element.16), channel_id=1, source_target_pairs={{0,5},{1,0},{2,3},{3,6},{4,1},{5,4},{6,7},{7,2},{8,9},{9,12},{10,1... | collective-permute-start | bytes 1597448 | tf_op jit(solution)/shard_map/ppermute | solution.py:538
  6.6 0.0 collective-permute-start.2
  6.6 1.5 %collective-permute-start.3 = (f32[1040,128]{1,0:T(8,128)S(1)}, f32[1040,128]{1,0:T(8,128)S(1)}, u32[]{:S(2)}, u32[]{:S(2)}) collective-permute-start(f32[1040,128]{1,0:T(8,128)S(1)} %get-tuple-element.16), channel_id=1, source_target_pairs={{0,3},{1,8},{2,11},{3,0},{4,7},{5,1},{6,2},{7,4},{8,12},{9,10},{10... | collective-permute-start | bytes 1597448 | tf_op jit(solution)/shard_map/ppermute | solution.py:540
  8.0 0.5 %collective-permute-start.4 = (f32[1040,128]{1,0:T(8,128)S(1)}, f32[1040,128]{1,0:T(8,128)S(1)}, u32[]{:S(2)}, u32[]{:S(2)}) collective-permute-start(f32[1040,128]{1,0:T(8,128)S(1)} %get-tuple-element.17), channel_id=1, source_target_pairs={{0,1},{1,0},{2,3},{3,2},{4,5},{5,4},{6,7},{7,6},{8,9},{9,8},{10,11... | collective-permute-start | bytes 1597448 | tf_op jit(solution)/shard_map/ppermute | solution.py:513
  8.5 0.0 collective-permute-start.5
  8.5 1.9 %collective-permute-done.5.refs_5_.refs_1_ = f32[128,512]{1,0:T(8,128)S(1)} collective-permute-done((f32[128,512]{1,0:T(8,128)S(1)}, f32[128,512]{1,0:T(8,128)S(1)}, u32[]{:S(2)}, u32[]{:S(2)}) %collective-permute-start.5) | collective-permute-done | bytes 262176 | tf_op jit(solution)/shard_map/ppermute | solution.py:513
  10.4 7.3 %collective-permute-done.1.refs_0_ = f32[1040,128]{1,0:T(8,128)S(1)} collective-permute-done((f32[1040,128]{1,0:T(8,128)S(1)}, f32[1040,128]{1,0:T(8,128)S(1)}, u32[]{:S(2)}, u32[]{:S(2)}) %collective-permute-start.1) | collective-permute-done | bytes 532512 | tf_op jit(solution)/shard_map/ppermute | solution.py:538
  17.8 0.0 collective-permute-done.2.refs_1_
  17.8 0.0 collective-permute-done.3.refs_2_
  17.8 0.0 collective-permute-done.4.refs_3_
  17.8 4.8 %shard_map.40 = (f32[512,128]{1,0:T(8,128)S(1)}, f32[528,128]{1,0:T(8,128)S(1)}, f32[1040,128]{1,0:T(8,128)S(1)}, f32[1024,128]{1,0:T(8,128)S(1)}) custom-call(f32[1040,128]{1,0:T(8,128)S(1)} %collective-permute-done.1.refs_0_, f32[1040,128]{1,0:T(8,128)S(1)} %collective-permute-done.2.refs_1_, f32[1040,128]{1,0:T(8,128)S(1)} %collective-permute-done.3.refs_2_, ...), custom_call_target="tpu_custom_call" | custom-call | tf_op jit(solution)/shard_map/pallas_call | solution.py:375
  22.6 1.9 %collective-permute-start.8 = (f32[528,128]{1,0:T(8,128)S(1)}, f32[528,128]{1,0:T(8,128)S(1)}, u32[]{:S(2)}, u32[]{:S(2)}) collective-permute-start(f32[528,128]{1,0:T(8,128)S(1)} %get-tuple-element.19.refs_0_), channel_id=1, source_target_pairs={{0,1},{1,0},{2,3},{3,2},{4,5},{5,7},{6,10},{7,6},{8,4},{9,8},{10,1... | collective-permute-start | bytes 811016 | tf_op jit(solution)/shard_map/ppermute | solution.py:558
  24.4 2.4 %collective-permute-start.10 = (f32[1040,128]{1,0:T(8,128)S(1)}, f32[1040,128]{1,0:T(8,128)S(1)}, u32[]{:S(2)}, u32[]{:S(2)}) collective-permute-start(f32[1040,128]{1,0:T(8,128)S(1)} %get-tuple-element.20), channel_id=1, source_target_pairs={{0,4},{1,0},{2,3},{3,7},{4,5},{5,1},{6,2},{7,6},{8,12},{9,8},{10,1... | collective-permute-start | bytes 1597448 | tf_op jit(solution)/shard_map/ppermute | solution.py:557
  26.9 0.0 collective-permute-start.6
  26.9 0.0 collective-permute-done.8.refs_1_
  26.9 0.5 %collective-permute-start.9 = (f32[528,128]{1,0:T(8,128)S(1)}, f32[528,128]{1,0:T(8,128)S(1)}, u32[]{:S(2)}, u32[]{:S(2)}) collective-permute-start(f32[528,128]{1,0:T(8,128)S(1)} %collective-permute-done.8.refs_1_), channel_id=1, source_target_pairs={{0,1},{1,5},{2,6},{3,2},{4,0},{5,4},{6,7},{7,3},{8,9},{9,13},{10,1... | collective-permute-start | bytes 811016 | tf_op jit(solution)/shard_map/ppermute | solution.py:559
  27.4 2.6 %collective-permute-start.13 = (f32[1024,128]{1,0:T(8,128)S(1)}, f32[1024,128]{1,0:T(8,128)S(1)}, u32[]{:S(2)}, u32[]{:S(2)}) collective-permute-start(f32[1024,128]{1,0:T(8,128)S(1)} %get-tuple-element.23.refs_2_), channel_id=1, source_target_pairs={{0,1},{1,0},{2,3},{3,2},{4,5},{5,4},{6,7},{7,6},{8,9},{9,8},{10,11... | collective-permute-start | bytes 1572872 | tf_op jit(solution)/shard_map/ppermute | solution.py:513
  30.0 0.0 collective-permute-done.6.refs_1_
  30.0 0.0 collective-permute-start.7
  30.0 6.8 %collective-permute-done.10.refs_3_.refs_4_ = f32[1040,128]{1,0:T(8,128)S(1)} collective-permute-done((f32[1040,128]{1,0:T(8,128)S(1)}, f32[1040,128]{1,0:T(8,128)S(1)}, u32[]{:S(2)}, u32[]{:S(2)}) %collective-permute-start.10) | collective-permute-done | bytes 532512 | tf_op jit(solution)/shard_map/ppermute | solution.py:557
  36.9 0.0 collective-permute-done.9.refs_2_.refs_6_
  36.9 0.1 collective-permute-start.12
  37.0 0.5 %collective-permute-start.14 = (f32[528,128]{1,0:T(8,128)S(1)}, f32[528,128]{1,0:T(8,128)S(1)}, u32[]{:S(2)}, u32[]{:S(2)}) collective-permute-start(f32[528,128]{1,0:T(8,128)S(1)} %collective-permute-done.9.refs_2_.refs_6_), channel_id=1, source_target_pairs={{0,1},{1,0},{2,3},{3,2},{4,5},{5,4},{6,7},{7,6},{8,9},{9,8},{10,11... | collective-permute-start | bytes 811016 | tf_op jit(solution)/shard_map/ppermute | solution.py:513
  37.5 2.0 %collective-permute-done.7.refs_2_.refs_5_ = f32[512,128]{1,0:T(8,128)S(1)} collective-permute-done((f32[512,128]{1,0:T(8,128)S(1)}, f32[512,128]{1,0:T(8,128)S(1)}, u32[]{:S(2)}, u32[]{:S(2)}) %collective-permute-start.7) | collective-permute-done | bytes 262176 | tf_op jit(solution)/shard_map/ppermute | solution.py:559
  39.5 0.1 collective-permute-start.11
  39.6 0.0 collective-permute-done.13.refs_3_
  39.6 0.0 collective-permute-done.12.other_b
  39.6 0.0 collective-permute-done.14.refs_7_
  39.6 1.2 %shard_map.43 = (f32[128,512]{1,0:T(8,128)S(1)}, bf16[512,512]{1,0:T(8,128)(2,1)S(1)}, bf16[512,512]{1,0:T(8,128)(2,1)S(1)}) custom-call(f32[512,128]{1,0:T(8,128)S(1)} %shard_map.41.own_a, f32[528,128]{1,0:T(8,128)S(1)} %shard_map.42.own_b, f32[528,128]{1,0:T(8,128)S(1)} %collective-permute-done.12.other_b, f32[128,512]{1,0:T(8,128)S(1)} %bitcast.9, ...), custom_call_target="tpu_custom_call" | custom-call | tf_op jit(solution)/shard_map/pallas_call | solution.py:375
  40.9 0.3 collective-permute-done.11.other_a
  41.1 1.2 %shard_map.44 = f32[128,512]{1,0:T(8,128)} custom-call(f32[512,128]{1,0:T(8,128)S(1)} %collective-permute-done.11.other_a, f32[528,128]{1,0:T(8,128)S(1)} %collective-permute-done.12.other_b, f32[128,512]{1,0:T(8,128)S(1)} %get-tuple-element.24.first_left, bf16[512,512]{1,0:T(8,128)(2,1)S(1)} %get-tuple-element.25.high_ref, ...), custom_call_target="tpu_custom_call" | custom-call | tf_op jit(solution)/shard_map/pallas_call | solution.py:375
  (2 shorter events, 0.0 us)
Async XLA Ops:
  1.6 2.1 %collective-permute-start = (f32[1040,128]{1,0:T(8,128)S(1)}, f32[1040,128]{1,0:T(8,128)S(1)}, u32[]{:S(2)}, u32[]{:S(2)}) collective-permute-start(f32[1040,128]{1,0:T(8,128)S(1)} %shard_map.38), channel_id=1, source_target_pairs={{0,1},{1,0},{2,3},{3,2},{4,5},{5,4},{6,7},{7,6},{8,9},{9,8},{10,11... | collective-permute-start | bytes 1597448 | tf_op jit(solution)/shard_map/ppermute | solution.py:513
  2.2 1.6 %copy-start = (f32[1,128,512]{2,1,0:T(8,128)S(1)}, f32[1,128,512]{2,1,0:T(8,128)}, u32[]{:S(2)}) copy-start(f32[1,128,512]{2,1,0:T(8,128)} %param.5) | copy-start | bytes 786436
  3.8 13.9 %collective-permute-start.1 = (f32[1040,128]{1,0:T(8,128)S(1)}, f32[1040,128]{1,0:T(8,128)S(1)}, u32[]{:S(2)}, u32[]{:S(2)}) collective-permute-start(f32[1040,128]{1,0:T(8,128)S(1)} %get-tuple-element.16), channel_id=1, source_target_pairs={{0,5},{1,0},{2,3},{3,6},{4,1},{5,4},{6,7},{7,2},{8,9},{9,12},{10,1... | collective-permute-start | bytes 1597448 | tf_op jit(solution)/shard_map/ppermute | solution.py:538
  6.6 11.2 %collective-permute-start.2 = (f32[1040,128]{1,0:T(8,128)S(1)}, f32[1040,128]{1,0:T(8,128)S(1)}, u32[]{:S(2)}, u32[]{:S(2)}) collective-permute-start(f32[1040,128]{1,0:T(8,128)S(1)} %get-tuple-element.17), channel_id=1, source_target_pairs={{0,1},{1,0},{2,3},{3,2},{4,20},{5,8},{6,11},{7,23},{8,5},{9,25},{1... | collective-permute-start | bytes 1597448 | tf_op jit(solution)/shard_map/ppermute | solution.py:539
  6.6 11.2 %collective-permute-start.3 = (f32[1040,128]{1,0:T(8,128)S(1)}, f32[1040,128]{1,0:T(8,128)S(1)}, u32[]{:S(2)}, u32[]{:S(2)}) collective-permute-start(f32[1040,128]{1,0:T(8,128)S(1)} %get-tuple-element.16), channel_id=1, source_target_pairs={{0,3},{1,8},{2,11},{3,0},{4,7},{5,1},{6,2},{7,4},{8,12},{9,10},{10... | collective-permute-start | bytes 1597448 | tf_op jit(solution)/shard_map/ppermute | solution.py:540
  8.0 9.7 %collective-permute-start.4 = (f32[1040,128]{1,0:T(8,128)S(1)}, f32[1040,128]{1,0:T(8,128)S(1)}, u32[]{:S(2)}, u32[]{:S(2)}) collective-permute-start(f32[1040,128]{1,0:T(8,128)S(1)} %get-tuple-element.17), channel_id=1, source_target_pairs={{0,1},{1,0},{2,3},{3,2},{4,5},{5,4},{6,7},{7,6},{8,9},{9,8},{10,11... | collective-permute-start | bytes 1597448 | tf_op jit(solution)/shard_map/ppermute | solution.py:513
  8.5 1.9 %collective-permute-start.5 = (f32[128,512]{1,0:T(8,128)S(1)}, f32[128,512]{1,0:T(8,128)S(1)}, u32[]{:S(2)}, u32[]{:S(2)}) collective-permute-start(f32[128,512]{1,0:T(8,128)S(1)} %bitcast.7), channel_id=1, source_target_pairs={{0,1},{1,0},{2,3},{3,2},{4,5},{5,4},{6,7},{7,6},{8,9},{9,8},{10,11... | collective-permute-start | bytes 786440 | tf_op jit(solution)/shard_map/ppermute | solution.py:513
  22.6 4.3 %collective-permute-start.8 = (f32[528,128]{1,0:T(8,128)S(1)}, f32[528,128]{1,0:T(8,128)S(1)}, u32[]{:S(2)}, u32[]{:S(2)}) collective-permute-start(f32[528,128]{1,0:T(8,128)S(1)} %get-tuple-element.19.refs_0_), channel_id=1, source_target_pairs={{0,1},{1,0},{2,3},{3,2},{4,5},{5,7},{6,10},{7,6},{8,4},{9,8},{10,1... | collective-permute-start | bytes 811016 | tf_op jit(solution)/shard_map/ppermute | solution.py:558
  24.4 12.4 %collective-permute-start.10 = (f32[1040,128]{1,0:T(8,128)S(1)}, f32[1040,128]{1,0:T(8,128)S(1)}, u32[]{:S(2)}, u32[]{:S(2)}) collective-permute-start(f32[1040,128]{1,0:T(8,128)S(1)} %get-tuple-element.20), channel_id=1, source_target_pairs={{0,4},{1,0},{2,3},{3,7},{4,5},{5,1},{6,2},{7,6},{8,12},{9,8},{10,1... | collective-permute-start | bytes 1597448 | tf_op jit(solution)/shard_map/ppermute | solution.py:557
  26.9 3.1 %collective-permute-start.6 = (f32[512,128]{1,0:T(8,128)S(1)}, f32[512,128]{1,0:T(8,128)S(1)}, u32[]{:S(2)}, u32[]{:S(2)}) collective-permute-start(f32[512,128]{1,0:T(8,128)S(1)} %get-tuple-element.18.refs_0_), channel_id=1, source_target_pairs={{0,1},{1,0},{2,3},{3,2},{4,5},{5,7},{6,10},{7,6},{8,4},{9,8},{10,1... | collective-permute-start | bytes 786440 | tf_op jit(solution)/shard_map/ppermute | solution.py:556
  26.9 10.0 %collective-permute-start.9 = (f32[528,128]{1,0:T(8,128)S(1)}, f32[528,128]{1,0:T(8,128)S(1)}, u32[]{:S(2)}, u32[]{:S(2)}) collective-permute-start(f32[528,128]{1,0:T(8,128)S(1)} %collective-permute-done.8.refs_1_), channel_id=1, source_target_pairs={{0,1},{1,5},{2,6},{3,2},{4,0},{5,4},{6,7},{7,3},{8,9},{9,13},{10,1... | collective-permute-start | bytes 811016 | tf_op jit(solution)/shard_map/ppermute | solution.py:559
  27.4 12.2 %collective-permute-start.13 = (f32[1024,128]{1,0:T(8,128)S(1)}, f32[1024,128]{1,0:T(8,128)S(1)}, u32[]{:S(2)}, u32[]{:S(2)}) collective-permute-start(f32[1024,128]{1,0:T(8,128)S(1)} %get-tuple-element.23.refs_2_), channel_id=1, source_target_pairs={{0,1},{1,0},{2,3},{3,2},{4,5},{5,4},{6,7},{7,6},{8,9},{9,8},{10,11... | collective-permute-start | bytes 1572872 | tf_op jit(solution)/shard_map/ppermute | solution.py:513
  30.0 9.5 %collective-permute-start.7 = (f32[512,128]{1,0:T(8,128)S(1)}, f32[512,128]{1,0:T(8,128)S(1)}, u32[]{:S(2)}, u32[]{:S(2)}) collective-permute-start(f32[512,128]{1,0:T(8,128)S(1)} %collective-permute-done.6.refs_1_), channel_id=1, source_target_pairs={{0,1},{1,5},{2,6},{3,2},{4,0},{5,4},{6,7},{7,3},{8,9},{9,13},{10,1... | collective-permute-start | bytes 786440 | tf_op jit(solution)/shard_map/ppermute | solution.py:559
  36.9 2.7 %collective-permute-start.12 = (f32[528,128]{1,0:T(8,128)S(1)}, f32[528,128]{1,0:T(8,128)S(1)}, u32[]{:S(2)}, u32[]{:S(2)}) collective-permute-start(f32[528,128]{1,0:T(8,128)S(1)} %shard_map.42.own_b), channel_id=1, source_target_pairs={{0,1},{1,0},{2,3},{3,2},{4,5},{5,4},{6,7},{7,6},{8,9},{9,8},{10,11... | collective-permute-start | bytes 811016 | tf_op jit(solution)/shard_map/ppermute | solution.py:513
  37.0 2.7 %collective-permute-start.14 = (f32[528,128]{1,0:T(8,128)S(1)}, f32[528,128]{1,0:T(8,128)S(1)}, u32[]{:S(2)}, u32[]{:S(2)}) collective-permute-start(f32[528,128]{1,0:T(8,128)S(1)} %collective-permute-done.9.refs_2_.refs_6_), channel_id=1, source_target_pairs={{0,1},{1,0},{2,3},{3,2},{4,5},{5,4},{6,7},{7,6},{8,9},{9,8},{10,11... | collective-permute-start | bytes 811016 | tf_op jit(solution)/shard_map/ppermute | solution.py:513
  39.5 1.6 %collective-permute-start.11 = (f32[512,128]{1,0:T(8,128)S(1)}, f32[512,128]{1,0:T(8,128)S(1)}, u32[]{:S(2)}, u32[]{:S(2)}) collective-permute-start(f32[512,128]{1,0:T(8,128)S(1)} %shard_map.41.own_a), channel_id=1, source_target_pairs={{0,1},{1,0},{2,3},{3,2},{4,5},{5,4},{6,7},{7,6},{8,9},{9,8},{10,11... | collective-permute-start | bytes 786440 | tf_op jit(solution)/shard_map/ppermute | solution.py:513

commit v13 on v12

--- a/solution.py
+++ b/solution.py
@@ -477,7 +477,11 @@
                     abreast = self.index(left, x + turn, 1)
                     hops[turn - 1].append((left_root, abreast))
                     relays[turn - 1].append((abreast, self.index(left ^ 1, x + turn, 1)))
-        return [self.chains(pairs) for pairs in hops], self.loops(direct), [self.loops(pairs) for pairs in relays]
+        return (
+            [(self.swaps(pairs), self.chains(pairs)) for pairs in hops],
+            self.loops(direct),
+            [self.loops(pairs) for pairs in relays],
+        )
 
     def turn(self):
         z, x, core = (lax.axis_index(name) for name in AXES[1:])
@@ -553,9 +557,9 @@
     )
 
     hops, outward, relays = plan.spread()
-    hopped = [[lax.ppermute(inverse[0], AXES, pairs) for pairs in hops]]
+    hopped = [[lax.ppermute(inverse[0], AXES, pairs) for pairs, _ in hops]]
     direct = lax.ppermute(direct, AXES, outward)
-    hopped.append([lax.ppermute(inverse[1], AXES, pairs) for pairs in hops])
+    hopped.append([lax.ppermute(inverse[1], AXES, pairs) for _, pairs in hops])
     relayed = [[lax.ppermute(array, AXES, pairs) for array, pairs in zip(arrays, relays)] for arrays in hopped]
     relayed[1], direct = lax.optimization_barrier((relayed[1], direct))
     arrived = [

time: 42.5 us -> 42.5 us (level)
  no operation moved by 1% of the time
where the time goes in v13:
time: 42.5 us; the launch traced here: 42.3 us
  waiting for transfers between devices  19.5 us (46%)
  starting transfers between devices  13.3 us (31%)
  Pallas kernels  8.26 us (19%)
  other arithmetic  1.17 us (3%)
    pallas_call x8, Pallas kernels, call(): pl.pallas_call(kernel, out_shape=[jax.ShapeDtypeStruct(shape[:2], *(shape...  8.26 us
    ppermute x1, waiting for transfers between devices, per_device(): lax.ppermute(outer, AXES, outward)  7.32 us
    ppermute x1, waiting for transfers between devices, per_device(): direct = lax.ppermute(direct, AXES, outward)  6.85 us
    ppermute x7, starting transfers between devices, swap_cores(): return lax.ppermute(array, 'grad', [(0, 1), (1, 0)])  4.28 us
    ppermute x7, waiting for transfers between devices, swap_cores(): return lax.ppermute(array, 'grad', [(0, 1), (1, 0)])  3.26 us
    ppermute x1, starting transfers between devices, per_device(): lax.ppermute(outer, AXES, outward)  2.74 us
    ppermute x1, starting transfers between devices, per_device(): direct = lax.ppermute(direct, AXES, outward)  2.44 us
    ppermute x2, waiting for transfers between devices, per_device(): lax.ppermute(array, AXES, pairs)  2.04 us
  transfers between devices with their start and end apart: 15, of which 6 were waited for; matrix products, arithmetic and copies ran while one was open for 0% of the time, Pallas kernels for 4%

profile of v13, /device:TPU:0, one launch (start us, length us, event | category | flops | bytes accessed | tf_op | source)
XLA Modules:
  0.0 42.3 jit_solution(2534059254909143823)
XLA Ops:
  0.0 1.2 %select_bitcast_fusion = (bf16[384,512]{1,0:T(8,128)(2,1)S(1)}, bf16[384,512]{1,0:T(8,128)(2,1)S(1)}) fusion(bf16[1,384,512]{2,1,0:T(8,128)(2,1)} %param.4, bf16[1,384,512]{2,1,0:T(8,128)(2,1)} %param.3, pred[]{:T(512)S(6)} %eq.4), kind=kLoop, calls=%fused_computation | loop fusion | flops 393216 | bytes 1572865 | tf_op jit(solution)/shard_map/jit(_where)/select_n | solution.py:531
  1.2 0.5 %shard_map.38 = f32[1040,128]{1,0:T(8,128)S(1)} custom-call(bf16[384,512]{1,0:T(8,128)(2,1)S(1)} %get-tuple-element.27.x_ref), custom_call_target="tpu_custom_call" | custom-call | tf_op jit(solution)/shard_map/pallas_call | solution.py:375
  1.6 0.5 %collective-permute-start = (f32[1040,128]{1,0:T(8,128)S(1)}, f32[1040,128]{1,0:T(8,128)S(1)}, u32[]{:S(2)}, u32[]{:S(2)}) collective-permute-start(f32[1040,128]{1,0:T(8,128)S(1)} %shard_map.38), channel_id=1, source_target_pairs={{0,1},{1,0},{2,3},{3,2},{4,5},{5,4},{6,7},{7,6},{8,9},{9,8},{10,11... | collective-permute-start | bytes 1597448 | tf_op jit(solution)/shard_map/ppermute | solution.py:517
  2.2 0.0 copy-start
  2.2 0.5 %shard_map.37.kept_ref = f32[1040,128]{1,0:T(8,128)S(1)} custom-call(bf16[384,512]{1,0:T(8,128)(2,1)S(1)} %get-tuple-element.28.x_ref), custom_call_target="tpu_custom_call" | custom-call | tf_op jit(solution)/shard_map/pallas_call | solution.py:375
  2.6 1.1 %collective-permute-done.other_ref = f32[1040,128]{1,0:T(8,128)S(1)} collective-permute-done((f32[1040,128]{1,0:T(8,128)S(1)}, f32[1040,128]{1,0:T(8,128)S(1)}, u32[]{:S(2)}, u32[]{:S(2)}) %collective-permute-start) | collective-permute-done | bytes 532512 | tf_op jit(solution)/shard_map/ppermute | solution.py:517
  3.7 0.0 copy-done
  3.7 0.1 shard_map.39
  3.8 2.7 %collective-permute-start.1 = (f32[1040,128]{1,0:T(8,128)S(1)}, f32[1040,128]{1,0:T(8,128)S(1)}, u32[]{:S(2)}, u32[]{:S(2)}) collective-permute-start(f32[1040,128]{1,0:T(8,128)S(1)} %get-tuple-element.16), channel_id=1, source_target_pairs={{0,5},{1,0},{2,3},{3,6},{4,1},{5,4},{6,7},{7,2},{8,9},{9,12},{10,1... | collective-permute-start | bytes 1597448 | tf_op jit(solution)/shard_map/ppermute | solution.py:542
  6.6 0.0 collective-permute-start.2
  6.6 1.5 %collective-permute-start.3 = (f32[1040,128]{1,0:T(8,128)S(1)}, f32[1040,128]{1,0:T(8,128)S(1)}, u32[]{:S(2)}, u32[]{:S(2)}) collective-permute-start(f32[1040,128]{1,0:T(8,128)S(1)} %get-tuple-element.16), channel_id=1, source_target_pairs={{0,3},{1,8},{2,11},{3,0},{4,7},{5,1},{6,2},{7,4},{8,12},{9,10},{10... | collective-permute-start | bytes 1597448 | tf_op jit(solution)/shard_map/ppermute | solution.py:544
  8.0 0.5 %collective-permute-start.4 = (f32[1040,128]{1,0:T(8,128)S(1)}, f32[1040,128]{1,0:T(8,128)S(1)}, u32[]{:S(2)}, u32[]{:S(2)}) collective-permute-start(f32[1040,128]{1,0:T(8,128)S(1)} %get-tuple-element.17), channel_id=1, source_target_pairs={{0,1},{1,0},{2,3},{3,2},{4,5},{5,4},{6,7},{7,6},{8,9},{9,8},{10,11... | collective-permute-start | bytes 1597448 | tf_op jit(solution)/shard_map/ppermute | solution.py:517
  8.5 0.0 collective-permute-start.5
  8.5 1.9 %collective-permute-done.5.refs_5_.refs_1_ = f32[128,512]{1,0:T(8,128)S(1)} collective-permute-done((f32[128,512]{1,0:T(8,128)S(1)}, f32[128,512]{1,0:T(8,128)S(1)}, u32[]{:S(2)}, u32[]{:S(2)}) %collective-permute-start.5) | collective-permute-done | bytes 262176 | tf_op jit(solution)/shard_map/ppermute | solution.py:517
  10.4 7.3 %collective-permute-done.1.refs_0_ = f32[1040,128]{1,0:T(8,128)S(1)} collective-permute-done((f32[1040,128]{1,0:T(8,128)S(1)}, f32[1040,128]{1,0:T(8,128)S(1)}, u32[]{:S(2)}, u32[]{:S(2)}) %collective-permute-start.1) | collective-permute-done | bytes 532512 | tf_op jit(solution)/shard_map/ppermute | solution.py:542
  17.8 0.0 collective-permute-done.2.refs_1_
  17.8 0.0 collective-permute-done.3.refs_2_
  17.8 0.0 collective-permute-done.4.refs_3_
  17.8 4.8 %shard_map.40 = (f32[512,128]{1,0:T(8,128)S(1)}, f32[528,128]{1,0:T(8,128)S(1)}, f32[1040,128]{1,0:T(8,128)S(1)}, f32[1024,128]{1,0:T(8,128)S(1)}) custom-call(f32[1040,128]{1,0:T(8,128)S(1)} %collective-permute-done.1.refs_0_, f32[1040,128]{1,0:T(8,128)S(1)} %collective-permute-done.2.refs_1_, f32[1040,128]{1,0:T(8,128)S(1)} %collective-permute-done.3.refs_2_, ...), custom_call_target="tpu_custom_call" | custom-call | tf_op jit(solution)/shard_map/pallas_call | solution.py:375
  22.6 1.9 %collective-permute-start.8 = (f32[528,128]{1,0:T(8,128)S(1)}, f32[528,128]{1,0:T(8,128)S(1)}, u32[]{:S(2)}, u32[]{:S(2)}) collective-permute-start(f32[528,128]{1,0:T(8,128)S(1)} %get-tuple-element.19.refs_0_), channel_id=1, source_target_pairs={{0,1},{1,0},{2,3},{3,2},{4,5},{5,7},{6,10},{7,6},{8,4},{9,8},{10,1... | collective-permute-start | bytes 811016 | tf_op jit(solution)/shard_map/ppermute | solution.py:562
  24.4 2.4 %collective-permute-start.10 = (f32[1040,128]{1,0:T(8,128)S(1)}, f32[1040,128]{1,0:T(8,128)S(1)}, u32[]{:S(2)}, u32[]{:S(2)}) collective-permute-start(f32[1040,128]{1,0:T(8,128)S(1)} %get-tuple-element.20), channel_id=1, source_target_pairs={{0,4},{1,0},{2,3},{3,7},{4,5},{5,1},{6,2},{7,6},{8,12},{9,8},{10,1... | collective-permute-start | bytes 1597448 | tf_op jit(solution)/shard_map/ppermute | solution.py:561
  26.9 0.0 collective-permute-start.6
  26.9 0.0 collective-permute-done.8.refs_1_
  26.9 0.5 %collective-permute-start.9 = (f32[528,128]{1,0:T(8,128)S(1)}, f32[528,128]{1,0:T(8,128)S(1)}, u32[]{:S(2)}, u32[]{:S(2)}) collective-permute-start(f32[528,128]{1,0:T(8,128)S(1)} %collective-permute-done.8.refs_1_), channel_id=1, source_target_pairs={{0,1},{1,5},{2,6},{3,2},{4,0},{5,4},{6,7},{7,3},{8,9},{9,13},{10,1... | collective-permute-start | bytes 811016 | tf_op jit(solution)/shard_map/ppermute | solution.py:563
  27.4 2.6 %collective-permute-start.13 = (f32[1024,128]{1,0:T(8,128)S(1)}, f32[1024,128]{1,0:T(8,128)S(1)}, u32[]{:S(2)}, u32[]{:S(2)}) collective-permute-start(f32[1024,128]{1,0:T(8,128)S(1)} %get-tuple-element.23.refs_2_), channel_id=1, source_target_pairs={{0,1},{1,0},{2,3},{3,2},{4,5},{5,4},{6,7},{7,6},{8,9},{9,8},{10,11... | collective-permute-start | bytes 1572872 | tf_op jit(solution)/shard_map/ppermute | solution.py:517
  30.0 0.0 collective-permute-done.6.refs_1_
  30.0 0.0 collective-permute-start.7
  30.0 6.8 %collective-permute-done.10.refs_3_.refs_4_ = f32[1040,128]{1,0:T(8,128)S(1)} collective-permute-done((f32[1040,128]{1,0:T(8,128)S(1)}, f32[1040,128]{1,0:T(8,128)S(1)}, u32[]{:S(2)}, u32[]{:S(2)}) %collective-permute-start.10) | collective-permute-done | bytes 532512 | tf_op jit(solution)/shard_map/ppermute | solution.py:561
  36.9 0.0 collective-permute-done.9.refs_2_.refs_6_
  36.9 0.1 collective-permute-start.12
  37.0 0.5 %collective-permute-start.14 = (f32[528,128]{1,0:T(8,128)S(1)}, f32[528,128]{1,0:T(8,128)S(1)}, u32[]{:S(2)}, u32[]{:S(2)}) collective-permute-start(f32[528,128]{1,0:T(8,128)S(1)} %collective-permute-done.9.refs_2_.refs_6_), channel_id=1, source_target_pairs={{0,1},{1,0},{2,3},{3,2},{4,5},{5,4},{6,7},{7,6},{8,9},{9,8},{10,11... | collective-permute-start | bytes 811016 | tf_op jit(solution)/shard_map/ppermute | solution.py:517
  37.5 2.0 %collective-permute-done.7.refs_2_.refs_5_ = f32[512,128]{1,0:T(8,128)S(1)} collective-permute-done((f32[512,128]{1,0:T(8,128)S(1)}, f32[512,128]{1,0:T(8,128)S(1)}, u32[]{:S(2)}, u32[]{:S(2)}) %collective-permute-start.7) | collective-permute-done | bytes 262176 | tf_op jit(solution)/shard_map/ppermute | solution.py:563
  39.5 0.1 collective-permute-start.11
  39.6 0.0 collective-permute-done.13.refs_3_
  39.6 0.0 collective-permute-done.12.other_b
  39.6 0.0 collective-permute-done.14.refs_7_
  39.6 1.2 %shard_map.43 = (f32[128,512]{1,0:T(8,128)S(1)}, bf16[512,512]{1,0:T(8,128)(2,1)S(1)}, bf16[512,512]{1,0:T(8,128)(2,1)S(1)}) custom-call(f32[512,128]{1,0:T(8,128)S(1)} %shard_map.41.own_a, f32[528,128]{1,0:T(8,128)S(1)} %shard_map.42.own_b, f32[528,128]{1,0:T(8,128)S(1)} %collective-permute-done.12.other_b, f32[128,512]{1,0:T(8,128)S(1)} %bitcast.9, ...), custom_call_target="tpu_custom_call" | custom-call | tf_op jit(solution)/shard_map/pallas_call | solution.py:375
  40.9 0.3 collective-permute-done.11.other_a
  41.1 1.2 %shard_map.44 = f32[128,512]{1,0:T(8,128)} custom-call(f32[512,128]{1,0:T(8,128)S(1)} %collective-permute-done.11.other_a, f32[528,128]{1,0:T(8,128)S(1)} %collective-permute-done.12.other_b, f32[128,512]{1,0:T(8,128)S(1)} %get-tuple-element.24.first_left, bf16[512,512]{1,0:T(8,128)(2,1)S(1)} %get-tuple-element.25.high_ref, ...), custom_call_target="tpu_custom_call" | custom-call | tf_op jit(solution)/shard_map/pallas_call | solution.py:375
  (2 shorter events, 0.0 us)
Async XLA Ops:
  1.6 2.1 %collective-permute-start = (f32[1040,128]{1,0:T(8,128)S(1)}, f32[1040,128]{1,0:T(8,128)S(1)}, u32[]{:S(2)}, u32[]{:S(2)}) collective-permute-start(f32[1040,128]{1,0:T(8,128)S(1)} %shard_map.38), channel_id=1, source_target_pairs={{0,1},{1,0},{2,3},{3,2},{4,5},{5,4},{6,7},{7,6},{8,9},{9,8},{10,11... | collective-permute-start | bytes 1597448 | tf_op jit(solution)/shard_map/ppermute | solution.py:517
  2.2 1.6 %copy-start = (f32[1,128,512]{2,1,0:T(8,128)S(1)}, f32[1,128,512]{2,1,0:T(8,128)}, u32[]{:S(2)}) copy-start(f32[1,128,512]{2,1,0:T(8,128)} %param.5) | copy-start | bytes 786436
  3.8 13.9 %collective-permute-start.1 = (f32[1040,128]{1,0:T(8,128)S(1)}, f32[1040,128]{1,0:T(8,128)S(1)}, u32[]{:S(2)}, u32[]{:S(2)}) collective-permute-start(f32[1040,128]{1,0:T(8,128)S(1)} %get-tuple-element.16), channel_id=1, source_target_pairs={{0,5},{1,0},{2,3},{3,6},{4,1},{5,4},{6,7},{7,2},{8,9},{9,12},{10,1... | collective-permute-start | bytes 1597448 | tf_op jit(solution)/shard_map/ppermute | solution.py:542
  6.6 11.2 %collective-permute-start.2 = (f32[1040,128]{1,0:T(8,128)S(1)}, f32[1040,128]{1,0:T(8,128)S(1)}, u32[]{:S(2)}, u32[]{:S(2)}) collective-permute-start(f32[1040,128]{1,0:T(8,128)S(1)} %get-tuple-element.17), channel_id=1, source_target_pairs={{0,1},{1,0},{2,3},{3,2},{4,20},{5,8},{6,11},{7,23},{8,5},{9,25},{1... | collective-permute-start | bytes 1597448 | tf_op jit(solution)/shard_map/ppermute | solution.py:543
  6.6 11.2 %collective-permute-start.3 = (f32[1040,128]{1,0:T(8,128)S(1)}, f32[1040,128]{1,0:T(8,128)S(1)}, u32[]{:S(2)}, u32[]{:S(2)}) collective-permute-start(f32[1040,128]{1,0:T(8,128)S(1)} %get-tuple-element.16), channel_id=1, source_target_pairs={{0,3},{1,8},{2,11},{3,0},{4,7},{5,1},{6,2},{7,4},{8,12},{9,10},{10... | collective-permute-start | bytes 1597448 | tf_op jit(solution)/shard_map/ppermute | solution.py:544
  8.0 9.7 %collective-permute-start.4 = (f32[1040,128]{1,0:T(8,128)S(1)}, f32[1040,128]{1,0:T(8,128)S(1)}, u32[]{:S(2)}, u32[]{:S(2)}) collective-permute-start(f32[1040,128]{1,0:T(8,128)S(1)} %get-tuple-element.17), channel_id=1, source_target_pairs={{0,1},{1,0},{2,3},{3,2},{4,5},{5,4},{6,7},{7,6},{8,9},{9,8},{10,11... | collective-permute-start | bytes 1597448 | tf_op jit(solution)/shard_map/ppermute | solution.py:517
  8.5 1.9 %collective-permute-start.5 = (f32[128,512]{1,0:T(8,128)S(1)}, f32[128,512]{1,0:T(8,128)S(1)}, u32[]{:S(2)}, u32[]{:S(2)}) collective-permute-start(f32[128,512]{1,0:T(8,128)S(1)} %bitcast.7), channel_id=1, source_target_pairs={{0,1},{1,0},{2,3},{3,2},{4,5},{5,4},{6,7},{7,6},{8,9},{9,8},{10,11... | collective-permute-start | bytes 786440 | tf_op jit(solution)/shard_map/ppermute | solution.py:517
  22.6 4.3 %collective-permute-start.8 = (f32[528,128]{1,0:T(8,128)S(1)}, f32[528,128]{1,0:T(8,128)S(1)}, u32[]{:S(2)}, u32[]{:S(2)}) collective-permute-start(f32[528,128]{1,0:T(8,128)S(1)} %get-tuple-element.19.refs_0_), channel_id=1, source_target_pairs={{0,1},{1,0},{2,3},{3,2},{4,5},{5,7},{6,10},{7,6},{8,4},{9,8},{10,1... | collective-permute-start | bytes 811016 | tf_op jit(solution)/shard_map/ppermute | solution.py:562
  24.4 12.4 %collective-permute-start.10 = (f32[1040,128]{1,0:T(8,128)S(1)}, f32[1040,128]{1,0:T(8,128)S(1)}, u32[]{:S(2)}, u32[]{:S(2)}) collective-permute-start(f32[1040,128]{1,0:T(8,128)S(1)} %get-tuple-element.20), channel_id=1, source_target_pairs={{0,4},{1,0},{2,3},{3,7},{4,5},{5,1},{6,2},{7,6},{8,12},{9,8},{10,1... | collective-permute-start | bytes 1597448 | tf_op jit(solution)/shard_map/ppermute | solution.py:561
  26.9 3.1 %collective-permute-start.6 = (f32[512,128]{1,0:T(8,128)S(1)}, f32[512,128]{1,0:T(8,128)S(1)}, u32[]{:S(2)}, u32[]{:S(2)}) collective-permute-start(f32[512,128]{1,0:T(8,128)S(1)} %get-tuple-element.18.refs_0_), channel_id=1, source_target_pairs={{0,1},{1,0},{2,3},{3,2},{4,8},{5,7},{6,10},{7,5},{8,4},{9,11},{10,... | collective-permute-start | bytes 786440 | tf_op jit(solution)/shard_map/ppermute | solution.py:560
  26.9 10.0 %collective-permute-start.9 = (f32[528,128]{1,0:T(8,128)S(1)}, f32[528,128]{1,0:T(8,128)S(1)}, u32[]{:S(2)}, u32[]{:S(2)}) collective-permute-start(f32[528,128]{1,0:T(8,128)S(1)} %collective-permute-done.8.refs_1_), channel_id=1, source_target_pairs={{0,1},{1,5},{2,6},{3,2},{4,0},{5,4},{6,7},{7,3},{8,9},{9,13},{10,1... | collective-permute-start | bytes 811016 | tf_op jit(solution)/shard_map/ppermute | solution.py:563
  27.4 12.2 %collective-permute-start.13 = (f32[1024,128]{1,0:T(8,128)S(1)}, f32[1024,128]{1,0:T(8,128)S(1)}, u32[]{:S(2)}, u32[]{:S(2)}) collective-permute-start(f32[1024,128]{1,0:T(8,128)S(1)} %get-tuple-element.23.refs_2_), channel_id=1, source_target_pairs={{0,1},{1,0},{2,3},{3,2},{4,5},{5,4},{6,7},{7,6},{8,9},{9,8},{10,11... | collective-permute-start | bytes 1572872 | tf_op jit(solution)/shard_map/ppermute | solution.py:517
  30.0 9.5 %collective-permute-start.7 = (f32[512,128]{1,0:T(8,128)S(1)}, f32[512,128]{1,0:T(8,128)S(1)}, u32[]{:S(2)}, u32[]{:S(2)}) collective-permute-start(f32[512,128]{1,0:T(8,128)S(1)} %collective-permute-done.6.refs_1_), channel_id=1, source_target_pairs={{0,1},{1,5},{2,6},{3,2},{4,0},{5,4},{6,7},{7,3},{8,9},{9,13},{10,1... | collective-permute-start | bytes 786440 | tf_op jit(solution)/shard_map/ppermute | solution.py:563
  36.9 2.7 %collective-permute-start.12 = (f32[528,128]{1,0:T(8,128)S(1)}, f32[528,128]{1,0:T(8,128)S(1)}, u32[]{:S(2)}, u32[]{:S(2)}) collective-permute-start(f32[528,128]{1,0:T(8,128)S(1)} %shard_map.42.own_b), channel_id=1, source_target_pairs={{0,1},{1,0},{2,3},{3,2},{4,5},{5,4},{6,7},{7,6},{8,9},{9,8},{10,11... | collective-permute-start | bytes 811016 | tf_op jit(solution)/shard_map/ppermute | solution.py:517
  37.0 2.7 %collective-permute-start.14 = (f32[528,128]{1,0:T(8,128)S(1)}, f32[528,128]{1,0:T(8,128)S(1)}, u32[]{:S(2)}, u32[]{:S(2)}) collective-permute-start(f32[528,128]{1,0:T(8,128)S(1)} %collective-permute-done.9.refs_2_.refs_6_), channel_id=1, source_target_pairs={{0,1},{1,0},{2,3},{3,2},{4,5},{5,4},{6,7},{7,6},{8,9},{9,8},{10,11... | collective-permute-start | bytes 811016 | tf_op jit(solution)/shard_map/ppermute | solution.py:517
  39.5 1.6 %collective-permute-start.11 = (f32[512,128]{1,0:T(8,128)S(1)}, f32[512,128]{1,0:T(8,128)S(1)}, u32[]{:S(2)}, u32[]{:S(2)}) collective-permute-start(f32[512,128]{1,0:T(8,128)S(1)} %shard_map.41.own_a), channel_id=1, source_target_pairs={{0,1},{1,0},{2,3},{3,2},{4,5},{5,4},{6,7},{7,6},{8,9},{9,8},{10,11... | collective-permute-start | bytes 786440 | tf_op jit(solution)/shard_map/ppermute | solution.py:517

commit v14 on v11

--- a/solution.py
+++ b/solution.py
@@ -197,16 +197,18 @@
     cols = lax.broadcasted_iota(jnp.int32, (order, order), 1)
     eye = jnp.where(rows == cols, 1.0, 0.0)
     total = eye - start * factor
-    power_halves = halves(total)
     middle = order // 2
-    for step in range(1, ITERS):
-        power = whole(*upper_square(power_halves))
+    square = whole(*upper_square(halves(total)))
+    power = whole(*upper_square(halves(square)))
+    total = total + 0.5 * (square + whole(*upper_square(halves(total + square))) - power)
+    for step in range(2, ITERS):
         power_halves = halves(power)
         top, corner = upper_times(halves(total), power_halves)
         known = total + power
         top, corner = top + known[:middle], corner + known[middle:, middle:]
         if step < ITERS - 1:
             total = whole(top, corner)
+            power = whole(*upper_square(power_halves))
 
     def block(i, j):
         if i < middle // LANE:

time: 42.5 us -> 42.3 us (level)
  no operation moved by 1% of the time
where the time goes in v14:
time: 42.3 us; the launch traced here: 42.2 us
  waiting for transfers between devices  19.5 us (46%)
  starting transfers between devices  13.3 us (31%)
  Pallas kernels  8.07 us (19%)
  other arithmetic  1.17 us (3%)
    pallas_call x8, Pallas kernels, call(): pl.pallas_call(kernel, out_shape=[jax.ShapeDtypeStruct(shape, jnp.float32...  8.07 us
    ppermute x1, waiting for transfers between devices, per_device(): lax.ppermute(outer, AXES, outward)  7.32 us
    ppermute x1, waiting for transfers between devices, per_device(): direct = lax.ppermute(direct, AXES, outward)  6.85 us
    ppermute x7, starting transfers between devices, swap_cores(): return lax.ppermute(array, 'grad', [(0, 1), (1, 0)])  4.28 us
    ppermute x7, waiting for transfers between devices, swap_cores(): return lax.ppermute(array, 'grad', [(0, 1), (1, 0)])  3.28 us
    ppermute x1, starting transfers between devices, per_device(): lax.ppermute(outer, AXES, outward)  2.74 us
    ppermute x1, starting transfers between devices, per_device(): direct = lax.ppermute(direct, AXES, outward)  2.43 us
    ppermute x2, waiting for transfers between devices, per_device(): lax.ppermute(array, AXES, pairs)  2.05 us
  transfers between devices with their start and end apart: 15, of which 6 were waited for; matrix products, arithmetic and copies ran while one was open for 0% of the time, Pallas kernels for 4%

profile of v14, /device:TPU:0, one launch (start us, length us, event | category | flops | bytes accessed | tf_op | source)
XLA Modules:
  0.0 42.2 jit_solution(9186506372269449824)
XLA Ops:
  0.0 1.2 %select_bitcast_fusion = (bf16[384,512]{1,0:T(8,128)(2,1)S(1)}, bf16[384,512]{1,0:T(8,128)(2,1)S(1)}) fusion(bf16[1,384,512]{2,1,0:T(8,128)(2,1)} %param.4, bf16[1,384,512]{2,1,0:T(8,128)(2,1)} %param.3, pred[]{:T(512)S(6)} %eq.4), kind=kLoop, calls=%fused_computation | loop fusion | flops 393216 | bytes 1572865 | tf_op jit(solution)/shard_map/jit(_where)/select_n | solution.py:509
  1.2 0.5 %shard_map.38 = f32[1040,128]{1,0:T(8,128)S(1)} custom-call(bf16[384,512]{1,0:T(8,128)(2,1)S(1)} %get-tuple-element.25.x_ref), custom_call_target="tpu_custom_call" | custom-call | tf_op jit(solution)/shard_map/pallas_call | solution.py:357
  1.6 0.5 %collective-permute-start = (f32[1040,128]{1,0:T(8,128)S(1)}, f32[1040,128]{1,0:T(8,128)S(1)}, u32[]{:S(2)}, u32[]{:S(2)}) collective-permute-start(f32[1040,128]{1,0:T(8,128)S(1)} %shard_map.38), channel_id=1, source_target_pairs={{0,1},{1,0},{2,3},{3,2},{4,5},{5,4},{6,7},{7,6},{8,9},{9,8},{10,11... | collective-permute-start | bytes 1597448 | tf_op jit(solution)/shard_map/ppermute | solution.py:495
  2.2 0.0 copy-start
  2.2 0.5 %shard_map.37.kept_ref = f32[1040,128]{1,0:T(8,128)S(1)} custom-call(bf16[384,512]{1,0:T(8,128)(2,1)S(1)} %get-tuple-element.26.x_ref), custom_call_target="tpu_custom_call" | custom-call | tf_op jit(solution)/shard_map/pallas_call | solution.py:357
  2.6 1.1 %collective-permute-done.other_ref = f32[1040,128]{1,0:T(8,128)S(1)} collective-permute-done((f32[1040,128]{1,0:T(8,128)S(1)}, f32[1040,128]{1,0:T(8,128)S(1)}, u32[]{:S(2)}, u32[]{:S(2)}) %collective-permute-start) | collective-permute-done | bytes 532512 | tf_op jit(solution)/shard_map/ppermute | solution.py:495
  3.7 0.0 copy-done
  3.7 0.1 shard_map.39
  3.8 2.7 %collective-permute-start.1 = (f32[1040,128]{1,0:T(8,128)S(1)}, f32[1040,128]{1,0:T(8,128)S(1)}, u32[]{:S(2)}, u32[]{:S(2)}) collective-permute-start(f32[1040,128]{1,0:T(8,128)S(1)} %get-tuple-element.15), channel_id=1, source_target_pairs={{0,5},{1,0},{2,3},{3,6},{4,1},{5,4},{6,7},{7,2},{8,9},{9,12},{10,1... | collective-permute-start | bytes 1597448 | tf_op jit(solution)/shard_map/ppermute | solution.py:520
  6.6 0.0 collective-permute-start.2
  6.6 1.5 %collective-permute-start.3 = (f32[1040,128]{1,0:T(8,128)S(1)}, f32[1040,128]{1,0:T(8,128)S(1)}, u32[]{:S(2)}, u32[]{:S(2)}) collective-permute-start(f32[1040,128]{1,0:T(8,128)S(1)} %get-tuple-element.15), channel_id=1, source_target_pairs={{0,3},{1,8},{2,11},{3,0},{4,7},{5,1},{6,2},{7,4},{8,12},{9,10},{10... | collective-permute-start | bytes 1597448 | tf_op jit(solution)/shard_map/ppermute | solution.py:522
  8.0 0.5 %collective-permute-start.4 = (f32[1040,128]{1,0:T(8,128)S(1)}, f32[1040,128]{1,0:T(8,128)S(1)}, u32[]{:S(2)}, u32[]{:S(2)}) collective-permute-start(f32[1040,128]{1,0:T(8,128)S(1)} %get-tuple-element.16), channel_id=1, source_target_pairs={{0,1},{1,0},{2,3},{3,2},{4,5},{5,4},{6,7},{7,6},{8,9},{9,8},{10,11... | collective-permute-start | bytes 1597448 | tf_op jit(solution)/shard_map/ppermute | solution.py:495
  8.5 0.0 collective-permute-start.5
  8.5 1.9 %collective-permute-done.5.refs_5_.refs_1_ = f32[128,512]{1,0:T(8,128)S(1)} collective-permute-done((f32[128,512]{1,0:T(8,128)S(1)}, f32[128,512]{1,0:T(8,128)S(1)}, u32[]{:S(2)}, u32[]{:S(2)}) %collective-permute-start.5) | collective-permute-done | bytes 262176 | tf_op jit(solution)/shard_map/ppermute | solution.py:495
  10.4 7.3 %collective-permute-done.1.refs_0_ = f32[1040,128]{1,0:T(8,128)S(1)} collective-permute-done((f32[1040,128]{1,0:T(8,128)S(1)}, f32[1040,128]{1,0:T(8,128)S(1)}, u32[]{:S(2)}, u32[]{:S(2)}) %collective-permute-start.1) | collective-permute-done | bytes 532512 | tf_op jit(solution)/shard_map/ppermute | solution.py:520
  17.8 0.0 collective-permute-done.2.refs_1_
  17.8 0.0 collective-permute-done.3.refs_2_
  17.8 0.0 collective-permute-done.4.refs_3_
  17.8 4.6 %shard_map.40 = (f32[512,128]{1,0:T(8,128)S(1)}, f32[528,128]{1,0:T(8,128)S(1)}, f32[1040,128]{1,0:T(8,128)S(1)}, f32[1024,128]{1,0:T(8,128)S(1)}) custom-call(f32[1040,128]{1,0:T(8,128)S(1)} %collective-permute-done.1.refs_0_, f32[1040,128]{1,0:T(8,128)S(1)} %collective-permute-done.2.refs_1_, f32[1040,128]{1,0:T(8,128)S(1)} %collective-permute-done.3.refs_2_, ...), custom_call_target="tpu_custom_call" | custom-call | tf_op jit(solution)/shard_map/pallas_call | solution.py:357
  22.4 1.9 %collective-permute-start.8 = (f32[528,128]{1,0:T(8,128)S(1)}, f32[528,128]{1,0:T(8,128)S(1)}, u32[]{:S(2)}, u32[]{:S(2)}) collective-permute-start(f32[528,128]{1,0:T(8,128)S(1)} %get-tuple-element.18.refs_0_), channel_id=1, source_target_pairs={{0,1},{1,0},{2,3},{3,2},{4,5},{5,7},{6,10},{7,6},{8,4},{9,8},{10,1... | collective-permute-start | bytes 811016 | tf_op jit(solution)/shard_map/ppermute | solution.py:540
  24.3 2.4 %collective-permute-start.10 = (f32[1040,128]{1,0:T(8,128)S(1)}, f32[1040,128]{1,0:T(8,128)S(1)}, u32[]{:S(2)}, u32[]{:S(2)}) collective-permute-start(f32[1040,128]{1,0:T(8,128)S(1)} %get-tuple-element.19), channel_id=1, source_target_pairs={{0,4},{1,0},{2,3},{3,7},{4,5},{5,1},{6,2},{7,6},{8,12},{9,8},{10,1... | collective-permute-start | bytes 1597448 | tf_op jit(solution)/shard_map/ppermute | solution.py:539
  26.7 0.0 collective-permute-start.6
  26.7 0.0 collective-permute-done.8.refs_1_
  26.7 0.5 %collective-permute-start.9 = (f32[528,128]{1,0:T(8,128)S(1)}, f32[528,128]{1,0:T(8,128)S(1)}, u32[]{:S(2)}, u32[]{:S(2)}) collective-permute-start(f32[528,128]{1,0:T(8,128)S(1)} %collective-permute-done.8.refs_1_), channel_id=1, source_target_pairs={{0,1},{1,5},{2,6},{3,2},{4,0},{5,4},{6,7},{7,3},{8,9},{9,13},{10,1... | collective-permute-start | bytes 811016 | tf_op jit(solution)/shard_map/ppermute | solution.py:541
  27.2 2.6 %collective-permute-start.13 = (f32[1024,128]{1,0:T(8,128)S(1)}, f32[1024,128]{1,0:T(8,128)S(1)}, u32[]{:S(2)}, u32[]{:S(2)}) collective-permute-start(f32[1024,128]{1,0:T(8,128)S(1)} %get-tuple-element.22.refs_2_), channel_id=1, source_target_pairs={{0,1},{1,0},{2,3},{3,2},{4,5},{5,4},{6,7},{7,6},{8,9},{9,8},{10,11... | collective-permute-start | bytes 1572872 | tf_op jit(solution)/shard_map/ppermute | solution.py:495
  29.8 0.0 collective-permute-done.6.refs_1_
  29.8 0.0 collective-permute-start.7
  29.8 6.8 %collective-permute-done.10.refs_3_.refs_4_ = f32[1040,128]{1,0:T(8,128)S(1)} collective-permute-done((f32[1040,128]{1,0:T(8,128)S(1)}, f32[1040,128]{1,0:T(8,128)S(1)}, u32[]{:S(2)}, u32[]{:S(2)}) %collective-permute-start.10) | collective-permute-done | bytes 532512 | tf_op jit(solution)/shard_map/ppermute | solution.py:539
  36.7 0.0 collective-permute-done.9.refs_2_.refs_6_
  36.7 0.0 collective-permute-start.14
  36.7 0.6 %collective-permute-start.12 = (f32[528,128]{1,0:T(8,128)S(1)}, f32[528,128]{1,0:T(8,128)S(1)}, u32[]{:S(2)}, u32[]{:S(2)}) collective-permute-start(f32[528,128]{1,0:T(8,128)S(1)} %shard_map.42.own_b), channel_id=1, source_target_pairs={{0,1},{1,0},{2,3},{3,2},{4,5},{5,4},{6,7},{7,6},{8,9},{9,8},{10,11... | collective-permute-start | bytes 811016 | tf_op jit(solution)/shard_map/ppermute | solution.py:495
  37.3 2.0 %collective-permute-done.7.refs_2_.refs_5_ = f32[512,128]{1,0:T(8,128)S(1)} collective-permute-done((f32[512,128]{1,0:T(8,128)S(1)}, f32[512,128]{1,0:T(8,128)S(1)}, u32[]{:S(2)}, u32[]{:S(2)}) %collective-permute-start.7) | collective-permute-done | bytes 262176 | tf_op jit(solution)/shard_map/ppermute | solution.py:541
  39.3 0.1 collective-permute-start.11
  39.4 0.0 collective-permute-done.13.refs_3_
  39.4 0.0 collective-permute-done.14.refs_7_
  39.4 1.2 %shard_map.43 = (f32[128,512]{1,0:T(8,128)S(1)}, f32[512,512]{1,0:T(8,128)S(1)}) custom-call(f32[512,128]{1,0:T(8,128)S(1)} %shard_map.41.own_a, f32[528,128]{1,0:T(8,128)S(1)} %shard_map.42.own_b, f32[128,512]{1,0:T(8,128)S(1)} %bitcast.9, f32[128,512]{1,0:T(8,128)S(1)} %collective-permute-done.5.refs_5_.refs_1_, ...), custom_call_target="tpu_custom_call" | custom-call | tf_op jit(solution)/shard_map/pallas_call | solution.py:357
  40.6 0.3 collective-permute-done.11.other_a
  40.9 0.0 collective-permute-done.12.other_b
  40.9 1.2 %shard_map.44 = f32[128,512]{1,0:T(8,128)} custom-call(f32[512,128]{1,0:T(8,128)S(1)} %collective-permute-done.11.other_a, f32[528,128]{1,0:T(8,128)S(1)} %collective-permute-done.12.other_b, f32[128,512]{1,0:T(8,128)S(1)} %get-tuple-element.23.first_left, f32[512,512]{1,0:T(8,128)S(1)} %get-tuple-element.24.first_right), custom_call_target="tpu_custom_call" | custom-call | tf_op jit(solution)/shard_map/pallas_call | solution.py:357
  (2 shorter events, 0.0 us)
Async XLA Ops:
  1.6 2.1 %collective-permute-start = (f32[1040,128]{1,0:T(8,128)S(1)}, f32[1040,128]{1,0:T(8,128)S(1)}, u32[]{:S(2)}, u32[]{:S(2)}) collective-permute-start(f32[1040,128]{1,0:T(8,128)S(1)} %shard_map.38), channel_id=1, source_target_pairs={{0,1},{1,0},{2,3},{3,2},{4,5},{5,4},{6,7},{7,6},{8,9},{9,8},{10,11... | collective-permute-start | bytes 1597448 | tf_op jit(solution)/shard_map/ppermute | solution.py:495
  2.2 1.6 %copy-start = (f32[1,128,512]{2,1,0:T(8,128)S(1)}, f32[1,128,512]{2,1,0:T(8,128)}, u32[]{:S(2)}) copy-start(f32[1,128,512]{2,1,0:T(8,128)} %param.5) | copy-start | bytes 786436
  3.8 13.9 %collective-permute-start.1 = (f32[1040,128]{1,0:T(8,128)S(1)}, f32[1040,128]{1,0:T(8,128)S(1)}, u32[]{:S(2)}, u32[]{:S(2)}) collective-permute-start(f32[1040,128]{1,0:T(8,128)S(1)} %get-tuple-element.15), channel_id=1, source_target_pairs={{0,5},{1,0},{2,3},{3,6},{4,1},{5,4},{6,7},{7,2},{8,9},{9,12},{10,1... | collective-permute-start | bytes 1597448 | tf_op jit(solution)/shard_map/ppermute | solution.py:520
  6.6 11.2 %collective-permute-start.2 = (f32[1040,128]{1,0:T(8,128)S(1)}, f32[1040,128]{1,0:T(8,128)S(1)}, u32[]{:S(2)}, u32[]{:S(2)}) collective-permute-start(f32[1040,128]{1,0:T(8,128)S(1)} %get-tuple-element.16), channel_id=1, source_target_pairs={{0,1},{1,0},{2,3},{3,2},{4,20},{5,8},{6,11},{7,23},{8,5},{9,25},{1... | collective-permute-start | bytes 1597448 | tf_op jit(solution)/shard_map/ppermute | solution.py:521
  6.6 11.2 %collective-permute-start.3 = (f32[1040,128]{1,0:T(8,128)S(1)}, f32[1040,128]{1,0:T(8,128)S(1)}, u32[]{:S(2)}, u32[]{:S(2)}) collective-permute-start(f32[1040,128]{1,0:T(8,128)S(1)} %get-tuple-element.15), channel_id=1, source_target_pairs={{0,3},{1,8},{2,11},{3,0},{4,7},{5,1},{6,2},{7,4},{8,12},{9,10},{10... | collective-permute-start | bytes 1597448 | tf_op jit(solution)/shard_map/ppermute | solution.py:522
  8.0 9.7 %collective-permute-start.4 = (f32[1040,128]{1,0:T(8,128)S(1)}, f32[1040,128]{1,0:T(8,128)S(1)}, u32[]{:S(2)}, u32[]{:S(2)}) collective-permute-start(f32[1040,128]{1,0:T(8,128)S(1)} %get-tuple-element.16), channel_id=1, source_target_pairs={{0,1},{1,0},{2,3},{3,2},{4,5},{5,4},{6,7},{7,6},{8,9},{9,8},{10,11... | collective-permute-start | bytes 1597448 | tf_op jit(solution)/shard_map/ppermute | solution.py:495
  8.5 1.9 %collective-permute-start.5 = (f32[128,512]{1,0:T(8,128)S(1)}, f32[128,512]{1,0:T(8,128)S(1)}, u32[]{:S(2)}, u32[]{:S(2)}) collective-permute-start(f32[128,512]{1,0:T(8,128)S(1)} %bitcast.7), channel_id=1, source_target_pairs={{0,1},{1,0},{2,3},{3,2},{4,5},{5,4},{6,7},{7,6},{8,9},{9,8},{10,11... | collective-permute-start | bytes 786440 | tf_op jit(solution)/shard_map/ppermute | solution.py:495
  22.4 4.3 %collective-permute-start.8 = (f32[528,128]{1,0:T(8,128)S(1)}, f32[528,128]{1,0:T(8,128)S(1)}, u32[]{:S(2)}, u32[]{:S(2)}) collective-permute-start(f32[528,128]{1,0:T(8,128)S(1)} %get-tuple-element.18.refs_0_), channel_id=1, source_target_pairs={{0,1},{1,0},{2,3},{3,2},{4,5},{5,7},{6,10},{7,6},{8,4},{9,8},{10,1... | collective-permute-start | bytes 811016 | tf_op jit(solution)/shard_map/ppermute | solution.py:540
  24.3 12.4 %collective-permute-start.10 = (f32[1040,128]{1,0:T(8,128)S(1)}, f32[1040,128]{1,0:T(8,128)S(1)}, u32[]{:S(2)}, u32[]{:S(2)}) collective-permute-start(f32[1040,128]{1,0:T(8,128)S(1)} %get-tuple-element.19), channel_id=1, source_target_pairs={{0,4},{1,0},{2,3},{3,7},{4,5},{5,1},{6,2},{7,6},{8,12},{9,8},{10,1... | collective-permute-start | bytes 1597448 | tf_op jit(solution)/shard_map/ppermute | solution.py:539
  26.7 3.1 %collective-permute-start.6 = (f32[512,128]{1,0:T(8,128)S(1)}, f32[512,128]{1,0:T(8,128)S(1)}, u32[]{:S(2)}, u32[]{:S(2)}) collective-permute-start(f32[512,128]{1,0:T(8,128)S(1)} %get-tuple-element.17.refs_0_), channel_id=1, source_target_pairs={{0,1},{1,0},{2,3},{3,2},{4,5},{5,7},{6,10},{7,6},{8,4},{9,8},{10,1... | collective-permute-start | bytes 786440 | tf_op jit(solution)/shard_map/ppermute | solution.py:538
  26.7 10.0 %collective-permute-start.9 = (f32[528,128]{1,0:T(8,128)S(1)}, f32[528,128]{1,0:T(8,128)S(1)}, u32[]{:S(2)}, u32[]{:S(2)}) collective-permute-start(f32[528,128]{1,0:T(8,128)S(1)} %collective-permute-done.8.refs_1_), channel_id=1, source_target_pairs={{0,1},{1,5},{2,6},{3,2},{4,0},{5,4},{6,7},{7,3},{8,9},{9,13},{10,1... | collective-permute-start | bytes 811016 | tf_op jit(solution)/shard_map/ppermute | solution.py:541
  27.2 12.2 %collective-permute-start.13 = (f32[1024,128]{1,0:T(8,128)S(1)}, f32[1024,128]{1,0:T(8,128)S(1)}, u32[]{:S(2)}, u32[]{:S(2)}) collective-permute-start(f32[1024,128]{1,0:T(8,128)S(1)} %get-tuple-element.22.refs_2_), channel_id=1, source_target_pairs={{0,1},{1,0},{2,3},{3,2},{4,5},{5,4},{6,7},{7,6},{8,9},{9,8},{10,11... | collective-permute-start | bytes 1572872 | tf_op jit(solution)/shard_map/ppermute | solution.py:495
  29.8 9.5 %collective-permute-start.7 = (f32[512,128]{1,0:T(8,128)S(1)}, f32[512,128]{1,0:T(8,128)S(1)}, u32[]{:S(2)}, u32[]{:S(2)}) collective-permute-start(f32[512,128]{1,0:T(8,128)S(1)} %collective-permute-done.6.refs_1_), channel_id=1, source_target_pairs={{0,1},{1,5},{2,6},{3,2},{4,0},{5,4},{6,7},{7,3},{8,9},{9,13},{10,1... | collective-permute-start | bytes 786440 | tf_op jit(solution)/shard_map/ppermute | solution.py:541
  36.7 2.8 %collective-permute-start.14 = (f32[528,128]{1,0:T(8,128)S(1)}, f32[528,128]{1,0:T(8,128)S(1)}, u32[]{:S(2)}, u32[]{:S(2)}) collective-permute-start(f32[528,128]{1,0:T(8,128)S(1)} %collective-permute-done.9.refs_2_.refs_6_), channel_id=1, source_target_pairs={{0,1},{1,0},{2,3},{3,2},{4,5},{5,4},{6,7},{7,6},{8,9},{9,8},{10,11... | collective-permute-start | bytes 811016 | tf_op jit(solution)/shard_map/ppermute | solution.py:495
  36.7 4.2 %collective-permute-start.12 = (f32[528,128]{1,0:T(8,128)S(1)}, f32[528,128]{1,0:T(8,128)S(1)}, u32[]{:S(2)}, u32[]{:S(2)}) collective-permute-start(f32[528,128]{1,0:T(8,128)S(1)} %shard_map.42.own_b), channel_id=1, source_target_pairs={{0,1},{1,0},{2,3},{3,2},{4,5},{5,4},{6,7},{7,6},{8,9},{9,8},{10,11... | collective-permute-start | bytes 811016 | tf_op jit(solution)/shard_map/ppermute | solution.py:495
  39.3 1.6 %collective-permute-start.11 = (f32[512,128]{1,0:T(8,128)S(1)}, f32[512,128]{1,0:T(8,128)S(1)}, u32[]{:S(2)}, u32[]{:S(2)}) collective-permute-start(f32[512,128]{1,0:T(8,128)S(1)} %shard_map.41.own_a), channel_id=1, source_target_pairs={{0,1},{1,0},{2,3},{3,2},{4,5},{5,4},{6,7},{7,6},{8,9},{9,8},{10,11... | collective-permute-start | bytes 786440 | tf_op jit(solution)/shard_map/ppermute | solution.py:495

commit v15 on v12

--- a/solution.py
+++ b/solution.py
@@ -202,16 +202,18 @@
     cols = lax.broadcasted_iota(jnp.int32, (order, order), 1)
     eye = jnp.where(rows == cols, 1.0, 0.0)
     total = eye - start * factor
-    power_halves = halves(total)
     middle = order // 2
-    for step in range(1, ITERS):
-        power = whole(*upper_square(power_halves))
+    square = whole(*upper_square(halves(total)))
+    power = whole(*upper_square(halves(square)))
+    total = total + 0.5 * (square + whole(*upper_square(halves(total + square))) - power)
+    for step in range(2, ITERS):
         power_halves = halves(power)
         top, corner = upper_times(halves(total), power_halves)
         known = total + power
         top, corner = top + known[:middle], corner + known[middle:, middle:]
         if step < ITERS - 1:
             total = whole(top, corner)
+            power = whole(*upper_square(power_halves))
 
     def block(i, j):
         if i < middle // LANE:

time: 42.5 us -> 42.3 us (level)
  no operation moved by 1% of the time
where the time goes in v15:
time: 42.3 us; the launch traced here: 42.2 us
  waiting for transfers between devices  19.5 us (46%)
  starting transfers between devices  13.3 us (31%)
  Pallas kernels  8.08 us (19%)
  other arithmetic  1.17 us (3%)
    pallas_call x8, Pallas kernels, call(): pl.pallas_call(kernel, out_shape=[jax.ShapeDtypeStruct(shape[:2], *(shape...  8.08 us
    ppermute x1, waiting for transfers between devices, per_device(): lax.ppermute(outer, AXES, outward)  7.32 us
    ppermute x1, waiting for transfers between devices, per_device(): direct = lax.ppermute(direct, AXES, outward)  6.85 us
    ppermute x7, starting transfers between devices, swap_cores(): return lax.ppermute(array, 'grad', [(0, 1), (1, 0)])  4.28 us
    ppermute x7, waiting for transfers between devices, swap_cores(): return lax.ppermute(array, 'grad', [(0, 1), (1, 0)])  3.26 us
    ppermute x1, starting transfers between devices, per_device(): lax.ppermute(outer, AXES, outward)  2.74 us
    ppermute x1, starting transfers between devices, per_device(): direct = lax.ppermute(direct, AXES, outward)  2.43 us
    ppermute x2, waiting for transfers between devices, per_device(): lax.ppermute(array, AXES, pairs)  2.05 us
  transfers between devices with their start and end apart: 15, of which 6 were waited for; matrix products, arithmetic and copies ran while one was open for 0% of the time, Pallas kernels for 4%

profile of v15, /device:TPU:0, one launch (start us, length us, event | category | flops | bytes accessed | tf_op | source)
XLA Modules:
  0.0 42.2 jit_solution(4341824907673454325)
XLA Ops:
  0.0 1.2 %select_bitcast_fusion = (bf16[384,512]{1,0:T(8,128)(2,1)S(1)}, bf16[384,512]{1,0:T(8,128)(2,1)S(1)}) fusion(bf16[1,384,512]{2,1,0:T(8,128)(2,1)} %param.4, bf16[1,384,512]{2,1,0:T(8,128)(2,1)} %param.3, pred[]{:T(512)S(6)} %eq.4), kind=kLoop, calls=%fused_computation | loop fusion | flops 393216 | bytes 1572865 | tf_op jit(solution)/shard_map/jit(_where)/select_n | solution.py:529
  1.2 0.5 %shard_map.38 = f32[1040,128]{1,0:T(8,128)S(1)} custom-call(bf16[384,512]{1,0:T(8,128)(2,1)S(1)} %get-tuple-element.27.x_ref), custom_call_target="tpu_custom_call" | custom-call | tf_op jit(solution)/shard_map/pallas_call | solution.py:377
  1.6 0.5 %collective-permute-start = (f32[1040,128]{1,0:T(8,128)S(1)}, f32[1040,128]{1,0:T(8,128)S(1)}, u32[]{:S(2)}, u32[]{:S(2)}) collective-permute-start(f32[1040,128]{1,0:T(8,128)S(1)} %shard_map.38), channel_id=1, source_target_pairs={{0,1},{1,0},{2,3},{3,2},{4,5},{5,4},{6,7},{7,6},{8,9},{9,8},{10,11... | collective-permute-start | bytes 1597448 | tf_op jit(solution)/shard_map/ppermute | solution.py:515
  2.2 0.0 copy-start
  2.2 0.5 %shard_map.37.kept_ref = f32[1040,128]{1,0:T(8,128)S(1)} custom-call(bf16[384,512]{1,0:T(8,128)(2,1)S(1)} %get-tuple-element.28.x_ref), custom_call_target="tpu_custom_call" | custom-call | tf_op jit(solution)/shard_map/pallas_call | solution.py:377
  2.6 1.1 %collective-permute-done.other_ref = f32[1040,128]{1,0:T(8,128)S(1)} collective-permute-done((f32[1040,128]{1,0:T(8,128)S(1)}, f32[1040,128]{1,0:T(8,128)S(1)}, u32[]{:S(2)}, u32[]{:S(2)}) %collective-permute-start) | collective-permute-done | bytes 532512 | tf_op jit(solution)/shard_map/ppermute | solution.py:515
  3.7 0.0 copy-done
  3.7 0.1 shard_map.39
  3.8 2.7 %collective-permute-start.1 = (f32[1040,128]{1,0:T(8,128)S(1)}, f32[1040,128]{1,0:T(8,128)S(1)}, u32[]{:S(2)}, u32[]{:S(2)}) collective-permute-start(f32[1040,128]{1,0:T(8,128)S(1)} %get-tuple-element.16), channel_id=1, source_target_pairs={{0,5},{1,0},{2,3},{3,6},{4,1},{5,4},{6,7},{7,2},{8,9},{9,12},{10,1... | collective-permute-start | bytes 1597448 | tf_op jit(solution)/shard_map/ppermute | solution.py:540
  6.6 0.0 collective-permute-start.2
  6.6 1.5 %collective-permute-start.3 = (f32[1040,128]{1,0:T(8,128)S(1)}, f32[1040,128]{1,0:T(8,128)S(1)}, u32[]{:S(2)}, u32[]{:S(2)}) collective-permute-start(f32[1040,128]{1,0:T(8,128)S(1)} %get-tuple-element.16), channel_id=1, source_target_pairs={{0,3},{1,8},{2,11},{3,0},{4,7},{5,1},{6,2},{7,4},{8,12},{9,10},{10... | collective-permute-start | bytes 1597448 | tf_op jit(solution)/shard_map/ppermute | solution.py:542
  8.0 0.5 %collective-permute-start.4 = (f32[1040,128]{1,0:T(8,128)S(1)}, f32[1040,128]{1,0:T(8,128)S(1)}, u32[]{:S(2)}, u32[]{:S(2)}) collective-permute-start(f32[1040,128]{1,0:T(8,128)S(1)} %get-tuple-element.17), channel_id=1, source_target_pairs={{0,1},{1,0},{2,3},{3,2},{4,5},{5,4},{6,7},{7,6},{8,9},{9,8},{10,11... | collective-permute-start | bytes 1597448 | tf_op jit(solution)/shard_map/ppermute | solution.py:515
  8.5 0.0 collective-permute-start.5
  8.5 1.9 %collective-permute-done.5.refs_5_.refs_1_ = f32[128,512]{1,0:T(8,128)S(1)} collective-permute-done((f32[128,512]{1,0:T(8,128)S(1)}, f32[128,512]{1,0:T(8,128)S(1)}, u32[]{:S(2)}, u32[]{:S(2)}) %collective-permute-start.5) | collective-permute-done | bytes 262176 | tf_op jit(solution)/shard_map/ppermute | solution.py:515
  10.4 7.3 %collective-permute-done.1.refs_0_ = f32[1040,128]{1,0:T(8,128)S(1)} collective-permute-done((f32[1040,128]{1,0:T(8,128)S(1)}, f32[1040,128]{1,0:T(8,128)S(1)}, u32[]{:S(2)}, u32[]{:S(2)}) %collective-permute-start.1) | collective-permute-done | bytes 532512 | tf_op jit(solution)/shard_map/ppermute | solution.py:540
  17.8 0.0 collective-permute-done.2.refs_1_
  17.8 0.0 collective-permute-done.3.refs_2_
  17.8 0.0 collective-permute-done.4.refs_3_
  17.8 4.6 %shard_map.40 = (f32[512,128]{1,0:T(8,128)S(1)}, f32[528,128]{1,0:T(8,128)S(1)}, f32[1040,128]{1,0:T(8,128)S(1)}, f32[1024,128]{1,0:T(8,128)S(1)}) custom-call(f32[1040,128]{1,0:T(8,128)S(1)} %collective-permute-done.1.refs_0_, f32[1040,128]{1,0:T(8,128)S(1)} %collective-permute-done.2.refs_1_, f32[1040,128]{1,0:T(8,128)S(1)} %collective-permute-done.3.refs_2_, ...), custom_call_target="tpu_custom_call" | custom-call | tf_op jit(solution)/shard_map/pallas_call | solution.py:377
  22.4 1.9 %collective-permute-start.8 = (f32[528,128]{1,0:T(8,128)S(1)}, f32[528,128]{1,0:T(8,128)S(1)}, u32[]{:S(2)}, u32[]{:S(2)}) collective-permute-start(f32[528,128]{1,0:T(8,128)S(1)} %get-tuple-element.19.refs_0_), channel_id=1, source_target_pairs={{0,1},{1,0},{2,3},{3,2},{4,5},{5,7},{6,10},{7,6},{8,4},{9,8},{10,1... | collective-permute-start | bytes 811016 | tf_op jit(solution)/shard_map/ppermute | solution.py:560
  24.3 2.4 %collective-permute-start.10 = (f32[1040,128]{1,0:T(8,128)S(1)}, f32[1040,128]{1,0:T(8,128)S(1)}, u32[]{:S(2)}, u32[]{:S(2)}) collective-permute-start(f32[1040,128]{1,0:T(8,128)S(1)} %get-tuple-element.20), channel_id=1, source_target_pairs={{0,4},{1,0},{2,3},{3,7},{4,5},{5,1},{6,2},{7,6},{8,12},{9,8},{10,1... | collective-permute-start | bytes 1597448 | tf_op jit(solution)/shard_map/ppermute | solution.py:559
  26.7 0.0 collective-permute-start.6
  26.7 0.0 collective-permute-done.8.refs_1_
  26.7 0.5 %collective-permute-start.9 = (f32[528,128]{1,0:T(8,128)S(1)}, f32[528,128]{1,0:T(8,128)S(1)}, u32[]{:S(2)}, u32[]{:S(2)}) collective-permute-start(f32[528,128]{1,0:T(8,128)S(1)} %collective-permute-done.8.refs_1_), channel_id=1, source_target_pairs={{0,1},{1,5},{2,6},{3,2},{4,0},{5,4},{6,7},{7,3},{8,9},{9,13},{10,1... | collective-permute-start | bytes 811016 | tf_op jit(solution)/shard_map/ppermute | solution.py:561
  27.2 2.6 %collective-permute-start.13 = (f32[1024,128]{1,0:T(8,128)S(1)}, f32[1024,128]{1,0:T(8,128)S(1)}, u32[]{:S(2)}, u32[]{:S(2)}) collective-permute-start(f32[1024,128]{1,0:T(8,128)S(1)} %get-tuple-element.23.refs_2_), channel_id=1, source_target_pairs={{0,1},{1,0},{2,3},{3,2},{4,5},{5,4},{6,7},{7,6},{8,9},{9,8},{10,11... | collective-permute-start | bytes 1572872 | tf_op jit(solution)/shard_map/ppermute | solution.py:515
  29.8 0.0 collective-permute-done.6.refs_1_
  29.8 0.0 collective-permute-start.7
  29.8 6.8 %collective-permute-done.10.refs_3_.refs_4_ = f32[1040,128]{1,0:T(8,128)S(1)} collective-permute-done((f32[1040,128]{1,0:T(8,128)S(1)}, f32[1040,128]{1,0:T(8,128)S(1)}, u32[]{:S(2)}, u32[]{:S(2)}) %collective-permute-start.10) | collective-permute-done | bytes 532512 | tf_op jit(solution)/shard_map/ppermute | solution.py:559
  36.7 0.0 collective-permute-done.9.refs_2_.refs_6_
  36.7 0.1 collective-permute-start.12
  36.8 0.5 %collective-permute-start.14 = (f32[528,128]{1,0:T(8,128)S(1)}, f32[528,128]{1,0:T(8,128)S(1)}, u32[]{:S(2)}, u32[]{:S(2)}) collective-permute-start(f32[528,128]{1,0:T(8,128)S(1)} %collective-permute-done.9.refs_2_.refs_6_), channel_id=1, source_target_pairs={{0,1},{1,0},{2,3},{3,2},{4,5},{5,4},{6,7},{7,6},{8,9},{9,8},{10,11... | collective-permute-start | bytes 811016 | tf_op jit(solution)/shard_map/ppermute | solution.py:515
  37.3 2.0 %collective-permute-done.7.refs_2_.refs_5_ = f32[512,128]{1,0:T(8,128)S(1)} collective-permute-done((f32[512,128]{1,0:T(8,128)S(1)}, f32[512,128]{1,0:T(8,128)S(1)}, u32[]{:S(2)}, u32[]{:S(2)}) %collective-permute-start.7) | collective-permute-done | bytes 262176 | tf_op jit(solution)/shard_map/ppermute | solution.py:561
  39.4 0.1 collective-permute-start.11
  39.4 0.0 collective-permute-done.13.refs_3_
  39.4 0.0 collective-permute-done.12.other_b
  39.5 0.0 collective-permute-done.14.refs_7_
  39.5 1.2 %shard_map.43 = (f32[128,512]{1,0:T(8,128)S(1)}, bf16[512,512]{1,0:T(8,128)(2,1)S(1)}, bf16[512,512]{1,0:T(8,128)(2,1)S(1)}) custom-call(f32[512,128]{1,0:T(8,128)S(1)} %shard_map.41.own_a, f32[528,128]{1,0:T(8,128)S(1)} %shard_map.42.own_b, f32[528,128]{1,0:T(8,128)S(1)} %collective-permute-done.12.other_b, f32[128,512]{1,0:T(8,128)S(1)} %bitcast.9, ...), custom_call_target="tpu_custom_call" | custom-call | tf_op jit(solution)/shard_map/pallas_call | solution.py:377
  40.7 0.3 collective-permute-done.11.other_a
  41.0 1.2 %shard_map.44 = f32[128,512]{1,0:T(8,128)} custom-call(f32[512,128]{1,0:T(8,128)S(1)} %collective-permute-done.11.other_a, f32[528,128]{1,0:T(8,128)S(1)} %collective-permute-done.12.other_b, f32[128,512]{1,0:T(8,128)S(1)} %get-tuple-element.24.first_left, bf16[512,512]{1,0:T(8,128)(2,1)S(1)} %get-tuple-element.25.high_ref, ...), custom_call_target="tpu_custom_call" | custom-call | tf_op jit(solution)/shard_map/pallas_call | solution.py:377
  (2 shorter events, 0.0 us)
Async XLA Ops:
  1.6 2.1 %collective-permute-start = (f32[1040,128]{1,0:T(8,128)S(1)}, f32[1040,128]{1,0:T(8,128)S(1)}, u32[]{:S(2)}, u32[]{:S(2)}) collective-permute-start(f32[1040,128]{1,0:T(8,128)S(1)} %shard_map.38), channel_id=1, source_target_pairs={{0,1},{1,0},{2,3},{3,2},{4,5},{5,4},{6,7},{7,6},{8,9},{9,8},{10,11... | collective-permute-start | bytes 1597448 | tf_op jit(solution)/shard_map/ppermute | solution.py:515
  2.2 1.6 %copy-start = (f32[1,128,512]{2,1,0:T(8,128)S(1)}, f32[1,128,512]{2,1,0:T(8,128)}, u32[]{:S(2)}) copy-start(f32[1,128,512]{2,1,0:T(8,128)} %param.5) | copy-start | bytes 786436
  3.8 13.9 %collective-permute-start.1 = (f32[1040,128]{1,0:T(8,128)S(1)}, f32[1040,128]{1,0:T(8,128)S(1)}, u32[]{:S(2)}, u32[]{:S(2)}) collective-permute-start(f32[1040,128]{1,0:T(8,128)S(1)} %get-tuple-element.16), channel_id=1, source_target_pairs={{0,5},{1,0},{2,3},{3,6},{4,1},{5,4},{6,7},{7,2},{8,9},{9,12},{10,1... | collective-permute-start | bytes 1597448 | tf_op jit(solution)/shard_map/ppermute | solution.py:540
  6.6 11.2 %collective-permute-start.2 = (f32[1040,128]{1,0:T(8,128)S(1)}, f32[1040,128]{1,0:T(8,128)S(1)}, u32[]{:S(2)}, u32[]{:S(2)}) collective-permute-start(f32[1040,128]{1,0:T(8,128)S(1)} %get-tuple-element.17), channel_id=1, source_target_pairs={{0,1},{1,0},{2,3},{3,2},{4,20},{5,8},{6,11},{7,23},{8,5},{9,25},{1... | collective-permute-start | bytes 1597448 | tf_op jit(solution)/shard_map/ppermute | solution.py:541
  6.6 11.2 %collective-permute-start.3 = (f32[1040,128]{1,0:T(8,128)S(1)}, f32[1040,128]{1,0:T(8,128)S(1)}, u32[]{:S(2)}, u32[]{:S(2)}) collective-permute-start(f32[1040,128]{1,0:T(8,128)S(1)} %get-tuple-element.16), channel_id=1, source_target_pairs={{0,3},{1,8},{2,11},{3,0},{4,7},{5,1},{6,2},{7,4},{8,12},{9,10},{10... | collective-permute-start | bytes 1597448 | tf_op jit(solution)/shard_map/ppermute | solution.py:542
  8.0 9.7 %collective-permute-start.4 = (f32[1040,128]{1,0:T(8,128)S(1)}, f32[1040,128]{1,0:T(8,128)S(1)}, u32[]{:S(2)}, u32[]{:S(2)}) collective-permute-start(f32[1040,128]{1,0:T(8,128)S(1)} %get-tuple-element.17), channel_id=1, source_target_pairs={{0,1},{1,0},{2,3},{3,2},{4,5},{5,4},{6,7},{7,6},{8,9},{9,8},{10,11... | collective-permute-start | bytes 1597448 | tf_op jit(solution)/shard_map/ppermute | solution.py:515
  8.5 1.9 %collective-permute-start.5 = (f32[128,512]{1,0:T(8,128)S(1)}, f32[128,512]{1,0:T(8,128)S(1)}, u32[]{:S(2)}, u32[]{:S(2)}) collective-permute-start(f32[128,512]{1,0:T(8,128)S(1)} %bitcast.7), channel_id=1, source_target_pairs={{0,1},{1,0},{2,3},{3,2},{4,5},{5,4},{6,7},{7,6},{8,9},{9,8},{10,11... | collective-permute-start | bytes 786440 | tf_op jit(solution)/shard_map/ppermute | solution.py:515
  22.4 4.3 %collective-permute-start.8 = (f32[528,128]{1,0:T(8,128)S(1)}, f32[528,128]{1,0:T(8,128)S(1)}, u32[]{:S(2)}, u32[]{:S(2)}) collective-permute-start(f32[528,128]{1,0:T(8,128)S(1)} %get-tuple-element.19.refs_0_), channel_id=1, source_target_pairs={{0,1},{1,0},{2,3},{3,2},{4,5},{5,7},{6,10},{7,6},{8,4},{9,8},{10,1... | collective-permute-start | bytes 811016 | tf_op jit(solution)/shard_map/ppermute | solution.py:560
  24.3 12.4 %collective-permute-start.10 = (f32[1040,128]{1,0:T(8,128)S(1)}, f32[1040,128]{1,0:T(8,128)S(1)}, u32[]{:S(2)}, u32[]{:S(2)}) collective-permute-start(f32[1040,128]{1,0:T(8,128)S(1)} %get-tuple-element.20), channel_id=1, source_target_pairs={{0,4},{1,0},{2,3},{3,7},{4,5},{5,1},{6,2},{7,6},{8,12},{9,8},{10,1... | collective-permute-start | bytes 1597448 | tf_op jit(solution)/shard_map/ppermute | solution.py:559
  26.7 3.1 %collective-permute-start.6 = (f32[512,128]{1,0:T(8,128)S(1)}, f32[512,128]{1,0:T(8,128)S(1)}, u32[]{:S(2)}, u32[]{:S(2)}) collective-permute-start(f32[512,128]{1,0:T(8,128)S(1)} %get-tuple-element.18.refs_0_), channel_id=1, source_target_pairs={{0,1},{1,0},{2,3},{3,2},{4,5},{5,7},{6,10},{7,6},{8,4},{9,8},{10,1... | collective-permute-start | bytes 786440 | tf_op jit(solution)/shard_map/ppermute | solution.py:558
  26.7 10.0 %collective-permute-start.9 = (f32[528,128]{1,0:T(8,128)S(1)}, f32[528,128]{1,0:T(8,128)S(1)}, u32[]{:S(2)}, u32[]{:S(2)}) collective-permute-start(f32[528,128]{1,0:T(8,128)S(1)} %collective-permute-done.8.refs_1_), channel_id=1, source_target_pairs={{0,1},{1,5},{2,6},{3,2},{4,0},{5,4},{6,7},{7,3},{8,9},{9,13},{10,1... | collective-permute-start | bytes 811016 | tf_op jit(solution)/shard_map/ppermute | solution.py:561
  27.2 12.2 %collective-permute-start.13 = (f32[1024,128]{1,0:T(8,128)S(1)}, f32[1024,128]{1,0:T(8,128)S(1)}, u32[]{:S(2)}, u32[]{:S(2)}) collective-permute-start(f32[1024,128]{1,0:T(8,128)S(1)} %get-tuple-element.23.refs_2_), channel_id=1, source_target_pairs={{0,1},{1,0},{2,3},{3,2},{4,5},{5,4},{6,7},{7,6},{8,9},{9,8},{10,11... | collective-permute-start | bytes 1572872 | tf_op jit(solution)/shard_map/ppermute | solution.py:515
  29.8 9.5 %collective-permute-start.7 = (f32[512,128]{1,0:T(8,128)S(1)}, f32[512,128]{1,0:T(8,128)S(1)}, u32[]{:S(2)}, u32[]{:S(2)}) collective-permute-start(f32[512,128]{1,0:T(8,128)S(1)} %collective-permute-done.6.refs_1_), channel_id=1, source_target_pairs={{0,1},{1,5},{2,6},{3,2},{4,0},{5,4},{6,7},{7,3},{8,9},{9,13},{10,1... | collective-permute-start | bytes 786440 | tf_op jit(solution)/shard_map/ppermute | solution.py:561
  36.7 2.7 %collective-permute-start.12 = (f32[528,128]{1,0:T(8,128)S(1)}, f32[528,128]{1,0:T(8,128)S(1)}, u32[]{:S(2)}, u32[]{:S(2)}) collective-permute-start(f32[528,128]{1,0:T(8,128)S(1)} %shard_map.42.own_b), channel_id=1, source_target_pairs={{0,1},{1,0},{2,3},{3,2},{4,5},{5,4},{6,7},{7,6},{8,9},{9,8},{10,11... | collective-permute-start | bytes 811016 | tf_op jit(solution)/shard_map/ppermute | solution.py:515
  36.8 2.7 %collective-permute-start.14 = (f32[528,128]{1,0:T(8,128)S(1)}, f32[528,128]{1,0:T(8,128)S(1)}, u32[]{:S(2)}, u32[]{:S(2)}) collective-permute-start(f32[528,128]{1,0:T(8,128)S(1)} %collective-permute-done.9.refs_2_.refs_6_), channel_id=1, source_target_pairs={{0,1},{1,0},{2,3},{3,2},{4,5},{5,4},{6,7},{7,6},{8,9},{9,8},{10,11... | collective-permute-start | bytes 811016 | tf_op jit(solution)/shard_map/ppermute | solution.py:515
  39.4 1.6 %collective-permute-start.11 = (f32[512,128]{1,0:T(8,128)S(1)}, f32[512,128]{1,0:T(8,128)S(1)}, u32[]{:S(2)}, u32[]{:S(2)}) collective-permute-start(f32[512,128]{1,0:T(8,128)S(1)} %shard_map.41.own_a), channel_id=1, source_target_pairs={{0,1},{1,0},{2,3},{3,2},{4,5},{5,4},{6,7},{7,6},{8,9},{9,8},{10,11... | collective-permute-start | bytes 786440 | tf_op jit(solution)/shard_map/ppermute | solution.py:515
